TPU v7x, 32 devices: a whole 2x2x4 slice. The times are simulated.
32 devices in a mesh: ctx: 8 (over y, x, core), head: 4 (over z).
Axes of the slice: x: 2, y: 2, z: 4, core: 2. Of those that a mesh axis runs over, the one named last changes fastest.
Arguments:
- queries: bfloat16 [4096, 2048], P(('ctx', 'head')), may hold values from -16 to 16
- keys: bfloat16 [4096, 512], P(('ctx', 'head')), may hold values from -4 to 4
- values: bfloat16 [4096, 512], P(('ctx', 'head')), may hold values from -6 to 6
- d_out: bfloat16 [4096, 2048], P(('ctx', 'head')), may hold values from -6 to 6
- lengths: int32 [32], replicated, may hold values from 1 to 2048, 4096 in all
Outputs:
- attn_out: bfloat16 [4096, 2048], P(('ctx', 'head'))
- grad_queries: bfloat16 [4096, 2048], P(('ctx', 'head'))
- grad_keys: bfloat16 [4096, 512], P(('ctx', 'head'))
- grad_values: bfloat16 [4096, 512], P(('ctx', 'head'))
Inputs may be any that keep to these rules, and one draw needn't show every extreme that they name: The 32 lengths sum to 4096; the longest is exactly 2048.
All inputs are finite; a program needn't handle non-finite values.
Results may differ from a plain program's by a relative error of at most 0.035.
Values may be sent and summed in bfloat16 or wider, within the bound.
No kernel may reach another device: no remote copies, remote signals or barrier semaphores. Data moves between devices by JAX's collectives and lax.ppermute only.
A program may use at most 128 MiB of HBM per device.

v0:
```python
import jax
import jax.numpy as jnp
from jax import lax
from jax.sharding import PartitionSpec as P

QH = 16
KVH = 4
HD = 128
REACH = 4


NEG_FILL = -1e30


def shifted(value, axis, steps):
    count = lax.axis_size(axis)
    first, last = (max(0, -steps), min(count, count - steps))
    return lax.ppermute(value, axis, [(source, source + steps) for source in range(first, last)])


def doc_starts(lengths, first, count):
    doc_ends = jnp.cumsum(lengths)
    positions = first + jnp.arange(count, dtype=jnp.int32)
    passed = doc_ends[None, :] <= positions[:, None]
    return jnp.sum(jnp.where(passed, lengths[None, :], 0), axis=1)


def visible_pairs(query_first, key_first, start_rows, block_rows):
    query_pos = query_first + jnp.arange(block_rows, dtype=jnp.int32)
    key_pos = key_first + jnp.arange(block_rows, dtype=jnp.int32)
    mask = (key_pos[None, :] <= query_pos[:, None]) & (key_pos[None, :] >= start_rows[:, None])
    return mask[:, None, None, :]


def block_live(query_first, key_first, tile_starts, tile_first, block_rows):
    lowest = jnp.maximum(query_first, key_first)
    picked = jnp.clip(lowest - tile_first, 0, tile_starts.shape[0] - 1)
    first_start = lax.dynamic_index_in_dim(tile_starts, picked, 0, keepdims=False)
    return (lowest <= query_first + block_rows - 1) & (first_start <= key_first + block_rows - 1)


def shards(queries, keys, values, d_out, lengths):
    heads_dev = lax.axis_size("head")
    tok_dev = queries.shape[0]
    copies = max(1, heads_dev // KVH)
    kv_local = max(1, KVH // heads_dev)
    q_local = QH // heads_dev
    group_size = q_local // kv_local
    scaling = HD ** (-0.5)

    def spread(array_in):
        if copies > 1:
            return jnp.repeat(array_in.reshape(tok_dev, KVH, HD), copies, axis=1).reshape(
                tok_dev, KVH * copies * HD
            )
        return array_in

    q_tile, k_tile, v_tile = (
        lax.all_to_all(queries, "head", split_axis=1, concat_axis=0, tiled=True),
        lax.all_to_all(spread(keys), "head", split_axis=1, concat_axis=0, tiled=True),
        lax.all_to_all(spread(values), "head", split_axis=1, concat_axis=0, tiled=True),
    )
    tile_rows = q_tile.shape[0]
    block_rows = min(1024, tile_rows)
    block_count = tile_rows // block_rows
    ctx_index = lax.axis_index("ctx")
    tile_first = ctx_index * tile_rows
    tile_starts = doc_starts(lengths, tile_first, tile_rows)
    query_blocks = [
        q_tile[number * block_rows : (number + 1) * block_rows].reshape(
            block_rows, kv_local, group_size, HD
        )
        for number in range(block_count)
    ]
    start_blocks = [
        tile_starts[number * block_rows : (number + 1) * block_rows]
        for number in range(block_count)
    ]
    query_firsts = [tile_first + number * block_rows for number in range(block_count)]
    key_pair = jnp.stack([k_tile, v_tile])
    key_tiles = [key_pair]
    moving = key_pair
    for offset in range(1, REACH + 1):
        moving = shifted(moving, "ctx", 1)
        key_tiles.append(moving)

    def split_keys(tile_pair):
        key_list = [
            tile_pair[0, number * block_rows : (number + 1) * block_rows].reshape(
                block_rows, kv_local, HD
            )
            for number in range(block_count)
        ]
        value_list = [
            tile_pair[1, number * block_rows : (number + 1) * block_rows].reshape(
                block_rows, kv_local, HD
            )
            for number in range(block_count)
        ]
        return (key_list, value_list)

    states = [
        (
            jnp.full((block_rows, kv_local, group_size), NEG_FILL, jnp.float32),
            jnp.zeros((block_rows, kv_local, group_size), jnp.float32),
            jnp.zeros((block_rows, kv_local, group_size, HD), jnp.float32),
        )
        for number in range(block_count)
    ]
    for offset in range(REACH + 1):
        key_list, value_list = split_keys(key_tiles[offset])
        key_start = (ctx_index - offset) * tile_rows
        for query_number in range(block_count):
            query_block = query_blocks[query_number]
            query_first = query_firsts[query_number]
            start_rows = start_blocks[query_number]
            for key_number in range(block_count):
                key_block = key_list[key_number]
                value_block = value_list[key_number]
                key_first = key_start + key_number * block_rows

                def forward_block(
                    current,
                    query_block=query_block,
                    query_first=query_first,
                    start_rows=start_rows,
                    key_block=key_block,
                    value_block=value_block,
                    key_first=key_first,
                ):
                    max_old, sum_old, acc_old = current
                    mask = visible_pairs(query_first, key_first, start_rows, block_rows)
                    scores = (
                        jnp.einsum(
                            "qkgd,ckd->qkgc",
                            query_block,
                            key_block,
                            preferred_element_type=jnp.float32,
                        )
                        * scaling
                    )
                    scores = jnp.where(mask, scores, NEG_FILL)
                    max_new = jnp.maximum(max_old, jnp.max(scores, axis=-1))
                    prob_raw = jnp.where(mask, jnp.exp(scores - max_new[..., None]), 0.0)
                    rescale = jnp.exp(max_old - max_new)
                    sum_new = sum_old * rescale + jnp.sum(prob_raw, axis=-1)
                    acc_new = acc_old * rescale[..., None] + jnp.einsum(
                        "qkgc,ckd->qkgd",
                        prob_raw.astype(jnp.bfloat16),
                        value_block,
                        preferred_element_type=jnp.float32,
                    )
                    return (max_new, sum_new, acc_new)

                live = block_live(query_first, key_first, tile_starts, tile_first, block_rows)
                states[query_number] = lax.cond(
                    live, forward_block, lambda unchanged: unchanged, states[query_number]
                )
    out_blocks = [(state[2] / state[1][..., None]).astype(jnp.bfloat16) for state in states]
    lse_blocks = [state[0] + jnp.log(state[1]) for state in states]
    grad_tile = lax.all_to_all(d_out, "head", split_axis=1, concat_axis=0, tiled=True)
    grad_blocks = [
        grad_tile[number * block_rows : (number + 1) * block_rows].reshape(
            block_rows, kv_local, group_size, HD
        )
        for number in range(block_count)
    ]
    delta_blocks = [
        jnp.sum(
            grad_blocks[number].astype(jnp.float32) * out_blocks[number].astype(jnp.float32),
            axis=-1,
        )
        for number in range(block_count)
    ]
    query_totals = [
        jnp.zeros((block_rows, kv_local, group_size, HD), jnp.float32)
        for number in range(block_count)
    ]
    partial_grads = []
    for offset in range(REACH + 1):
        key_list, value_list = split_keys(key_tiles[offset])
        key_start = (ctx_index - offset) * tile_rows
        key_sums = [
            jnp.zeros((block_rows, kv_local, HD), jnp.float32) for number in range(block_count)
        ]
        value_sums = [
            jnp.zeros((block_rows, kv_local, HD), jnp.float32) for number in range(block_count)
        ]
        for query_number in range(block_count):
            query_block = query_blocks[query_number]
            grad_block = grad_blocks[query_number]
            query_first = query_firsts[query_number]
            start_rows = start_blocks[query_number]
            lse_rows = lse_blocks[query_number]
            delta_rows = delta_blocks[query_number]
            for key_number in range(block_count):
                key_block = key_list[key_number]
                value_block = value_list[key_number]
                key_first = key_start + key_number * block_rows

                def backward_block(
                    current,
                    query_block=query_block,
                    grad_block=grad_block,
                    query_first=query_first,
                    start_rows=start_rows,
                    lse_rows=lse_rows,
                    delta_rows=delta_rows,
                    key_block=key_block,
                    value_block=value_block,
                    key_first=key_first,
                ):
                    query_grad, key_grad, value_grad = current
                    mask = visible_pairs(query_first, key_first, start_rows, block_rows)
                    scores = (
                        jnp.einsum(
                            "qkgd,ckd->qkgc",
                            query_block,
                            key_block,
                            preferred_element_type=jnp.float32,
                        )
                        * scaling
                    )
                    prob_raw = jnp.where(mask, jnp.exp(scores - lse_rows[..., None]), 0.0)
                    weights = prob_raw.astype(jnp.bfloat16)
                    value_grad = value_grad + jnp.einsum(
                        "qkgc,qkgd->ckd", weights, grad_block, preferred_element_type=jnp.float32
                    )
                    prob_grad = jnp.einsum(
                        "qkgd,ckd->qkgc",
                        grad_block,
                        value_block,
                        preferred_element_type=jnp.float32,
                    )
                    score_grad = (prob_raw * (prob_grad - delta_rows[..., None]) * scaling).astype(
                        jnp.bfloat16
                    )
                    query_grad = query_grad + jnp.einsum(
                        "qkgc,ckd->qkgd", score_grad, key_block, preferred_element_type=jnp.float32
                    )
                    key_grad = key_grad + jnp.einsum(
                        "qkgc,qkgd->ckd",
                        score_grad,
                        query_block,
                        preferred_element_type=jnp.float32,
                    )
                    return (query_grad, key_grad, value_grad)

                live = block_live(query_first, key_first, tile_starts, tile_first, block_rows)
                current = (query_totals[query_number], key_sums[key_number], value_sums[key_number])
                query_totals[query_number], key_sums[key_number], value_sums[key_number] = lax.cond(
                    live, backward_block, lambda unchanged: unchanged, current
                )
        key_whole = jnp.concatenate(key_sums, axis=0).reshape(tile_rows, kv_local * HD)
        value_whole = jnp.concatenate(value_sums, axis=0).reshape(tile_rows, kv_local * HD)
        partial_grads.append(jnp.stack([key_whole, value_whole]))
    grad_total = partial_grads[REACH]
    for offset in range(REACH - 1, -1, -1):
        grad_total = (
            shifted(grad_total.astype(jnp.bfloat16), "ctx", -1).astype(grad_total.dtype)
            + partial_grads[offset]
        )
    out_tile = jnp.concatenate(out_blocks, axis=0).reshape(tile_rows, q_local * HD)
    query_tile = (
        jnp.concatenate(query_totals, axis=0).reshape(tile_rows, q_local * HD).astype(jnp.bfloat16)
    )
    attn_out, grad_queries = (
        lax.all_to_all(out_tile, "head", split_axis=0, concat_axis=1, tiled=True),
        lax.all_to_all(query_tile, "head", split_axis=0, concat_axis=1, tiled=True),
    )
    token_grads = lax.all_to_all(
        grad_total.astype(jnp.bfloat16), "head", split_axis=1, concat_axis=2, tiled=True
    ).astype(grad_total.dtype)
    if copies > 1:
        token_grads = jnp.sum(token_grads.reshape(2, tok_dev, KVH, copies, HD), axis=3).reshape(
            2, tok_dev, KVH * HD
        )
    token_grads = token_grads.astype(jnp.bfloat16)
    return (attn_out, grad_queries, token_grads[0], token_grads[1])


def solution(mesh):
    return jax.shard_map(
        shards,
        mesh=mesh,
        in_specs=(
            P(("ctx", "head"), None),
            P(("ctx", "head"), None),
            P(("ctx", "head"), None),
            P(("ctx", "head"), None),
            P(),
        ),
        out_specs=(
            P(("ctx", "head"), None),
            P(("ctx", "head"), None),
            P(("ctx", "head"), None),
            P(("ctx", "head"), None),
        ),
        check_vma=False,
    )
```

profile of v0, /device:TPU:6, one launch (start us, length us, event | category | flops | bytes accessed | tf_op | source)
XLA Modules:
  0.0 181.9 jit_solution(12370410441505309113)
XLA Ops:
  2.2 4.9 %all-to-all-start = ((bf16[128,4,128]{2,0,1:T(8,128)(2,1)}), bf16[128,4,128]{2,0,1:T(8,128)(2,1)S(1)}, u32[]{:S(2)}, u32[]{:S(2)}) async-start(bf16[128,4,128]{2,0,1:T(8,128)(2,1)} %copy_bitcast_fusion.5), calls=%async_computation | async-start | bytes 262144 | tf_op jit(solution)/shard_map/all_to_all | solution.py:60
  7.1 1.6 copy_bitcast_fusion.4
  8.7 4.5 %all-to-all-done = bf16[128,4,128]{2,0,1:T(8,128)(2,1)S(1)} async-done(((bf16[128,4,128]{2,0,1:T(8,128)(2,1)}), bf16[128,4,128]{2,0,1:T(8,128)(2,1)S(1)}, u32[]{:S(2)}, u32[]{:S(2)}) %all-to-all-start) | async-done | bytes 131104 | tf_op jit(solution)/shard_map/all_to_all | solution.py:60
  13.2 3.9 %all-to-all-start.2 = ((bf16[128,4,128]{2,0,1:T(8,128)(2,1)}), bf16[128,4,128]{2,0,1:T(8,128)(2,1)}, u32[]{:S(2)}, u32[]{:S(2)}) async-start(bf16[128,4,128]{2,0,1:T(8,128)(2,1)} %copy_bitcast_fusion.4), calls=%async_computation.2 | async-start | bytes 262144 | tf_op jit(solution)/shard_map/all_to_all | solution.py:61
  17.1 1.9 %copy.345 = bf16[16,4,8,512]{3,2,0,1:T(8,128)(2,1)} copy(bf16[16,4,8,512]{3,2,1,0:T(8,128)(2,1)} %bitcast.941) | data formatting | bytes 1048576 | tf_op jit(solution)/shard_map/all_to_all | solution.py:59
  19.0 4.1 %all-to-all-done.2 = bf16[128,4,128]{2,0,1:T(8,128)(2,1)} async-done(((bf16[128,4,128]{2,0,1:T(8,128)(2,1)}), bf16[128,4,128]{2,0,1:T(8,128)(2,1)}, u32[]{:S(2)}, u32[]{:S(2)}) %all-to-all-start.2) | async-done | bytes 131104 | tf_op jit(solution)/shard_map/all_to_all | solution.py:61
  23.1 3.5 %all-to-all-start.1 = ((bf16[128,4,512]{2,0,1:T(8,128)(2,1)}), bf16[128,4,512]{2,0,1:T(8,128)(2,1)S(1)}, u32[]{:S(2)}, u32[]{:S(2)}) async-start(bf16[128,4,512]{2,0,1:T(8,128)(2,1)} %bitcast.918), calls=%async_computation.1 | async-start | bytes 1048576 | tf_op jit(solution)/shard_map/all_to_all | solution.py:59
  27.5 1.9 %collective-permute-start = (bf16[2,512,128]{2,1,0:T(8,128)(2,1)S(1)}, bf16[2,512,128]{2,1,0:T(8,128)(2,1)S(1)}, u32[]{:S(2)}, u32[]{:S(2)}) collective-permute-start(bf16[2,512,128]{2,1,0:T(8,128)(2,1)S(1)} %pad_maximum_fusion), channel_id=1, source_target_pairs={{0,4},{4,8},{8,12},{12,16},{16,20},{20,24},{24,28},{1,5},{5,9},{9,... | collective-permute-start | bytes 786440 | tf_op jit(solution)/shard_map/ppermute | solution.py:18
  29.4 5.8 %collective-permute-done = bf16[2,512,128]{2,1,0:T(8,128)(2,1)S(1)} collective-permute-done((bf16[2,512,128]{2,1,0:T(8,128)(2,1)S(1)}, bf16[2,512,128]{2,1,0:T(8,128)(2,1)S(1)}, u32[]{:S(2)}, u32[]{:S(2)}) %collective-permute-start) | collective-permute-done | bytes 262176 | tf_op jit(solution)/shard_map/ppermute | solution.py:18
  35.2 1.9 %collective-permute-start.1 = (bf16[2,512,128]{2,1,0:T(8,128)(2,1)S(1)}, bf16[2,512,128]{2,1,0:T(8,128)(2,1)S(1)}, u32[]{:S(2)}, u32[]{:S(2)}) collective-permute-start(bf16[2,512,128]{2,1,0:T(8,128)(2,1)S(1)} %collective-permute-done), channel_id=1, source_target_pairs={{0,4},{4,8},{8,12},{12,16},{16,20},{20,24},{24,28},{1,5},{5,9},{9,... | collective-permute-start | bytes 786440 | tf_op jit(solution)/shard_map/ppermute | solution.py:18
  38.1 1.9 %copy.344 = bf16[16,4,8,512]{3,2,0,1:T(8,128)(2,1)} copy(bf16[16,4,8,512]{3,2,1,0:T(8,128)(2,1)} %bitcast.942) | data formatting | bytes 1048576 | tf_op jit(solution)/shard_map/all_to_all | solution.py:161
  40.0 5.1 %all-to-all-start.4 = ((bf16[128,4,512]{2,0,1:T(8,128)(2,1)}), bf16[128,4,512]{2,0,1:T(8,128)(2,1)S(1)}, u32[]{:S(2)}, u32[]{:S(2)}) async-start(bf16[128,4,512]{2,0,1:T(8,128)(2,1)} %bitcast.917), calls=%async_computation.4 | async-start | bytes 1048576 | tf_op jit(solution)/shard_map/all_to_all | solution.py:161
  45.1 1.9 %collective-permute-start.2 = (bf16[2,512,128]{2,1,0:T(8,128)(2,1)S(1)}, bf16[2,512,128]{2,1,0:T(8,128)(2,1)S(1)}, u32[]{:S(2)}, u32[]{:S(2)}) collective-permute-start(bf16[2,512,128]{2,1,0:T(8,128)(2,1)S(1)} %collective-permute-done.1), channel_id=1, source_target_pairs={{0,4},{4,8},{8,12},{12,16},{16,20},{20,24},{24,28},{1,5},{5,9},{9,... | collective-permute-start | bytes 786440 | tf_op jit(solution)/shard_map/ppermute | solution.py:18
  51.6 1.3 collective-permute-done.2
  52.8 1.9 %collective-permute-start.3 = (bf16[2,512,128]{2,1,0:T(8,128)(2,1)S(1)}, bf16[2,512,128]{2,1,0:T(8,128)(2,1)S(1)}, u32[]{:S(2)}, u32[]{:S(2)}) collective-permute-start(bf16[2,512,128]{2,1,0:T(8,128)(2,1)S(1)} %collective-permute-done.2), channel_id=1, source_target_pairs={{0,4},{4,8},{8,12},{12,16},{16,20},{20,24},{24,28},{1,5},{5,9},{9,... | collective-permute-start | bytes 786440 | tf_op jit(solution)/shard_map/ppermute | solution.py:18
  55.5 4.7 %conditional.10 = (f32[512,1,4]{0,2,1:T(4,128)S(1)}, f32[512,1,4]{0,2,1:T(4,128)S(1)}, f32[512,1,4,128]{3,0,2,1:T(8,128)S(1)}) conditional(s32[]{:T(128)} %convert_element_type.120, () %tuple.100, (s32[]{:T(128)}, s32[512]{0:T(512)S(1)}, bf16[512,1,128]{2,0,1:T(8,128)(2,1)S(1)}, bf16[512,1,4,128]{3,2,0,1:T(4,128)(2,1)S(1)}, ...), branch_computations={%region_2.3_spmd, %region_3.6_spmd} | conditional | flops 551561728 | bytes 15570972 | solution.py:156
  56.7 1.0 fusion.2
  57.7 2.4 %fusion.13 = f32[512,1,4,128]{3,0,2,1:T(8,128)S(1)} fusion(f32[512,512,4]{1,0,2:T(8,128)S(1)} %get-tuple-element.790, f32[512,4]{0,1:T(4,128)S(1)} %get-tuple-element.788, pred[512,512]{0,1:T(8,128)(4,1)S(1)} %compare_and_fusion, f32[512,4]{0,1:T(4,128)S(1)} %get-tuple-element.787, bf16[512,1,128]{2,0,1:T(8,128)(2,1)} %get-tuple-element.222), kind=kOutput, calls=%fused_computation.10 | convolution fusion | flops 273940480 | bytes 5652480 | tf_op jit(solution)/shard_map/cond/branch_1_fun/qkgc,ckd->qkgd/dot_general | solution.py:147
  60.2 4.0 %conditional.11 = ((f32[512,1,4]{0,2,1:T(4,128)S(1)}, f32[512,1,4]{0,2,1:T(4,128)S(1)}, f32[512,1,4,128]{3,0,2,1:T(8,128)S(1)})) conditional(s32[]{:T(128)} %convert_element_type.119, (f32[512,1,4]{0,2,1:T(4,128)S(1)}, f32[512,1,4]{0,2,1:T(4,128)S(1)}, f32[512,1,4,128]{3,0,2,1:T(8,128)S(1)}) %conditional.10, (s32[]{:T(128)}, s32[]{:T(128)}, ...), branch_computations={%region_6.7_spmd, %region_7.10_spmd} | conditional | flops 551820288 | bytes 16656424 | solution.py:156
  61.4 1.7 fusion.35
  63.1 1.0 fusion.27
  66.9 2.3 %multiply_reduce_fusion = (f32[512,4]{1,0:T(8,128)S(1)}, bf16[512,1,4,128]{3,2,0,1:T(4,128)(2,1)}) fusion(bf16[512,1,4,128]{3,2,0,1:T(4,128)(2,1)S(1)} %reshape.1005, f32[512,1,4,128]{3,2,0,1:T(4,128)S(1)} %get-tuple-element.744, f32[512,4]{1,0:T(8,128)S(1)} %copy.168), kind=kLoop, calls=%fused_computation.310 | loop fusion | flops 1570816 | bytes 2113536 | tf_op jit(solution)/shard_map/reduce_sum | solution.py:169
  69.2 9.1 %conditional.15 = (f32[512,1,4,128]{3,0,2,1:T(8,128)S(1)}, f32[1,512,128]{2,1,0:T(8,128)S(1)}, f32[1,512,128]{2,1,0:T(8,128)S(1)}) conditional(s32[]{:T(128)} %convert_element_type.120, () %tuple.106, (s32[]{:T(128)}, s32[512]{0:T(512)S(1)}, bf16[512,1,128]{2,0,1:T(8,128)(2,1)S(1)}, bf16[512,1,4,128]{3,2,0,1:T(4,128)(2,1)S(1)}, ...), branch_computations={%region_23.24_spmd, %region_24.25_spmd} | conditional | flops 1354498560 | bytes 23771164 | solution.py:251
  73.3 0.9 fusion.106
  74.3 2.6 %fusion.92 = bf16[512,1,4,512]{0,3,2,1:T(8,128)(2,1)S(1)} fusion(f32[512,512,4]{1,0,2:T(8,128)S(1)} %fusion.115, f32[512,4]{0,1:T(4,128)S(1)} %bitcast.952, f32[512,4]{0,1:T(4,128)S(1)} %bitcast.958, pred[512,512]{0,1:T(8,128)(4,1)S(1)} %compare_and_fusion.4, bf16[512,1,4,128]{3,2,0,1:T(4,128)(2,1)S(1)} %get-tuple-element.695, ...), kind=kOutput, calls=%fused_computation.102 | convolution fusion | flops 275775488 | bytes 7225344 | tf_op jit(solution)/shard_map/cond/branch_1_fun/qkgd,ckd->qkgc/dot_general | solution.py:229
  79.2 6.7 %conditional.16 = (f32[512,1,4,128]{3,0,2,1:T(8,128)S(1)}, f32[1,512,128]{2,1,0:T(8,128)}, f32[1,512,128]{2,1,0:T(8,128)S(1)}) conditional(s32[]{:T(128)} %convert_element_type.119, f32[512,1,4,128]{3,0,2,1:T(8,128)S(1)} %get-tuple-element.356, (s32[]{:T(128)}, s32[]{:T(128)}, s32[512]{0:T(512)S(1)}, bf16[512,1,128]{2,0,1:T(8,128)(2,1)S(1)}, ...), branch_computations={%region_25.26_spmd, %region_26.27_spmd} | conditional | flops 1354761216 | bytes 25413748 | solution.py:251
  81.8 1.7 fusion.127
  83.5 1.4 fusion.147
  87.7 7.4 %conditional.19 = (f32[512,1,4,128]{3,0,2,1:T(8,128)S(1)}, bf16[1,512,128]{2,0,1:T(2,128)(2,1)S(1)}, bf16[1,512,128]{2,0,1:T(2,128)(2,1)S(1)}) conditional(s32[]{:T(128)} %convert_element_type.116, f32[512,1,4,128]{3,0,2,1:T(8,128)S(1)} %get-tuple-element.359, (s32[]{:T(128)}, s32[]{:T(128)}, s32[512]{0:T(512)S(1)}, ...), branch_computations={%region_31.32_spmd, %region_32.33_spmd} | conditional | flops 1354892288 | bytes 25118780 | solution.py:251
  95.1 1.3 pad_maximum_fusion.1
  96.4 35.6 %collective-permute-start.4 = (bf16[2,512,128]{2,0,1:T(2,128)(2,1)}, bf16[2,512,128]{2,0,1:T(2,128)(2,1)}, u32[]{:S(2)}, u32[]{:S(2)}) collective-permute-start(bf16[2,512,128]{2,0,1:T(2,128)(2,1)} %pad_maximum_fusion.1), channel_id=1, source_target_pairs={{4,0},{8,4},{12,8},{16,12},{20,16},{24,20},{28,24},{5,1},{9,5},{13... | collective-permute-start | bytes 786440 | tf_op jit(solution)/shard_map/ppermute | solution.py:18
  132.0 1.0 all_to_all.94
  133.0 3.6 %all-to-all-start.3 = ((bf16[4,128,512]{2,1,0:T(8,128)(2,1)}), bf16[4,128,512]{2,1,0:T(8,128)(2,1)S(1)}, u32[]{:S(2)}, u32[]{:S(2)}) async-start(bf16[4,128,512]{2,1,0:T(8,128)(2,1)} %all_to_all.94), calls=%async_computation.3 | async-start | bytes 1048576 | tf_op jit(solution)/shard_map/all_to_all | solution.py:268
  136.7 1.7 fusion.313
  138.4 3.3 %collective-permute-start.5 = (bf16[2,512,128]{2,0,1:T(2,128)(2,1)S(1)}, bf16[2,512,128]{2,0,1:T(2,128)(2,1)S(1)}, u32[]{:S(2)}, u32[]{:S(2)}) collective-permute-start(bf16[2,512,128]{2,0,1:T(2,128)(2,1)S(1)} %fusion.313), channel_id=1, source_target_pairs={{4,0},{8,4},{12,8},{16,12},{20,16},{24,20},{28,24},{5,1},{9,5},{13... | collective-permute-start | bytes 786440 | tf_op jit(solution)/shard_map/ppermute | solution.py:18
  141.7 3.9 %collective-permute-done.5 = bf16[2,512,128]{2,0,1:T(2,128)(2,1)S(1)} collective-permute-done((bf16[2,512,128]{2,0,1:T(2,128)(2,1)S(1)}, bf16[2,512,128]{2,0,1:T(2,128)(2,1)S(1)}, u32[]{:S(2)}, u32[]{:S(2)}) %collective-permute-start.5) | collective-permute-done | bytes 262176 | tf_op jit(solution)/shard_map/ppermute | solution.py:18
  146.2 3.8 %collective-permute-start.6 = (bf16[2,512,128]{2,0,1:T(2,128)(2,1)S(1)}, bf16[2,512,128]{2,0,1:T(2,128)(2,1)S(1)}, u32[]{:S(2)}, u32[]{:S(2)}) collective-permute-start(bf16[2,512,128]{2,0,1:T(2,128)(2,1)S(1)} %fusion.314), channel_id=1, source_target_pairs={{4,0},{8,4},{12,8},{16,12},{20,16},{24,20},{28,24},{5,1},{9,5},{13... | collective-permute-start | bytes 786440 | tf_op jit(solution)/shard_map/ppermute | solution.py:18
  150.5 1.0 convert_element_type.125
  151.5 3.7 %all-to-all-start.5 = ((bf16[4,128,512]{2,1,0:T(8,128)(2,1)}), bf16[4,128,512]{2,1,0:T(8,128)(2,1)S(1)}, u32[]{:S(2)}, u32[]{:S(2)}) async-start(bf16[4,128,512]{2,1,0:T(8,128)(2,1)} %convert_element_type.125), calls=%async_computation.5 | async-start | bytes 1048576 | tf_op jit(solution)/shard_map/all_to_all | solution.py:269
  155.2 1.6 fusion.315
  156.7 2.8 %collective-permute-start.7 = (bf16[2,512,128]{2,0,1:T(2,128)(2,1)S(1)}, bf16[2,512,128]{2,0,1:T(2,128)(2,1)S(1)}, u32[]{:S(2)}, u32[]{:S(2)}) collective-permute-start(bf16[2,512,128]{2,0,1:T(2,128)(2,1)S(1)} %fusion.315), channel_id=1, source_target_pairs={{4,0},{8,4},{12,8},{16,12},{20,16},{24,20},{28,24},{5,1},{9,5},{13... | collective-permute-start | bytes 786440 | tf_op jit(solution)/shard_map/ppermute | solution.py:18
  159.5 3.9 %collective-permute-done.7 = bf16[2,512,128]{2,0,1:T(2,128)(2,1)S(1)} collective-permute-done((bf16[2,512,128]{2,0,1:T(2,128)(2,1)S(1)}, bf16[2,512,128]{2,0,1:T(2,128)(2,1)S(1)}, u32[]{:S(2)}, u32[]{:S(2)}) %collective-permute-start.7) | collective-permute-done | bytes 262176 | tf_op jit(solution)/shard_map/ppermute | solution.py:18
  163.4 1.3 fusion.316
  164.7 3.8 %all-to-all-done.5 = bf16[4,128,512]{2,1,0:T(8,128)(2,1)S(1)} async-done(((bf16[4,128,512]{2,1,0:T(8,128)(2,1)}), bf16[4,128,512]{2,1,0:T(8,128)(2,1)S(1)}, u32[]{:S(2)}, u32[]{:S(2)}) %all-to-all-start.5) | async-done | bytes 524320 | tf_op jit(solution)/shard_map/all_to_all | solution.py:269
  168.5 3.4 %all-to-all-start.6 = ((bf16[2,512,128]{2,0,1:T(2,128)(2,1)}), bf16[2,512,128]{2,0,1:T(2,128)(2,1)S(1)}, u32[]{:S(2)}, u32[]{:S(2)}) async-start(bf16[2,512,128]{2,0,1:T(2,128)(2,1)} %fusion.316), calls=%async_computation.6 | async-start | bytes 524288 | tf_op jit(solution)/shard_map/all_to_all | solution.py:271
  172.2 1.0 copy.201
  173.4 1.0 copy.202
  174.5 5.6 %all-to-all-done.6 = bf16[2,512,128]{2,0,1:T(2,128)(2,1)S(1)} async-done(((bf16[2,512,128]{2,0,1:T(2,128)(2,1)}), bf16[2,512,128]{2,0,1:T(2,128)(2,1)S(1)}, u32[]{:S(2)}, u32[]{:S(2)}) %all-to-all-start.6) | async-done | bytes 262176 | tf_op jit(solution)/shard_map/all_to_all | solution.py:271
  (111 shorter events, 23.4 us)
Async XLA Ops:
  0.6 0.9 copy-start
  0.6 44.4 %copy-start.25 = (s32[32]{0:T(128)S(1)}, s32[32]{0:T(128)}, u32[]{:S(2)}) copy-start(s32[32]{0:T(128)} %param.29) | copy-start | bytes 388
  2.2 10.9 %all-to-all-start = ((bf16[128,4,128]{2,0,1:T(8,128)(2,1)}), bf16[128,4,128]{2,0,1:T(8,128)(2,1)S(1)}, u32[]{:S(2)}, u32[]{:S(2)}) async-start(bf16[128,4,128]{2,0,1:T(8,128)(2,1)} %copy_bitcast_fusion.5), calls=%async_computation | async-start | bytes 262144 | tf_op jit(solution)/shard_map/all_to_all | solution.py:60
  13.2 9.9 %all-to-all-start.2 = ((bf16[128,4,128]{2,0,1:T(8,128)(2,1)}), bf16[128,4,128]{2,0,1:T(8,128)(2,1)}, u32[]{:S(2)}, u32[]{:S(2)}) async-start(bf16[128,4,128]{2,0,1:T(8,128)(2,1)} %copy_bitcast_fusion.4), calls=%async_computation.2 | async-start | bytes 262144 | tf_op jit(solution)/shard_map/all_to_all | solution.py:61
  23.1 16.9 %all-to-all-start.1 = ((bf16[128,4,512]{2,0,1:T(8,128)(2,1)}), bf16[128,4,512]{2,0,1:T(8,128)(2,1)S(1)}, u32[]{:S(2)}, u32[]{:S(2)}) async-start(bf16[128,4,512]{2,0,1:T(8,128)(2,1)} %bitcast.918), calls=%async_computation.1 | async-start | bytes 1048576 | tf_op jit(solution)/shard_map/all_to_all | solution.py:59
  27.5 7.7 %collective-permute-start = (bf16[2,512,128]{2,1,0:T(8,128)(2,1)S(1)}, bf16[2,512,128]{2,1,0:T(8,128)(2,1)S(1)}, u32[]{:S(2)}, u32[]{:S(2)}) collective-permute-start(bf16[2,512,128]{2,1,0:T(8,128)(2,1)S(1)} %pad_maximum_fusion), channel_id=1, source_target_pairs={{0,4},{4,8},{8,12},{12,16},{16,20},{20,24},{24,28},{1,5},{5,9},{9,... | collective-permute-start | bytes 786440 | tf_op jit(solution)/shard_map/ppermute | solution.py:18
  35.2 9.9 %collective-permute-start.1 = (bf16[2,512,128]{2,1,0:T(8,128)(2,1)S(1)}, bf16[2,512,128]{2,1,0:T(8,128)(2,1)S(1)}, u32[]{:S(2)}, u32[]{:S(2)}) collective-permute-start(bf16[2,512,128]{2,1,0:T(8,128)(2,1)S(1)} %collective-permute-done), channel_id=1, source_target_pairs={{0,4},{4,8},{8,12},{12,16},{16,20},{20,24},{24,28},{1,5},{5,9},{9,... | collective-permute-start | bytes 786440 | tf_op jit(solution)/shard_map/ppermute | solution.py:18
  40.0 15.3 %all-to-all-start.4 = ((bf16[128,4,512]{2,0,1:T(8,128)(2,1)}), bf16[128,4,512]{2,0,1:T(8,128)(2,1)S(1)}, u32[]{:S(2)}, u32[]{:S(2)}) async-start(bf16[128,4,512]{2,0,1:T(8,128)(2,1)} %bitcast.917), calls=%async_computation.4 | async-start | bytes 1048576 | tf_op jit(solution)/shard_map/all_to_all | solution.py:161
  45.1 7.7 %collective-permute-start.2 = (bf16[2,512,128]{2,1,0:T(8,128)(2,1)S(1)}, bf16[2,512,128]{2,1,0:T(8,128)(2,1)S(1)}, u32[]{:S(2)}, u32[]{:S(2)}) collective-permute-start(bf16[2,512,128]{2,1,0:T(8,128)(2,1)S(1)} %collective-permute-done.1), channel_id=1, source_target_pairs={{0,4},{4,8},{8,12},{12,16},{16,20},{20,24},{24,28},{1,5},{5,9},{9,... | collective-permute-start | bytes 786440 | tf_op jit(solution)/shard_map/ppermute | solution.py:18
  51.6 8.6 %copy-start.5 = (bf16[512,1,128]{2,0,1:T(8,128)(2,1)}, bf16[512,1,128]{2,0,1:T(8,128)(2,1)S(1)}, u32[]{:S(2)}) copy-start(bf16[512,1,128]{2,0,1:T(8,128)(2,1)S(1)} %get-tuple-element.818) | copy-start | bytes 393220
  52.8 12.5 %collective-permute-start.3 = (bf16[2,512,128]{2,1,0:T(8,128)(2,1)S(1)}, bf16[2,512,128]{2,1,0:T(8,128)(2,1)S(1)}, u32[]{:S(2)}, u32[]{:S(2)}) collective-permute-start(bf16[2,512,128]{2,1,0:T(8,128)(2,1)S(1)} %collective-permute-done.2), channel_id=1, source_target_pairs={{0,4},{4,8},{8,12},{12,16},{16,20},{20,24},{24,28},{1,5},{5,9},{9,... | collective-permute-start | bytes 786440 | tf_op jit(solution)/shard_map/ppermute | solution.py:18
  54.8 9.4 %copy-start.3 = (bf16[512,1,128]{2,0,1:T(8,128)(2,1)}, bf16[512,1,128]{2,0,1:T(8,128)(2,1)S(1)}, u32[]{:S(2)}) copy-start(bf16[512,1,128]{2,0,1:T(8,128)(2,1)S(1)} %get-tuple-element.816) | copy-start | bytes 393220
  54.8 9.4 %copy-start.15 = (bf16[512,1,128]{2,0,1:T(8,128)(2,1)}, bf16[512,1,128]{2,0,1:T(8,128)(2,1)S(1)}, u32[]{:S(2)}) copy-start(bf16[512,1,128]{2,0,1:T(8,128)(2,1)S(1)} %get-tuple-element.815) | copy-start | bytes 393220
  55.4 4.7 %copy-start.17 = (bf16[512,1,128]{2,0,1:T(8,128)(2,1)S(1)}, bf16[512,1,128]{2,0,1:T(8,128)(2,1)}, u32[]{:S(2)}) copy-start(bf16[512,1,128]{2,0,1:T(8,128)(2,1)} %get-tuple-element.817) | copy-start | bytes 393220
  66.8 11.6 %copy-start.19 = (f32[512,1,4]{0,2,1:T(4,128)}, f32[512,1,4]{0,2,1:T(4,128)S(1)}, u32[]{:S(2)}) copy-start(f32[512,1,4]{0,2,1:T(4,128)S(1)} %get-tuple-element.746) | copy-start | bytes 24580
  69.2 9.1 %copy-start.6 = (bf16[512,1,128]{2,0,1:T(8,128)(2,1)S(1)}, bf16[512,1,128]{2,0,1:T(8,128)(2,1)}, u32[]{:S(2)}) copy-start(bf16[512,1,128]{2,0,1:T(8,128)(2,1)} %copy-done.5) | copy-start | bytes 393220
  78.4 0.7 copy-start.7
  78.4 0.8 copy-start.9
  78.4 7.5 %copy-start.4 = (bf16[512,1,128]{2,0,1:T(8,128)(2,1)S(1)}, bf16[512,1,128]{2,0,1:T(8,128)(2,1)}, u32[]{:S(2)}) copy-start(bf16[512,1,128]{2,0,1:T(8,128)(2,1)} %copy-done.3) | copy-start | bytes 393220
  79.2 0.6 copy-start.20
  79.9 1.0 copy-start.21
  80.9 1.0 copy-start.18
  85.9 0.7 copy-start.11
  86.9 0.7 copy-start.13
  86.9 0.8 copy-start.14
  87.7 44.3 %copy-start.2 = (bf16[512,1,4,128]{3,2,0,1:T(4,128)(2,1)S(1)}, bf16[512,1,4,128]{3,2,0,1:T(4,128)(2,1)}, u32[]{:S(2)}) copy-start(bf16[512,1,4,128]{3,2,0,1:T(4,128)(2,1)} %get-tuple-element.778) | copy-start | bytes 1572868
  96.4 40.3 %collective-permute-start.4 = (bf16[2,512,128]{2,0,1:T(2,128)(2,1)}, bf16[2,512,128]{2,0,1:T(2,128)(2,1)}, u32[]{:S(2)}, u32[]{:S(2)}) collective-permute-start(bf16[2,512,128]{2,0,1:T(2,128)(2,1)} %pad_maximum_fusion.1), channel_id=1, source_target_pairs={{4,0},{8,4},{12,8},{16,12},{20,16},{24,20},{28,24},{5,1},{9,5},{13... | collective-permute-start | bytes 786440 | tf_op jit(solution)/shard_map/ppermute | solution.py:18
  133.0 22.1 %copy-start.12 = (f32[1,512,128]{2,1,0:T(8,128)S(1)}, f32[1,512,128]{2,1,0:T(8,128)}, u32[]{:S(2)}) copy-start(f32[1,512,128]{2,1,0:T(8,128)} %copy-done.11) | copy-start | bytes 786436
  133.0 18.4 %all-to-all-start.3 = ((bf16[4,128,512]{2,1,0:T(8,128)(2,1)}), bf16[4,128,512]{2,1,0:T(8,128)(2,1)S(1)}, u32[]{:S(2)}, u32[]{:S(2)}) async-start(bf16[4,128,512]{2,1,0:T(8,128)(2,1)} %all_to_all.94), calls=%async_computation.3 | async-start | bytes 1048576 | tf_op jit(solution)/shard_map/all_to_all | solution.py:268
  136.6 26.8 %copy-start.8 = (f32[1,512,128]{2,1,0:T(8,128)S(1)}, f32[1,512,128]{2,1,0:T(8,128)}, u32[]{:S(2)}) copy-start(f32[1,512,128]{2,1,0:T(8,128)} %copy-done.7) | copy-start | bytes 786436
  136.7 26.8 %copy-start.10 = (f32[1,512,128]{2,1,0:T(8,128)S(1)}, f32[1,512,128]{2,1,0:T(8,128)}, u32[]{:S(2)}) copy-start(f32[1,512,128]{2,1,0:T(8,128)} %copy-done.9) | copy-start | bytes 786436
  138.4 7.2 %collective-permute-start.5 = (bf16[2,512,128]{2,0,1:T(2,128)(2,1)S(1)}, bf16[2,512,128]{2,0,1:T(2,128)(2,1)S(1)}, u32[]{:S(2)}, u32[]{:S(2)}) collective-permute-start(bf16[2,512,128]{2,0,1:T(2,128)(2,1)S(1)} %fusion.313), channel_id=1, source_target_pairs={{4,0},{8,4},{12,8},{16,12},{20,16},{24,20},{28,24},{5,1},{9,5},{13... | collective-permute-start | bytes 786440 | tf_op jit(solution)/shard_map/ppermute | solution.py:18
  146.2 9.0 %collective-permute-start.6 = (bf16[2,512,128]{2,0,1:T(2,128)(2,1)S(1)}, bf16[2,512,128]{2,0,1:T(2,128)(2,1)S(1)}, u32[]{:S(2)}, u32[]{:S(2)}) collective-permute-start(bf16[2,512,128]{2,0,1:T(2,128)(2,1)S(1)} %fusion.314), channel_id=1, source_target_pairs={{4,0},{8,4},{12,8},{16,12},{20,16},{24,20},{28,24},{5,1},{9,5},{13... | collective-permute-start | bytes 786440 | tf_op jit(solution)/shard_map/ppermute | solution.py:18
  151.5 17.0 %all-to-all-start.5 = ((bf16[4,128,512]{2,1,0:T(8,128)(2,1)}), bf16[4,128,512]{2,1,0:T(8,128)(2,1)S(1)}, u32[]{:S(2)}, u32[]{:S(2)}) async-start(bf16[4,128,512]{2,1,0:T(8,128)(2,1)} %convert_element_type.125), calls=%async_computation.5 | async-start | bytes 1048576 | tf_op jit(solution)/shard_map/all_to_all | solution.py:269
  155.1 26.4 %copy-start.1 = (bf16[128,512]{1,0:T(8,128)(2,1)S(1)}, bf16[128,512]{1,0:T(8,128)(2,1)}, u32[]{:S(2)}) copy-start(bf16[128,512]{1,0:T(8,128)(2,1)} %param.26) | copy-start | bytes 393220
  156.7 6.7 %collective-permute-start.7 = (bf16[2,512,128]{2,0,1:T(2,128)(2,1)S(1)}, bf16[2,512,128]{2,0,1:T(2,128)(2,1)S(1)}, u32[]{:S(2)}, u32[]{:S(2)}) collective-permute-start(bf16[2,512,128]{2,0,1:T(2,128)(2,1)S(1)} %fusion.315), channel_id=1, source_target_pairs={{4,0},{8,4},{12,8},{16,12},{20,16},{24,20},{28,24},{5,1},{9,5},{13... | collective-permute-start | bytes 786440 | tf_op jit(solution)/shard_map/ppermute | solution.py:18
  168.5 11.6 %all-to-all-start.6 = ((bf16[2,512,128]{2,0,1:T(2,128)(2,1)}), bf16[2,512,128]{2,0,1:T(2,128)(2,1)S(1)}, u32[]{:S(2)}, u32[]{:S(2)}) async-start(bf16[2,512,128]{2,0,1:T(2,128)(2,1)} %fusion.316), calls=%async_computation.6 | async-start | bytes 524288 | tf_op jit(solution)/shard_map/all_to_all | solution.py:271
where the time goes:
time: 185 us; the launch traced here: 182 us
  starting transfers between devices  81.2 us (44%)
  waiting for transfers between devices  33.1 us (18%)
  local copies, waits for them, and re-layouts  21.3 us (12%)
  matrix products  17.2 us (9%)
  other arithmetic  13.3 us (7%)
  loops' own time  11 us (6%)
  between operations  4.77 us (3%)
    ppermute x8, starting transfers between devices, shifted(): lax.ppermute(value, axis, [(source, source + steps) for source in range(f...  53.2 us
    ppermute x8, waiting for transfers between devices, shifted(): lax.ppermute(value, axis, [(source, source + steps) for source in range(f...  14.8 us
    another operation x5, loops' own time, shards(): lax.cond(live, backward_block, lambda unchanged: unchanged, current)  10.5 us
    all_to_all x1, waiting for transfers between devices, shards(): lax.all_to_all(grad_total.astype(jnp.bfloat16), 'head', split_axis=1, con...  5.58 us
    unnamed x40, local copies, waits for them, and re-layouts  5.18 us
    convert_element_type x4, other arithmetic, shards(): grad_total.astype(jnp.bfloat16)  5.13 us
    all_to_all x1, starting transfers between devices, shards(): lax.all_to_all(d_out, 'head', split_axis=1, concat_axis=0, tiled=True)  5.06 us
    all_to_all x1, starting transfers between devices, shards(): lax.all_to_all(spread(keys), 'head', split_axis=1, concat_axis=0, tiled=T...  4.87 us
  transfers between devices with their start and end apart: 15, of which 9 were waited for; matrix products, arithmetic and copies ran while one was open for 15% of the time, Pallas kernels for 0%

commit v1 on v0

--- a/solution.py
+++ b/solution.py
@@ -1,6 +1,11 @@
+import functools
+import math
+
 import jax
 import jax.numpy as jnp
 from jax import lax
+from jax.experimental import pallas as pl
+from jax.experimental.pallas import tpu as pltpu
 from jax.sharding import PartitionSpec as P
 
 QH = 16
@@ -279,22 +284,259 @@
     return (attn_out, grad_queries, token_grads[0], token_grads[1])
 
 
+KEY_ROWS = 256
+CONTRACT_LAST = (((1,), (1,)), ((), ()))
+CONTRACT_FIRST = (((0,), (0,)), ((), ()))
+VMEM = pl.BlockSpec(memory_space=pltpu.VMEM)
+SMEM = pl.BlockSpec(memory_space=pltpu.SMEM)
+
+
+def flipped(value, axis, bits):
+    count = lax.axis_size(axis)
+    return lax.ppermute(value, axis, [(source, source ^ bits) for source in range(count)])
+
+
+def pack_heads_kernel(cores, wide, left_ref, right_ref, *out_refs):
+    part = lax.axis_index("ctx") // cores
+    for flip, out_ref in enumerate(out_refs):
+        columns = pl.ds(pl.multiple_of((part ^ flip) * wide, HD), wide)
+        out_ref[:, :wide] = left_ref[:, columns]
+        out_ref[:, wide:] = right_ref[:, columns]
+
+
+def unpack_heads_kernel(cores, wide, *refs):
+    in_refs, (left_ref, right_ref) = refs[:KVH], refs[KVH:]
+    part = lax.axis_index("ctx") // cores
+    for flip, in_ref in enumerate(in_refs):
+        columns = pl.ds(pl.multiple_of((part ^ flip) * wide, HD), wide)
+        left_ref[:, columns] = in_ref[:, :wide]
+        right_ref[:, columns] = in_ref[:, wide:]
+
+
+def pack_heads(left, right, cores):
+    rows, wide = left.shape[0], left.shape[1] // KVH
+    return pl.pallas_call(
+        functools.partial(pack_heads_kernel, cores, wide),
+        out_shape=[jax.ShapeDtypeStruct((rows, 2 * wide), left.dtype)] * KVH,
+        in_specs=[VMEM] * 2,
+        out_specs=[VMEM] * KVH,
+    )(left, right)
+
+
+def unpack_heads(pieces, cores):
+    rows, wide = pieces[0].shape[0], pieces[0].shape[1] // 2
+    return pl.pallas_call(
+        functools.partial(unpack_heads_kernel, cores, wide),
+        out_shape=[jax.ShapeDtypeStruct((rows, wide * KVH), pieces[0].dtype)] * 2,
+        in_specs=[VMEM] * KVH,
+        out_specs=[VMEM] * 2,
+    )(*pieces)
+
+
+def attention_kernel(cores, heads, tok, *refs):
+    group = QH // KVH
+    lanes = group * tok
+    tile_rows = heads * tok
+    kv_count = heads * cores
+    lengths_ref, refs = refs[0], refs[1:]
+    qd_refs, refs = refs[:KVH], refs[KVH:]
+    kv_refs, refs = refs[:kv_count], refs[kv_count:]
+    od_refs, refs = refs[:KVH], refs[KVH:]
+    dkv_refs, refs = refs[:kv_count], refs[kv_count:]
+    k_all, v_all, q_all, g_all, o_all, dq_all, dk_acc, dv_acc, score, acc = refs
+    scaling = HD ** (-0.5)
+    log_scale = scaling * math.log2(math.e)
+
+    ctx_index, head_index = lax.axis_index("ctx"), lax.axis_index("head")
+    part, core = ctx_index // cores, ctx_index % cores
+
+    def rows_of(head_flip, core_flip, part_flip):
+        tile = (part ^ part_flip) * cores + (core ^ core_flip)
+        return pl.ds(pl.multiple_of((tile * heads + (head_index ^ head_flip)) * tok, tok), tok)
+
+    for number, kv_ref in enumerate(kv_refs):
+        for flip in range(KVH):
+            rows = rows_of(number // cores, number % cores, flip)
+            k_all[rows, :] = kv_ref[flip, :, :HD]
+            v_all[rows, :] = kv_ref[flip, :, HD:]
+    for flip, qd_ref in enumerate(qd_refs):
+        for member in range(group):
+            rows = slice(member * tok, (member + 1) * tok)
+            q_all[flip, rows, :] = qd_ref[:, member * HD : (member + 1) * HD]
+            g_all[flip, rows, :] = qd_ref[:, (group + member) * HD : (group + member + 1) * HD]
+    dk_acc[...] = jnp.zeros_like(dk_acc)
+    dv_acc[...] = jnp.zeros_like(dv_acc)
+
+    def fold(values, combine):
+        return combine(values.reshape(KEY_ROWS // 8, 8, lanes), axis=0)
+
+    def query_block(flip, _):
+        first = ((part ^ flip) * cores + core) * tile_rows + head_index * tok
+        last = first + tok - 1
+        query_pos = first + lax.broadcasted_iota(jnp.int32, (1, lanes), 1) % tok
+
+        def document(number, carry):
+            end, low, start_row = carry
+            length = lengths_ref[number]
+            end = end + length
+            return (
+                end,
+                low + jnp.where(end <= first, length, 0),
+                start_row + jnp.where(end <= query_pos, length, 0),
+            )
+
+        _, low, start_row = lax.fori_loop(
+            0,
+            lengths_ref.shape[0],
+            document,
+            (jnp.int32(0), jnp.int32(0), jnp.zeros((1, lanes), jnp.int32)),
+        )
+        key_block = low // KEY_ROWS
+        count = last // KEY_ROWS + 1 - key_block
+        q = q_all[flip]
+        g = g_all[flip]
+
+        def key_rows(step):
+            return pl.ds(pl.multiple_of((key_block + step) * KEY_ROWS, KEY_ROWS), KEY_ROWS)
+
+        def score_rows(step):
+            return pl.ds(pl.multiple_of(step * KEY_ROWS, KEY_ROWS), KEY_ROWS)
+
+        def scores_step(step, top):
+            raw = lax.dot_general(
+                k_all[key_rows(step), :], q, CONTRACT_LAST, preferred_element_type=jnp.float32
+            )
+            offset = (key_block + step) * KEY_ROWS
+            key_pos = lax.broadcasted_iota(jnp.int32, (KEY_ROWS, lanes), 0)
+            mask = (key_pos <= query_pos - offset) & (key_pos >= start_row - offset)
+            raw = jnp.where(mask, raw, NEG_FILL)
+            score[score_rows(step), :] = raw
+            return jnp.maximum(top, fold(raw, jnp.max))
+
+        top = lax.fori_loop(
+            0, count, scores_step, jnp.full((8, lanes), NEG_FILL, jnp.float32)
+        )
+        top = jnp.max(top, axis=0, keepdims=True)
+        acc[...] = jnp.zeros_like(acc)
+
+        def out_step(step, total):
+            prob = jnp.exp2((score[score_rows(step), :] - top) * log_scale)
+            score[score_rows(step), :] = prob
+            acc[...] += lax.dot_general(
+                v_all[key_rows(step), :],
+                prob.astype(jnp.bfloat16),
+                CONTRACT_FIRST,
+                preferred_element_type=jnp.float32,
+            )
+            return total + fold(prob, jnp.sum)
+
+        total = lax.fori_loop(0, count, out_step, jnp.zeros((8, lanes), jnp.float32))
+        inverse = 1.0 / jnp.sum(total, axis=0, keepdims=True)
+        out = (acc[...] * inverse).T.astype(jnp.bfloat16)
+        o_all[flip] = out
+        delta = jnp.sum((out.astype(jnp.float32) * g.astype(jnp.float32)).T, axis=0, keepdims=True)
+        acc[...] = jnp.zeros_like(acc)
+
+        def grad_step(step, _):
+            rows = key_rows(step)
+            prob = score[score_rows(step), :] * inverse
+            prob_grad = lax.dot_general(
+                v_all[rows, :], g, CONTRACT_LAST, preferred_element_type=jnp.float32
+            )
+            score_grad = (prob * (prob_grad - delta)).astype(jnp.bfloat16)
+            dv_acc[rows, :] += jnp.dot(
+                prob.astype(jnp.bfloat16), g, preferred_element_type=jnp.float32
+            )
+            dk_acc[rows, :] += jnp.dot(score_grad, q, preferred_element_type=jnp.float32)
+            acc[...] += lax.dot_general(
+                k_all[rows, :], score_grad, CONTRACT_FIRST, preferred_element_type=jnp.float32
+            )
+            return 0
+
+        lax.fori_loop(0, count, grad_step, 0)
+        dq_all[flip] = (acc[...] * scaling).T.astype(jnp.bfloat16)
+        return 0
+
+    lax.fori_loop(0, KVH, query_block, 0)
+
+    for flip, od_ref in enumerate(od_refs):
+        for member in range(group):
+            rows = slice(member * tok, (member + 1) * tok)
+            od_ref[:, member * HD : (member + 1) * HD] = o_all[flip, rows, :]
+            od_ref[:, (group + member) * HD : (group + member + 1) * HD] = dq_all[flip, rows, :]
+    for number, dkv_ref in enumerate(dkv_refs):
+        for flip in range(KVH):
+            rows = rows_of(number // cores, number % cores, flip)
+            dkv_ref[flip, :, :HD] = (dk_acc[rows, :] * scaling).astype(jnp.bfloat16)
+            dkv_ref[flip, :, HD:] = dv_acc[rows, :].astype(jnp.bfloat16)
+
+
+def attention(lengths, qd, kv, cores, heads):
+    tok, group = qd[0].shape[0], QH // KVH
+    total = KVH * cores * heads * tok
+    window = (REACH * heads * tok + tok) // KEY_ROWS * KEY_ROWS + 2 * KEY_ROWS
+    lanes = group * tok
+    bf16, f32 = jnp.bfloat16, jnp.float32
+    results = pl.pallas_call(
+        functools.partial(attention_kernel, cores, heads, tok),
+        out_shape=[jax.ShapeDtypeStruct(a.shape, a.dtype) for a in qd]
+        + [jax.ShapeDtypeStruct(a.shape, a.dtype) for a in kv],
+        in_specs=[SMEM] + [VMEM] * (len(qd) + len(kv)),
+        out_specs=[VMEM] * (len(qd) + len(kv)),
+        scratch_shapes=[
+            pltpu.VMEM((total, HD), bf16),
+            pltpu.VMEM((total, HD), bf16),
+            pltpu.VMEM((KVH, lanes, HD), bf16),
+            pltpu.VMEM((KVH, lanes, HD), bf16),
+            pltpu.VMEM((KVH, lanes, HD), bf16),
+            pltpu.VMEM((KVH, lanes, HD), bf16),
+            pltpu.VMEM((total, HD), f32),
+            pltpu.VMEM((total, HD), f32),
+            pltpu.VMEM((window, lanes), f32),
+            pltpu.VMEM((HD, lanes), f32),
+        ],
+        compiler_params=pltpu.CompilerParams(vmem_limit_bytes=40 * 1024 * 1024),
+    )(lengths, *qd, *kv)
+    return results[: len(qd)], results[len(qd) :]
+
+
+def part_shards(queries, keys, values, d_out, lengths):
+    heads = lax.axis_size("head")
+    cores = lax.axis_size("ctx") // KVH
+
+    def exchange(pieces):
+        return [pieces[0]] + [flipped(pieces[s], "ctx", s * cores) for s in range(1, KVH)]
+
+    kv_mine = jnp.stack(exchange(pack_heads(keys, values, cores)))
+    qd = exchange(pack_heads(queries, d_out, cores))
+    near, far = flipped(kv_mine, "head", 1), flipped(kv_mine, "head", 2)
+    gathered = [kv_mine, near, far, flipped(far, "head", 1)]
+    kv = []
+    for piece in gathered:
+        kv += [piece, flipped(piece, "ctx", 1)]
+    od, dkv = attention(lengths, qd, kv, cores, heads)
+
+    def summed(*terms):
+        return sum(term.astype(jnp.float32) for term in terms).astype(jnp.bfloat16)
+
+    both = [(dkv[2 * h], flipped(dkv[2 * h + 1], "ctx", 1)) for h in range(heads)]
+    third = flipped(summed(*both[3]), "head", 1)
+    second = flipped(summed(*both[2], third), "head", 2)
+    first = flipped(summed(*both[1]), "head", 1)
+    kv_total = summed(*both[0], first, second)
+    attn_out, grad_queries = unpack_heads(exchange(od), cores)
+    grad_keys, grad_values = unpack_heads(exchange([kv_total[s] for s in range(KVH)]), cores)
+    return attn_out, grad_queries, grad_keys, grad_values
+
+
 def solution(mesh):
+    ctx_dev, head_dev = mesh.shape["ctx"], mesh.shape["head"]
+    local = part_shards if ctx_dev == 2 * KVH and head_dev == 4 else shards
+    rows = P(("ctx", "head"), None)
     return jax.shard_map(
-        shards,
+        local,
         mesh=mesh,
-        in_specs=(
-            P(("ctx", "head"), None),
-            P(("ctx", "head"), None),
-            P(("ctx", "head"), None),
-            P(("ctx", "head"), None),
-            P(),
-        ),
-        out_specs=(
-            P(("ctx", "head"), None),
-            P(("ctx", "head"), None),
-            P(("ctx", "head"), None),
-            P(("ctx", "head"), None),
-        ),
+        in_specs=(rows, rows, rows, rows, P()),
+        out_specs=(rows, rows, rows, rows),
         check_vma=False,
     )

time: 185 us -> 93.1 us (0.50)
  the two profiles are of different devices: /device:TPU:6 before, /device:TPU:0 now
where the time goes in v1:
time: 93.1 us; the launch traced here: 92.8 us
  waiting for transfers between devices  34.4 us (37%)
  Pallas kernels  27.2 us (29%)
  starting transfers between devices  26.1 us (28%)
  local copies, waits for them, and re-layouts  3.01 us (3%)
  other arithmetic  1.24 us (1%)
    ppermute x26, waiting for transfers between devices, flipped(): lax.ppermute(value, axis, [(source, source ^ bits) for source in range(co...  34.4 us
    ppermute x26, starting transfers between devices, flipped(): lax.ppermute(value, axis, [(source, source ^ bits) for source in range(co...  26.1 us
    pallas_call x1, Pallas kernels, attention(): pl.pallas_call(functools.partial(attention_kernel, cores, heads, tok), ou...  19.3 us
    pallas_call x2, Pallas kernels, pack_heads(): pl.pallas_call(functools.partial(pack_heads_kernel, cores, wide), out_sha...  3.95 us
    pallas_call x2, Pallas kernels, unpack_heads(): pl.pallas_call(functools.partial(unpack_heads_kernel, cores, wide), out_s...  3.91 us
    unnamed x18, local copies, waits for them, and re-layouts  2.36 us
  transfers between devices with their start and end apart: 26, of which 13 were waited for; matrix products, arithmetic and copies ran while one was open for 1% of the time, Pallas kernels for 5%

profile of v1, /device:TPU:0, one launch (start us, length us, event | category | flops | bytes accessed | tf_op | source)
XLA Modules:
  0.0 92.8 jit_solution(3042003093319917064)
XLA Ops:
  0.6 1.7 %shard_map.85 = (bf16[128,256]{1,0:T(8,128)(2,1)}, bf16[128,256]{1,0:T(8,128)(2,1)}, bf16[128,256]{1,0:T(8,128)(2,1)}, bf16[128,256]{1,0:T(8,128)(2,1)}) custom-call(bf16[128,512]{1,0:T(8,128)(2,1)} %left_ref.3, bf16[128,512]{1,0:T(8,128)(2,1)} %right_ref.3), custom_call_target="tpu_custom_call" | custom-call | tf_op jit(solution)/shard_map/pallas_call | solution.py:318
  2.3 2.9 %collective-permute-start.3 = (bf16[128,256]{1,0:T(8,128)(2,1)}, bf16[128,256]{1,0:T(8,128)(2,1)S(1)}, u32[]{:S(2)}, u32[]{:S(2)}) collective-permute-start(bf16[128,256]{1,0:T(8,128)(2,1)} %get-tuple-element.33), channel_id=1, source_target_pairs={{0,8},{4,12},{8,0},{12,4},{16,24},{20,28},{24,16},{28,20},{1,9},{5... | collective-permute-start | bytes 196616 | tf_op jit(solution)/shard_map/ppermute | solution.py:296
  5.3 1.5 %collective-permute-start.4 = (bf16[128,256]{1,0:T(8,128)(2,1)}, bf16[128,256]{1,0:T(8,128)(2,1)S(1)}, u32[]{:S(2)}, u32[]{:S(2)}) collective-permute-start(bf16[128,256]{1,0:T(8,128)(2,1)} %get-tuple-element.34), channel_id=1, source_target_pairs={{0,16},{4,20},{8,24},{12,28},{16,0},{20,4},{24,8},{28,12},{1,17},{... | collective-permute-start | bytes 196616 | tf_op jit(solution)/shard_map/ppermute | solution.py:296
  6.8 1.2 %collective-permute-done.3 = bf16[128,256]{1,0:T(8,128)(2,1)S(1)} collective-permute-done((bf16[128,256]{1,0:T(8,128)(2,1)}, bf16[128,256]{1,0:T(8,128)(2,1)S(1)}, u32[]{:S(2)}, u32[]{:S(2)}) %collective-permute-start.3) | collective-permute-done | bytes 65568 | tf_op jit(solution)/shard_map/ppermute | solution.py:296
  8.0 1.8 %collective-permute-done.4 = bf16[128,256]{1,0:T(8,128)(2,1)S(1)} collective-permute-done((bf16[128,256]{1,0:T(8,128)(2,1)}, bf16[128,256]{1,0:T(8,128)(2,1)S(1)}, u32[]{:S(2)}, u32[]{:S(2)}) %collective-permute-start.4) | collective-permute-done | bytes 65568 | tf_op jit(solution)/shard_map/ppermute | solution.py:296
  9.8 2.4 %collective-permute-done.5 = bf16[128,256]{1,0:T(8,128)(2,1)S(1)} collective-permute-done((bf16[128,256]{1,0:T(8,128)(2,1)}, bf16[128,256]{1,0:T(8,128)(2,1)S(1)}, u32[]{:S(2)}, u32[]{:S(2)}) %collective-permute-start.5) | collective-permute-done | bytes 65568 | tf_op jit(solution)/shard_map/ppermute | solution.py:296
  12.2 0.9 pad_maximum_fusion.refs_5_
  13.1 2.7 %collective-permute-start.9 = (bf16[4,128,256]{2,1,0:T(8,128)(2,1)S(1)}, bf16[4,128,256]{2,1,0:T(8,128)(2,1)S(1)}, u32[]{:S(2)}, u32[]{:S(2)}) collective-permute-start(bf16[4,128,256]{2,1,0:T(8,128)(2,1)S(1)} %pad_maximum_fusion.refs_5_), channel_id=1, source_target_pairs={{0,2},{1,3},{2,0},{3,1},{4,6},{5,7},{6,4},{7,5},{8,10},{9,11},{10,... | collective-permute-start | bytes 786440 | tf_op jit(solution)/shard_map/ppermute | solution.py:296
  15.7 2.2 %shard_map.84 = (bf16[128,1024]{1,0:T(8,128)(2,1)}, bf16[128,1024]{1,0:T(8,128)(2,1)}, bf16[128,1024]{1,0:T(8,128)(2,1)}, bf16[128,1024]{1,0:T(8,128)(2,1)}) custom-call(bf16[128,2048]{1,0:T(8,128)(2,1)} %left_ref.2, bf16[128,2048]{1,0:T(8,128)(2,1)} %right_ref.2), custom_call_target="tpu_custom_call" | custom-call | tf_op jit(solution)/shard_map/pallas_call | solution.py:318
  17.9 0.5 collective-permute-start
  18.5 0.5 collective-permute-start.1
  19.0 1.6 %collective-permute-start.7 = (bf16[4,128,256]{2,1,0:T(8,128)(2,1)S(1)}, bf16[4,128,256]{2,1,0:T(8,128)(2,1)S(1)}, u32[]{:S(2)}, u32[]{:S(2)}) collective-permute-start(bf16[4,128,256]{2,1,0:T(8,128)(2,1)S(1)} %pad_maximum_fusion.refs_5_), channel_id=1, source_target_pairs={{0,1},{1,0},{2,3},{3,2},{4,5},{5,4},{6,7},{7,6},{8,9},{9,8},{10,11... | collective-permute-start | bytes 786440 | tf_op jit(solution)/shard_map/ppermute | solution.py:296
  20.6 5.5 %collective-permute-done.9.refs_9_ = bf16[4,128,256]{2,1,0:T(8,128)(2,1)S(1)} collective-permute-done((bf16[4,128,256]{2,1,0:T(8,128)(2,1)S(1)}, bf16[4,128,256]{2,1,0:T(8,128)(2,1)S(1)}, u32[]{:S(2)}, u32[]{:S(2)}) %collective-permute-start.9) | collective-permute-done | bytes 262176 | tf_op jit(solution)/shard_map/ppermute | solution.py:296
  26.1 0.6 collective-permute-start.11
  26.7 1.0 %collective-permute-start.2 = (bf16[128,1024]{1,0:T(8,128)(2,1)}, bf16[128,1024]{1,0:T(8,128)(2,1)S(1)}, u32[]{:S(2)}, u32[]{:S(2)}) collective-permute-start(bf16[128,1024]{1,0:T(8,128)(2,1)} %get-tuple-element.31), channel_id=1, source_target_pairs={{0,24},{4,28},{8,16},{12,20},{16,8},{20,12},{24,0},{28,4},{1,25},{... | collective-permute-start | bytes 786440 | tf_op jit(solution)/shard_map/ppermute | solution.py:296
  27.7 0.5 collective-permute-start.10
  28.2 2.9 %collective-permute-done.7.refs_7_ = bf16[4,128,256]{2,1,0:T(8,128)(2,1)S(1)} collective-permute-done((bf16[4,128,256]{2,1,0:T(8,128)(2,1)S(1)}, bf16[4,128,256]{2,1,0:T(8,128)(2,1)S(1)}, u32[]{:S(2)}, u32[]{:S(2)}) %collective-permute-start.7) | collective-permute-done | bytes 262176 | tf_op jit(solution)/shard_map/ppermute | solution.py:296
  31.1 4.0 %collective-permute-done.11.refs_11_ = bf16[4,128,256]{2,1,0:T(8,128)(2,1)S(1)} collective-permute-done((bf16[4,128,256]{2,1,0:T(8,128)(2,1)S(1)}, bf16[4,128,256]{2,1,0:T(8,128)(2,1)S(1)}, u32[]{:S(2)}, u32[]{:S(2)}) %collective-permute-start.11) | collective-permute-done | bytes 262176 | tf_op jit(solution)/shard_map/ppermute | solution.py:296
  35.0 0.7 collective-permute-done.2.refs_4_
  35.8 0.8 collective-permute-done.12.refs_12_
  36.6 0.9 %copy-done.1 = bf16[128,1024]{1,0:T(8,128)(2,1)S(1)} copy-done((bf16[128,1024]{1,0:T(8,128)(2,1)S(1)}, bf16[128,1024]{1,0:T(8,128)(2,1)}, u32[]{:S(2)}) %copy-start.1) | copy-done | bytes 262168
  37.5 19.3 %shard_map.86 = (bf16[128,1024]{1,0:T(8,128)(2,1)S(1)}, bf16[128,1024]{1,0:T(8,128)(2,1)S(1)}, bf16[128,1024]{1,0:T(8,128)(2,1)S(1)}, bf16[128,1024]{1,0:T(8,128...) custom-call(s32[32]{0:T(128)S(1)} %copy-done.2, ...), custom_call_target="tpu_custom_call" | custom-call | tf_op jit(solution)/shard_map/pallas_call | solution.py:480
  56.9 0.1 collective-permute-start.20
  57.0 0.5 collective-permute-start.17
  57.5 0.1 collective-permute-start.19
  57.5 0.9 %collective-permute-done.20 = bf16[4,128,256]{2,1,0:T(8,128)(2,1)S(1)} collective-permute-done((bf16[4,128,256]{2,1,0:T(8,128)(2,1)S(1)}, bf16[4,128,256]{2,1,0:T(8,128)(2,1)S(1)}, u32[]{:S(2)}, u32[]{:S(2)}) %collective-permute-start.20) | collective-permute-done | bytes 262176 | tf_op jit(solution)/shard_map/ppermute | solution.py:296
  58.6 0.2 collective-permute-start.16
  58.9 1.9 %collective-permute-start.18 = (bf16[4,128,256]{2,1,0:T(8,128)(2,1)S(1)}, bf16[4,128,256]{2,1,0:T(8,128)(2,1)S(1)}, u32[]{:S(2)}, u32[]{:S(2)}) collective-permute-start(bf16[4,128,256]{2,1,0:T(8,128)(2,1)S(1)} %add_convert_fusion.3), channel_id=1, source_target_pairs={{0,1},{1,0},{2,3},{3,2},{4,5},{5,4},{6,7},{7,6},{8,9},{9,8},{10,11... | collective-permute-start | bytes 786440 | tf_op jit(solution)/shard_map/ppermute | solution.py:296
  60.8 7.0 %collective-permute-done.21 = bf16[4,128,256]{2,1,0:T(8,128)(2,1)S(1)} collective-permute-done((bf16[4,128,256]{2,1,0:T(8,128)(2,1)S(1)}, bf16[4,128,256]{2,1,0:T(8,128)(2,1)S(1)}, u32[]{:S(2)}, u32[]{:S(2)}) %collective-permute-start.21) | collective-permute-done | bytes 262176 | tf_op jit(solution)/shard_map/ppermute | solution.py:296
  67.8 0.1 add_convert_fusion.1
  67.9 4.5 %collective-permute-start.22 = (bf16[4,128,256]{2,1,0:T(8,128)(2,1)S(1)}, bf16[4,128,256]{2,1,0:T(8,128)(2,1)S(1)}, u32[]{:S(2)}, u32[]{:S(2)}) collective-permute-start(bf16[4,128,256]{2,1,0:T(8,128)(2,1)S(1)} %add_convert_fusion.1), channel_id=1, source_target_pairs={{0,2},{1,3},{2,0},{3,1},{4,6},{5,7},{6,4},{7,5},{8,10},{9,11},{10,... | collective-permute-start | bytes 786440 | tf_op jit(solution)/shard_map/ppermute | solution.py:296
  72.4 0.9 collective-permute-start.13
  73.3 0.6 collective-permute-start.14
  74.0 1.9 %collective-permute-start.15 = (bf16[128,1024]{1,0:T(8,128)(2,1)S(1)}, bf16[128,1024]{1,0:T(8,128)(2,1)S(1)}, u32[]{:S(2)}, u32[]{:S(2)}) collective-permute-start(bf16[128,1024]{1,0:T(8,128)(2,1)S(1)} %get-tuple-element.39), channel_id=1, source_target_pairs={{0,24},{4,28},{8,16},{12,20},{16,8},{20,12},{24,0},{28,4},{1,25},{... | collective-permute-start | bytes 786440 | tf_op jit(solution)/shard_map/ppermute | solution.py:296
  75.9 1.3 %collective-permute-done.18 = bf16[4,128,256]{2,1,0:T(8,128)(2,1)S(1)} collective-permute-done((bf16[4,128,256]{2,1,0:T(8,128)(2,1)S(1)}, bf16[4,128,256]{2,1,0:T(8,128)(2,1)S(1)}, u32[]{:S(2)}, u32[]{:S(2)}) %collective-permute-start.18) | collective-permute-done | bytes 262176 | tf_op jit(solution)/shard_map/ppermute | solution.py:296
  77.2 5.8 %collective-permute-done.22 = bf16[4,128,256]{2,1,0:T(8,128)(2,1)S(1)} collective-permute-done((bf16[4,128,256]{2,1,0:T(8,128)(2,1)S(1)}, bf16[4,128,256]{2,1,0:T(8,128)(2,1)S(1)}, u32[]{:S(2)}, u32[]{:S(2)}) %collective-permute-start.22) | collective-permute-done | bytes 262176 | tf_op jit(solution)/shard_map/ppermute | solution.py:296
  83.0 0.1 add_convert_fusion
  83.2 0.6 slice_bitcast_fusion
  83.8 1.0 %collective-permute-start.25 = (bf16[128,256]{1,0:T(8,128)(2,1)S(1)}, bf16[128,256]{1,0:T(8,128)(2,1)S(1)}, u32[]{:S(2)}, u32[]{:S(2)}) collective-permute-start(bf16[128,256]{1,0:T(8,128)(2,1)S(1)} %get-tuple-element.52), channel_id=1, source_target_pairs={{0,24},{4,28},{8,16},{12,20},{16,8},{20,12},{24,0},{28,4},{1,25},{... | collective-permute-start | bytes 196616 | tf_op jit(solution)/shard_map/ppermute | solution.py:296
  84.8 1.4 %collective-permute-start.24 = (bf16[128,256]{1,0:T(8,128)(2,1)S(1)}, bf16[128,256]{1,0:T(8,128)(2,1)S(1)}, u32[]{:S(2)}, u32[]{:S(2)}) collective-permute-start(bf16[128,256]{1,0:T(8,128)(2,1)S(1)} %get-tuple-element.53), channel_id=1, source_target_pairs={{0,16},{4,20},{8,24},{12,28},{16,0},{20,4},{24,8},{28,12},{1,17},{... | collective-permute-start | bytes 196616 | tf_op jit(solution)/shard_map/ppermute | solution.py:296
  86.2 1.1 %collective-permute-start.23 = (bf16[128,256]{1,0:T(8,128)(2,1)S(1)}, bf16[128,256]{1,0:T(8,128)(2,1)S(1)}, u32[]{:S(2)}, u32[]{:S(2)}) collective-permute-start(bf16[128,256]{1,0:T(8,128)(2,1)S(1)} %get-tuple-element.54), channel_id=1, source_target_pairs={{0,8},{4,12},{8,0},{12,4},{16,24},{20,28},{24,16},{28,20},{1,9},{5... | collective-permute-start | bytes 196616 | tf_op jit(solution)/shard_map/ppermute | solution.py:296
  87.4 0.7 copy-done.4
  88.0 0.1 copy-done.5
  88.1 2.2 %shard_map.87 = (bf16[128,2048]{1,0:T(8,128)(2,1)}, bf16[128,2048]{1,0:T(8,128)(2,1)}) custom-call(bf16[128,1024]{1,0:T(8,128)(2,1)} %copy-done, bf16[128,1024]{1,0:T(8,128)(2,1)} %copy-done.3, bf16[128,1024]{1,0:T(8,128)(2,1)} %copy-done.4, bf16[128,1024]{1,0:T(8,128)(2,1)} %copy-done.5), custom_call_target="tpu_custom_call" | custom-call | tf_op jit(solution)/shard_map/pallas_call | solution.py:328
  90.4 0.1 collective-permute-done.23.refs_1_
  90.5 0.5 copy-done.6
  91.0 0.1 copy-done.8
  91.1 1.7 %shard_map.88 = (bf16[128,512]{1,0:T(8,128)(2,1)}, bf16[128,512]{1,0:T(8,128)(2,1)}) custom-call(bf16[128,256]{1,0:T(8,128)(2,1)} %get-tuple-element.55.refs_0_, bf16[128,256]{1,0:T(8,128)(2,1)} %copy-done.8, bf16[128,256]{1,0:T(8,128)(2,1)} %copy-done.7, bf16[128,256]{1,0:T(8,128)(2,1)} %copy-done.6), custom_call_target="tpu_custom_call" | custom-call | tf_op jit(solution)/shard_map/pallas_call | solution.py:328
  (33 shorter events, 0.3 us)
Async XLA Ops:
  2.3 5.6 %collective-permute-start.3 = (bf16[128,256]{1,0:T(8,128)(2,1)}, bf16[128,256]{1,0:T(8,128)(2,1)S(1)}, u32[]{:S(2)}, u32[]{:S(2)}) collective-permute-start(bf16[128,256]{1,0:T(8,128)(2,1)} %get-tuple-element.33), channel_id=1, source_target_pairs={{0,8},{4,12},{8,0},{12,4},{16,24},{20,28},{24,16},{28,20},{1,9},{5... | collective-permute-start | bytes 196616 | tf_op jit(solution)/shard_map/ppermute | solution.py:296
  5.3 4.5 %collective-permute-start.4 = (bf16[128,256]{1,0:T(8,128)(2,1)}, bf16[128,256]{1,0:T(8,128)(2,1)S(1)}, u32[]{:S(2)}, u32[]{:S(2)}) collective-permute-start(bf16[128,256]{1,0:T(8,128)(2,1)} %get-tuple-element.34), channel_id=1, source_target_pairs={{0,16},{4,20},{8,24},{12,28},{16,0},{20,4},{24,8},{28,12},{1,17},{... | collective-permute-start | bytes 196616 | tf_op jit(solution)/shard_map/ppermute | solution.py:296
  6.8 5.4 %collective-permute-start.5 = (bf16[128,256]{1,0:T(8,128)(2,1)}, bf16[128,256]{1,0:T(8,128)(2,1)S(1)}, u32[]{:S(2)}, u32[]{:S(2)}) collective-permute-start(bf16[128,256]{1,0:T(8,128)(2,1)} %get-tuple-element.35), channel_id=1, source_target_pairs={{0,24},{4,28},{8,16},{12,20},{16,8},{20,12},{24,0},{28,4},{1,25},{... | collective-permute-start | bytes 196616 | tf_op jit(solution)/shard_map/ppermute | solution.py:296
  13.1 13.0 %collective-permute-start.9 = (bf16[4,128,256]{2,1,0:T(8,128)(2,1)S(1)}, bf16[4,128,256]{2,1,0:T(8,128)(2,1)S(1)}, u32[]{:S(2)}, u32[]{:S(2)}) collective-permute-start(bf16[4,128,256]{2,1,0:T(8,128)(2,1)S(1)} %pad_maximum_fusion.refs_5_), channel_id=1, source_target_pairs={{0,2},{1,3},{2,0},{3,1},{4,6},{5,7},{6,4},{7,5},{8,10},{9,11},{10,... | collective-permute-start | bytes 786440 | tf_op jit(solution)/shard_map/ppermute | solution.py:296
  17.9 9.7 %collective-permute-start = (bf16[128,1024]{1,0:T(8,128)(2,1)}, bf16[128,1024]{1,0:T(8,128)(2,1)S(1)}, u32[]{:S(2)}, u32[]{:S(2)}) collective-permute-start(bf16[128,1024]{1,0:T(8,128)(2,1)} %get-tuple-element.29), channel_id=1, source_target_pairs={{0,8},{4,12},{8,0},{12,4},{16,24},{20,28},{24,16},{28,20},{1,9},{5... | collective-permute-start | bytes 786440 | tf_op jit(solution)/shard_map/ppermute | solution.py:296
  18.5 9.2 %collective-permute-start.1 = (bf16[128,1024]{1,0:T(8,128)(2,1)}, bf16[128,1024]{1,0:T(8,128)(2,1)S(1)}, u32[]{:S(2)}, u32[]{:S(2)}) collective-permute-start(bf16[128,1024]{1,0:T(8,128)(2,1)} %get-tuple-element.30), channel_id=1, source_target_pairs={{0,16},{4,20},{8,24},{12,28},{16,0},{20,4},{24,8},{28,12},{1,17},{... | collective-permute-start | bytes 786440 | tf_op jit(solution)/shard_map/ppermute | solution.py:296
  19.0 12.1 %collective-permute-start.7 = (bf16[4,128,256]{2,1,0:T(8,128)(2,1)S(1)}, bf16[4,128,256]{2,1,0:T(8,128)(2,1)S(1)}, u32[]{:S(2)}, u32[]{:S(2)}) collective-permute-start(bf16[4,128,256]{2,1,0:T(8,128)(2,1)S(1)} %pad_maximum_fusion.refs_5_), channel_id=1, source_target_pairs={{0,1},{1,0},{2,3},{3,2},{4,5},{5,4},{6,7},{7,6},{8,9},{9,8},{10,11... | collective-permute-start | bytes 786440 | tf_op jit(solution)/shard_map/ppermute | solution.py:296
  26.1 9.0 %collective-permute-start.11 = (bf16[4,128,256]{2,1,0:T(8,128)(2,1)S(1)}, bf16[4,128,256]{2,1,0:T(8,128)(2,1)S(1)}, u32[]{:S(2)}, u32[]{:S(2)}) collective-permute-start(bf16[4,128,256]{2,1,0:T(8,128)(2,1)S(1)} %collective-permute-done.9.refs_9_), channel_id=1, source_target_pairs={{0,1},{1,0},{2,3},{3,2},{4,5},{5,4},{6,7},{7,6},{8,9},{9,8},{10,11... | collective-permute-start | bytes 786440 | tf_op jit(solution)/shard_map/ppermute | solution.py:296
  26.7 9.9 %copy-start.2 = (s32[32]{0:T(128)S(1)}, s32[32]{0:T(128)}, u32[]{:S(2)}) copy-start(s32[32]{0:T(128)} %refs_0_.1) | copy-start | bytes 388
  26.7 9.1 %collective-permute-start.2 = (bf16[128,1024]{1,0:T(8,128)(2,1)}, bf16[128,1024]{1,0:T(8,128)(2,1)S(1)}, u32[]{:S(2)}, u32[]{:S(2)}) collective-permute-start(bf16[128,1024]{1,0:T(8,128)(2,1)} %get-tuple-element.31), channel_id=1, source_target_pairs={{0,24},{4,28},{8,16},{12,20},{16,8},{20,12},{24,0},{28,4},{1,25},{... | collective-permute-start | bytes 786440 | tf_op jit(solution)/shard_map/ppermute | solution.py:296
  27.7 8.1 %collective-permute-start.6 = (bf16[4,128,256]{2,1,0:T(8,128)(2,1)S(1)}, bf16[4,128,256]{2,1,0:T(8,128)(2,1)S(1)}, u32[]{:S(2)}, u32[]{:S(2)}) collective-permute-start(bf16[4,128,256]{2,1,0:T(8,128)(2,1)S(1)} %pad_maximum_fusion.refs_5_), channel_id=1, source_target_pairs={{0,4},{4,0},{8,12},{12,8},{16,20},{20,16},{24,28},{28,24},{1,5},{5... | collective-permute-start | bytes 786440 | tf_op jit(solution)/shard_map/ppermute | solution.py:296
  27.7 8.1 %collective-permute-start.10 = (bf16[4,128,256]{2,1,0:T(8,128)(2,1)S(1)}, bf16[4,128,256]{2,1,0:T(8,128)(2,1)S(1)}, u32[]{:S(2)}, u32[]{:S(2)}) collective-permute-start(bf16[4,128,256]{2,1,0:T(8,128)(2,1)S(1)} %collective-permute-done.9.refs_9_), channel_id=1, source_target_pairs={{0,4},{4,0},{8,12},{12,8},{16,20},{20,16},{24,28},{28,24},{1,5},{5... | collective-permute-start | bytes 786440 | tf_op jit(solution)/shard_map/ppermute | solution.py:296
  31.1 4.7 %collective-permute-start.8 = (bf16[4,128,256]{2,1,0:T(8,128)(2,1)S(1)}, bf16[4,128,256]{2,1,0:T(8,128)(2,1)S(1)}, u32[]{:S(2)}, u32[]{:S(2)}) collective-permute-start(bf16[4,128,256]{2,1,0:T(8,128)(2,1)S(1)} %collective-permute-done.7.refs_7_), channel_id=1, source_target_pairs={{0,4},{4,0},{8,12},{12,8},{16,20},{20,16},{24,28},{28,24},{1,5},{5... | collective-permute-start | bytes 786440 | tf_op jit(solution)/shard_map/ppermute | solution.py:296
  35.0 1.5 %collective-permute-start.12 = (bf16[4,128,256]{2,1,0:T(8,128)(2,1)S(1)}, bf16[4,128,256]{2,1,0:T(8,128)(2,1)S(1)}, u32[]{:S(2)}, u32[]{:S(2)}) collective-permute-start(bf16[4,128,256]{2,1,0:T(8,128)(2,1)S(1)} %collective-permute-done.11.refs_11_), channel_id=1, source_target_pairs={{0,4},{4,0},{8,12},{12,8},{16,20},{20,16},{24,28},{28,24},{1,5},{5... | collective-permute-start | bytes 786440 | tf_op jit(solution)/shard_map/ppermute | solution.py:296
  36.6 1.0 %copy-start.1 = (bf16[128,1024]{1,0:T(8,128)(2,1)S(1)}, bf16[128,1024]{1,0:T(8,128)(2,1)}, u32[]{:S(2)}) copy-start(bf16[128,1024]{1,0:T(8,128)(2,1)} %get-tuple-element.28.refs_1_) | copy-start | bytes 786436
  56.9 1.7 %copy-start = (bf16[128,1024]{1,0:T(8,128)(2,1)}, bf16[128,1024]{1,0:T(8,128)(2,1)S(1)}, u32[]{:S(2)}) copy-start(bf16[128,1024]{1,0:T(8,128)(2,1)S(1)} %get-tuple-element.36.refs_0_) | copy-start | bytes 786436
  56.9 1.6 %collective-permute-start.20 = (bf16[4,128,256]{2,1,0:T(8,128)(2,1)S(1)}, bf16[4,128,256]{2,1,0:T(8,128)(2,1)S(1)}, u32[]{:S(2)}, u32[]{:S(2)}) collective-permute-start(bf16[4,128,256]{2,1,0:T(8,128)(2,1)S(1)} %get-tuple-element.49), channel_id=1, source_target_pairs={{0,4},{4,0},{8,12},{12,8},{16,20},{20,16},{24,28},{28,24},{1,5},{5... | collective-permute-start | bytes 786440 | tf_op jit(solution)/shard_map/ppermute | solution.py:296
  57.0 1.9 %collective-permute-start.17 = (bf16[4,128,256]{2,1,0:T(8,128)(2,1)S(1)}, bf16[4,128,256]{2,1,0:T(8,128)(2,1)S(1)}, u32[]{:S(2)}, u32[]{:S(2)}) collective-permute-start(bf16[4,128,256]{2,1,0:T(8,128)(2,1)S(1)} %get-tuple-element.45), channel_id=1, source_target_pairs={{0,4},{4,0},{8,12},{12,8},{16,20},{20,16},{24,28},{28,24},{1,5},{5... | collective-permute-start | bytes 786440 | tf_op jit(solution)/shard_map/ppermute | solution.py:296
  57.5 3.3 %collective-permute-start.19 = (bf16[4,128,256]{2,1,0:T(8,128)(2,1)S(1)}, bf16[4,128,256]{2,1,0:T(8,128)(2,1)S(1)}, u32[]{:S(2)}, u32[]{:S(2)}) collective-permute-start(bf16[4,128,256]{2,1,0:T(8,128)(2,1)S(1)} %get-tuple-element.47), channel_id=1, source_target_pairs={{0,4},{4,0},{8,12},{12,8},{16,20},{20,16},{24,28},{28,24},{1,5},{5... | collective-permute-start | bytes 786440 | tf_op jit(solution)/shard_map/ppermute | solution.py:296
  58.6 9.2 %collective-permute-start.21 = (bf16[4,128,256]{2,1,0:T(8,128)(2,1)S(1)}, bf16[4,128,256]{2,1,0:T(8,128)(2,1)S(1)}, u32[]{:S(2)}, u32[]{:S(2)}) collective-permute-start(bf16[4,128,256]{2,1,0:T(8,128)(2,1)S(1)} %add_convert_fusion.2), channel_id=1, source_target_pairs={{0,1},{1,0},{2,3},{3,2},{4,5},{5,4},{6,7},{7,6},{8,9},{9,8},{10,11... | collective-permute-start | bytes 786440 | tf_op jit(solution)/shard_map/ppermute | solution.py:296
  58.6 15.3 %collective-permute-start.16 = (bf16[4,128,256]{2,1,0:T(8,128)(2,1)S(1)}, bf16[4,128,256]{2,1,0:T(8,128)(2,1)S(1)}, u32[]{:S(2)}, u32[]{:S(2)}) collective-permute-start(bf16[4,128,256]{2,1,0:T(8,128)(2,1)S(1)} %get-tuple-element.43), channel_id=1, source_target_pairs={{0,4},{4,0},{8,12},{12,8},{16,20},{20,16},{24,28},{28,24},{1,5},{5... | collective-permute-start | bytes 786440 | tf_op jit(solution)/shard_map/ppermute | solution.py:296
  58.9 18.3 %collective-permute-start.18 = (bf16[4,128,256]{2,1,0:T(8,128)(2,1)S(1)}, bf16[4,128,256]{2,1,0:T(8,128)(2,1)S(1)}, u32[]{:S(2)}, u32[]{:S(2)}) collective-permute-start(bf16[4,128,256]{2,1,0:T(8,128)(2,1)S(1)} %add_convert_fusion.3), channel_id=1, source_target_pairs={{0,1},{1,0},{2,3},{3,2},{4,5},{5,4},{6,7},{7,6},{8,9},{9,8},{10,11... | collective-permute-start | bytes 786440 | tf_op jit(solution)/shard_map/ppermute | solution.py:296
  67.9 15.2 %collective-permute-start.22 = (bf16[4,128,256]{2,1,0:T(8,128)(2,1)S(1)}, bf16[4,128,256]{2,1,0:T(8,128)(2,1)S(1)}, u32[]{:S(2)}, u32[]{:S(2)}) collective-permute-start(bf16[4,128,256]{2,1,0:T(8,128)(2,1)S(1)} %add_convert_fusion.1), channel_id=1, source_target_pairs={{0,2},{1,3},{2,0},{3,1},{4,6},{5,7},{6,4},{7,5},{8,10},{9,11},{10,... | collective-permute-start | bytes 786440 | tf_op jit(solution)/shard_map/ppermute | solution.py:296
  72.4 13.8 %collective-permute-start.13 = (bf16[128,1024]{1,0:T(8,128)(2,1)S(1)}, bf16[128,1024]{1,0:T(8,128)(2,1)S(1)}, u32[]{:S(2)}, u32[]{:S(2)}) collective-permute-start(bf16[128,1024]{1,0:T(8,128)(2,1)S(1)} %get-tuple-element.37), channel_id=1, source_target_pairs={{0,8},{4,12},{8,0},{12,4},{16,24},{20,28},{24,16},{28,20},{1,9},{5... | collective-permute-start | bytes 786440 | tf_op jit(solution)/shard_map/ppermute | solution.py:296
  73.3 14.0 %collective-permute-start.14 = (bf16[128,1024]{1,0:T(8,128)(2,1)S(1)}, bf16[128,1024]{1,0:T(8,128)(2,1)S(1)}, u32[]{:S(2)}, u32[]{:S(2)}) collective-permute-start(bf16[128,1024]{1,0:T(8,128)(2,1)S(1)} %get-tuple-element.38), channel_id=1, source_target_pairs={{0,16},{4,20},{8,24},{12,28},{16,0},{20,4},{24,8},{28,12},{1,17},{... | collective-permute-start | bytes 786440 | tf_op jit(solution)/shard_map/ppermute | solution.py:296
  74.0 13.4 %collective-permute-start.15 = (bf16[128,1024]{1,0:T(8,128)(2,1)S(1)}, bf16[128,1024]{1,0:T(8,128)(2,1)S(1)}, u32[]{:S(2)}, u32[]{:S(2)}) collective-permute-start(bf16[128,1024]{1,0:T(8,128)(2,1)S(1)} %get-tuple-element.39), channel_id=1, source_target_pairs={{0,24},{4,28},{8,16},{12,20},{16,8},{20,12},{24,0},{28,4},{1,25},{... | collective-permute-start | bytes 786440 | tf_op jit(solution)/shard_map/ppermute | solution.py:296
  83.8 6.5 %collective-permute-start.25 = (bf16[128,256]{1,0:T(8,128)(2,1)S(1)}, bf16[128,256]{1,0:T(8,128)(2,1)S(1)}, u32[]{:S(2)}, u32[]{:S(2)}) collective-permute-start(bf16[128,256]{1,0:T(8,128)(2,1)S(1)} %get-tuple-element.52), channel_id=1, source_target_pairs={{0,24},{4,28},{8,16},{12,20},{16,8},{20,12},{24,0},{28,4},{1,25},{... | collective-permute-start | bytes 196616 | tf_op jit(solution)/shard_map/ppermute | solution.py:296
  84.8 5.6 %collective-permute-start.24 = (bf16[128,256]{1,0:T(8,128)(2,1)S(1)}, bf16[128,256]{1,0:T(8,128)(2,1)S(1)}, u32[]{:S(2)}, u32[]{:S(2)}) collective-permute-start(bf16[128,256]{1,0:T(8,128)(2,1)S(1)} %get-tuple-element.53), channel_id=1, source_target_pairs={{0,16},{4,20},{8,24},{12,28},{16,0},{20,4},{24,8},{28,12},{1,17},{... | collective-permute-start | bytes 196616 | tf_op jit(solution)/shard_map/ppermute | solution.py:296
  86.2 1.1 %copy-start.3 = (bf16[128,1024]{1,0:T(8,128)(2,1)}, bf16[128,1024]{1,0:T(8,128)(2,1)S(1)}, u32[]{:S(2)}) copy-start(bf16[128,1024]{1,0:T(8,128)(2,1)S(1)} %collective-permute-done.13.refs_1_) | copy-start | bytes 786436
  86.2 4.3 %collective-permute-start.23 = (bf16[128,256]{1,0:T(8,128)(2,1)S(1)}, bf16[128,256]{1,0:T(8,128)(2,1)S(1)}, u32[]{:S(2)}, u32[]{:S(2)}) collective-permute-start(bf16[128,256]{1,0:T(8,128)(2,1)S(1)} %get-tuple-element.54), channel_id=1, source_target_pairs={{0,8},{4,12},{8,0},{12,4},{16,24},{20,28},{24,16},{28,20},{1,9},{5... | collective-permute-start | bytes 196616 | tf_op jit(solution)/shard_map/ppermute | solution.py:296
  87.3 0.7 copy-start.4
  87.3 0.8 copy-start.5
  90.4 0.6 copy-start.6
  90.4 0.6 copy-start.7
  90.5 0.6 copy-start.8

commit v2 on v0

--- a/solution.py
+++ b/solution.py
@@ -1,6 +1,11 @@
+import functools
+import math
+
 import jax
 import jax.numpy as jnp
 from jax import lax
+from jax.experimental import pallas as pl
+from jax.experimental.pallas import tpu as pltpu
 from jax.sharding import PartitionSpec as P
 
 QH = 16
@@ -279,22 +284,339 @@
     return (attn_out, grad_queries, token_grads[0], token_grads[1])
 
 
+CHUNKS = ((0, 1, 2, 3),)
+CONTRACT_LAST = (((1,), (1,)), ((), ()))
+CONTRACT_FIRST = (((0,), (0,)), ((), ()))
+VMEM = pl.BlockSpec(memory_space=pltpu.VMEM)
+SMEM = pl.BlockSpec(memory_space=pltpu.SMEM)
+
+
+def flipped(value, axis, bits):
+    count = lax.axis_size(axis)
+    return lax.ppermute(value, axis, [(source, source ^ bits) for source in range(count)])
+
+
+def pack_heads_kernel(cores, wide, left_ref, right_ref, *out_refs):
+    part = lax.axis_index("ctx") // cores
+    for flip, out_ref in enumerate(out_refs):
+        columns = pl.ds(pl.multiple_of((part ^ flip) * wide, HD), wide)
+        out_ref[:, :wide] = left_ref[:, columns]
+        out_ref[:, wide:] = right_ref[:, columns]
+
+
+def unpack_heads_kernel(cores, wide, *refs):
+    in_refs, (left_ref, right_ref) = refs[:KVH], refs[KVH:]
+    part = lax.axis_index("ctx") // cores
+    for flip, in_ref in enumerate(in_refs):
+        columns = pl.ds(pl.multiple_of((part ^ flip) * wide, HD), wide)
+        left_ref[:, columns] = in_ref[:, :wide]
+        right_ref[:, columns] = in_ref[:, wide:]
+
+
+def pack_heads(left, right, cores):
+    rows, wide = left.shape[0], left.shape[1] // KVH
+    return pl.pallas_call(
+        functools.partial(pack_heads_kernel, cores, wide),
+        out_shape=[jax.ShapeDtypeStruct((rows, 2 * wide), left.dtype)] * KVH,
+        in_specs=[VMEM] * 2,
+        out_specs=[VMEM] * KVH,
+    )(left, right)
+
+
+def unpack_heads(pieces, cores):
+    rows, wide = pieces[0].shape[0], pieces[0].shape[1] // 2
+    return pl.pallas_call(
+        functools.partial(unpack_heads_kernel, cores, wide),
+        out_shape=[jax.ShapeDtypeStruct((rows, wide * KVH), pieces[0].dtype)] * 2,
+        in_specs=[VMEM] * KVH,
+        out_specs=[VMEM] * 2,
+    )(*pieces)
+
+
+KEY_ROWS = 256
+BATCH = 4
+GRAD_BATCH = 4
+MARKS = 128
+HIDDEN = -(2.0**100)
+
+
+def attention_kernel(cores, heads, tok, *refs):
+    group = QH // KVH
+    lanes = group * tok
+    tile_rows = heads * tok
+    kv_count = heads * cores * len(CHUNKS)
+    lengths_ref, marks_ref, refs = refs[0], refs[1], refs[2:]
+    docs = lengths_ref.shape[0]
+    qd_refs, refs = refs[:KVH], refs[KVH:]
+    kv_refs, refs = refs[:kv_count], refs[kv_count:]
+    od_refs, refs = refs[:KVH], refs[KVH:]
+    dkv_refs, refs = refs[: cores * len(CHUNKS)], refs[cores * len(CHUNKS) :]
+    k_all, v_all, q_wide, g_wide, dk_acc, dv_acc, score, prob, tops, acc, table = refs
+    scaling = HD ** (-0.5)
+    log_scale = scaling * math.log2(math.e)
+    f32, bf16 = jnp.float32, jnp.bfloat16
+
+    ctx_index, head_index = lax.axis_index("ctx"), lax.axis_index("head")
+    part, core = ctx_index // cores, ctx_index % cores
+
+    def rows_of(head_flip, core_flip, part_flip):
+        tile = (part ^ part_flip) * cores + (core ^ core_flip)
+        return pl.ds(pl.multiple_of((tile * heads + (head_index ^ head_flip)) * tok, tok), tok)
+
+    for chunk_number, chunk in enumerate(CHUNKS):
+        for number in range(heads * cores):
+            kv_ref = kv_refs[chunk_number * heads * cores + number]
+            for place, flip in enumerate(chunk):
+                rows = rows_of(number // cores, number % cores, flip)
+                k_all[rows, :] = kv_ref[place, :, :HD]
+                v_all[rows, :] = kv_ref[place, :, HD:]
+    feature = lax.broadcasted_iota(jnp.int32, (tok, MARKS), 1)
+    for flip, qd_ref in enumerate(qd_refs):
+        own_marks = marks_ref[rows_of(0, 0, flip), :].astype(f32)
+        bias = jnp.where(feature < docs, (1.0 - own_marks) * HIDDEN, 0.0).astype(bf16)
+        for member in range(group):
+            rows = slice(member * tok, (member + 1) * tok)
+            q_wide[flip, rows, :HD] = qd_ref[:, member * HD : (member + 1) * HD]
+            q_wide[flip, rows, HD:] = bias
+            g_wide[flip, rows, :HD] = qd_ref[:, (group + member) * HD : (group + member + 1) * HD]
+    dk_acc[...] = jnp.zeros_like(dk_acc)
+    dv_acc[...] = jnp.zeros_like(dv_acc)
+    tops[...] = jnp.full_like(tops, NEG_FILL)
+    acc[...] = jnp.zeros_like(acc)
+
+    def entry(number, flip, row, limit):
+        table[0, number] = flip
+        table[1, number] = row
+        table[2, number] = limit
+
+    total = jnp.int32(0)
+    for flip in range(KVH):
+        first = ((part ^ flip) * cores + core) * tile_rows + head_index * tok
+        end, low = jnp.int32(0), jnp.int32(0)
+        for number in range(docs):
+            length = lengths_ref[number]
+            end = end + length
+            low = low + jnp.where(end <= first, length, 0)
+        count = (first + tok - low // tok * tok + KEY_ROWS - 1) // KEY_ROWS
+        begin = jnp.maximum(first + tok - count * KEY_ROWS, 0)
+
+        def listed(step, _, flip=flip, first=first, begin=begin, total=total):
+            row = begin + step * KEY_ROWS
+            entry(total + step, flip, row, first - row)
+            return 0
+
+        lax.fori_loop(0, count, listed, 0)
+        total = total + count
+    for spare in range(BATCH - 1):
+        entry(total + spare, 0, 0, -(1 << 20))
+    rounds = (total + BATCH - 1) // BATCH
+
+    def sweep(body, batch):
+        def one_round(number, _):
+            body([number * batch + place for place in range(batch)])
+            return 0
+
+        lax.fori_loop(0, rounds * (BATCH // batch), one_round, 0)
+
+    def key_rows(item):
+        return pl.ds(pl.multiple_of(table[1, item], tok), KEY_ROWS)
+
+    def score_rows(item):
+        return pl.ds(pl.multiple_of(item * KEY_ROWS, KEY_ROWS), KEY_ROWS)
+
+    def wide(ref, rows):
+        return jnp.concatenate([ref[rows, :], marks_ref[rows, :]], axis=1)
+
+    key_row = lax.broadcasted_iota(jnp.int32, (KEY_ROWS, lanes), 0)
+    query_row = lax.broadcasted_iota(jnp.int32, (1, lanes), 1) % tok
+
+    def scores_round(items):
+        raws = [
+            lax.dot_general(
+                wide(k_all, key_rows(item)),
+                q_wide[table[0, item]],
+                CONTRACT_LAST,
+                preferred_element_type=f32,
+            )
+            for item in items
+        ]
+        for item, raw in zip(items, raws):
+            raw = jnp.where(key_row <= query_row + table[2, item], raw, NEG_FILL)
+            score[score_rows(item), :] = raw
+            flip = table[0, item]
+            tops[flip] = jnp.maximum(
+                tops[flip], jnp.max(raw.reshape(KEY_ROWS // 8, 8, lanes), axis=0)
+            )
+
+    sweep(scores_round, BATCH)
+    for flip in range(KVH):
+        tops[flip] = jnp.broadcast_to(jnp.max(tops[flip], axis=0, keepdims=True), (8, lanes))
+
+    ones = jnp.ones((acc.shape[1] - HD, KEY_ROWS), bf16)
+
+    def out_round(items):
+        weights = [
+            jnp.exp2((score[score_rows(item), :] - tops[table[0, item], :1]) * log_scale).astype(bf16)
+            for item in items
+        ]
+        for item, weight in zip(items, weights):
+            prob[score_rows(item), :] = weight
+        parts = [
+            jnp.dot(
+                jnp.concatenate([v_all[key_rows(item), :].T, ones], axis=0),
+                weight,
+                preferred_element_type=f32,
+            )
+            for item, weight in zip(items, weights)
+        ]
+        for item, value in zip(items, parts):
+            acc[table[0, item]] += value
+
+    sweep(out_round, BATCH)
+    feature = lax.broadcasted_iota(jnp.int32, (lanes, MARKS), 1)
+    for flip in range(KVH):
+        inverse = 1.0 / acc[flip, HD : HD + 1, :]
+        out = (acc[flip, :HD, :] * inverse).T.astype(bf16)
+        g = g_wide[flip, :, :HD].astype(f32)
+        g_scaled = (g * jnp.broadcast_to(inverse, (HD, lanes)).T).astype(bf16)
+        delta = jnp.sum(out.astype(f32) * g_scaled.astype(f32), axis=1, keepdims=True)
+        high = delta.astype(bf16).astype(f32)
+        extra = jnp.where(feature == docs, -high, jnp.where(feature == docs + 1, high - delta, 0.0))
+        g_wide[flip, :, :HD] = g_scaled
+        g_wide[flip, :, HD:] = extra.astype(bf16)
+        for member in range(group):
+            rows = slice(member * tok, (member + 1) * tok)
+            od_refs[flip][:, member * HD : (member + 1) * HD] = out[rows, :]
+        acc[flip] = jnp.zeros_like(acc[flip])
+
+    def grad_round(items):
+        weights = [prob[score_rows(item), :] for item in items]
+        slopes = [
+            lax.dot_general(
+                wide(v_all, key_rows(item)),
+                g_wide[table[0, item]],
+                CONTRACT_LAST,
+                preferred_element_type=f32,
+            )
+            for item in items
+        ]
+        score_grads = [
+            (weight.astype(f32) * slope).astype(bf16) for weight, slope in zip(weights, slopes)
+        ]
+        for item, weight, score_grad in zip(items, weights, score_grads):
+            flip, rows = table[0, item], key_rows(item)
+            dv_acc[rows, :] += jnp.dot(weight, g_wide[flip, :, :HD], preferred_element_type=f32)
+            dk_acc[rows, :] += jnp.dot(score_grad, q_wide[flip, :, :HD], preferred_element_type=f32)
+            acc[flip, :HD, :] += lax.dot_general(
+                k_all[rows, :], score_grad, CONTRACT_FIRST, preferred_element_type=f32
+            )
+
+    sweep(grad_round, GRAD_BATCH)
+
+    for flip, od_ref in enumerate(od_refs):
+        turned = (acc[flip, :HD, :] * scaling).T.astype(bf16)
+        for member in range(group):
+            rows = slice(member * tok, (member + 1) * tok)
+            od_ref[:, (group + member) * HD : (group + member + 1) * HD] = turned[rows, :]
+    for chunk_number, chunk in enumerate(CHUNKS):
+        for core_flip in range(cores):
+            dkv_ref = dkv_refs[chunk_number * cores + core_flip]
+            for head_flip in range(heads):
+                for place, flip in enumerate(chunk):
+                    rows = rows_of(head_flip, core_flip, flip)
+                    dkv_ref[head_flip, place, :, :HD] = (dk_acc[rows, :] * scaling).astype(bf16)
+                    dkv_ref[head_flip, place, :, HD:] = dv_acc[rows, :].astype(bf16)
+
+
+def document_marks(lengths, total):
+    docs = lengths.shape[0]
+    ends = jnp.cumsum(lengths)
+    begins = jnp.pad(ends - lengths, (0, MARKS - docs))
+    lane = jnp.arange(MARKS)
+    ends = jnp.where(lane < docs, jnp.pad(ends, (0, MARKS - docs)), jnp.where(lane < docs + 2, total, 0))
+    position = jnp.arange(total, dtype=jnp.int32)[:, None]
+    return ((position >= begins[None, :]) & (position < ends[None, :])).astype(jnp.bfloat16)
+
+
+def attention(lengths, qd, kv, cores, heads):
+    tok, group = qd[0].shape[0], QH // KVH
+    total = KVH * cores * heads * tok
+    lanes = group * tok
+    reach = REACH * heads * tok
+    pair = sum(-(-(keys + tok) // KEY_ROWS) for keys in (reach, reach // 2))
+    items = -(-KVH // 2 * pair // BATCH) * BATCH
+    bf16, f32 = jnp.bfloat16, jnp.float32
+    results = pl.pallas_call(
+        functools.partial(attention_kernel, cores, heads, tok),
+        out_shape=[jax.ShapeDtypeStruct(a.shape, a.dtype) for a in qd]
+        + [
+            jax.ShapeDtypeStruct((heads, len(chunk), tok, 2 * HD), bf16)
+            for chunk in CHUNKS
+            for _ in range(cores)
+        ],
+        in_specs=[SMEM] + [VMEM] * (1 + len(qd) + len(kv)),
+        out_specs=[VMEM] * (len(qd) + cores * len(CHUNKS)),
+        scratch_shapes=[
+            pltpu.VMEM((total, HD), bf16),
+            pltpu.VMEM((total, HD), bf16),
+            pltpu.VMEM((KVH, lanes, HD + MARKS), bf16),
+            pltpu.VMEM((KVH, lanes, HD + MARKS), bf16),
+            pltpu.VMEM((total, HD), f32),
+            pltpu.VMEM((total, HD), f32),
+            pltpu.VMEM((items * KEY_ROWS, lanes), f32),
+            pltpu.VMEM((items * KEY_ROWS, lanes), bf16),
+            pltpu.VMEM((KVH, 8, lanes), f32),
+            pltpu.VMEM((KVH, HD + 16, lanes), f32),
+            pltpu.SMEM((3, items + BATCH), jnp.int32),
+        ],
+        compiler_params=pltpu.CompilerParams(vmem_limit_bytes=48 * 1024 * 1024),
+    )(lengths, document_marks(lengths, total), *qd, *kv)
+    return results[: len(qd)], results[len(qd) :]
+
+
+def part_shards(queries, keys, values, d_out, lengths):
+    heads = lax.axis_size("head")
+    cores = lax.axis_size("ctx") // KVH
+
+    def exchange(pieces):
+        return [pieces[0]] + [flipped(pieces[s], "ctx", s * cores) for s in range(1, KVH)]
+
+    pieces = exchange(pack_heads(keys, values, cores))
+    qd = exchange(pack_heads(queries, d_out, cores))
+    kv = []
+    for chunk in CHUNKS:
+        own = jnp.stack([pieces[flip] for flip in chunk])
+        far = flipped(own, "head", 2)
+        near = flipped(own, "head", 1)
+        for piece in (own, near, far, flipped(far, "head", 1)):
+            kv += [piece, flipped(piece, "ctx", 1)]
+    od, dkv = attention(lengths, qd, kv, cores, heads)
+
+    def summed(*terms):
+        return sum(term.astype(jnp.float32) for term in terms).astype(jnp.bfloat16)
+
+    grads = [None] * KVH
+    for number in reversed(range(len(CHUNKS))):
+        both = (dkv[number * cores], flipped(dkv[number * cores + 1], "ctx", 1))
+        third = flipped(summed(*(term[3] for term in both)), "head", 1)
+        second = flipped(summed(*(term[2] for term in both), third), "head", 2)
+        first, _ = lax.optimization_barrier((summed(*(term[1] for term in both)), third))
+        first = flipped(first, "head", 1)
+        for place, flip in enumerate(CHUNKS[number]):
+            grads[flip] = summed(*(term[0, place] for term in both), first[place], second[place])
+    attn_out, grad_queries = unpack_heads(exchange(od), cores)
+    grad_keys, grad_values = unpack_heads(exchange(grads), cores)
+    return attn_out, grad_queries, grad_keys, grad_values
+
+
 def solution(mesh):
+    ctx_dev, head_dev = mesh.shape["ctx"], mesh.shape["head"]
+    local = part_shards if ctx_dev == 2 * KVH and head_dev == 4 else shards
+    rows = P(("ctx", "head"), None)
     return jax.shard_map(
-        shards,
+        local,
         mesh=mesh,
-        in_specs=(
-            P(("ctx", "head"), None),
-            P(("ctx", "head"), None),
-            P(("ctx", "head"), None),
-            P(("ctx", "head"), None),
-            P(),
-        ),
-        out_specs=(
-            P(("ctx", "head"), None),
-            P(("ctx", "head"), None),
-            P(("ctx", "head"), None),
-            P(("ctx", "head"), None),
-        ),
+        in_specs=(rows, rows, rows, rows, P()),
+        out_specs=(rows, rows, rows, rows),
         check_vma=False,
     )

time: 185 us -> 88.1 us (0.48)
  the two profiles are of different devices: /device:TPU:6 before, /device:TPU:0 now
where the time goes in v2:
time: 88.1 us; the launch traced here: 88 us
  waiting for transfers between devices  38.1 us (43%)
  Pallas kernels  23.8 us (27%)
  starting transfers between devices  20.4 us (23%)
  other arithmetic  3.43 us (4%)
  local copies, waits for them, and re-layouts  1.51 us (2%)
    ppermute x23, waiting for transfers between devices, flipped(): lax.ppermute(value, axis, [(source, source ^ bits) for source in range(co...  38.1 us
    ppermute x23, starting transfers between devices, flipped(): lax.ppermute(value, axis, [(source, source ^ bits) for source in range(co...  20.4 us
    pallas_call x1, Pallas kernels, attention(): pl.pallas_call(functools.partial(attention_kernel, cores, heads, tok), ou...  15.9 us
    pallas_call x2, Pallas kernels, pack_heads(): pl.pallas_call(functools.partial(pack_heads_kernel, cores, wide), out_sha...  3.95 us
    pallas_call x2, Pallas kernels, unpack_heads(): pl.pallas_call(functools.partial(unpack_heads_kernel, cores, wide), out_s...  3.91 us
  transfers between devices with their start and end apart: 23, of which 11 were waited for; matrix products, arithmetic and copies ran while one was open for 3% of the time, Pallas kernels for 5%

profile of v2, /device:TPU:0, one launch (start us, length us, event | category | flops | bytes accessed | tf_op | source)
XLA Modules:
  0.0 88.0 jit_solution(800904347539869872)
XLA Ops:
  0.6 1.7 %shard_map.85 = (bf16[128,256]{1,0:T(8,128)(2,1)}, bf16[128,256]{1,0:T(8,128)(2,1)}, bf16[128,256]{1,0:T(8,128)(2,1)}, bf16[128,256]{1,0:T(8,128)(2,1)}) custom-call(bf16[128,512]{1,0:T(8,128)(2,1)} %left_ref.3, bf16[128,512]{1,0:T(8,128)(2,1)} %right_ref.3), custom_call_target="tpu_custom_call" | custom-call | tf_op jit(solution)/shard_map/pallas_call | solution.py:318
  2.4 2.9 %collective-permute-start.3 = (bf16[128,256]{1,0:T(8,128)(2,1)}, bf16[128,256]{1,0:T(8,128)(2,1)S(1)}, u32[]{:S(2)}, u32[]{:S(2)}) collective-permute-start(bf16[128,256]{1,0:T(8,128)(2,1)} %get-tuple-element.28), channel_id=1, source_target_pairs={{0,8},{4,12},{8,0},{12,4},{16,24},{20,28},{24,16},{28,20},{1,9},{5... | collective-permute-start | bytes 196616 | tf_op jit(solution)/shard_map/ppermute | solution.py:296
  5.3 1.5 %collective-permute-start.4 = (bf16[128,256]{1,0:T(8,128)(2,1)}, bf16[128,256]{1,0:T(8,128)(2,1)S(1)}, u32[]{:S(2)}, u32[]{:S(2)}) collective-permute-start(bf16[128,256]{1,0:T(8,128)(2,1)} %get-tuple-element.29), channel_id=1, source_target_pairs={{0,16},{4,20},{8,24},{12,28},{16,0},{20,4},{24,8},{28,12},{1,17},{... | collective-permute-start | bytes 196616 | tf_op jit(solution)/shard_map/ppermute | solution.py:296
  6.8 1.2 %collective-permute-done.3 = bf16[128,256]{1,0:T(8,128)(2,1)S(1)} collective-permute-done((bf16[128,256]{1,0:T(8,128)(2,1)}, bf16[128,256]{1,0:T(8,128)(2,1)S(1)}, u32[]{:S(2)}, u32[]{:S(2)}) %collective-permute-start.3) | collective-permute-done | bytes 65568 | tf_op jit(solution)/shard_map/ppermute | solution.py:296
  8.0 1.8 %collective-permute-done.4 = bf16[128,256]{1,0:T(8,128)(2,1)S(1)} collective-permute-done((bf16[128,256]{1,0:T(8,128)(2,1)}, bf16[128,256]{1,0:T(8,128)(2,1)S(1)}, u32[]{:S(2)}, u32[]{:S(2)}) %collective-permute-start.4) | collective-permute-done | bytes 65568 | tf_op jit(solution)/shard_map/ppermute | solution.py:296
  9.8 2.4 %collective-permute-done.5 = bf16[128,256]{1,0:T(8,128)(2,1)S(1)} collective-permute-done((bf16[128,256]{1,0:T(8,128)(2,1)}, bf16[128,256]{1,0:T(8,128)(2,1)S(1)}, u32[]{:S(2)}, u32[]{:S(2)}) %collective-permute-start.5) | collective-permute-done | bytes 65568 | tf_op jit(solution)/shard_map/ppermute | solution.py:296
  12.2 0.9 pad_maximum_fusion.refs_6_
  13.1 2.7 %collective-permute-start.9 = (bf16[4,128,256]{2,1,0:T(8,128)(2,1)S(1)}, bf16[4,128,256]{2,1,0:T(8,128)(2,1)S(1)}, u32[]{:S(2)}, u32[]{:S(2)}) collective-permute-start(bf16[4,128,256]{2,1,0:T(8,128)(2,1)S(1)} %pad_maximum_fusion.refs_6_), channel_id=1, source_target_pairs={{0,2},{1,3},{2,0},{3,1},{4,6},{5,7},{6,4},{7,5},{8,10},{9,11},{10,... | collective-permute-start | bytes 786440 | tf_op jit(solution)/shard_map/ppermute | solution.py:296
  15.7 2.2 %shard_map.84 = (bf16[128,1024]{1,0:T(8,128)(2,1)}, bf16[128,1024]{1,0:T(8,128)(2,1)}, bf16[128,1024]{1,0:T(8,128)(2,1)}, bf16[128,1024]{1,0:T(8,128)(2,1)}) custom-call(bf16[128,2048]{1,0:T(8,128)(2,1)} %left_ref.2, bf16[128,2048]{1,0:T(8,128)(2,1)} %right_ref.2), custom_call_target="tpu_custom_call" | custom-call | tf_op jit(solution)/shard_map/pallas_call | solution.py:318
  18.0 0.5 collective-permute-start
  18.5 0.5 collective-permute-start.1
  19.0 1.6 %collective-permute-start.7 = (bf16[4,128,256]{2,1,0:T(8,128)(2,1)S(1)}, bf16[4,128,256]{2,1,0:T(8,128)(2,1)S(1)}, u32[]{:S(2)}, u32[]{:S(2)}) collective-permute-start(bf16[4,128,256]{2,1,0:T(8,128)(2,1)S(1)} %pad_maximum_fusion.refs_6_), channel_id=1, source_target_pairs={{0,1},{1,0},{2,3},{3,2},{4,5},{5,4},{6,7},{7,6},{8,9},{9,8},{10,11... | collective-permute-start | bytes 786440 | tf_op jit(solution)/shard_map/ppermute | solution.py:296
  20.6 5.5 %collective-permute-done.9.refs_10_ = bf16[4,128,256]{2,1,0:T(8,128)(2,1)S(1)} collective-permute-done((bf16[4,128,256]{2,1,0:T(8,128)(2,1)S(1)}, bf16[4,128,256]{2,1,0:T(8,128)(2,1)S(1)}, u32[]{:S(2)}, u32[]{:S(2)}) %collective-permute-start.9) | collective-permute-done | bytes 262176 | tf_op jit(solution)/shard_map/ppermute | solution.py:296
  26.1 0.6 collective-permute-start.11
  26.7 1.0 %collective-permute-start.2 = (bf16[128,1024]{1,0:T(8,128)(2,1)}, bf16[128,1024]{1,0:T(8,128)(2,1)S(1)}, u32[]{:S(2)}, u32[]{:S(2)}) collective-permute-start(bf16[128,1024]{1,0:T(8,128)(2,1)} %get-tuple-element.26), channel_id=1, source_target_pairs={{0,24},{4,28},{8,16},{12,20},{16,8},{20,12},{24,0},{28,4},{1,25},{... | collective-permute-start | bytes 786440 | tf_op jit(solution)/shard_map/ppermute | solution.py:296
  27.7 0.1 copy.10
  27.8 0.1 reduce-window.9
  27.8 0.1 reduce
  28.0 0.1 collective-permute-start.6
  28.1 0.5 collective-permute-start.10
  28.6 2.5 %collective-permute-done.7.refs_8_ = bf16[4,128,256]{2,1,0:T(8,128)(2,1)S(1)} collective-permute-done((bf16[4,128,256]{2,1,0:T(8,128)(2,1)S(1)}, bf16[4,128,256]{2,1,0:T(8,128)(2,1)S(1)}, u32[]{:S(2)}, u32[]{:S(2)}) %collective-permute-start.7) | collective-permute-done | bytes 262176 | tf_op jit(solution)/shard_map/ppermute | solution.py:296
  31.1 4.0 %collective-permute-done.11.refs_12_ = bf16[4,128,256]{2,1,0:T(8,128)(2,1)S(1)} collective-permute-done((bf16[4,128,256]{2,1,0:T(8,128)(2,1)S(1)}, bf16[4,128,256]{2,1,0:T(8,128)(2,1)S(1)}, u32[]{:S(2)}, u32[]{:S(2)}) %collective-permute-start.11) | collective-permute-done | bytes 262176 | tf_op jit(solution)/shard_map/ppermute | solution.py:296
  35.0 1.4 %fusion.1.refs_1_ = bf16[4096,128]{1,0:T(8,128)(2,1)} fusion(s32[128]{0:T(128)S(1)} %compare_select_fusion.1, s32[128]{0:T(128)S(1)} %pad.7), kind=kLoop, calls=%fused_computation.3 | loop fusion | flops 2097152 | bytes 1049600 | tf_op jit(solution)/shard_map/convert_element_type | solution.py:538
  36.4 0.1 collective-permute-done.12.refs_13_
  36.6 15.9 %shard_map.86 = (bf16[128,1024]{1,0:T(8,128)(2,1)S(1)}, bf16[128,1024]{1,0:T(8,128)(2,1)S(1)}, bf16[128,1024]{1,0:T(8,128)(2,1)S(1)}, bf16[128,1024]{1,0:T(8,128...) custom-call(s32[32]{0:T(128)S(1)} %copy-done.2, bf16[4096,128]{1,0:T(8,128)(2,1)} %fusion.1.refs_1_, ...), custom_call_target="tpu_custom_call" | custom-call | tf_op jit(solution)/shard_map/pallas_call | solution.py:549
  52.5 2.9 %collective-permute-done.16 = bf16[4,4,128,256]{3,2,1,0:T(8,128)(2,1)S(1)} collective-permute-done((bf16[4,4,128,256]{3,2,1,0:T(8,128)(2,1)}, bf16[4,4,128,256]{3,2,1,0:T(8,128)(2,1)S(1)}, u32[]{:S(2)}, u32[]{:S(2)}) %collective-permute-start.16) | collective-permute-done | bytes 1048608 | tf_op jit(solution)/shard_map/ppermute | solution.py:296
  55.3 0.1 fusion.3
  55.5 0.1 collective-permute-start.17
  55.6 8.3 %collective-permute-done.17 = bf16[4,128,256]{2,1,0:T(8,128)(2,1)S(1)} collective-permute-done((bf16[4,128,256]{2,1,0:T(8,128)(2,1)S(1)}, bf16[4,128,256]{2,1,0:T(8,128)(2,1)S(1)}, u32[]{:S(2)}, u32[]{:S(2)}) %collective-permute-start.17) | collective-permute-done | bytes 262176 | tf_op jit(solution)/shard_map/ppermute | solution.py:296
  63.9 0.1 fusion.2
  64.0 0.1 collective-permute-start.19
  64.1 1.3 %collective-permute-start.18 = (bf16[4,128,256]{2,1,0:T(8,128)(2,1)S(1)}, bf16[4,128,256]{2,1,0:T(8,128)(2,1)S(1)}, u32[]{:S(2)}, u32[]{:S(2)}) collective-permute-start(bf16[4,128,256]{2,1,0:T(8,128)(2,1)S(1)} %get-tuple-element.39), channel_id=1, source_target_pairs={{0,1},{1,0},{2,3},{3,2},{4,5},{5,4},{6,7},{7,6},{8,9},{9,8},{10,11... | collective-permute-start | bytes 786440 | tf_op jit(solution)/shard_map/ppermute | solution.py:296
  65.4 0.9 %collective-permute-start.13 = (bf16[128,1024]{1,0:T(8,128)(2,1)S(1)}, bf16[128,1024]{1,0:T(8,128)(2,1)S(1)}, u32[]{:S(2)}, u32[]{:S(2)}) collective-permute-start(bf16[128,1024]{1,0:T(8,128)(2,1)S(1)} %get-tuple-element.32), channel_id=1, source_target_pairs={{0,8},{4,12},{8,0},{12,4},{16,24},{20,28},{24,16},{28,20},{1,9},{5... | collective-permute-start | bytes 786440 | tf_op jit(solution)/shard_map/ppermute | solution.py:296
  66.4 1.3 %collective-permute-start.14 = (bf16[128,1024]{1,0:T(8,128)(2,1)S(1)}, bf16[128,1024]{1,0:T(8,128)(2,1)S(1)}, u32[]{:S(2)}, u32[]{:S(2)}) collective-permute-start(bf16[128,1024]{1,0:T(8,128)(2,1)S(1)} %get-tuple-element.33), channel_id=1, source_target_pairs={{0,16},{4,20},{8,24},{12,28},{16,0},{20,4},{24,8},{28,12},{1,17},{... | collective-permute-start | bytes 786440 | tf_op jit(solution)/shard_map/ppermute | solution.py:296
  67.7 1.2 %collective-permute-start.15 = (bf16[128,1024]{1,0:T(8,128)(2,1)S(1)}, bf16[128,1024]{1,0:T(8,128)(2,1)S(1)}, u32[]{:S(2)}, u32[]{:S(2)}) collective-permute-start(bf16[128,1024]{1,0:T(8,128)(2,1)S(1)} %get-tuple-element.34), channel_id=1, source_target_pairs={{0,24},{4,28},{8,16},{12,20},{16,8},{20,12},{24,0},{28,4},{1,25},{... | collective-permute-start | bytes 786440 | tf_op jit(solution)/shard_map/ppermute | solution.py:296
  68.9 9.2 %collective-permute-done.19 = bf16[4,128,256]{2,1,0:T(8,128)(2,1)S(1)} collective-permute-done((bf16[4,128,256]{2,1,0:T(8,128)(2,1)S(1)}, bf16[4,128,256]{2,1,0:T(8,128)(2,1)S(1)}, u32[]{:S(2)}, u32[]{:S(2)}) %collective-permute-start.19) | collective-permute-done | bytes 262176 | tf_op jit(solution)/shard_map/ppermute | solution.py:296
  78.1 0.8 fusion.5
  78.9 2.0 %collective-permute-start.22 = (bf16[128,256]{1,0:T(8,128)(2,1)S(1)}, bf16[128,256]{1,0:T(8,128)(2,1)S(1)}, u32[]{:S(2)}, u32[]{:S(2)}) collective-permute-start(bf16[128,256]{1,0:T(8,128)(2,1)S(1)} %get-tuple-element.42), channel_id=1, source_target_pairs={{0,24},{4,28},{8,16},{12,20},{16,8},{20,12},{24,0},{28,4},{1,25},{... | collective-permute-start | bytes 196616 | tf_op jit(solution)/shard_map/ppermute | solution.py:296
  80.9 0.5 collective-permute-start.21
  81.4 1.0 %collective-permute-start.20 = (bf16[128,256]{1,0:T(8,128)(2,1)S(1)}, bf16[128,256]{1,0:T(8,128)(2,1)S(1)}, u32[]{:S(2)}, u32[]{:S(2)}) collective-permute-start(bf16[128,256]{1,0:T(8,128)(2,1)S(1)} %get-tuple-element.44), channel_id=1, source_target_pairs={{0,8},{4,12},{8,0},{12,4},{16,24},{20,28},{24,16},{28,20},{1,9},{5... | collective-permute-start | bytes 196616 | tf_op jit(solution)/shard_map/ppermute | solution.py:296
  82.4 0.7 copy-done.4
  83.1 0.1 copy-done.5
  83.2 2.2 %shard_map.87 = (bf16[128,2048]{1,0:T(8,128)(2,1)}, bf16[128,2048]{1,0:T(8,128)(2,1)}) custom-call(bf16[128,1024]{1,0:T(8,128)(2,1)} %copy-done.1, bf16[128,1024]{1,0:T(8,128)(2,1)} %copy-done.3, bf16[128,1024]{1,0:T(8,128)(2,1)} %copy-done.4, bf16[128,1024]{1,0:T(8,128)(2,1)} %copy-done.5), custom_call_target="tpu_custom_call" | custom-call | tf_op jit(solution)/shard_map/pallas_call | solution.py:328
  85.4 0.2 collective-permute-done.20.refs_1_
  85.7 0.4 copy-done.6
  86.0 0.0 copy-done.7
  86.1 0.2 copy-done.8
  86.3 1.7 %shard_map.88 = (bf16[128,512]{1,0:T(8,128)(2,1)}, bf16[128,512]{1,0:T(8,128)(2,1)}) custom-call(bf16[128,256]{1,0:T(8,128)(2,1)} %get-tuple-element.45.refs_0_, bf16[128,256]{1,0:T(8,128)(2,1)} %copy-done.8, bf16[128,256]{1,0:T(8,128)(2,1)} %copy-done.7, bf16[128,256]{1,0:T(8,128)(2,1)} %copy-done.6), custom_call_target="tpu_custom_call" | custom-call | tf_op jit(solution)/shard_map/pallas_call | solution.py:328
  (32 shorter events, 0.1 us)
Async XLA Ops:
  0.6 27.1 %copy-start.2 = (s32[32]{0:T(128)S(1)}, s32[32]{0:T(128)}, u32[]{:S(2)}) copy-start(s32[32]{0:T(128)} %refs_0_.1) | copy-start | bytes 388
  2.4 5.6 %collective-permute-start.3 = (bf16[128,256]{1,0:T(8,128)(2,1)}, bf16[128,256]{1,0:T(8,128)(2,1)S(1)}, u32[]{:S(2)}, u32[]{:S(2)}) collective-permute-start(bf16[128,256]{1,0:T(8,128)(2,1)} %get-tuple-element.28), channel_id=1, source_target_pairs={{0,8},{4,12},{8,0},{12,4},{16,24},{20,28},{24,16},{28,20},{1,9},{5... | collective-permute-start | bytes 196616 | tf_op jit(solution)/shard_map/ppermute | solution.py:296
  5.3 4.5 %collective-permute-start.4 = (bf16[128,256]{1,0:T(8,128)(2,1)}, bf16[128,256]{1,0:T(8,128)(2,1)S(1)}, u32[]{:S(2)}, u32[]{:S(2)}) collective-permute-start(bf16[128,256]{1,0:T(8,128)(2,1)} %get-tuple-element.29), channel_id=1, source_target_pairs={{0,16},{4,20},{8,24},{12,28},{16,0},{20,4},{24,8},{28,12},{1,17},{... | collective-permute-start | bytes 196616 | tf_op jit(solution)/shard_map/ppermute | solution.py:296
  6.8 5.4 %collective-permute-start.5 = (bf16[128,256]{1,0:T(8,128)(2,1)}, bf16[128,256]{1,0:T(8,128)(2,1)S(1)}, u32[]{:S(2)}, u32[]{:S(2)}) collective-permute-start(bf16[128,256]{1,0:T(8,128)(2,1)} %get-tuple-element.30), channel_id=1, source_target_pairs={{0,24},{4,28},{8,16},{12,20},{16,8},{20,12},{24,0},{28,4},{1,25},{... | collective-permute-start | bytes 196616 | tf_op jit(solution)/shard_map/ppermute | solution.py:296
  13.1 13.0 %collective-permute-start.9 = (bf16[4,128,256]{2,1,0:T(8,128)(2,1)S(1)}, bf16[4,128,256]{2,1,0:T(8,128)(2,1)S(1)}, u32[]{:S(2)}, u32[]{:S(2)}) collective-permute-start(bf16[4,128,256]{2,1,0:T(8,128)(2,1)S(1)} %pad_maximum_fusion.refs_6_), channel_id=1, source_target_pairs={{0,2},{1,3},{2,0},{3,1},{4,6},{5,7},{6,4},{7,5},{8,10},{9,11},{10,... | collective-permute-start | bytes 786440 | tf_op jit(solution)/shard_map/ppermute | solution.py:296
  18.0 18.6 %copy-start = (bf16[128,1024]{1,0:T(8,128)(2,1)S(1)}, bf16[128,1024]{1,0:T(8,128)(2,1)}, u32[]{:S(2)}) copy-start(bf16[128,1024]{1,0:T(8,128)(2,1)} %get-tuple-element.23.refs_2_) | copy-start | bytes 786436
  18.0 10.0 %collective-permute-start = (bf16[128,1024]{1,0:T(8,128)(2,1)}, bf16[128,1024]{1,0:T(8,128)(2,1)S(1)}, u32[]{:S(2)}, u32[]{:S(2)}) collective-permute-start(bf16[128,1024]{1,0:T(8,128)(2,1)} %get-tuple-element.24), channel_id=1, source_target_pairs={{0,8},{4,12},{8,0},{12,4},{16,24},{20,28},{24,16},{28,20},{1,9},{5... | collective-permute-start | bytes 786440 | tf_op jit(solution)/shard_map/ppermute | solution.py:296
  18.5 9.6 %collective-permute-start.1 = (bf16[128,1024]{1,0:T(8,128)(2,1)}, bf16[128,1024]{1,0:T(8,128)(2,1)S(1)}, u32[]{:S(2)}, u32[]{:S(2)}) collective-permute-start(bf16[128,1024]{1,0:T(8,128)(2,1)} %get-tuple-element.25), channel_id=1, source_target_pairs={{0,16},{4,20},{8,24},{12,28},{16,0},{20,4},{24,8},{28,12},{1,17},{... | collective-permute-start | bytes 786440 | tf_op jit(solution)/shard_map/ppermute | solution.py:296
  19.0 12.1 %collective-permute-start.7 = (bf16[4,128,256]{2,1,0:T(8,128)(2,1)S(1)}, bf16[4,128,256]{2,1,0:T(8,128)(2,1)S(1)}, u32[]{:S(2)}, u32[]{:S(2)}) collective-permute-start(bf16[4,128,256]{2,1,0:T(8,128)(2,1)S(1)} %pad_maximum_fusion.refs_6_), channel_id=1, source_target_pairs={{0,1},{1,0},{2,3},{3,2},{4,5},{5,4},{6,7},{7,6},{8,9},{9,8},{10,11... | collective-permute-start | bytes 786440 | tf_op jit(solution)/shard_map/ppermute | solution.py:296
  26.1 8.9 %collective-permute-start.11 = (bf16[4,128,256]{2,1,0:T(8,128)(2,1)S(1)}, bf16[4,128,256]{2,1,0:T(8,128)(2,1)S(1)}, u32[]{:S(2)}, u32[]{:S(2)}) collective-permute-start(bf16[4,128,256]{2,1,0:T(8,128)(2,1)S(1)} %collective-permute-done.9.refs_10_), channel_id=1, source_target_pairs={{0,1},{1,0},{2,3},{3,2},{4,5},{5,4},{6,7},{7,6},{8,9},{9,8},{10,11... | collective-permute-start | bytes 786440 | tf_op jit(solution)/shard_map/ppermute | solution.py:296
  26.7 9.7 %collective-permute-start.2 = (bf16[128,1024]{1,0:T(8,128)(2,1)}, bf16[128,1024]{1,0:T(8,128)(2,1)S(1)}, u32[]{:S(2)}, u32[]{:S(2)}) collective-permute-start(bf16[128,1024]{1,0:T(8,128)(2,1)} %get-tuple-element.26), channel_id=1, source_target_pairs={{0,24},{4,28},{8,16},{12,20},{16,8},{20,12},{24,0},{28,4},{1,25},{... | collective-permute-start | bytes 786440 | tf_op jit(solution)/shard_map/ppermute | solution.py:296
  28.0 8.4 %collective-permute-start.6 = (bf16[4,128,256]{2,1,0:T(8,128)(2,1)S(1)}, bf16[4,128,256]{2,1,0:T(8,128)(2,1)S(1)}, u32[]{:S(2)}, u32[]{:S(2)}) collective-permute-start(bf16[4,128,256]{2,1,0:T(8,128)(2,1)S(1)} %pad_maximum_fusion.refs_6_), channel_id=1, source_target_pairs={{0,4},{4,0},{8,12},{12,8},{16,20},{20,16},{24,28},{28,24},{1,5},{5... | collective-permute-start | bytes 786440 | tf_op jit(solution)/shard_map/ppermute | solution.py:296
  28.1 8.3 %collective-permute-start.10 = (bf16[4,128,256]{2,1,0:T(8,128)(2,1)S(1)}, bf16[4,128,256]{2,1,0:T(8,128)(2,1)S(1)}, u32[]{:S(2)}, u32[]{:S(2)}) collective-permute-start(bf16[4,128,256]{2,1,0:T(8,128)(2,1)S(1)} %collective-permute-done.9.refs_10_), channel_id=1, source_target_pairs={{0,4},{4,0},{8,12},{12,8},{16,20},{20,16},{24,28},{28,24},{1,5},{5... | collective-permute-start | bytes 786440 | tf_op jit(solution)/shard_map/ppermute | solution.py:296
  31.1 5.4 %collective-permute-start.8 = (bf16[4,128,256]{2,1,0:T(8,128)(2,1)S(1)}, bf16[4,128,256]{2,1,0:T(8,128)(2,1)S(1)}, u32[]{:S(2)}, u32[]{:S(2)}) collective-permute-start(bf16[4,128,256]{2,1,0:T(8,128)(2,1)S(1)} %collective-permute-done.7.refs_8_), channel_id=1, source_target_pairs={{0,4},{4,0},{8,12},{12,8},{16,20},{20,16},{24,28},{28,24},{1,5},{5... | collective-permute-start | bytes 786440 | tf_op jit(solution)/shard_map/ppermute | solution.py:296
  35.0 1.5 %collective-permute-start.12 = (bf16[4,128,256]{2,1,0:T(8,128)(2,1)S(1)}, bf16[4,128,256]{2,1,0:T(8,128)(2,1)S(1)}, u32[]{:S(2)}, u32[]{:S(2)}) collective-permute-start(bf16[4,128,256]{2,1,0:T(8,128)(2,1)S(1)} %collective-permute-done.11.refs_12_), channel_id=1, source_target_pairs={{0,4},{4,0},{8,12},{12,8},{16,20},{20,16},{24,28},{28,24},{1,5},{5... | collective-permute-start | bytes 786440 | tf_op jit(solution)/shard_map/ppermute | solution.py:296
  52.5 11.5 %copy-start.1 = (bf16[128,1024]{1,0:T(8,128)(2,1)}, bf16[128,1024]{1,0:T(8,128)(2,1)S(1)}, u32[]{:S(2)}) copy-start(bf16[128,1024]{1,0:T(8,128)(2,1)S(1)} %get-tuple-element.31.refs_0_) | copy-start | bytes 786436
  52.5 2.9 %collective-permute-start.16 = (bf16[4,4,128,256]{3,2,1,0:T(8,128)(2,1)}, bf16[4,4,128,256]{3,2,1,0:T(8,128)(2,1)S(1)}, u32[]{:S(2)}, u32[]{:S(2)}) collective-permute-start(bf16[4,4,128,256]{3,2,1,0:T(8,128)(2,1)} %get-tuple-element.38), channel_id=1, source_target_pairs={{0,4},{4,0},{8,12},{12,8},{16,20},{20,16},{24,28},{28,24},{1,5},{5... | collective-permute-start | bytes 3145736 | tf_op jit(solution)/shard_map/ppermute | solution.py:296
  55.5 8.4 %collective-permute-start.17 = (bf16[4,128,256]{2,1,0:T(8,128)(2,1)S(1)}, bf16[4,128,256]{2,1,0:T(8,128)(2,1)S(1)}, u32[]{:S(2)}, u32[]{:S(2)}) collective-permute-start(bf16[4,128,256]{2,1,0:T(8,128)(2,1)S(1)} %get-tuple-element.47), channel_id=1, source_target_pairs={{0,1},{1,0},{2,3},{3,2},{4,5},{5,4},{6,7},{7,6},{8,9},{9,8},{10,11... | collective-permute-start | bytes 786440 | tf_op jit(solution)/shard_map/ppermute | solution.py:296
  64.0 14.1 %collective-permute-start.19 = (bf16[4,128,256]{2,1,0:T(8,128)(2,1)S(1)}, bf16[4,128,256]{2,1,0:T(8,128)(2,1)S(1)}, u32[]{:S(2)}, u32[]{:S(2)}) collective-permute-start(bf16[4,128,256]{2,1,0:T(8,128)(2,1)S(1)} %fusion.2), channel_id=1, source_target_pairs={{0,2},{1,3},{2,0},{3,1},{4,6},{5,7},{6,4},{7,5},{8,10},{9,11},{10,... | collective-permute-start | bytes 786440 | tf_op jit(solution)/shard_map/ppermute | solution.py:296
  64.1 14.0 %collective-permute-start.18 = (bf16[4,128,256]{2,1,0:T(8,128)(2,1)S(1)}, bf16[4,128,256]{2,1,0:T(8,128)(2,1)S(1)}, u32[]{:S(2)}, u32[]{:S(2)}) collective-permute-start(bf16[4,128,256]{2,1,0:T(8,128)(2,1)S(1)} %get-tuple-element.39), channel_id=1, source_target_pairs={{0,1},{1,0},{2,3},{3,2},{4,5},{5,4},{6,7},{7,6},{8,9},{9,8},{10,11... | collective-permute-start | bytes 786440 | tf_op jit(solution)/shard_map/ppermute | solution.py:296
  65.4 16.0 %collective-permute-start.13 = (bf16[128,1024]{1,0:T(8,128)(2,1)S(1)}, bf16[128,1024]{1,0:T(8,128)(2,1)S(1)}, u32[]{:S(2)}, u32[]{:S(2)}) collective-permute-start(bf16[128,1024]{1,0:T(8,128)(2,1)S(1)} %get-tuple-element.32), channel_id=1, source_target_pairs={{0,8},{4,12},{8,0},{12,4},{16,24},{20,28},{24,16},{28,20},{1,9},{5... | collective-permute-start | bytes 786440 | tf_op jit(solution)/shard_map/ppermute | solution.py:296
  66.4 16.0 %collective-permute-start.14 = (bf16[128,1024]{1,0:T(8,128)(2,1)S(1)}, bf16[128,1024]{1,0:T(8,128)(2,1)S(1)}, u32[]{:S(2)}, u32[]{:S(2)}) collective-permute-start(bf16[128,1024]{1,0:T(8,128)(2,1)S(1)} %get-tuple-element.33), channel_id=1, source_target_pairs={{0,16},{4,20},{8,24},{12,28},{16,0},{20,4},{24,8},{28,12},{1,17},{... | collective-permute-start | bytes 786440 | tf_op jit(solution)/shard_map/ppermute | solution.py:296
  67.7 14.7 %collective-permute-start.15 = (bf16[128,1024]{1,0:T(8,128)(2,1)S(1)}, bf16[128,1024]{1,0:T(8,128)(2,1)S(1)}, u32[]{:S(2)}, u32[]{:S(2)}) collective-permute-start(bf16[128,1024]{1,0:T(8,128)(2,1)S(1)} %get-tuple-element.34), channel_id=1, source_target_pairs={{0,24},{4,28},{8,16},{12,20},{16,8},{20,12},{24,0},{28,4},{1,25},{... | collective-permute-start | bytes 786440 | tf_op jit(solution)/shard_map/ppermute | solution.py:296
  78.9 6.5 %collective-permute-start.22 = (bf16[128,256]{1,0:T(8,128)(2,1)S(1)}, bf16[128,256]{1,0:T(8,128)(2,1)S(1)}, u32[]{:S(2)}, u32[]{:S(2)}) collective-permute-start(bf16[128,256]{1,0:T(8,128)(2,1)S(1)} %get-tuple-element.42), channel_id=1, source_target_pairs={{0,24},{4,28},{8,16},{12,20},{16,8},{20,12},{24,0},{28,4},{1,25},{... | collective-permute-start | bytes 196616 | tf_op jit(solution)/shard_map/ppermute | solution.py:296
  80.9 4.5 %collective-permute-start.21 = (bf16[128,256]{1,0:T(8,128)(2,1)S(1)}, bf16[128,256]{1,0:T(8,128)(2,1)S(1)}, u32[]{:S(2)}, u32[]{:S(2)}) collective-permute-start(bf16[128,256]{1,0:T(8,128)(2,1)S(1)} %get-tuple-element.43), channel_id=1, source_target_pairs={{0,16},{4,20},{8,24},{12,28},{16,0},{20,4},{24,8},{28,12},{1,17},{... | collective-permute-start | bytes 196616 | tf_op jit(solution)/shard_map/ppermute | solution.py:296
  81.4 1.0 %copy-start.3 = (bf16[128,1024]{1,0:T(8,128)(2,1)}, bf16[128,1024]{1,0:T(8,128)(2,1)S(1)}, u32[]{:S(2)}) copy-start(bf16[128,1024]{1,0:T(8,128)(2,1)S(1)} %collective-permute-done.13.refs_1_) | copy-start | bytes 786436
  81.4 4.3 %collective-permute-start.20 = (bf16[128,256]{1,0:T(8,128)(2,1)S(1)}, bf16[128,256]{1,0:T(8,128)(2,1)S(1)}, u32[]{:S(2)}, u32[]{:S(2)}) collective-permute-start(bf16[128,256]{1,0:T(8,128)(2,1)S(1)} %get-tuple-element.44), channel_id=1, source_target_pairs={{0,8},{4,12},{8,0},{12,4},{16,24},{20,28},{24,16},{28,20},{1,9},{5... | collective-permute-start | bytes 196616 | tf_op jit(solution)/shard_map/ppermute | solution.py:296
  82.4 0.7 copy-start.4
  82.4 0.8 copy-start.5
  85.4 0.6 copy-start.6
  85.4 0.6 copy-start.7
  85.7 0.6 copy-start.8

commit v3 on v2

--- a/solution.py
+++ b/solution.py
@@ -289,6 +289,7 @@
 CONTRACT_FIRST = (((0,), (0,)), ((), ()))
 VMEM = pl.BlockSpec(memory_space=pltpu.VMEM)
 SMEM = pl.BlockSpec(memory_space=pltpu.SMEM)
+SMALL = pltpu.CompilerParams(vmem_limit_bytes=8 * 1024 * 1024)
 
 
 def flipped(value, axis, bits):
@@ -296,41 +297,83 @@
     return lax.ppermute(value, axis, [(source, source ^ bits) for source in range(count)])
 
 
-def pack_heads_kernel(cores, wide, left_ref, right_ref, *out_refs):
-    part = lax.axis_index("ctx") // cores
-    for flip, out_ref in enumerate(out_refs):
-        columns = pl.ds(pl.multiple_of((part ^ flip) * wide, HD), wide)
-        out_ref[:, :wide] = left_ref[:, columns]
-        out_ref[:, wide:] = right_ref[:, columns]
-
-
-def unpack_heads_kernel(cores, wide, *refs):
-    in_refs, (left_ref, right_ref) = refs[:KVH], refs[KVH:]
-    part = lax.axis_index("ctx") // cores
-    for flip, in_ref in enumerate(in_refs):
-        columns = pl.ds(pl.multiple_of((part ^ flip) * wide, HD), wide)
-        left_ref[:, columns] = in_ref[:, :wide]
-        right_ref[:, columns] = in_ref[:, wide:]
-
-
-def pack_heads(left, right, cores):
-    rows, wide = left.shape[0], left.shape[1] // KVH
+def piece_columns(pieces, flip, wide):
+    index = lax.axis_index("ctx") // (lax.axis_size("ctx") // pieces)
+    return pl.ds(pl.multiple_of((index ^ flip) * wide, HD), wide)
+
+
+def split_heads_kernel(pieces, wide, left_ref, right_ref, *piece_refs):
+    for flip, piece_ref in enumerate(piece_refs):
+        columns = piece_columns(pieces, flip, wide)
+        piece_ref[:, :wide] = left_ref[:, columns]
+        piece_ref[:, wide:] = right_ref[:, columns]
+
+
+def join_heads_kernel(pieces, wide, *refs):
+    piece_refs, (left_ref, right_ref) = refs[:pieces], refs[pieces:]
+    for flip, piece_ref in enumerate(piece_refs):
+        columns = piece_columns(pieces, flip, wide)
+        left_ref[:, columns] = piece_ref[:, :wide]
+        right_ref[:, columns] = piece_ref[:, wide:]
+
+
+def split_heads(left, right, pieces):
+    rows, wide = left.shape[0], left.shape[1] // pieces
     return pl.pallas_call(
-        functools.partial(pack_heads_kernel, cores, wide),
-        out_shape=[jax.ShapeDtypeStruct((rows, 2 * wide), left.dtype)] * KVH,
+        functools.partial(split_heads_kernel, pieces, wide),
+        out_shape=[jax.ShapeDtypeStruct((rows, 2 * wide), left.dtype)] * pieces,
         in_specs=[VMEM] * 2,
-        out_specs=[VMEM] * KVH,
+        out_specs=[VMEM] * pieces,
+        compiler_params=SMALL,
     )(left, right)
 
 
-def unpack_heads(pieces, cores):
-    rows, wide = pieces[0].shape[0], pieces[0].shape[1] // 2
+def join_heads(parts):
+    pieces = len(parts)
+    rows, wide = parts[0].shape[0], parts[0].shape[1] // 2
     return pl.pallas_call(
-        functools.partial(unpack_heads_kernel, cores, wide),
-        out_shape=[jax.ShapeDtypeStruct((rows, wide * KVH), pieces[0].dtype)] * 2,
-        in_specs=[VMEM] * KVH,
+        functools.partial(join_heads_kernel, pieces, wide),
+        out_shape=[jax.ShapeDtypeStruct((rows, wide * pieces), parts[0].dtype)] * 2,
+        in_specs=[VMEM] * pieces,
         out_specs=[VMEM] * 2,
-    )(*pieces)
+        compiler_params=SMALL,
+    )(*parts)
+
+
+def prepare_kernel(pieces, wide, lengths_ref, left_ref, right_ref, *out_refs):
+    piece_refs, marks_ref = out_refs[:pieces], out_refs[pieces]
+    split_heads_kernel(pieces, wide, left_ref, right_ref, *piece_refs)
+    total, docs = marks_ref.shape[0], lengths_ref.shape[0]
+    lane = lax.broadcasted_iota(jnp.int32, (1, MARKS), 1)
+    begins = jnp.zeros((1, MARKS), jnp.int32)
+    ends = jnp.where(lane < docs, total, 0)
+    end = jnp.int32(0)
+    for number in range(docs):
+        begins = jnp.where(lane == number, end, begins)
+        end = end + lengths_ref[number]
+        ends = jnp.where(lane == number, end, ends)
+
+    def some_rows(step, _):
+        rows = pl.ds(pl.multiple_of(step * KEY_ROWS, KEY_ROWS), KEY_ROWS)
+        position = step * KEY_ROWS + lax.broadcasted_iota(jnp.int32, (KEY_ROWS, MARKS), 0)
+        inside = (position >= begins) & (position < ends)
+        marks_ref[rows, :] = jnp.where(inside, 1.0, 0.0).astype(jnp.bfloat16)
+        return 0
+
+    lax.fori_loop(0, total // KEY_ROWS, some_rows, 0)
+
+
+def prepare(lengths, left, right, pieces, total):
+    rows, wide = left.shape[0], left.shape[1] // pieces
+    results = pl.pallas_call(
+        functools.partial(prepare_kernel, pieces, wide),
+        out_shape=[jax.ShapeDtypeStruct((rows, 2 * wide), left.dtype)] * pieces
+        + [jax.ShapeDtypeStruct((total, MARKS), jnp.bfloat16)],
+        in_specs=[SMEM] + [VMEM] * 2,
+        out_specs=[VMEM] * (pieces + 1),
+        compiler_params=SMALL,
+    )(lengths, left, right)
+    return results[:pieces], results[pieces]
 
 
 KEY_ROWS = 256
@@ -351,7 +394,7 @@
     kv_refs, refs = refs[:kv_count], refs[kv_count:]
     od_refs, refs = refs[:KVH], refs[KVH:]
     dkv_refs, refs = refs[: cores * len(CHUNKS)], refs[cores * len(CHUNKS) :]
-    k_all, v_all, q_wide, g_wide, dk_acc, dv_acc, score, prob, tops, acc, table = refs
+    k_all, v_all, q_wide, g_all, dk_acc, dv_acc, score, prob, tops, acc, table = refs
     scaling = HD ** (-0.5)
     log_scale = scaling * math.log2(math.e)
     f32, bf16 = jnp.float32, jnp.bfloat16
@@ -378,7 +421,7 @@
             rows = slice(member * tok, (member + 1) * tok)
             q_wide[flip, rows, :HD] = qd_ref[:, member * HD : (member + 1) * HD]
             q_wide[flip, rows, HD:] = bias
-            g_wide[flip, rows, :HD] = qd_ref[:, (group + member) * HD : (group + member + 1) * HD]
+            g_all[flip, rows, :] = qd_ref[:, (group + member) * HD : (group + member + 1) * HD]
     dk_acc[...] = jnp.zeros_like(dk_acc)
     dv_acc[...] = jnp.zeros_like(dv_acc)
     tops[...] = jnp.full_like(tops, NEG_FILL)
@@ -473,39 +516,41 @@
             acc[table[0, item]] += value
 
     sweep(out_round, BATCH)
-    feature = lax.broadcasted_iota(jnp.int32, (lanes, MARKS), 1)
     for flip in range(KVH):
         inverse = 1.0 / acc[flip, HD : HD + 1, :]
-        out = (acc[flip, :HD, :] * inverse).T.astype(bf16)
-        g = g_wide[flip, :, :HD].astype(f32)
-        g_scaled = (g * jnp.broadcast_to(inverse, (HD, lanes)).T).astype(bf16)
-        delta = jnp.sum(out.astype(f32) * g_scaled.astype(f32), axis=1, keepdims=True)
-        high = delta.astype(bf16).astype(f32)
-        extra = jnp.where(feature == docs, -high, jnp.where(feature == docs + 1, high - delta, 0.0))
-        g_wide[flip, :, :HD] = g_scaled
-        g_wide[flip, :, HD:] = extra.astype(bf16)
+        turned = (acc[flip, :HD, :] * inverse).astype(bf16)
+        out = turned.T
+        g_turned = g_all[flip].T.astype(f32)
+        delta = jnp.sum(turned.astype(f32) * g_turned, axis=0, keepdims=True)
+        acc[flip, HD : HD + 1, :] = inverse
+        acc[flip, HD + 1 : HD + 2, :] = delta
+        acc[flip, :HD, :] = jnp.zeros((HD, lanes), f32)
         for member in range(group):
             rows = slice(member * tok, (member + 1) * tok)
             od_refs[flip][:, member * HD : (member + 1) * HD] = out[rows, :]
-        acc[flip] = jnp.zeros_like(acc[flip])
 
     def grad_round(items):
-        weights = [prob[score_rows(item), :] for item in items]
         slopes = [
             lax.dot_general(
-                wide(v_all, key_rows(item)),
-                g_wide[table[0, item]],
+                v_all[key_rows(item), :],
+                g_all[table[0, item]],
                 CONTRACT_LAST,
                 preferred_element_type=f32,
             )
             for item in items
         ]
+        probs = [
+            prob[score_rows(item), :].astype(f32) * acc[table[0, item], HD : HD + 1, :]
+            for item in items
+        ]
+        weights = [value.astype(bf16) for value in probs]
         score_grads = [
-            (weight.astype(f32) * slope).astype(bf16) for weight, slope in zip(weights, slopes)
+            (value * (slope - acc[table[0, item], HD + 1 : HD + 2, :])).astype(bf16)
+            for item, value, slope in zip(items, probs, slopes)
         ]
         for item, weight, score_grad in zip(items, weights, score_grads):
             flip, rows = table[0, item], key_rows(item)
-            dv_acc[rows, :] += jnp.dot(weight, g_wide[flip, :, :HD], preferred_element_type=f32)
+            dv_acc[rows, :] += jnp.dot(weight, g_all[flip], preferred_element_type=f32)
             dk_acc[rows, :] += jnp.dot(score_grad, q_wide[flip, :, :HD], preferred_element_type=f32)
             acc[flip, :HD, :] += lax.dot_general(
                 k_all[rows, :], score_grad, CONTRACT_FIRST, preferred_element_type=f32
@@ -514,7 +559,7 @@
     sweep(grad_round, GRAD_BATCH)
 
     for flip, od_ref in enumerate(od_refs):
-        turned = (acc[flip, :HD, :] * scaling).T.astype(bf16)
+        turned = (acc[flip, :HD, :] * scaling).astype(bf16).T
         for member in range(group):
             rows = slice(member * tok, (member + 1) * tok)
             od_ref[:, (group + member) * HD : (group + member + 1) * HD] = turned[rows, :]
@@ -528,17 +573,7 @@
                     dkv_ref[head_flip, place, :, HD:] = dv_acc[rows, :].astype(bf16)
 
 
-def document_marks(lengths, total):
-    docs = lengths.shape[0]
-    ends = jnp.cumsum(lengths)
-    begins = jnp.pad(ends - lengths, (0, MARKS - docs))
-    lane = jnp.arange(MARKS)
-    ends = jnp.where(lane < docs, jnp.pad(ends, (0, MARKS - docs)), jnp.where(lane < docs + 2, total, 0))
-    position = jnp.arange(total, dtype=jnp.int32)[:, None]
-    return ((position >= begins[None, :]) & (position < ends[None, :])).astype(jnp.bfloat16)
-
-
-def attention(lengths, qd, kv, cores, heads):
+def attention(lengths, marks, qd, kv, cores, heads):
     tok, group = qd[0].shape[0], QH // KVH
     total = KVH * cores * heads * tok
     lanes = group * tok
@@ -560,7 +595,7 @@
             pltpu.VMEM((total, HD), bf16),
             pltpu.VMEM((total, HD), bf16),
             pltpu.VMEM((KVH, lanes, HD + MARKS), bf16),
-            pltpu.VMEM((KVH, lanes, HD + MARKS), bf16),
+            pltpu.VMEM((KVH, lanes, HD), bf16),
             pltpu.VMEM((total, HD), f32),
             pltpu.VMEM((total, HD), f32),
             pltpu.VMEM((items * KEY_ROWS, lanes), f32),
@@ -569,43 +604,40 @@
             pltpu.VMEM((KVH, HD + 16, lanes), f32),
             pltpu.SMEM((3, items + BATCH), jnp.int32),
         ],
-        compiler_params=pltpu.CompilerParams(vmem_limit_bytes=48 * 1024 * 1024),
-    )(lengths, document_marks(lengths, total), *qd, *kv)
+        compiler_params=pltpu.CompilerParams(vmem_limit_bytes=36 * 1024 * 1024),
+    )(lengths, marks, *qd, *kv)
     return results[: len(qd)], results[len(qd) :]
 
 
 def part_shards(queries, keys, values, d_out, lengths):
-    heads = lax.axis_size("head")
-    cores = lax.axis_size("ctx") // KVH
+    heads, ctx = lax.axis_size("head"), lax.axis_size("ctx")
+    cores = ctx // KVH
+    total = queries.shape[0] * heads * ctx
 
     def exchange(pieces):
-        return [pieces[0]] + [flipped(pieces[s], "ctx", s * cores) for s in range(1, KVH)]
-
-    pieces = exchange(pack_heads(keys, values, cores))
-    qd = exchange(pack_heads(queries, d_out, cores))
+        span = ctx // len(pieces)
+        return [pieces[0]] + [flipped(p, "ctx", (s + 1) * span) for s, p in enumerate(pieces[1:])]
+
+    kv_mine = jnp.stack(exchange(split_heads(keys, values, KVH)))
+    qd, marks = prepare(lengths, queries, d_out, KVH, total)
+    qd = exchange(qd)
+    near, far = flipped(kv_mine, "head", 1), flipped(kv_mine, "head", 2)
     kv = []
-    for chunk in CHUNKS:
-        own = jnp.stack([pieces[flip] for flip in chunk])
-        far = flipped(own, "head", 2)
-        near = flipped(own, "head", 1)
-        for piece in (own, near, far, flipped(far, "head", 1)):
-            kv += [piece, flipped(piece, "ctx", 1)]
-    od, dkv = attention(lengths, qd, kv, cores, heads)
+    for piece in (kv_mine, near, far, flipped(far, "head", 1)):
+        kv += [piece, flipped(piece, "ctx", 1)]
+    od, dkv = attention(lengths, marks, qd, kv, cores, heads)
 
     def summed(*terms):
         return sum(term.astype(jnp.float32) for term in terms).astype(jnp.bfloat16)
 
-    grads = [None] * KVH
-    for number in reversed(range(len(CHUNKS))):
-        both = (dkv[number * cores], flipped(dkv[number * cores + 1], "ctx", 1))
-        third = flipped(summed(*(term[3] for term in both)), "head", 1)
-        second = flipped(summed(*(term[2] for term in both), third), "head", 2)
-        first, _ = lax.optimization_barrier((summed(*(term[1] for term in both)), third))
-        first = flipped(first, "head", 1)
-        for place, flip in enumerate(CHUNKS[number]):
-            grads[flip] = summed(*(term[0, place] for term in both), first[place], second[place])
-    attn_out, grad_queries = unpack_heads(exchange(od), cores)
-    grad_keys, grad_values = unpack_heads(exchange(grads), cores)
+    both = (dkv[0], flipped(dkv[1], "ctx", 1))
+    third = flipped(summed(*(term[3] for term in both)), "head", 1)
+    second = flipped(summed(*(term[2] for term in both), third), "head", 2)
+    first, _ = lax.optimization_barrier((summed(*(term[1] for term in both)), third))
+    first = flipped(first, "head", 1)
+    grads = [summed(*(term[0, s] for term in both), first[s], second[s]) for s in range(KVH)]
+    attn_out, grad_queries = join_heads(exchange(od))
+    grad_keys, grad_values = join_heads(exchange(grads))
     return attn_out, grad_queries, grad_keys, grad_values
 
 

time: 88.1 us -> 83.4 us (0.947); the launches traced: 88 us -> 84.5 us
  Pallas kernels: 23.8 us -> 15.2 us
  starting transfers between devices: 20.4 us -> 24.2 us
  other arithmetic: 3.43 us -> 0.41 us
  waiting for transfers between devices: 38.1 us -> 41.1 us
  local copies, waits for them, and re-layouts: 1.51 us -> 2.85 us
    pallas_call x4, Pallas kernels: 7.86 us -> 2.99 us  [the longest x2 1.82 us: join_heads(): pl.pallas_call(functools.partial(join_heads_kernel, pieces, wide), out_sh...]
    ppermute x23, starting transfers between devices: 20.4 us -> 24.2 us  [flipped(): lax.ppermute(value, axis, [(source, source ^ bits) for source in range(co...]
    pallas_call x1, Pallas kernels: 15.9 us -> 12.2 us  [attention(): pl.pallas_call(functools.partial(attention_kernel, cores, heads, tok), ou...]
    ppermute x23, waiting for transfers between devices: 38.1 us -> 41.1 us  [flipped(): lax.ppermute(value, axis, [(source, source ^ bits) for source in range(co...]
    unnamed x18 -> x10, local copies, waits for them, and re-layouts: 1.42 us -> 2.85 us
    convert_element_type x1 -> x0, other arithmetic: 1.38 us -> none  [document_marks(): ((position >= begins[None, :]) & (position < ends[None, :])).astype(jnp.b...]
    another operation x3 -> x1, other arithmetic: 1.04 us -> 0.04 us  [part_shards(): kv_mine = jnp.stack(exchange(split_heads(keys, values, KVH)))]
  transfers between devices with their start and end apart: 23 -> 23, of which waited for: 11 -> 15; matrix products, arithmetic and copies ran while one was open for 3% -> 0% of each run, Pallas kernels for 5% -> 3%
where the time goes in v3:
time: 83.4 us; the launch traced here: 84.5 us
  waiting for transfers between devices  41.1 us (49%)
  starting transfers between devices  24.2 us (29%)
  Pallas kernels  15.2 us (18%)
  local copies, waits for them, and re-layouts  2.85 us (3%)
    ppermute x23, waiting for transfers between devices, flipped(): lax.ppermute(value, axis, [(source, source ^ bits) for source in range(co...  41.1 us
    ppermute x23, starting transfers between devices, flipped(): lax.ppermute(value, axis, [(source, source ^ bits) for source in range(co...  24.2 us
    pallas_call x1, Pallas kernels, attention(): pl.pallas_call(functools.partial(attention_kernel, cores, heads, tok), ou...  12.2 us
    unnamed x10, local copies, waits for them, and re-layouts  2.85 us
    pallas_call x2, Pallas kernels, join_heads(): pl.pallas_call(functools.partial(join_heads_kernel, pieces, wide), out_sh...  1.82 us
  transfers between devices with their start and end apart: 23, of which 15 were waited for; matrix products, arithmetic and copies ran while one was open for 0% of the time, Pallas kernels for 3%

profile of v3, /device:TPU:0, one launch (start us, length us, event | category | flops | bytes accessed | tf_op | source)
XLA Modules:
  0.0 84.5 jit_solution(11053161342078796444)
XLA Ops:
  0.6 0.9 %copy-done.2 = bf16[128,512]{1,0:T(8,128)(2,1)S(1)} copy-done((bf16[128,512]{1,0:T(8,128)(2,1)S(1)}, bf16[128,512]{1,0:T(8,128)(2,1)}, u32[]{:S(2)}) %copy-start.2) | copy-done | bytes 131096
  1.5 0.9 %copy-done.3 = bf16[128,512]{1,0:T(8,128)(2,1)S(1)} copy-done((bf16[128,512]{1,0:T(8,128)(2,1)S(1)}, bf16[128,512]{1,0:T(8,128)(2,1)}, u32[]{:S(2)}) %copy-start.3) | copy-done | bytes 131096
  2.5 3.0 %collective-permute-start.3 = (bf16[128,256]{1,0:T(8,128)(2,1)S(1)}, bf16[128,256]{1,0:T(8,128)(2,1)S(1)}, u32[]{:S(2)}, u32[]{:S(2)}) collective-permute-start(bf16[128,256]{1,0:T(8,128)(2,1)S(1)} %get-tuple-element.30), channel_id=1, source_target_pairs={{0,8},{4,12},{8,0},{12,4},{16,24},{20,28},{24,16},{28,20},{1,9},{5... | collective-permute-start | bytes 196616 | tf_op jit(solution)/shard_map/ppermute | solution.py:297
  5.5 1.5 %collective-permute-start.4 = (bf16[128,256]{1,0:T(8,128)(2,1)S(1)}, bf16[128,256]{1,0:T(8,128)(2,1)S(1)}, u32[]{:S(2)}, u32[]{:S(2)}) collective-permute-start(bf16[128,256]{1,0:T(8,128)(2,1)S(1)} %get-tuple-element.31), channel_id=1, source_target_pairs={{0,16},{4,20},{8,24},{12,28},{16,0},{20,4},{24,8},{28,12},{1,17},{... | collective-permute-start | bytes 196616 | tf_op jit(solution)/shard_map/ppermute | solution.py:297
  7.0 0.0 collective-permute-start.5
  7.0 0.8 collective-permute-done.3
  7.9 1.9 %collective-permute-done.4 = bf16[128,256]{1,0:T(8,128)(2,1)S(1)} collective-permute-done((bf16[128,256]{1,0:T(8,128)(2,1)S(1)}, bf16[128,256]{1,0:T(8,128)(2,1)S(1)}, u32[]{:S(2)}, u32[]{:S(2)}) %collective-permute-start.4) | collective-permute-done | bytes 65568 | tf_op jit(solution)/shard_map/ppermute | solution.py:297
  9.8 2.4 %collective-permute-done.5 = bf16[128,256]{1,0:T(8,128)(2,1)S(1)} collective-permute-done((bf16[128,256]{1,0:T(8,128)(2,1)S(1)}, bf16[128,256]{1,0:T(8,128)(2,1)S(1)}, u32[]{:S(2)}, u32[]{:S(2)}) %collective-permute-start.5) | collective-permute-done | bytes 65568 | tf_op jit(solution)/shard_map/ppermute | solution.py:297
  12.2 2.7 %collective-permute-start.9 = (bf16[4,128,256]{2,1,0:T(8,128)(2,1)S(1)}, bf16[4,128,256]{2,1,0:T(8,128)(2,1)S(1)}, u32[]{:S(2)}, u32[]{:S(2)}) collective-permute-start(bf16[4,128,256]{2,1,0:T(8,128)(2,1)S(1)} %pad_maximum_fusion.refs_6_), channel_id=1, source_target_pairs={{0,2},{1,3},{2,0},{3,1},{4,6},{5,7},{6,4},{7,5},{8,10},{9,11},{10,... | collective-permute-start | bytes 786440 | tf_op jit(solution)/shard_map/ppermute | solution.py:297
  14.9 1.0 %copy-done.1 = bf16[128,2048]{1,0:T(8,128)(2,1)S(1)} copy-done((bf16[128,2048]{1,0:T(8,128)(2,1)S(1)}, bf16[128,2048]{1,0:T(8,128)(2,1)}, u32[]{:S(2)}) %copy-start.1) | copy-done | bytes 524312
  15.9 1.1 %shard_map.84 = (bf16[128,1024]{1,0:T(8,128)(2,1)S(1)}, bf16[128,1024]{1,0:T(8,128)(2,1)S(1)}, bf16[128,1024]{1,0:T(8,128)(2,1)S(1)}, bf16[128,1024]{1,0:T(8,128)(2,1)S(1)}, bf16[4096,128]{1,0:T(8,128)(2,1)S(1)}) custom-call(s32[32]{0:T(128)S(1)} %copy-done.4, bf16[128,2048]{1,0:T(8,128)(2,1)S(1)} %copy-done, bf16[128,2048]{1,0:T(8,128)(2,1)S(1)} %copy-done.1), custom_call_target="tpu_custom_call" | custom-call | tf_op jit(solution)/shard_map/pallas_call | solution.py:368
  17.1 0.6 collective-permute-start
  17.7 0.5 collective-permute-start.1
  18.2 1.6 %collective-permute-start.7 = (bf16[4,128,256]{2,1,0:T(8,128)(2,1)S(1)}, bf16[4,128,256]{2,1,0:T(8,128)(2,1)S(1)}, u32[]{:S(2)}, u32[]{:S(2)}) collective-permute-start(bf16[4,128,256]{2,1,0:T(8,128)(2,1)S(1)} %pad_maximum_fusion.refs_6_), channel_id=1, source_target_pairs={{0,1},{1,0},{2,3},{3,2},{4,5},{5,4},{6,7},{7,6},{8,9},{9,8},{10,11... | collective-permute-start | bytes 786440 | tf_op jit(solution)/shard_map/ppermute | solution.py:297
  19.7 5.5 %collective-permute-done.9.refs_10_ = bf16[4,128,256]{2,1,0:T(8,128)(2,1)S(1)} collective-permute-done((bf16[4,128,256]{2,1,0:T(8,128)(2,1)S(1)}, bf16[4,128,256]{2,1,0:T(8,128)(2,1)S(1)}, u32[]{:S(2)}, u32[]{:S(2)}) %collective-permute-start.9) | collective-permute-done | bytes 262176 | tf_op jit(solution)/shard_map/ppermute | solution.py:297
  25.3 0.6 collective-permute-start.11
  25.9 1.0 %collective-permute-start.2 = (bf16[128,1024]{1,0:T(8,128)(2,1)S(1)}, bf16[128,1024]{1,0:T(8,128)(2,1)S(1)}, u32[]{:S(2)}, u32[]{:S(2)}) collective-permute-start(bf16[128,1024]{1,0:T(8,128)(2,1)S(1)} %get-tuple-element.28), channel_id=1, source_target_pairs={{0,24},{4,28},{8,16},{12,20},{16,8},{20,12},{24,0},{28,4},{1,25},{... | collective-permute-start | bytes 786440 | tf_op jit(solution)/shard_map/ppermute | solution.py:297
  26.9 0.0 collective-permute-done.1.refs_4_
  26.9 0.5 collective-permute-start.10
  27.4 3.1 %collective-permute-done.7.refs_8_ = bf16[4,128,256]{2,1,0:T(8,128)(2,1)S(1)} collective-permute-done((bf16[4,128,256]{2,1,0:T(8,128)(2,1)S(1)}, bf16[4,128,256]{2,1,0:T(8,128)(2,1)S(1)}, u32[]{:S(2)}, u32[]{:S(2)}) %collective-permute-start.7) | collective-permute-done | bytes 262176 | tf_op jit(solution)/shard_map/ppermute | solution.py:297
  30.5 0.0 collective-permute-start.8
  30.5 3.8 %collective-permute-done.11.refs_12_ = bf16[4,128,256]{2,1,0:T(8,128)(2,1)S(1)} collective-permute-done((bf16[4,128,256]{2,1,0:T(8,128)(2,1)S(1)}, bf16[4,128,256]{2,1,0:T(8,128)(2,1)S(1)}, u32[]{:S(2)}, u32[]{:S(2)}) %collective-permute-start.11) | collective-permute-done | bytes 262176 | tf_op jit(solution)/shard_map/ppermute | solution.py:297
  34.3 0.0 collective-permute-start.12
  34.3 0.4 collective-permute-done.2.refs_5_
  34.7 1.1 %collective-permute-done.12.refs_13_ = bf16[4,128,256]{2,1,0:T(8,128)(2,1)S(1)} collective-permute-done((bf16[4,128,256]{2,1,0:T(8,128)(2,1)S(1)}, bf16[4,128,256]{2,1,0:T(8,128)(2,1)S(1)}, u32[]{:S(2)}, u32[]{:S(2)}) %collective-permute-start.12) | collective-permute-done | bytes 262176 | tf_op jit(solution)/shard_map/ppermute | solution.py:297
  35.8 12.2 %shard_map.86 = (bf16[128,1024]{1,0:T(8,128)(2,1)S(1)}, bf16[128,1024]{1,0:T(8,128)(2,1)S(1)}, bf16[128,1024]{1,0:T(8,128)(2,1)S(1)}, bf16[128,1024]{1,0:T(8,128...) custom-call(s32[32]{0:T(128)S(1)} %copy-done.4, ...), custom_call_target="tpu_custom_call" | custom-call | tf_op jit(solution)/shard_map/pallas_call | solution.py:584
  48.0 0.1 collective-permute-start.16
  48.1 2.6 %collective-permute-done.16 = bf16[4,4,128,256]{3,2,1,0:T(8,128)(2,1)S(1)} collective-permute-done((bf16[4,4,128,256]{3,2,1,0:T(8,128)(2,1)S(1)}, bf16[4,4,128,256]{3,2,1,0:T(8,128)(2,1)S(1)}, u32[]{:S(2)}, u32[]{:S(2)}) %collective-permute-start.16) | collective-permute-done | bytes 1048608 | tf_op jit(solution)/shard_map/ppermute | solution.py:297
  50.8 0.1 fusion.1
  50.9 0.1 collective-permute-start.17
  51.0 8.3 %collective-permute-done.17 = bf16[4,128,256]{2,1,0:T(8,128)(2,1)S(1)} collective-permute-done((bf16[4,128,256]{2,1,0:T(8,128)(2,1)S(1)}, bf16[4,128,256]{2,1,0:T(8,128)(2,1)S(1)}, u32[]{:S(2)}, u32[]{:S(2)}) %collective-permute-start.17) | collective-permute-done | bytes 262176 | tf_op jit(solution)/shard_map/ppermute | solution.py:297
  59.3 0.1 fusion
  59.4 4.7 %collective-permute-start.19 = (bf16[4,128,256]{2,1,0:T(8,128)(2,1)S(1)}, bf16[4,128,256]{2,1,0:T(8,128)(2,1)S(1)}, u32[]{:S(2)}, u32[]{:S(2)}) collective-permute-start(bf16[4,128,256]{2,1,0:T(8,128)(2,1)S(1)} %fusion), channel_id=1, source_target_pairs={{0,2},{1,3},{2,0},{3,1},{4,6},{5,7},{6,4},{7,5},{8,10},{9,11},{10,... | collective-permute-start | bytes 786440 | tf_op jit(solution)/shard_map/ppermute | solution.py:297
  64.1 0.3 collective-permute-start.18
  64.4 0.9 %collective-permute-start.13 = (bf16[128,1024]{1,0:T(8,128)(2,1)S(1)}, bf16[128,1024]{1,0:T(8,128)(2,1)S(1)}, u32[]{:S(2)}, u32[]{:S(2)}) collective-permute-start(bf16[128,1024]{1,0:T(8,128)(2,1)S(1)} %get-tuple-element.34), channel_id=1, source_target_pairs={{0,8},{4,12},{8,0},{12,4},{16,24},{20,28},{24,16},{28,20},{1,9},{5... | collective-permute-start | bytes 786440 | tf_op jit(solution)/shard_map/ppermute | solution.py:297
  65.4 0.6 collective-permute-start.14
  66.0 1.9 %collective-permute-start.15 = (bf16[128,1024]{1,0:T(8,128)(2,1)S(1)}, bf16[128,1024]{1,0:T(8,128)(2,1)S(1)}, u32[]{:S(2)}, u32[]{:S(2)}) collective-permute-start(bf16[128,1024]{1,0:T(8,128)(2,1)S(1)} %get-tuple-element.36), channel_id=1, source_target_pairs={{0,24},{4,28},{8,16},{12,20},{16,8},{20,12},{24,0},{28,4},{1,25},{... | collective-permute-start | bytes 786440 | tf_op jit(solution)/shard_map/ppermute | solution.py:297
  67.9 7.7 %collective-permute-done.19 = bf16[4,128,256]{2,1,0:T(8,128)(2,1)S(1)} collective-permute-done((bf16[4,128,256]{2,1,0:T(8,128)(2,1)S(1)}, bf16[4,128,256]{2,1,0:T(8,128)(2,1)S(1)}, u32[]{:S(2)}, u32[]{:S(2)}) %collective-permute-start.19) | collective-permute-done | bytes 262176 | tf_op jit(solution)/shard_map/ppermute | solution.py:297
  75.6 1.2 %collective-permute-done.18 = bf16[4,128,256]{2,1,0:T(8,128)(2,1)S(1)} collective-permute-done((bf16[4,128,256]{2,1,0:T(8,128)(2,1)S(1)}, bf16[4,128,256]{2,1,0:T(8,128)(2,1)S(1)}, u32[]{:S(2)}, u32[]{:S(2)}) %collective-permute-start.18) | collective-permute-done | bytes 262176 | tf_op jit(solution)/shard_map/ppermute | solution.py:297
  76.9 0.1 fusion.3
  77.0 1.0 %collective-permute-start.22 = (bf16[128,256]{1,0:T(8,128)(2,1)S(1)}, bf16[128,256]{1,0:T(8,128)(2,1)S(1)}, u32[]{:S(2)}, u32[]{:S(2)}) collective-permute-start(bf16[128,256]{1,0:T(8,128)(2,1)S(1)} %get-tuple-element.44), channel_id=1, source_target_pairs={{0,24},{4,28},{8,16},{12,20},{16,8},{20,12},{24,0},{28,4},{1,25},{... | collective-permute-start | bytes 196616 | tf_op jit(solution)/shard_map/ppermute | solution.py:297
  78.0 1.4 %collective-permute-start.21 = (bf16[128,256]{1,0:T(8,128)(2,1)S(1)}, bf16[128,256]{1,0:T(8,128)(2,1)S(1)}, u32[]{:S(2)}, u32[]{:S(2)}) collective-permute-start(bf16[128,256]{1,0:T(8,128)(2,1)S(1)} %get-tuple-element.45), channel_id=1, source_target_pairs={{0,16},{4,20},{8,24},{12,28},{16,0},{20,4},{24,8},{28,12},{1,17},{... | collective-permute-start | bytes 196616 | tf_op jit(solution)/shard_map/ppermute | solution.py:297
  79.5 1.1 %collective-permute-start.20 = (bf16[128,256]{1,0:T(8,128)(2,1)S(1)}, bf16[128,256]{1,0:T(8,128)(2,1)S(1)}, u32[]{:S(2)}, u32[]{:S(2)}) collective-permute-start(bf16[128,256]{1,0:T(8,128)(2,1)S(1)} %get-tuple-element.46), channel_id=1, source_target_pairs={{0,8},{4,12},{8,0},{12,4},{16,24},{20,28},{24,16},{28,20},{1,9},{5... | collective-permute-start | bytes 196616 | tf_op jit(solution)/shard_map/ppermute | solution.py:297
  80.6 1.1 %shard_map.87 = (bf16[128,2048]{1,0:T(8,128)(2,1)}, bf16[128,2048]{1,0:T(8,128)(2,1)}) custom-call(bf16[128,1024]{1,0:T(8,128)(2,1)S(1)} %get-tuple-element.33.refs_0_, bf16[128,1024]{1,0:T(8,128)(2,1)S(1)} %collective-permute-done.13.refs_1_, bf16[128,1024]{1,0:T(8,128)(2,1)S(1)} %collective-permute-done.14.refs_2_, ...), custom_call_target="tpu_custom_call" | custom-call | tf_op jit(solution)/shard_map/pallas_call | solution.py:334
  81.6 0.7 collective-permute-done.22.refs_3_
  82.3 0.6 collective-permute-done.21.refs_2_
  82.9 0.8 collective-permute-done.20.refs_1_
  83.7 0.8 shard_map.88
  (17 shorter events, 0.1 us)
Async XLA Ops:
  0.6 0.9 %copy-start.2 = (bf16[128,512]{1,0:T(8,128)(2,1)S(1)}, bf16[128,512]{1,0:T(8,128)(2,1)}, u32[]{:S(2)}) copy-start(bf16[128,512]{1,0:T(8,128)(2,1)} %left_ref.3) | copy-start | bytes 393220
  1.5 0.9 %copy-start.3 = (bf16[128,512]{1,0:T(8,128)(2,1)S(1)}, bf16[128,512]{1,0:T(8,128)(2,1)}, u32[]{:S(2)}) copy-start(bf16[128,512]{1,0:T(8,128)(2,1)} %right_ref.3) | copy-start | bytes 393220
  2.4 12.4 %copy-start = (bf16[128,2048]{1,0:T(8,128)(2,1)S(1)}, bf16[128,2048]{1,0:T(8,128)(2,1)}, u32[]{:S(2)}) copy-start(bf16[128,2048]{1,0:T(8,128)(2,1)} %left_ref.2) | copy-start | bytes 1572868
  2.5 5.4 %collective-permute-start.3 = (bf16[128,256]{1,0:T(8,128)(2,1)S(1)}, bf16[128,256]{1,0:T(8,128)(2,1)S(1)}, u32[]{:S(2)}, u32[]{:S(2)}) collective-permute-start(bf16[128,256]{1,0:T(8,128)(2,1)S(1)} %get-tuple-element.30), channel_id=1, source_target_pairs={{0,8},{4,12},{8,0},{12,4},{16,24},{20,28},{24,16},{28,20},{1,9},{5... | collective-permute-start | bytes 196616 | tf_op jit(solution)/shard_map/ppermute | solution.py:297
  5.5 4.3 %collective-permute-start.4 = (bf16[128,256]{1,0:T(8,128)(2,1)S(1)}, bf16[128,256]{1,0:T(8,128)(2,1)S(1)}, u32[]{:S(2)}, u32[]{:S(2)}) collective-permute-start(bf16[128,256]{1,0:T(8,128)(2,1)S(1)} %get-tuple-element.31), channel_id=1, source_target_pairs={{0,16},{4,20},{8,24},{12,28},{16,0},{20,4},{24,8},{28,12},{1,17},{... | collective-permute-start | bytes 196616 | tf_op jit(solution)/shard_map/ppermute | solution.py:297
  7.0 5.2 %collective-permute-start.5 = (bf16[128,256]{1,0:T(8,128)(2,1)S(1)}, bf16[128,256]{1,0:T(8,128)(2,1)S(1)}, u32[]{:S(2)}, u32[]{:S(2)}) collective-permute-start(bf16[128,256]{1,0:T(8,128)(2,1)S(1)} %get-tuple-element.32), channel_id=1, source_target_pairs={{0,24},{4,28},{8,16},{12,20},{16,8},{20,12},{24,0},{28,4},{1,25},{... | collective-permute-start | bytes 196616 | tf_op jit(solution)/shard_map/ppermute | solution.py:297
  12.2 2.7 %copy-start.4 = (s32[32]{0:T(128)S(1)}, s32[32]{0:T(128)}, u32[]{:S(2)}) copy-start(s32[32]{0:T(128)} %refs_0_.1) | copy-start | bytes 388
  12.2 13.0 %collective-permute-start.9 = (bf16[4,128,256]{2,1,0:T(8,128)(2,1)S(1)}, bf16[4,128,256]{2,1,0:T(8,128)(2,1)S(1)}, u32[]{:S(2)}, u32[]{:S(2)}) collective-permute-start(bf16[4,128,256]{2,1,0:T(8,128)(2,1)S(1)} %pad_maximum_fusion.refs_6_), channel_id=1, source_target_pairs={{0,2},{1,3},{2,0},{3,1},{4,6},{5,7},{6,4},{7,5},{8,10},{9,11},{10,... | collective-permute-start | bytes 786440 | tf_op jit(solution)/shard_map/ppermute | solution.py:297
  14.9 1.0 %copy-start.1 = (bf16[128,2048]{1,0:T(8,128)(2,1)S(1)}, bf16[128,2048]{1,0:T(8,128)(2,1)}, u32[]{:S(2)}) copy-start(bf16[128,2048]{1,0:T(8,128)(2,1)} %right_ref.2) | copy-start | bytes 1572868
  17.1 9.8 %collective-permute-start = (bf16[128,1024]{1,0:T(8,128)(2,1)S(1)}, bf16[128,1024]{1,0:T(8,128)(2,1)S(1)}, u32[]{:S(2)}, u32[]{:S(2)}) collective-permute-start(bf16[128,1024]{1,0:T(8,128)(2,1)S(1)} %get-tuple-element.26), channel_id=1, source_target_pairs={{0,8},{4,12},{8,0},{12,4},{16,24},{20,28},{24,16},{28,20},{1,9},{5... | collective-permute-start | bytes 786440 | tf_op jit(solution)/shard_map/ppermute | solution.py:297
  17.7 9.2 %collective-permute-start.1 = (bf16[128,1024]{1,0:T(8,128)(2,1)S(1)}, bf16[128,1024]{1,0:T(8,128)(2,1)S(1)}, u32[]{:S(2)}, u32[]{:S(2)}) collective-permute-start(bf16[128,1024]{1,0:T(8,128)(2,1)S(1)} %get-tuple-element.27), channel_id=1, source_target_pairs={{0,16},{4,20},{8,24},{12,28},{16,0},{20,4},{24,8},{28,12},{1,17},{... | collective-permute-start | bytes 786440 | tf_op jit(solution)/shard_map/ppermute | solution.py:297
  18.2 12.3 %collective-permute-start.7 = (bf16[4,128,256]{2,1,0:T(8,128)(2,1)S(1)}, bf16[4,128,256]{2,1,0:T(8,128)(2,1)S(1)}, u32[]{:S(2)}, u32[]{:S(2)}) collective-permute-start(bf16[4,128,256]{2,1,0:T(8,128)(2,1)S(1)} %pad_maximum_fusion.refs_6_), channel_id=1, source_target_pairs={{0,1},{1,0},{2,3},{3,2},{4,5},{5,4},{6,7},{7,6},{8,9},{9,8},{10,11... | collective-permute-start | bytes 786440 | tf_op jit(solution)/shard_map/ppermute | solution.py:297
  25.3 9.0 %collective-permute-start.11 = (bf16[4,128,256]{2,1,0:T(8,128)(2,1)S(1)}, bf16[4,128,256]{2,1,0:T(8,128)(2,1)S(1)}, u32[]{:S(2)}, u32[]{:S(2)}) collective-permute-start(bf16[4,128,256]{2,1,0:T(8,128)(2,1)S(1)} %collective-permute-done.9.refs_10_), channel_id=1, source_target_pairs={{0,1},{1,0},{2,3},{3,2},{4,5},{5,4},{6,7},{7,6},{8,9},{9,8},{10,11... | collective-permute-start | bytes 786440 | tf_op jit(solution)/shard_map/ppermute | solution.py:297
  25.9 8.8 %collective-permute-start.2 = (bf16[128,1024]{1,0:T(8,128)(2,1)S(1)}, bf16[128,1024]{1,0:T(8,128)(2,1)S(1)}, u32[]{:S(2)}, u32[]{:S(2)}) collective-permute-start(bf16[128,1024]{1,0:T(8,128)(2,1)S(1)} %get-tuple-element.28), channel_id=1, source_target_pairs={{0,24},{4,28},{8,16},{12,20},{16,8},{20,12},{24,0},{28,4},{1,25},{... | collective-permute-start | bytes 786440 | tf_op jit(solution)/shard_map/ppermute | solution.py:297
  26.9 7.9 %collective-permute-start.6 = (bf16[4,128,256]{2,1,0:T(8,128)(2,1)S(1)}, bf16[4,128,256]{2,1,0:T(8,128)(2,1)S(1)}, u32[]{:S(2)}, u32[]{:S(2)}) collective-permute-start(bf16[4,128,256]{2,1,0:T(8,128)(2,1)S(1)} %pad_maximum_fusion.refs_6_), channel_id=1, source_target_pairs={{0,4},{4,0},{8,12},{12,8},{16,20},{20,16},{24,28},{28,24},{1,5},{5... | collective-permute-start | bytes 786440 | tf_op jit(solution)/shard_map/ppermute | solution.py:297
  26.9 7.9 %collective-permute-start.10 = (bf16[4,128,256]{2,1,0:T(8,128)(2,1)S(1)}, bf16[4,128,256]{2,1,0:T(8,128)(2,1)S(1)}, u32[]{:S(2)}, u32[]{:S(2)}) collective-permute-start(bf16[4,128,256]{2,1,0:T(8,128)(2,1)S(1)} %collective-permute-done.9.refs_10_), channel_id=1, source_target_pairs={{0,4},{4,0},{8,12},{12,8},{16,20},{20,16},{24,28},{28,24},{1,5},{5... | collective-permute-start | bytes 786440 | tf_op jit(solution)/shard_map/ppermute | solution.py:297
  30.5 4.2 %collective-permute-start.8 = (bf16[4,128,256]{2,1,0:T(8,128)(2,1)S(1)}, bf16[4,128,256]{2,1,0:T(8,128)(2,1)S(1)}, u32[]{:S(2)}, u32[]{:S(2)}) collective-permute-start(bf16[4,128,256]{2,1,0:T(8,128)(2,1)S(1)} %collective-permute-done.7.refs_8_), channel_id=1, source_target_pairs={{0,4},{4,0},{8,12},{12,8},{16,20},{20,16},{24,28},{28,24},{1,5},{5... | collective-permute-start | bytes 786440 | tf_op jit(solution)/shard_map/ppermute | solution.py:297
  34.3 1.5 %collective-permute-start.12 = (bf16[4,128,256]{2,1,0:T(8,128)(2,1)S(1)}, bf16[4,128,256]{2,1,0:T(8,128)(2,1)S(1)}, u32[]{:S(2)}, u32[]{:S(2)}) collective-permute-start(bf16[4,128,256]{2,1,0:T(8,128)(2,1)S(1)} %collective-permute-done.11.refs_12_), channel_id=1, source_target_pairs={{0,4},{4,0},{8,12},{12,8},{16,20},{20,16},{24,28},{28,24},{1,5},{5... | collective-permute-start | bytes 786440 | tf_op jit(solution)/shard_map/ppermute | solution.py:297
  48.0 2.7 %collective-permute-start.16 = (bf16[4,4,128,256]{3,2,1,0:T(8,128)(2,1)S(1)}, bf16[4,4,128,256]{3,2,1,0:T(8,128)(2,1)S(1)}, u32[]{:S(2)}, u32[]{:S(2)}) collective-permute-start(bf16[4,4,128,256]{3,2,1,0:T(8,128)(2,1)S(1)} %get-tuple-element.40), channel_id=1, source_target_pairs={{0,4},{4,0},{8,12},{12,8},{16,20},{20,16},{24,28},{28,24},{1,5},{5... | collective-permute-start | bytes 3145736 | tf_op jit(solution)/shard_map/ppermute | solution.py:297
  50.9 8.4 %collective-permute-start.17 = (bf16[4,128,256]{2,1,0:T(8,128)(2,1)S(1)}, bf16[4,128,256]{2,1,0:T(8,128)(2,1)S(1)}, u32[]{:S(2)}, u32[]{:S(2)}) collective-permute-start(bf16[4,128,256]{2,1,0:T(8,128)(2,1)S(1)} %get-tuple-element.49), channel_id=1, source_target_pairs={{0,1},{1,0},{2,3},{3,2},{4,5},{5,4},{6,7},{7,6},{8,9},{9,8},{10,11... | collective-permute-start | bytes 786440 | tf_op jit(solution)/shard_map/ppermute | solution.py:297
  59.4 16.2 %collective-permute-start.19 = (bf16[4,128,256]{2,1,0:T(8,128)(2,1)S(1)}, bf16[4,128,256]{2,1,0:T(8,128)(2,1)S(1)}, u32[]{:S(2)}, u32[]{:S(2)}) collective-permute-start(bf16[4,128,256]{2,1,0:T(8,128)(2,1)S(1)} %fusion), channel_id=1, source_target_pairs={{0,2},{1,3},{2,0},{3,1},{4,6},{5,7},{6,4},{7,5},{8,10},{9,11},{10,... | collective-permute-start | bytes 786440 | tf_op jit(solution)/shard_map/ppermute | solution.py:297
  64.1 12.7 %collective-permute-start.18 = (bf16[4,128,256]{2,1,0:T(8,128)(2,1)S(1)}, bf16[4,128,256]{2,1,0:T(8,128)(2,1)S(1)}, u32[]{:S(2)}, u32[]{:S(2)}) collective-permute-start(bf16[4,128,256]{2,1,0:T(8,128)(2,1)S(1)} %get-tuple-element.41), channel_id=1, source_target_pairs={{0,1},{1,0},{2,3},{3,2},{4,5},{5,4},{6,7},{7,6},{8,9},{9,8},{10,11... | collective-permute-start | bytes 786440 | tf_op jit(solution)/shard_map/ppermute | solution.py:297
  64.4 15.0 %collective-permute-start.13 = (bf16[128,1024]{1,0:T(8,128)(2,1)S(1)}, bf16[128,1024]{1,0:T(8,128)(2,1)S(1)}, u32[]{:S(2)}, u32[]{:S(2)}) collective-permute-start(bf16[128,1024]{1,0:T(8,128)(2,1)S(1)} %get-tuple-element.34), channel_id=1, source_target_pairs={{0,8},{4,12},{8,0},{12,4},{16,24},{20,28},{24,16},{28,20},{1,9},{5... | collective-permute-start | bytes 786440 | tf_op jit(solution)/shard_map/ppermute | solution.py:297
  65.4 15.2 %collective-permute-start.14 = (bf16[128,1024]{1,0:T(8,128)(2,1)S(1)}, bf16[128,1024]{1,0:T(8,128)(2,1)S(1)}, u32[]{:S(2)}, u32[]{:S(2)}) collective-permute-start(bf16[128,1024]{1,0:T(8,128)(2,1)S(1)} %get-tuple-element.35), channel_id=1, source_target_pairs={{0,16},{4,20},{8,24},{12,28},{16,0},{20,4},{24,8},{28,12},{1,17},{... | collective-permute-start | bytes 786440 | tf_op jit(solution)/shard_map/ppermute | solution.py:297
  66.0 14.6 %collective-permute-start.15 = (bf16[128,1024]{1,0:T(8,128)(2,1)S(1)}, bf16[128,1024]{1,0:T(8,128)(2,1)S(1)}, u32[]{:S(2)}, u32[]{:S(2)}) collective-permute-start(bf16[128,1024]{1,0:T(8,128)(2,1)S(1)} %get-tuple-element.36), channel_id=1, source_target_pairs={{0,24},{4,28},{8,16},{12,20},{16,8},{20,12},{24,0},{28,4},{1,25},{... | collective-permute-start | bytes 786440 | tf_op jit(solution)/shard_map/ppermute | solution.py:297
  77.0 5.3 %collective-permute-start.22 = (bf16[128,256]{1,0:T(8,128)(2,1)S(1)}, bf16[128,256]{1,0:T(8,128)(2,1)S(1)}, u32[]{:S(2)}, u32[]{:S(2)}) collective-permute-start(bf16[128,256]{1,0:T(8,128)(2,1)S(1)} %get-tuple-element.44), channel_id=1, source_target_pairs={{0,24},{4,28},{8,16},{12,20},{16,8},{20,12},{24,0},{28,4},{1,25},{... | collective-permute-start | bytes 196616 | tf_op jit(solution)/shard_map/ppermute | solution.py:297
  78.0 4.9 %collective-permute-start.21 = (bf16[128,256]{1,0:T(8,128)(2,1)S(1)}, bf16[128,256]{1,0:T(8,128)(2,1)S(1)}, u32[]{:S(2)}, u32[]{:S(2)}) collective-permute-start(bf16[128,256]{1,0:T(8,128)(2,1)S(1)} %get-tuple-element.45), channel_id=1, source_target_pairs={{0,16},{4,20},{8,24},{12,28},{16,0},{20,4},{24,8},{28,12},{1,17},{... | collective-permute-start | bytes 196616 | tf_op jit(solution)/shard_map/ppermute | solution.py:297
  79.5 4.3 %collective-permute-start.20 = (bf16[128,256]{1,0:T(8,128)(2,1)S(1)}, bf16[128,256]{1,0:T(8,128)(2,1)S(1)}, u32[]{:S(2)}, u32[]{:S(2)}) collective-permute-start(bf16[128,256]{1,0:T(8,128)(2,1)S(1)} %get-tuple-element.46), channel_id=1, source_target_pairs={{0,8},{4,12},{8,0},{12,4},{16,24},{20,28},{24,16},{28,20},{1,9},{5... | collective-permute-start | bytes 196616 | tf_op jit(solution)/shard_map/ppermute | solution.py:297

commit v4 on v3

--- a/solution.py
+++ b/solution.py
@@ -292,9 +292,14 @@
 SMALL = pltpu.CompilerParams(vmem_limit_bytes=8 * 1024 * 1024)
 
 
-def flipped(value, axis, bits):
-    count = lax.axis_size(axis)
-    return lax.ppermute(value, axis, [(source, source ^ bits) for source in range(count)])
+def flipped(value, ctx_bits, head_bits):
+    ctx, heads = lax.axis_size("ctx"), lax.axis_size("head")
+    pairs = [
+        (c * heads + h, (c ^ ctx_bits) * heads + (h ^ head_bits))
+        for c in range(ctx)
+        for h in range(heads)
+    ]
+    return lax.ppermute(value, ("ctx", "head"), pairs)
 
 
 def piece_columns(pieces, flip, wide):
@@ -378,7 +383,6 @@
 
 KEY_ROWS = 256
 BATCH = 4
-GRAD_BATCH = 4
 MARKS = 128
 HIDDEN = -(2.0**100)
 
@@ -452,14 +456,20 @@
         total = total + count
     for spare in range(BATCH - 1):
         entry(total + spare, 0, 0, -(1 << 20))
-    rounds = (total + BATCH - 1) // BATCH
-
-    def sweep(body, batch):
+    rounds = (total + 1) // BATCH
+    left_over = (total - rounds * BATCH + 1) // 2
+
+    def sweep(body):
         def one_round(number, _):
-            body([number * batch + place for place in range(batch)])
+            body([number * BATCH + place for place in range(BATCH)])
             return 0
 
-        lax.fori_loop(0, rounds * (BATCH // batch), one_round, 0)
+        def one_pair(number, _):
+            body([rounds * BATCH + number * 2 + place for place in range(2)])
+            return 0
+
+        lax.fori_loop(0, rounds, one_round, 0)
+        lax.fori_loop(0, left_over, one_pair, 0)
 
     def key_rows(item):
         return pl.ds(pl.multiple_of(table[1, item], tok), KEY_ROWS)
@@ -491,7 +501,7 @@
                 tops[flip], jnp.max(raw.reshape(KEY_ROWS // 8, 8, lanes), axis=0)
             )
 
-    sweep(scores_round, BATCH)
+    sweep(scores_round)
     for flip in range(KVH):
         tops[flip] = jnp.broadcast_to(jnp.max(tops[flip], axis=0, keepdims=True), (8, lanes))
 
@@ -515,7 +525,7 @@
         for item, value in zip(items, parts):
             acc[table[0, item]] += value
 
-    sweep(out_round, BATCH)
+    sweep(out_round)
     for flip in range(KVH):
         inverse = 1.0 / acc[flip, HD : HD + 1, :]
         turned = (acc[flip, :HD, :] * inverse).astype(bf16)
@@ -556,7 +566,7 @@
                 k_all[rows, :], score_grad, CONTRACT_FIRST, preferred_element_type=f32
             )
 
-    sweep(grad_round, GRAD_BATCH)
+    sweep(grad_round)
 
     for flip, od_ref in enumerate(od_refs):
         turned = (acc[flip, :HD, :] * scaling).astype(bf16).T
@@ -613,31 +623,52 @@
     heads, ctx = lax.axis_size("head"), lax.axis_size("ctx")
     cores = ctx // KVH
     total = queries.shape[0] * heads * ctx
+    together = lax.optimization_barrier
+
+    def over_part(piece, flip):
+        return flipped(piece, flip * cores, 0)
 
     def exchange(pieces):
-        span = ctx // len(pieces)
-        return [pieces[0]] + [flipped(p, "ctx", (s + 1) * span) for s, p in enumerate(pieces[1:])]
-
-    kv_mine = jnp.stack(exchange(split_heads(keys, values, KVH)))
+        return [pieces[0]] + [over_part(piece, s + 1) for s, piece in enumerate(pieces[1:])]
+
+    def summed(*terms):
+        return sum(term.astype(jnp.float32) for term in terms).astype(jnp.bfloat16)
+
+    kv_pieces = split_heads(keys, values, KVH)
+    far_own = flipped(kv_pieces[0][None], 0, 2)
+    kv_pieces = exchange(kv_pieces)
+    kv_mine = jnp.stack(kv_pieces)
+    far_rest = flipped(jnp.stack(kv_pieces[1:]), 0, 2)
+    far = jnp.concatenate([far_own, far_rest])
     qd, marks = prepare(lengths, queries, d_out, KVH, total)
     qd = exchange(qd)
-    near, far = flipped(kv_mine, "head", 1), flipped(kv_mine, "head", 2)
+    near = flipped(kv_mine, 0, 1)
     kv = []
-    for piece in (kv_mine, near, far, flipped(far, "head", 1)):
-        kv += [piece, flipped(piece, "ctx", 1)]
+    for piece in (kv_mine, near, far, flipped(far, 0, 1)):
+        kv += [piece, flipped(piece, 1, 0)]
     od, dkv = attention(lengths, marks, qd, kv, cores, heads)
 
-    def summed(*terms):
-        return sum(term.astype(jnp.float32) for term in terms).astype(jnp.bfloat16)
-
-    both = (dkv[0], flipped(dkv[1], "ctx", 1))
-    third = flipped(summed(*(term[3] for term in both)), "head", 1)
-    second = flipped(summed(*(term[2] for term in both), third), "head", 2)
-    first, _ = lax.optimization_barrier((summed(*(term[1] for term in both)), third))
-    first = flipped(first, "head", 1)
-    grads = [summed(*(term[0, s] for term in both), first[s], second[s]) for s in range(KVH)]
-    attn_out, grad_queries = join_heads(exchange(od))
-    grad_keys, grad_values = join_heads(exchange(grads))
+    both = (dkv[0], flipped(dkv[1], 1, 0))
+    third = flipped(summed(*(term[3] for term in both)), 0, 1)
+    first, _ = together((summed(*(term[1] for term in both)), third))
+    first, rest, od_moved = together(
+        (
+            flipped(first, 0, 1),
+            flipped(summed(*(term[2, 1:] for term in both), third[1:]), 0, 2),
+            exchange(od)[1:],
+        )
+    )
+    own, grads = together(
+        (
+            summed(*(term[2, 0] for term in both), third[0]),
+            [summed(*(term[0, s] for term in both), first[s], rest[s - 1]) for s in (1, 2, 3)],
+        )
+    )
+    own = flipped(own, 0, 2)
+    grads = [over_part(grad, s + 1) for s, grad in enumerate(grads)]
+    attn_out, grad_queries = join_heads([od[0], *od_moved])
+    grads = [summed(*(term[0, 0] for term in both), first[0], own), *grads]
+    grad_keys, grad_values = join_heads(grads)
     return attn_out, grad_queries, grad_keys, grad_values
 
 

time: 83.4 us -> 79.3 us (0.951); the launches traced: 84.5 us -> 78 us
  waiting for transfers between devices: 41.1 us -> 31.9 us
  starting transfers between devices: 24.2 us -> 28.1 us
  Pallas kernels: 15.2 us -> 12.8 us
  local copies, waits for them, and re-layouts: 2.85 us -> 3.91 us
    ppermute x23 -> x25, waiting for transfers between devices: 41.1 us -> 31.9 us  [flipped(): return lax.ppermute(value, ('ctx', 'head'), pairs)]
    ppermute x23 -> x25, starting transfers between devices: 24.2 us -> 28.1 us  [flipped(): return lax.ppermute(value, ('ctx', 'head'), pairs)]
    pallas_call x1, Pallas kernels: 12.2 us -> 9.84 us  [attention(): pl.pallas_call(functools.partial(attention_kernel, cores, heads, tok), ou...]
    unnamed x10 -> x11, local copies, waits for them, and re-layouts: 2.85 us -> 3.89 us
  transfers between devices with their start and end apart: 23 -> 25, of which waited for: 15 -> 12; matrix products, arithmetic and copies ran while one was open for 0% -> 0% of each run, Pallas kernels for 3% -> 3%
where the time goes in v4:
time: 79.3 us; the launch traced here: 78 us
  waiting for transfers between devices  31.9 us (40%)
  starting transfers between devices  28.1 us (35%)
  Pallas kernels  12.8 us (16%)
  local copies, waits for them, and re-layouts  3.91 us (5%)
    ppermute x25, waiting for transfers between devices, flipped(): return lax.ppermute(value, ('ctx', 'head'), pairs)  31.9 us
    ppermute x25, starting transfers between devices, flipped(): return lax.ppermute(value, ('ctx', 'head'), pairs)  28.1 us
    pallas_call x1, Pallas kernels, attention(): pl.pallas_call(functools.partial(attention_kernel, cores, heads, tok), ou...  9.84 us
    unnamed x11, local copies, waits for them, and re-layouts  3.89 us
    pallas_call x2, Pallas kernels, join_heads(): pl.pallas_call(functools.partial(join_heads_kernel, pieces, wide), out_sh...  1.81 us
  transfers between devices with their start and end apart: 25, of which 12 were waited for; matrix products, arithmetic and copies ran while one was open for 0% of the time, Pallas kernels for 3%

profile of v4, /device:TPU:0, one launch (start us, length us, event | category | flops | bytes accessed | tf_op | source)
XLA Modules:
  0.0 78.0 jit_solution(7902054671132548862)
XLA Ops:
  0.6 0.9 %copy-done.2 = bf16[128,512]{1,0:T(8,128)(2,1)S(1)} copy-done((bf16[128,512]{1,0:T(8,128)(2,1)S(1)}, bf16[128,512]{1,0:T(8,128)(2,1)}, u32[]{:S(2)}) %copy-start.2) | copy-done | bytes 131096
  1.5 0.9 %copy-done.3 = bf16[128,512]{1,0:T(8,128)(2,1)S(1)} copy-done((bf16[128,512]{1,0:T(8,128)(2,1)S(1)}, bf16[128,512]{1,0:T(8,128)(2,1)}, u32[]{:S(2)}) %copy-start.3) | copy-done | bytes 131096
  2.5 3.0 %collective-permute-start.3 = (bf16[128,256]{1,0:T(8,128)(2,1)S(1)}, bf16[128,256]{1,0:T(8,128)(2,1)S(1)}, u32[]{:S(2)}, u32[]{:S(2)}) collective-permute-start(bf16[128,256]{1,0:T(8,128)(2,1)S(1)} %get-tuple-element.39), channel_id=1, source_target_pairs={{0,8},{1,9},{2,10},{3,11},{4,12},{5,13},{6,14},{7,15},{8,0},{9,1},... | collective-permute-start | bytes 196616 | tf_op jit(solution)/shard_map/ppermute | solution.py:302
  5.5 1.5 %collective-permute-start.4 = (bf16[128,256]{1,0:T(8,128)(2,1)S(1)}, bf16[128,256]{1,0:T(8,128)(2,1)S(1)}, u32[]{:S(2)}, u32[]{:S(2)}) collective-permute-start(bf16[128,256]{1,0:T(8,128)(2,1)S(1)} %get-tuple-element.40), channel_id=1, source_target_pairs={{0,16},{1,17},{2,18},{3,19},{4,20},{5,21},{6,22},{7,23},{8,24},{9,... | collective-permute-start | bytes 196616 | tf_op jit(solution)/shard_map/ppermute | solution.py:302
  7.0 0.0 collective-permute-start.5
  7.0 3.0 %collective-permute-start.9 = (bf16[1,128,256]{2,1,0:T(8,128)(2,1)S(1)}, bf16[1,128,256]{2,1,0:T(8,128)(2,1)S(1)}, u32[]{:S(2)}, u32[]{:S(2)}) collective-permute-start(bf16[1,128,256]{2,1,0:T(8,128)(2,1)S(1)} %bitcast.48), channel_id=1, source_target_pairs={{0,2},{1,3},{2,0},{3,1},{4,6},{5,7},{6,4},{7,5},{8,10},{9,11},{10,... | collective-permute-start | bytes 196616 | tf_op jit(solution)/shard_map/ppermute | solution.py:302
  10.1 1.0 %copy-done = bf16[128,2048]{1,0:T(8,128)(2,1)S(1)} copy-done((bf16[128,2048]{1,0:T(8,128)(2,1)S(1)}, bf16[128,2048]{1,0:T(8,128)(2,1)}, u32[]{:S(2)}) %copy-start) | copy-done | bytes 524312
  11.1 1.0 %copy-done.1 = bf16[128,2048]{1,0:T(8,128)(2,1)S(1)} copy-done((bf16[128,2048]{1,0:T(8,128)(2,1)S(1)}, bf16[128,2048]{1,0:T(8,128)(2,1)}, u32[]{:S(2)}) %copy-start.1) | copy-done | bytes 524312
  12.2 1.1 %shard_map.84 = (bf16[128,1024]{1,0:T(8,128)(2,1)S(1)}, bf16[128,1024]{1,0:T(8,128)(2,1)S(1)}, bf16[128,1024]{1,0:T(8,128)(2,1)S(1)}, bf16[128,1024]{1,0:T(8,128)(2,1)S(1)}, bf16[4096,128]{1,0:T(8,128)(2,1)S(1)}) custom-call(s32[32]{0:T(128)S(1)} %copy-done.4, bf16[128,2048]{1,0:T(8,128)(2,1)S(1)} %copy-done, bf16[128,2048]{1,0:T(8,128)(2,1)S(1)} %copy-done.1), custom_call_target="tpu_custom_call" | custom-call | tf_op jit(solution)/shard_map/pallas_call | solution.py:373
  13.3 1.6 %collective-permute-start = (bf16[128,1024]{1,0:T(8,128)(2,1)S(1)}, bf16[128,1024]{1,0:T(8,128)(2,1)S(1)}, u32[]{:S(2)}, u32[]{:S(2)}) collective-permute-start(bf16[128,1024]{1,0:T(8,128)(2,1)S(1)} %get-tuple-element.35), channel_id=1, source_target_pairs={{0,8},{1,9},{2,10},{3,11},{4,12},{5,13},{6,14},{7,15},{8,0},{9,1},... | collective-permute-start | bytes 786440 | tf_op jit(solution)/shard_map/ppermute | solution.py:302
  14.9 0.0 collective-permute-done.3
  14.9 1.5 %collective-permute-start.1 = (bf16[128,1024]{1,0:T(8,128)(2,1)S(1)}, bf16[128,1024]{1,0:T(8,128)(2,1)S(1)}, u32[]{:S(2)}, u32[]{:S(2)}) collective-permute-start(bf16[128,1024]{1,0:T(8,128)(2,1)S(1)} %get-tuple-element.36), channel_id=1, source_target_pairs={{0,16},{1,17},{2,18},{3,19},{4,20},{5,21},{6,22},{7,23},{8,24},{9,... | collective-permute-start | bytes 786440 | tf_op jit(solution)/shard_map/ppermute | solution.py:302
  16.4 0.0 collective-permute-done.4
  16.4 0.0 collective-permute-done.5
  16.4 0.7 collective-permute-start.10
  17.2 1.6 %collective-permute-start.7 = (bf16[4,128,256]{2,1,0:T(8,128)(2,1)S(1)}, bf16[4,128,256]{2,1,0:T(8,128)(2,1)S(1)}, u32[]{:S(2)}, u32[]{:S(2)}) collective-permute-start(bf16[4,128,256]{2,1,0:T(8,128)(2,1)S(1)} %pad_maximum_fusion.refs_6_), channel_id=1, source_target_pairs={{0,1},{1,0},{2,3},{3,2},{4,5},{5,4},{6,7},{7,6},{8,9},{9,8},{10,11... | collective-permute-start | bytes 786440 | tf_op jit(solution)/shard_map/ppermute | solution.py:302
  18.8 7.8 %collective-permute-done.10 = bf16[3,128,256]{2,1,0:T(8,128)(2,1)S(1)} collective-permute-done((bf16[3,128,256]{2,1,0:T(8,128)(2,1)S(1)}, bf16[3,128,256]{2,1,0:T(8,128)(2,1)S(1)}, u32[]{:S(2)}, u32[]{:S(2)}) %collective-permute-start.10) | collective-permute-done | bytes 196640 | tf_op jit(solution)/shard_map/ppermute | solution.py:302
  26.7 0.3 collective-permute-start.12
  27.0 0.5 collective-permute-start.2
  27.5 0.5 collective-permute-start.11
  28.0 0.1 collective-permute-done.7.refs_8_
  28.1 5.4 %collective-permute-done.12.refs_12_ = bf16[4,128,256]{2,1,0:T(8,128)(2,1)S(1)} collective-permute-done((bf16[4,128,256]{2,1,0:T(8,128)(2,1)S(1)}, bf16[4,128,256]{2,1,0:T(8,128)(2,1)S(1)}, u32[]{:S(2)}, u32[]{:S(2)}) %collective-permute-start.12) | collective-permute-done | bytes 262176 | tf_op jit(solution)/shard_map/ppermute | solution.py:302
  33.4 0.8 %collective-permute-done.2.refs_5_ = bf16[128,1024]{1,0:T(8,128)(2,1)S(1)} collective-permute-done((bf16[128,1024]{1,0:T(8,128)(2,1)S(1)}, bf16[128,1024]{1,0:T(8,128)(2,1)S(1)}, u32[]{:S(2)}, u32[]{:S(2)}) %collective-permute-start.2) | collective-permute-done | bytes 262176 | tf_op jit(solution)/shard_map/ppermute | solution.py:302
  34.2 0.7 collective-permute-done.13.refs_13_
  35.0 9.8 %shard_map.86 = (bf16[128,1024]{1,0:T(8,128)(2,1)S(1)}, bf16[128,1024]{1,0:T(8,128)(2,1)S(1)}, bf16[128,1024]{1,0:T(8,128)(2,1)S(1)}, bf16[128,1024]{1,0:T(8,128...) custom-call(s32[32]{0:T(128)S(1)} %copy-done.4, ...), custom_call_target="tpu_custom_call" | custom-call | tf_op jit(solution)/shard_map/pallas_call | solution.py:594
  44.8 1.6 %collective-permute-start.14 = (bf16[4,4,128,256]{3,2,1,0:T(8,128)(2,1)S(1)}, bf16[4,4,128,256]{3,2,1,0:T(8,128)(2,1)S(1)}, u32[]{:S(2)}, u32[]{:S(2)}) collective-permute-start(bf16[4,4,128,256]{3,2,1,0:T(8,128)(2,1)S(1)} %get-tuple-element.44), channel_id=1, source_target_pairs={{0,4},{1,5},{2,6},{3,7},{4,0},{5,1},{6,2},{7,3},{8,12},{9,13},{10,... | collective-permute-start | bytes 3145736 | tf_op jit(solution)/shard_map/ppermute | solution.py:302
  46.4 2.3 %collective-permute-done.14 = bf16[4,4,128,256]{3,2,1,0:T(8,128)(2,1)S(1)} collective-permute-done((bf16[4,4,128,256]{3,2,1,0:T(8,128)(2,1)S(1)}, bf16[4,4,128,256]{3,2,1,0:T(8,128)(2,1)S(1)}, u32[]{:S(2)}, u32[]{:S(2)}) %collective-permute-start.14) | collective-permute-done | bytes 1048608 | tf_op jit(solution)/shard_map/ppermute | solution.py:302
  48.7 0.1 fusion.2
  48.8 0.3 collective-permute-start.15
  49.1 0.5 collective-permute-start.18
  49.6 0.5 collective-permute-start.19
  50.1 2.4 %collective-permute-start.20 = (bf16[128,1024]{1,0:T(8,128)(2,1)S(1)}, bf16[128,1024]{1,0:T(8,128)(2,1)S(1)}, u32[]{:S(2)}, u32[]{:S(2)}) collective-permute-start(bf16[128,1024]{1,0:T(8,128)(2,1)S(1)} %get-tuple-element.48), channel_id=1, source_target_pairs={{0,24},{1,25},{2,26},{3,27},{4,28},{5,29},{6,30},{7,31},{8,16},{9,... | collective-permute-start | bytes 786440 | tf_op jit(solution)/shard_map/ppermute | solution.py:302
  52.6 4.9 %collective-permute-done.15 = bf16[4,128,256]{2,1,0:T(8,128)(2,1)S(1)} collective-permute-done((bf16[4,128,256]{2,1,0:T(8,128)(2,1)S(1)}, bf16[4,128,256]{2,1,0:T(8,128)(2,1)S(1)}, u32[]{:S(2)}, u32[]{:S(2)}) %collective-permute-start.15) | collective-permute-done | bytes 262176 | tf_op jit(solution)/shard_map/ppermute | solution.py:302
  57.5 0.3 collective-permute-start.16
  57.7 0.1 fusion
  57.8 3.3 %collective-permute-start.17 = (bf16[3,128,256]{2,1,0:T(8,128)(2,1)S(1)}, bf16[3,128,256]{2,1,0:T(8,128)(2,1)S(1)}, u32[]{:S(2)}, u32[]{:S(2)}) collective-permute-start(bf16[3,128,256]{2,1,0:T(8,128)(2,1)S(1)} %fusion), channel_id=1, source_target_pairs={{0,2},{1,3},{2,0},{3,1},{4,6},{5,7},{6,4},{7,5},{8,10},{9,11},{10,... | collective-permute-start | bytes 589832 | tf_op jit(solution)/shard_map/ppermute | solution.py:302
  61.1 2.3 %collective-permute-done.19.refs_2_ = bf16[128,1024]{1,0:T(8,128)(2,1)S(1)} collective-permute-done((bf16[128,1024]{1,0:T(8,128)(2,1)S(1)}, bf16[128,1024]{1,0:T(8,128)(2,1)S(1)}, u32[]{:S(2)}, u32[]{:S(2)}) %collective-permute-start.19) | collective-permute-done | bytes 262176 | tf_op jit(solution)/shard_map/ppermute | solution.py:302
  63.4 4.0 %collective-permute-done.17 = bf16[3,128,256]{2,1,0:T(8,128)(2,1)S(1)} collective-permute-done((bf16[3,128,256]{2,1,0:T(8,128)(2,1)S(1)}, bf16[3,128,256]{2,1,0:T(8,128)(2,1)S(1)}, u32[]{:S(2)}, u32[]{:S(2)}) %collective-permute-start.17) | collective-permute-done | bytes 196640 | tf_op jit(solution)/shard_map/ppermute | solution.py:302
  67.4 2.1 %collective-permute-done.16 = bf16[4,128,256]{2,1,0:T(8,128)(2,1)S(1)} collective-permute-done((bf16[4,128,256]{2,1,0:T(8,128)(2,1)S(1)}, bf16[4,128,256]{2,1,0:T(8,128)(2,1)S(1)}, u32[]{:S(2)}, u32[]{:S(2)}) %collective-permute-start.16) | collective-permute-done | bytes 262176 | tf_op jit(solution)/shard_map/ppermute | solution.py:302
  69.4 0.1 fusion.3
  69.6 1.4 %collective-permute-start.21 = (bf16[128,256]{1,0:T(8,128)(2,1)S(1)}, bf16[128,256]{1,0:T(8,128)(2,1)S(1)}, u32[]{:S(2)}, u32[]{:S(2)}) collective-permute-start(bf16[128,256]{1,0:T(8,128)(2,1)S(1)} %get-tuple-element.56), channel_id=1, source_target_pairs={{0,2},{1,3},{2,0},{3,1},{4,6},{5,7},{6,4},{7,5},{8,10},{9,11},{10,... | collective-permute-start | bytes 196616 | tf_op jit(solution)/shard_map/ppermute | solution.py:302
  71.0 0.5 collective-permute-start.22
  71.5 0.5 collective-permute-start.23
  72.0 2.5 %collective-permute-start.24 = (bf16[128,256]{1,0:T(8,128)(2,1)S(1)}, bf16[128,256]{1,0:T(8,128)(2,1)S(1)}, u32[]{:S(2)}, u32[]{:S(2)}) collective-permute-start(bf16[128,256]{1,0:T(8,128)(2,1)S(1)} %get-tuple-element.59), channel_id=1, source_target_pairs={{0,24},{1,25},{2,26},{3,27},{4,28},{5,29},{6,30},{7,31},{8,16},{9,... | collective-permute-start | bytes 196616 | tf_op jit(solution)/shard_map/ppermute | solution.py:302
  74.5 1.1 %shard_map.87 = (bf16[128,2048]{1,0:T(8,128)(2,1)}, bf16[128,2048]{1,0:T(8,128)(2,1)}) custom-call(bf16[128,1024]{1,0:T(8,128)(2,1)S(1)} %get-tuple-element.42.refs_0_, bf16[128,1024]{1,0:T(8,128)(2,1)S(1)} %collective-permute-done.18.refs_1_, bf16[128,1024]{1,0:T(8,128)(2,1)S(1)} %collective-permute-done.19.refs_2_, ...), custom_call_target="tpu_custom_call" | custom-call | tf_op jit(solution)/shard_map/pallas_call | solution.py:339
  75.6 0.2 collective-permute-done.23.refs_2_
  75.8 1.4 %collective-permute-done.24.refs_3_ = bf16[128,256]{1,0:T(8,128)(2,1)S(1)} collective-permute-done((bf16[128,256]{1,0:T(8,128)(2,1)S(1)}, bf16[128,256]{1,0:T(8,128)(2,1)S(1)}, u32[]{:S(2)}, u32[]{:S(2)}) %collective-permute-start.24) | collective-permute-done | bytes 65568 | tf_op jit(solution)/shard_map/ppermute | solution.py:302
  77.2 0.8 shard_map.88
  (25 shorter events, 0.2 us)
Async XLA Ops:
  0.6 0.9 %copy-start.2 = (bf16[128,512]{1,0:T(8,128)(2,1)S(1)}, bf16[128,512]{1,0:T(8,128)(2,1)}, u32[]{:S(2)}) copy-start(bf16[128,512]{1,0:T(8,128)(2,1)} %left_ref.3) | copy-start | bytes 393220
  1.5 0.9 %copy-start.3 = (bf16[128,512]{1,0:T(8,128)(2,1)S(1)}, bf16[128,512]{1,0:T(8,128)(2,1)}, u32[]{:S(2)}) copy-start(bf16[128,512]{1,0:T(8,128)(2,1)} %right_ref.3) | copy-start | bytes 393220
  2.5 12.4 %collective-permute-start.3 = (bf16[128,256]{1,0:T(8,128)(2,1)S(1)}, bf16[128,256]{1,0:T(8,128)(2,1)S(1)}, u32[]{:S(2)}, u32[]{:S(2)}) collective-permute-start(bf16[128,256]{1,0:T(8,128)(2,1)S(1)} %get-tuple-element.39), channel_id=1, source_target_pairs={{0,8},{1,9},{2,10},{3,11},{4,12},{5,13},{6,14},{7,15},{8,0},{9,1},... | collective-permute-start | bytes 196616 | tf_op jit(solution)/shard_map/ppermute | solution.py:302
  5.5 10.9 %collective-permute-start.4 = (bf16[128,256]{1,0:T(8,128)(2,1)S(1)}, bf16[128,256]{1,0:T(8,128)(2,1)S(1)}, u32[]{:S(2)}, u32[]{:S(2)}) collective-permute-start(bf16[128,256]{1,0:T(8,128)(2,1)S(1)} %get-tuple-element.40), channel_id=1, source_target_pairs={{0,16},{1,17},{2,18},{3,19},{4,20},{5,21},{6,22},{7,23},{8,24},{9,... | collective-permute-start | bytes 196616 | tf_op jit(solution)/shard_map/ppermute | solution.py:302
  7.0 9.4 %collective-permute-start.5 = (bf16[128,256]{1,0:T(8,128)(2,1)S(1)}, bf16[128,256]{1,0:T(8,128)(2,1)S(1)}, u32[]{:S(2)}, u32[]{:S(2)}) collective-permute-start(bf16[128,256]{1,0:T(8,128)(2,1)S(1)} %get-tuple-element.41), channel_id=1, source_target_pairs={{0,24},{1,25},{2,26},{3,27},{4,28},{5,29},{6,30},{7,31},{8,16},{9,... | collective-permute-start | bytes 196616 | tf_op jit(solution)/shard_map/ppermute | solution.py:302
  7.0 3.0 %copy-start.4 = (s32[32]{0:T(128)S(1)}, s32[32]{0:T(128)}, u32[]{:S(2)}) copy-start(s32[32]{0:T(128)} %refs_0_.1) | copy-start | bytes 388
  7.0 11.8 %collective-permute-start.9 = (bf16[1,128,256]{2,1,0:T(8,128)(2,1)S(1)}, bf16[1,128,256]{2,1,0:T(8,128)(2,1)S(1)}, u32[]{:S(2)}, u32[]{:S(2)}) collective-permute-start(bf16[1,128,256]{2,1,0:T(8,128)(2,1)S(1)} %bitcast.48), channel_id=1, source_target_pairs={{0,2},{1,3},{2,0},{3,1},{4,6},{5,7},{6,4},{7,5},{8,10},{9,11},{10,... | collective-permute-start | bytes 196616 | tf_op jit(solution)/shard_map/ppermute | solution.py:302
  10.1 1.0 %copy-start = (bf16[128,2048]{1,0:T(8,128)(2,1)S(1)}, bf16[128,2048]{1,0:T(8,128)(2,1)}, u32[]{:S(2)}) copy-start(bf16[128,2048]{1,0:T(8,128)(2,1)} %left_ref.2) | copy-start | bytes 1572868
  11.1 1.0 %copy-start.1 = (bf16[128,2048]{1,0:T(8,128)(2,1)S(1)}, bf16[128,2048]{1,0:T(8,128)(2,1)}, u32[]{:S(2)}) copy-start(bf16[128,2048]{1,0:T(8,128)(2,1)} %right_ref.2) | copy-start | bytes 1572868
  13.3 14.1 %collective-permute-start = (bf16[128,1024]{1,0:T(8,128)(2,1)S(1)}, bf16[128,1024]{1,0:T(8,128)(2,1)S(1)}, u32[]{:S(2)}, u32[]{:S(2)}) collective-permute-start(bf16[128,1024]{1,0:T(8,128)(2,1)S(1)} %get-tuple-element.35), channel_id=1, source_target_pairs={{0,8},{1,9},{2,10},{3,11},{4,12},{5,13},{6,14},{7,15},{8,0},{9,1},... | collective-permute-start | bytes 786440 | tf_op jit(solution)/shard_map/ppermute | solution.py:302
  14.9 12.6 %collective-permute-start.1 = (bf16[128,1024]{1,0:T(8,128)(2,1)S(1)}, bf16[128,1024]{1,0:T(8,128)(2,1)S(1)}, u32[]{:S(2)}, u32[]{:S(2)}) collective-permute-start(bf16[128,1024]{1,0:T(8,128)(2,1)S(1)} %get-tuple-element.36), channel_id=1, source_target_pairs={{0,16},{1,17},{2,18},{3,19},{4,20},{5,21},{6,22},{7,23},{8,24},{9,... | collective-permute-start | bytes 786440 | tf_op jit(solution)/shard_map/ppermute | solution.py:302
  16.4 10.2 %collective-permute-start.10 = (bf16[3,128,256]{2,1,0:T(8,128)(2,1)S(1)}, bf16[3,128,256]{2,1,0:T(8,128)(2,1)S(1)}, u32[]{:S(2)}, u32[]{:S(2)}) collective-permute-start(bf16[3,128,256]{2,1,0:T(8,128)(2,1)S(1)} %pad_maximum_fusion.1), channel_id=1, source_target_pairs={{0,2},{1,3},{2,0},{3,1},{4,6},{5,7},{6,4},{7,5},{8,10},{9,11},{10,... | collective-permute-start | bytes 589832 | tf_op jit(solution)/shard_map/ppermute | solution.py:302
  17.2 10.9 %collective-permute-start.7 = (bf16[4,128,256]{2,1,0:T(8,128)(2,1)S(1)}, bf16[4,128,256]{2,1,0:T(8,128)(2,1)S(1)}, u32[]{:S(2)}, u32[]{:S(2)}) collective-permute-start(bf16[4,128,256]{2,1,0:T(8,128)(2,1)S(1)} %pad_maximum_fusion.refs_6_), channel_id=1, source_target_pairs={{0,1},{1,0},{2,3},{3,2},{4,5},{5,4},{6,7},{7,6},{8,9},{9,8},{10,11... | collective-permute-start | bytes 786440 | tf_op jit(solution)/shard_map/ppermute | solution.py:302
  26.7 6.8 %collective-permute-start.12 = (bf16[4,128,256]{2,1,0:T(8,128)(2,1)S(1)}, bf16[4,128,256]{2,1,0:T(8,128)(2,1)S(1)}, u32[]{:S(2)}, u32[]{:S(2)}) collective-permute-start(bf16[4,128,256]{2,1,0:T(8,128)(2,1)S(1)} %constant_dynamic-update-slice_fusion.refs_10_), channel_id=1, source_target_pairs={{0,1},{1,0},{2,3},{3,2},{4,5},{5,4},{6,7},{7,6},{8,9},{9,8},{10,11... | collective-permute-start | bytes 786440 | tf_op jit(solution)/shard_map/ppermute | solution.py:302
  27.0 7.3 %collective-permute-start.2 = (bf16[128,1024]{1,0:T(8,128)(2,1)S(1)}, bf16[128,1024]{1,0:T(8,128)(2,1)S(1)}, u32[]{:S(2)}, u32[]{:S(2)}) collective-permute-start(bf16[128,1024]{1,0:T(8,128)(2,1)S(1)} %get-tuple-element.37), channel_id=1, source_target_pairs={{0,24},{1,25},{2,26},{3,27},{4,28},{5,29},{6,30},{7,31},{8,16},{9,... | collective-permute-start | bytes 786440 | tf_op jit(solution)/shard_map/ppermute | solution.py:302
  27.4 6.8 %collective-permute-start.6 = (bf16[4,128,256]{2,1,0:T(8,128)(2,1)S(1)}, bf16[4,128,256]{2,1,0:T(8,128)(2,1)S(1)}, u32[]{:S(2)}, u32[]{:S(2)}) collective-permute-start(bf16[4,128,256]{2,1,0:T(8,128)(2,1)S(1)} %pad_maximum_fusion.refs_6_), channel_id=1, source_target_pairs={{0,4},{1,5},{2,6},{3,7},{4,0},{5,1},{6,2},{7,3},{8,12},{9,13},{10,... | collective-permute-start | bytes 786440 | tf_op jit(solution)/shard_map/ppermute | solution.py:302
  27.5 6.8 %collective-permute-start.11 = (bf16[4,128,256]{2,1,0:T(8,128)(2,1)S(1)}, bf16[4,128,256]{2,1,0:T(8,128)(2,1)S(1)}, u32[]{:S(2)}, u32[]{:S(2)}) collective-permute-start(bf16[4,128,256]{2,1,0:T(8,128)(2,1)S(1)} %constant_dynamic-update-slice_fusion.refs_10_), channel_id=1, source_target_pairs={{0,4},{1,5},{2,6},{3,7},{4,0},{5,1},{6,2},{7,3},{8,12},{9,13},{10,... | collective-permute-start | bytes 786440 | tf_op jit(solution)/shard_map/ppermute | solution.py:302
  28.1 6.2 %collective-permute-start.8 = (bf16[4,128,256]{2,1,0:T(8,128)(2,1)S(1)}, bf16[4,128,256]{2,1,0:T(8,128)(2,1)S(1)}, u32[]{:S(2)}, u32[]{:S(2)}) collective-permute-start(bf16[4,128,256]{2,1,0:T(8,128)(2,1)S(1)} %collective-permute-done.7.refs_8_), channel_id=1, source_target_pairs={{0,4},{1,5},{2,6},{3,7},{4,0},{5,1},{6,2},{7,3},{8,12},{9,13},{10,... | collective-permute-start | bytes 786440 | tf_op jit(solution)/shard_map/ppermute | solution.py:302
  33.4 1.5 %collective-permute-start.13 = (bf16[4,128,256]{2,1,0:T(8,128)(2,1)S(1)}, bf16[4,128,256]{2,1,0:T(8,128)(2,1)S(1)}, u32[]{:S(2)}, u32[]{:S(2)}) collective-permute-start(bf16[4,128,256]{2,1,0:T(8,128)(2,1)S(1)} %collective-permute-done.12.refs_12_), channel_id=1, source_target_pairs={{0,4},{1,5},{2,6},{3,7},{4,0},{5,1},{6,2},{7,3},{8,12},{9,13},{10,... | collective-permute-start | bytes 786440 | tf_op jit(solution)/shard_map/ppermute | solution.py:302
  44.8 3.8 %collective-permute-start.14 = (bf16[4,4,128,256]{3,2,1,0:T(8,128)(2,1)S(1)}, bf16[4,4,128,256]{3,2,1,0:T(8,128)(2,1)S(1)}, u32[]{:S(2)}, u32[]{:S(2)}) collective-permute-start(bf16[4,4,128,256]{3,2,1,0:T(8,128)(2,1)S(1)} %get-tuple-element.44), channel_id=1, source_target_pairs={{0,4},{1,5},{2,6},{3,7},{4,0},{5,1},{6,2},{7,3},{8,12},{9,13},{10,... | collective-permute-start | bytes 3145736 | tf_op jit(solution)/shard_map/ppermute | solution.py:302
  48.8 8.7 %collective-permute-start.15 = (bf16[4,128,256]{2,1,0:T(8,128)(2,1)S(1)}, bf16[4,128,256]{2,1,0:T(8,128)(2,1)S(1)}, u32[]{:S(2)}, u32[]{:S(2)}) collective-permute-start(bf16[4,128,256]{2,1,0:T(8,128)(2,1)S(1)} %get-tuple-element.66), channel_id=1, source_target_pairs={{0,1},{1,0},{2,3},{3,2},{4,5},{5,4},{6,7},{7,6},{8,9},{9,8},{10,11... | collective-permute-start | bytes 786440 | tf_op jit(solution)/shard_map/ppermute | solution.py:302
  49.1 12.0 %collective-permute-start.18 = (bf16[128,1024]{1,0:T(8,128)(2,1)S(1)}, bf16[128,1024]{1,0:T(8,128)(2,1)S(1)}, u32[]{:S(2)}, u32[]{:S(2)}) collective-permute-start(bf16[128,1024]{1,0:T(8,128)(2,1)S(1)} %get-tuple-element.46), channel_id=1, source_target_pairs={{0,8},{1,9},{2,10},{3,11},{4,12},{5,13},{6,14},{7,15},{8,0},{9,1},... | collective-permute-start | bytes 786440 | tf_op jit(solution)/shard_map/ppermute | solution.py:302
  49.6 13.8 %collective-permute-start.19 = (bf16[128,1024]{1,0:T(8,128)(2,1)S(1)}, bf16[128,1024]{1,0:T(8,128)(2,1)S(1)}, u32[]{:S(2)}, u32[]{:S(2)}) collective-permute-start(bf16[128,1024]{1,0:T(8,128)(2,1)S(1)} %get-tuple-element.47), channel_id=1, source_target_pairs={{0,16},{1,17},{2,18},{3,19},{4,20},{5,21},{6,22},{7,23},{8,24},{9,... | collective-permute-start | bytes 786440 | tf_op jit(solution)/shard_map/ppermute | solution.py:302
  50.1 13.3 %collective-permute-start.20 = (bf16[128,1024]{1,0:T(8,128)(2,1)S(1)}, bf16[128,1024]{1,0:T(8,128)(2,1)S(1)}, u32[]{:S(2)}, u32[]{:S(2)}) collective-permute-start(bf16[128,1024]{1,0:T(8,128)(2,1)S(1)} %get-tuple-element.48), channel_id=1, source_target_pairs={{0,24},{1,25},{2,26},{3,27},{4,28},{5,29},{6,30},{7,31},{8,16},{9,... | collective-permute-start | bytes 786440 | tf_op jit(solution)/shard_map/ppermute | solution.py:302
  57.5 12.0 %collective-permute-start.16 = (bf16[4,128,256]{2,1,0:T(8,128)(2,1)S(1)}, bf16[4,128,256]{2,1,0:T(8,128)(2,1)S(1)}, u32[]{:S(2)}, u32[]{:S(2)}) collective-permute-start(bf16[4,128,256]{2,1,0:T(8,128)(2,1)S(1)} %get-tuple-element.45), channel_id=1, source_target_pairs={{0,1},{1,0},{2,3},{3,2},{4,5},{5,4},{6,7},{7,6},{8,9},{9,8},{10,11... | collective-permute-start | bytes 786440 | tf_op jit(solution)/shard_map/ppermute | solution.py:302
  57.8 9.5 %collective-permute-start.17 = (bf16[3,128,256]{2,1,0:T(8,128)(2,1)S(1)}, bf16[3,128,256]{2,1,0:T(8,128)(2,1)S(1)}, u32[]{:S(2)}, u32[]{:S(2)}) collective-permute-start(bf16[3,128,256]{2,1,0:T(8,128)(2,1)S(1)} %fusion), channel_id=1, source_target_pairs={{0,2},{1,3},{2,0},{3,1},{4,6},{5,7},{6,4},{7,5},{8,10},{9,11},{10,... | collective-permute-start | bytes 589832 | tf_op jit(solution)/shard_map/ppermute | solution.py:302
  69.6 6.0 %collective-permute-start.21 = (bf16[128,256]{1,0:T(8,128)(2,1)S(1)}, bf16[128,256]{1,0:T(8,128)(2,1)S(1)}, u32[]{:S(2)}, u32[]{:S(2)}) collective-permute-start(bf16[128,256]{1,0:T(8,128)(2,1)S(1)} %get-tuple-element.56), channel_id=1, source_target_pairs={{0,2},{1,3},{2,0},{3,1},{4,6},{5,7},{6,4},{7,5},{8,10},{9,11},{10,... | collective-permute-start | bytes 196616 | tf_op jit(solution)/shard_map/ppermute | solution.py:302
  71.0 4.6 %collective-permute-start.22 = (bf16[128,256]{1,0:T(8,128)(2,1)S(1)}, bf16[128,256]{1,0:T(8,128)(2,1)S(1)}, u32[]{:S(2)}, u32[]{:S(2)}) collective-permute-start(bf16[128,256]{1,0:T(8,128)(2,1)S(1)} %get-tuple-element.57), channel_id=1, source_target_pairs={{0,8},{1,9},{2,10},{3,11},{4,12},{5,13},{6,14},{7,15},{8,0},{9,1},... | collective-permute-start | bytes 196616 | tf_op jit(solution)/shard_map/ppermute | solution.py:302
  71.5 4.3 %collective-permute-start.23 = (bf16[128,256]{1,0:T(8,128)(2,1)S(1)}, bf16[128,256]{1,0:T(8,128)(2,1)S(1)}, u32[]{:S(2)}, u32[]{:S(2)}) collective-permute-start(bf16[128,256]{1,0:T(8,128)(2,1)S(1)} %get-tuple-element.58), channel_id=1, source_target_pairs={{0,16},{1,17},{2,18},{3,19},{4,20},{5,21},{6,22},{7,23},{8,24},{9,... | collective-permute-start | bytes 196616 | tf_op jit(solution)/shard_map/ppermute | solution.py:302
  72.0 5.2 %collective-permute-start.24 = (bf16[128,256]{1,0:T(8,128)(2,1)S(1)}, bf16[128,256]{1,0:T(8,128)(2,1)S(1)}, u32[]{:S(2)}, u32[]{:S(2)}) collective-permute-start(bf16[128,256]{1,0:T(8,128)(2,1)S(1)} %get-tuple-element.59), channel_id=1, source_target_pairs={{0,24},{1,25},{2,26},{3,27},{4,28},{5,29},{6,30},{7,31},{8,16},{9,... | collective-permute-start | bytes 196616 | tf_op jit(solution)/shard_map/ppermute | solution.py:302

commit v5 on v4

--- a/solution.py
+++ b/solution.py
@@ -302,16 +302,16 @@
     return lax.ppermute(value, ("ctx", "head"), pairs)
 
 
-def piece_columns(pieces, flip, wide):
+def piece_columns(pieces, flip, wide, offset=0):
     index = lax.axis_index("ctx") // (lax.axis_size("ctx") // pieces)
-    return pl.ds(pl.multiple_of((index ^ flip) * wide, HD), wide)
-
-
-def split_heads_kernel(pieces, wide, left_ref, right_ref, *piece_refs):
+    return pl.ds(pl.multiple_of(((index ^ flip) + offset) * wide, HD), wide)
+
+
+def split_heads_kernel(pieces, wide, both_ref, *piece_refs):
     for flip, piece_ref in enumerate(piece_refs):
-        columns = piece_columns(pieces, flip, wide)
-        piece_ref[:, :wide] = left_ref[:, columns]
-        piece_ref[:, wide:] = right_ref[:, columns]
+        for side in range(2):
+            columns = piece_columns(pieces, flip, wide, side * pieces)
+            piece_ref[:, side * wide : (side + 1) * wide] = both_ref[:, columns]
 
 
 def join_heads_kernel(pieces, wide, *refs):
@@ -327,10 +327,10 @@
     return pl.pallas_call(
         functools.partial(split_heads_kernel, pieces, wide),
         out_shape=[jax.ShapeDtypeStruct((rows, 2 * wide), left.dtype)] * pieces,
-        in_specs=[VMEM] * 2,
+        in_specs=[VMEM],
         out_specs=[VMEM] * pieces,
         compiler_params=SMALL,
-    )(left, right)
+    )(jnp.concatenate([left, right], axis=1))
 
 
 def join_heads(parts):
@@ -345,9 +345,9 @@
     )(*parts)
 
 
-def prepare_kernel(pieces, wide, lengths_ref, left_ref, right_ref, *out_refs):
+def prepare_kernel(pieces, wide, lengths_ref, both_ref, *out_refs):
     piece_refs, marks_ref = out_refs[:pieces], out_refs[pieces]
-    split_heads_kernel(pieces, wide, left_ref, right_ref, *piece_refs)
+    split_heads_kernel(pieces, wide, both_ref, *piece_refs)
     total, docs = marks_ref.shape[0], lengths_ref.shape[0]
     lane = lax.broadcasted_iota(jnp.int32, (1, MARKS), 1)
     begins = jnp.zeros((1, MARKS), jnp.int32)
@@ -374,10 +374,10 @@
         functools.partial(prepare_kernel, pieces, wide),
         out_shape=[jax.ShapeDtypeStruct((rows, 2 * wide), left.dtype)] * pieces
         + [jax.ShapeDtypeStruct((total, MARKS), jnp.bfloat16)],
-        in_specs=[SMEM] + [VMEM] * 2,
+        in_specs=[SMEM, VMEM],
         out_specs=[VMEM] * (pieces + 1),
         compiler_params=SMALL,
-    )(lengths, left, right)
+    )(lengths, jnp.concatenate([left, right], axis=1))
     return results[:pieces], results[pieces]
 
 

time: 79.3 us -> 77.4 us (0.976); the launches traced: 78 us -> 77.7 us
  local copies, waits for them, and re-layouts: 3.91 us -> 0.03 us
  other arithmetic: 0.44 us -> 2.61 us
  Pallas kernels: 12.8 us -> 14.2 us
  starting transfers between devices: 28.1 us -> 29.2 us
  waiting for transfers between devices: 31.9 us -> 30.9 us
    unnamed x11 -> x5, local copies, waits for them, and re-layouts: 3.89 us -> 0.01 us
    concatenate x0 -> x2, other arithmetic: none -> 2.16 us  [the longest x1 1.12 us: prepare(): jnp.concatenate([left, right], axis=1)]
    pallas_call x1, Pallas kernels: 9.84 us -> 11.2 us  [attention(): pl.pallas_call(functools.partial(attention_kernel, cores, heads, tok), ou...]
    ppermute x25, starting transfers between devices: 28.1 us -> 29.2 us  [flipped(): return lax.ppermute(value, ('ctx', 'head'), pairs)]
    ppermute x25, waiting for transfers between devices: 31.9 us -> 30.9 us  [flipped(): return lax.ppermute(value, ('ctx', 'head'), pairs)]
  transfers between devices with their start and end apart: 25 -> 25, of which waited for: 12 -> 11; matrix products, arithmetic and copies ran while one was open for 0% -> 2% of each run, Pallas kernels for 3% -> 3%
where the time goes in v5:
time: 77.4 us; the launch traced here: 77.7 us
  waiting for transfers between devices  30.9 us (40%)
  starting transfers between devices  29.2 us (38%)
  Pallas kernels  14.2 us (18%)
  other arithmetic  2.61 us (3%)
    ppermute x25, waiting for transfers between devices, flipped(): return lax.ppermute(value, ('ctx', 'head'), pairs)  30.9 us
    ppermute x25, starting transfers between devices, flipped(): return lax.ppermute(value, ('ctx', 'head'), pairs)  29.2 us
    pallas_call x1, Pallas kernels, attention(): pl.pallas_call(functools.partial(attention_kernel, cores, heads, tok), ou...  11.2 us
    pallas_call x2, Pallas kernels, join_heads(): pl.pallas_call(functools.partial(join_heads_kernel, pieces, wide), out_sh...  1.81 us
  transfers between devices with their start and end apart: 25, of which 11 were waited for; matrix products, arithmetic and copies ran while one was open for 2% of the time, Pallas kernels for 3%

profile of v5, /device:TPU:0, one launch (start us, length us, event | category | flops | bytes accessed | tf_op | source)
XLA Modules:
  0.0 77.7 jit_solution(6591442074051210205)
XLA Ops:
  0.6 1.0 %pad_maximum_fusion.1.both_ref = bf16[128,1024]{1,0:T(8,128)(2,1)S(1)} fusion(bf16[128,512]{1,0:T(8,128)(2,1)} %param.7, bf16[128,512]{1,0:T(8,128)(2,1)} %param.6), kind=kLoop, calls=%fused_computation.7 | loop fusion | flops 524288 | bytes 524288 | tf_op jit(solution)/shard_map/concatenate | solution.py:333
  1.7 0.1 shard_map.85
  1.8 4.1 %collective-permute-start.9 = (bf16[1,128,256]{2,1,0:T(8,128)(2,1)S(1)}, bf16[1,128,256]{2,1,0:T(8,128)(2,1)S(1)}, u32[]{:S(2)}, u32[]{:S(2)}) collective-permute-start(bf16[1,128,256]{2,1,0:T(8,128)(2,1)S(1)} %bitcast.48), channel_id=1, source_target_pairs={{0,2},{1,3},{2,0},{3,1},{4,6},{5,7},{6,4},{7,5},{8,10},{9,11},{10,... | collective-permute-start | bytes 196616 | tf_op jit(solution)/shard_map/ppermute | solution.py:302
  5.9 1.5 %collective-permute-start.3 = (bf16[128,256]{1,0:T(8,128)(2,1)S(1)}, bf16[128,256]{1,0:T(8,128)(2,1)S(1)}, u32[]{:S(2)}, u32[]{:S(2)}) collective-permute-start(bf16[128,256]{1,0:T(8,128)(2,1)S(1)} %get-tuple-element.39), channel_id=1, source_target_pairs={{0,8},{1,9},{2,10},{3,11},{4,12},{5,13},{6,14},{7,15},{8,0},{9,1},... | collective-permute-start | bytes 196616 | tf_op jit(solution)/shard_map/ppermute | solution.py:302
  7.4 1.5 %collective-permute-start.4 = (bf16[128,256]{1,0:T(8,128)(2,1)S(1)}, bf16[128,256]{1,0:T(8,128)(2,1)S(1)}, u32[]{:S(2)}, u32[]{:S(2)}) collective-permute-start(bf16[128,256]{1,0:T(8,128)(2,1)S(1)} %get-tuple-element.40), channel_id=1, source_target_pairs={{0,16},{1,17},{2,18},{3,19},{4,20},{5,21},{6,22},{7,23},{8,24},{9,... | collective-permute-start | bytes 196616 | tf_op jit(solution)/shard_map/ppermute | solution.py:302
  8.9 0.5 collective-permute-start.5
  9.4 1.1 %pad_maximum_fusion.both_ref = bf16[128,4096]{1,0:T(8,128)(2,1)S(1)} fusion(bf16[128,2048]{1,0:T(8,128)(2,1)S(1)} %copy-done.1, bf16[128,2048]{1,0:T(8,128)(2,1)} %param.5), kind=kLoop, calls=%fused_computation | loop fusion | flops 2097152 | bytes 2097152 | tf_op jit(solution)/shard_map/concatenate | solution.py:380
  10.5 1.1 %shard_map.84 = (bf16[128,1024]{1,0:T(8,128)(2,1)S(1)}, bf16[128,1024]{1,0:T(8,128)(2,1)S(1)}, bf16[128,1024]{1,0:T(8,128)(2,1)S(1)}, bf16[128,1024]{1,0:T(8,128)(2,1)S(1)}, bf16[4096,128]{1,0:T(8,128)(2,1)S(1)}) custom-call(s32[32]{0:T(128)S(1)} %copy-done, bf16[128,4096]{1,0:T(8,128)(2,1)S(1)} %pad_maximum_fusion.both_ref), custom_call_target="tpu_custom_call" | custom-call | tf_op jit(solution)/shard_map/pallas_call | solution.py:373
  11.7 1.6 %collective-permute-start = (bf16[128,1024]{1,0:T(8,128)(2,1)S(1)}, bf16[128,1024]{1,0:T(8,128)(2,1)S(1)}, u32[]{:S(2)}, u32[]{:S(2)}) collective-permute-start(bf16[128,1024]{1,0:T(8,128)(2,1)S(1)} %get-tuple-element.35), channel_id=1, source_target_pairs={{0,8},{1,9},{2,10},{3,11},{4,12},{5,13},{6,14},{7,15},{8,0},{9,1},... | collective-permute-start | bytes 786440 | tf_op jit(solution)/shard_map/ppermute | solution.py:302
  13.2 0.0 collective-permute-done.3
  13.2 1.5 %collective-permute-start.1 = (bf16[128,1024]{1,0:T(8,128)(2,1)S(1)}, bf16[128,1024]{1,0:T(8,128)(2,1)S(1)}, u32[]{:S(2)}, u32[]{:S(2)}) collective-permute-start(bf16[128,1024]{1,0:T(8,128)(2,1)S(1)} %get-tuple-element.36), channel_id=1, source_target_pairs={{0,16},{1,17},{2,18},{3,19},{4,20},{5,21},{6,22},{7,23},{8,24},{9,... | collective-permute-start | bytes 786440 | tf_op jit(solution)/shard_map/ppermute | solution.py:302
  14.7 0.0 collective-permute-done.4
  14.7 0.0 collective-permute-done.5
  14.8 0.4 collective-permute-start.10
  15.2 1.6 %collective-permute-start.7 = (bf16[4,128,256]{2,1,0:T(8,128)(2,1)S(1)}, bf16[4,128,256]{2,1,0:T(8,128)(2,1)S(1)}, u32[]{:S(2)}, u32[]{:S(2)}) collective-permute-start(bf16[4,128,256]{2,1,0:T(8,128)(2,1)S(1)} %pad_maximum_fusion.2.refs_6_), channel_id=1, source_target_pairs={{0,1},{1,0},{2,3},{3,2},{4,5},{5,4},{6,7},{7,6},{8,9},{9,8},{10,11... | collective-permute-start | bytes 786440 | tf_op jit(solution)/shard_map/ppermute | solution.py:302
  16.9 8.1 %collective-permute-done.10 = bf16[3,128,256]{2,1,0:T(8,128)(2,1)S(1)} collective-permute-done((bf16[3,128,256]{2,1,0:T(8,128)(2,1)S(1)}, bf16[3,128,256]{2,1,0:T(8,128)(2,1)S(1)}, u32[]{:S(2)}, u32[]{:S(2)}) %collective-permute-start.10) | collective-permute-done | bytes 196640 | tf_op jit(solution)/shard_map/ppermute | solution.py:302
  25.0 0.3 collective-permute-start.12
  25.3 0.5 collective-permute-start.2
  25.8 0.0 collective-permute-done.refs_3_
  25.8 0.5 collective-permute-start.11
  26.3 0.1 collective-permute-start.8
  26.4 5.1 %collective-permute-done.12.refs_12_ = bf16[4,128,256]{2,1,0:T(8,128)(2,1)S(1)} collective-permute-done((bf16[4,128,256]{2,1,0:T(8,128)(2,1)S(1)}, bf16[4,128,256]{2,1,0:T(8,128)(2,1)S(1)}, u32[]{:S(2)}, u32[]{:S(2)}) %collective-permute-start.12) | collective-permute-done | bytes 262176 | tf_op jit(solution)/shard_map/ppermute | solution.py:302
  31.5 1.1 %collective-permute-done.2.refs_5_ = bf16[128,1024]{1,0:T(8,128)(2,1)S(1)} collective-permute-done((bf16[128,1024]{1,0:T(8,128)(2,1)S(1)}, bf16[128,1024]{1,0:T(8,128)(2,1)S(1)}, u32[]{:S(2)}, u32[]{:S(2)}) %collective-permute-start.2) | collective-permute-done | bytes 262176 | tf_op jit(solution)/shard_map/ppermute | solution.py:302
  32.6 0.4 collective-permute-done.13.refs_13_
  33.0 11.2 %shard_map.86 = (bf16[128,1024]{1,0:T(8,128)(2,1)S(1)}, bf16[128,1024]{1,0:T(8,128)(2,1)S(1)}, bf16[128,1024]{1,0:T(8,128)(2,1)S(1)}, bf16[128,1024]{1,0:T(8,128...) custom-call(s32[32]{0:T(128)S(1)} %copy-done, ...), custom_call_target="tpu_custom_call" | custom-call | tf_op jit(solution)/shard_map/pallas_call | solution.py:594
  44.2 0.1 collective-permute-start.14
  44.3 2.6 %collective-permute-done.14 = bf16[4,4,128,256]{3,2,1,0:T(8,128)(2,1)S(1)} collective-permute-done((bf16[4,4,128,256]{3,2,1,0:T(8,128)(2,1)S(1)}, bf16[4,4,128,256]{3,2,1,0:T(8,128)(2,1)S(1)}, u32[]{:S(2)}, u32[]{:S(2)}) %collective-permute-start.14) | collective-permute-done | bytes 1048608 | tf_op jit(solution)/shard_map/ppermute | solution.py:302
  46.9 0.1 fusion.2
  47.1 2.5 %collective-permute-start.15 = (bf16[4,128,256]{2,1,0:T(8,128)(2,1)S(1)}, bf16[4,128,256]{2,1,0:T(8,128)(2,1)S(1)}, u32[]{:S(2)}, u32[]{:S(2)}) collective-permute-start(bf16[4,128,256]{2,1,0:T(8,128)(2,1)S(1)} %get-tuple-element.66), channel_id=1, source_target_pairs={{0,1},{1,0},{2,3},{3,2},{4,5},{5,4},{6,7},{7,6},{8,9},{9,8},{10,11... | collective-permute-start | bytes 786440 | tf_op jit(solution)/shard_map/ppermute | solution.py:302
  49.6 0.5 collective-permute-start.18
  50.1 0.5 collective-permute-start.19
  50.6 2.5 %collective-permute-start.20 = (bf16[128,1024]{1,0:T(8,128)(2,1)S(1)}, bf16[128,1024]{1,0:T(8,128)(2,1)S(1)}, u32[]{:S(2)}, u32[]{:S(2)}) collective-permute-start(bf16[128,1024]{1,0:T(8,128)(2,1)S(1)} %get-tuple-element.48), channel_id=1, source_target_pairs={{0,24},{1,25},{2,26},{3,27},{4,28},{5,29},{6,30},{7,31},{8,16},{9,... | collective-permute-start | bytes 786440 | tf_op jit(solution)/shard_map/ppermute | solution.py:302
  53.1 3.1 %collective-permute-done.15 = bf16[4,128,256]{2,1,0:T(8,128)(2,1)S(1)} collective-permute-done((bf16[4,128,256]{2,1,0:T(8,128)(2,1)S(1)}, bf16[4,128,256]{2,1,0:T(8,128)(2,1)S(1)}, u32[]{:S(2)}, u32[]{:S(2)}) %collective-permute-start.15) | collective-permute-done | bytes 262176 | tf_op jit(solution)/shard_map/ppermute | solution.py:302
  56.2 1.7 %collective-permute-start.16 = (bf16[4,128,256]{2,1,0:T(8,128)(2,1)S(1)}, bf16[4,128,256]{2,1,0:T(8,128)(2,1)S(1)}, u32[]{:S(2)}, u32[]{:S(2)}) collective-permute-start(bf16[4,128,256]{2,1,0:T(8,128)(2,1)S(1)} %get-tuple-element.45), channel_id=1, source_target_pairs={{0,1},{1,0},{2,3},{3,2},{4,5},{5,4},{6,7},{7,6},{8,9},{9,8},{10,11... | collective-permute-start | bytes 786440 | tf_op jit(solution)/shard_map/ppermute | solution.py:302
  57.9 0.1 fusion
  58.0 1.4 %collective-permute-start.17 = (bf16[3,128,256]{2,1,0:T(8,128)(2,1)S(1)}, bf16[3,128,256]{2,1,0:T(8,128)(2,1)S(1)}, u32[]{:S(2)}, u32[]{:S(2)}) collective-permute-start(bf16[3,128,256]{2,1,0:T(8,128)(2,1)S(1)} %fusion), channel_id=1, source_target_pairs={{0,2},{1,3},{2,0},{3,1},{4,6},{5,7},{6,4},{7,5},{8,10},{9,11},{10,... | collective-permute-start | bytes 589832 | tf_op jit(solution)/shard_map/ppermute | solution.py:302
  59.4 4.1 %collective-permute-done.19.refs_2_ = bf16[128,1024]{1,0:T(8,128)(2,1)S(1)} collective-permute-done((bf16[128,1024]{1,0:T(8,128)(2,1)S(1)}, bf16[128,1024]{1,0:T(8,128)(2,1)S(1)}, u32[]{:S(2)}, u32[]{:S(2)}) %collective-permute-start.19) | collective-permute-done | bytes 262176 | tf_op jit(solution)/shard_map/ppermute | solution.py:302
  63.5 3.7 %collective-permute-done.17 = bf16[3,128,256]{2,1,0:T(8,128)(2,1)S(1)} collective-permute-done((bf16[3,128,256]{2,1,0:T(8,128)(2,1)S(1)}, bf16[3,128,256]{2,1,0:T(8,128)(2,1)S(1)}, u32[]{:S(2)}, u32[]{:S(2)}) %collective-permute-start.17) | collective-permute-done | bytes 196640 | tf_op jit(solution)/shard_map/ppermute | solution.py:302
  67.2 1.1 %collective-permute-done.16 = bf16[4,128,256]{2,1,0:T(8,128)(2,1)S(1)} collective-permute-done((bf16[4,128,256]{2,1,0:T(8,128)(2,1)S(1)}, bf16[4,128,256]{2,1,0:T(8,128)(2,1)S(1)}, u32[]{:S(2)}, u32[]{:S(2)}) %collective-permute-start.16) | collective-permute-done | bytes 262176 | tf_op jit(solution)/shard_map/ppermute | solution.py:302
  68.2 0.1 fusion.3
  68.4 2.4 %collective-permute-start.21 = (bf16[128,256]{1,0:T(8,128)(2,1)S(1)}, bf16[128,256]{1,0:T(8,128)(2,1)S(1)}, u32[]{:S(2)}, u32[]{:S(2)}) collective-permute-start(bf16[128,256]{1,0:T(8,128)(2,1)S(1)} %get-tuple-element.56), channel_id=1, source_target_pairs={{0,2},{1,3},{2,0},{3,1},{4,6},{5,7},{6,4},{7,5},{8,10},{9,11},{10,... | collective-permute-start | bytes 196616 | tf_op jit(solution)/shard_map/ppermute | solution.py:302
  70.7 0.5 collective-permute-start.22
  71.3 0.5 collective-permute-start.23
  71.8 2.5 %collective-permute-start.24 = (bf16[128,256]{1,0:T(8,128)(2,1)S(1)}, bf16[128,256]{1,0:T(8,128)(2,1)S(1)}, u32[]{:S(2)}, u32[]{:S(2)}) collective-permute-start(bf16[128,256]{1,0:T(8,128)(2,1)S(1)} %get-tuple-element.59), channel_id=1, source_target_pairs={{0,24},{1,25},{2,26},{3,27},{4,28},{5,29},{6,30},{7,31},{8,16},{9,... | collective-permute-start | bytes 196616 | tf_op jit(solution)/shard_map/ppermute | solution.py:302
  74.2 1.1 %shard_map.87 = (bf16[128,2048]{1,0:T(8,128)(2,1)}, bf16[128,2048]{1,0:T(8,128)(2,1)}) custom-call(bf16[128,1024]{1,0:T(8,128)(2,1)S(1)} %get-tuple-element.42.refs_0_, bf16[128,1024]{1,0:T(8,128)(2,1)S(1)} %collective-permute-done.18.refs_1_, bf16[128,1024]{1,0:T(8,128)(2,1)S(1)} %collective-permute-done.19.refs_2_, ...), custom_call_target="tpu_custom_call" | custom-call | tf_op jit(solution)/shard_map/pallas_call | solution.py:339
  75.3 0.2 collective-permute-done.23.refs_2_
  75.5 1.4 %collective-permute-done.24.refs_3_ = bf16[128,256]{1,0:T(8,128)(2,1)S(1)} collective-permute-done((bf16[128,256]{1,0:T(8,128)(2,1)S(1)}, bf16[128,256]{1,0:T(8,128)(2,1)S(1)}, u32[]{:S(2)}, u32[]{:S(2)}) %collective-permute-start.24) | collective-permute-done | bytes 65568 | tf_op jit(solution)/shard_map/ppermute | solution.py:302
  76.9 0.8 shard_map.88
  (21 shorter events, 0.2 us)
Async XLA Ops:
  0.6 8.8 %copy-start.1 = (bf16[128,2048]{1,0:T(8,128)(2,1)S(1)}, bf16[128,2048]{1,0:T(8,128)(2,1)}, u32[]{:S(2)}) copy-start(bf16[128,2048]{1,0:T(8,128)(2,1)} %param.8) | copy-start | bytes 1572868
  1.8 15.1 %collective-permute-start.9 = (bf16[1,128,256]{2,1,0:T(8,128)(2,1)S(1)}, bf16[1,128,256]{2,1,0:T(8,128)(2,1)S(1)}, u32[]{:S(2)}, u32[]{:S(2)}) collective-permute-start(bf16[1,128,256]{2,1,0:T(8,128)(2,1)S(1)} %bitcast.48), channel_id=1, source_target_pairs={{0,2},{1,3},{2,0},{3,1},{4,6},{5,7},{6,4},{7,5},{8,10},{9,11},{10,... | collective-permute-start | bytes 196616 | tf_op jit(solution)/shard_map/ppermute | solution.py:302
  5.9 7.3 %collective-permute-start.3 = (bf16[128,256]{1,0:T(8,128)(2,1)S(1)}, bf16[128,256]{1,0:T(8,128)(2,1)S(1)}, u32[]{:S(2)}, u32[]{:S(2)}) collective-permute-start(bf16[128,256]{1,0:T(8,128)(2,1)S(1)} %get-tuple-element.39), channel_id=1, source_target_pairs={{0,8},{1,9},{2,10},{3,11},{4,12},{5,13},{6,14},{7,15},{8,0},{9,1},... | collective-permute-start | bytes 196616 | tf_op jit(solution)/shard_map/ppermute | solution.py:302
  7.4 7.4 %collective-permute-start.4 = (bf16[128,256]{1,0:T(8,128)(2,1)S(1)}, bf16[128,256]{1,0:T(8,128)(2,1)S(1)}, u32[]{:S(2)}, u32[]{:S(2)}) collective-permute-start(bf16[128,256]{1,0:T(8,128)(2,1)S(1)} %get-tuple-element.40), channel_id=1, source_target_pairs={{0,16},{1,17},{2,18},{3,19},{4,20},{5,21},{6,22},{7,23},{8,24},{9,... | collective-permute-start | bytes 196616 | tf_op jit(solution)/shard_map/ppermute | solution.py:302
  8.9 1.6 %copy-start = (s32[32]{0:T(128)S(1)}, s32[32]{0:T(128)}, u32[]{:S(2)}) copy-start(s32[32]{0:T(128)} %refs_0_.1) | copy-start | bytes 388
  8.9 5.8 %collective-permute-start.5 = (bf16[128,256]{1,0:T(8,128)(2,1)S(1)}, bf16[128,256]{1,0:T(8,128)(2,1)S(1)}, u32[]{:S(2)}, u32[]{:S(2)}) collective-permute-start(bf16[128,256]{1,0:T(8,128)(2,1)S(1)} %get-tuple-element.41), channel_id=1, source_target_pairs={{0,24},{1,25},{2,26},{3,27},{4,28},{5,29},{6,30},{7,31},{8,16},{9,... | collective-permute-start | bytes 196616 | tf_op jit(solution)/shard_map/ppermute | solution.py:302
  11.7 14.1 %collective-permute-start = (bf16[128,1024]{1,0:T(8,128)(2,1)S(1)}, bf16[128,1024]{1,0:T(8,128)(2,1)S(1)}, u32[]{:S(2)}, u32[]{:S(2)}) collective-permute-start(bf16[128,1024]{1,0:T(8,128)(2,1)S(1)} %get-tuple-element.35), channel_id=1, source_target_pairs={{0,8},{1,9},{2,10},{3,11},{4,12},{5,13},{6,14},{7,15},{8,0},{9,1},... | collective-permute-start | bytes 786440 | tf_op jit(solution)/shard_map/ppermute | solution.py:302
  13.2 12.6 %collective-permute-start.1 = (bf16[128,1024]{1,0:T(8,128)(2,1)S(1)}, bf16[128,1024]{1,0:T(8,128)(2,1)S(1)}, u32[]{:S(2)}, u32[]{:S(2)}) collective-permute-start(bf16[128,1024]{1,0:T(8,128)(2,1)S(1)} %get-tuple-element.36), channel_id=1, source_target_pairs={{0,16},{1,17},{2,18},{3,19},{4,20},{5,21},{6,22},{7,23},{8,24},{9,... | collective-permute-start | bytes 786440 | tf_op jit(solution)/shard_map/ppermute | solution.py:302
  14.8 10.2 %collective-permute-start.10 = (bf16[3,128,256]{2,1,0:T(8,128)(2,1)S(1)}, bf16[3,128,256]{2,1,0:T(8,128)(2,1)S(1)}, u32[]{:S(2)}, u32[]{:S(2)}) collective-permute-start(bf16[3,128,256]{2,1,0:T(8,128)(2,1)S(1)} %pad_maximum_fusion.3), channel_id=1, source_target_pairs={{0,2},{1,3},{2,0},{3,1},{4,6},{5,7},{6,4},{7,5},{8,10},{9,11},{10,... | collective-permute-start | bytes 589832 | tf_op jit(solution)/shard_map/ppermute | solution.py:302
  15.2 11.1 %collective-permute-start.7 = (bf16[4,128,256]{2,1,0:T(8,128)(2,1)S(1)}, bf16[4,128,256]{2,1,0:T(8,128)(2,1)S(1)}, u32[]{:S(2)}, u32[]{:S(2)}) collective-permute-start(bf16[4,128,256]{2,1,0:T(8,128)(2,1)S(1)} %pad_maximum_fusion.2.refs_6_), channel_id=1, source_target_pairs={{0,1},{1,0},{2,3},{3,2},{4,5},{5,4},{6,7},{7,6},{8,9},{9,8},{10,11... | collective-permute-start | bytes 786440 | tf_op jit(solution)/shard_map/ppermute | solution.py:302
  25.0 6.5 %collective-permute-start.12 = (bf16[4,128,256]{2,1,0:T(8,128)(2,1)S(1)}, bf16[4,128,256]{2,1,0:T(8,128)(2,1)S(1)}, u32[]{:S(2)}, u32[]{:S(2)}) collective-permute-start(bf16[4,128,256]{2,1,0:T(8,128)(2,1)S(1)} %constant_dynamic-update-slice_fusion.refs_10_), channel_id=1, source_target_pairs={{0,1},{1,0},{2,3},{3,2},{4,5},{5,4},{6,7},{7,6},{8,9},{9,8},{10,11... | collective-permute-start | bytes 786440 | tf_op jit(solution)/shard_map/ppermute | solution.py:302
  25.3 7.3 %collective-permute-start.2 = (bf16[128,1024]{1,0:T(8,128)(2,1)S(1)}, bf16[128,1024]{1,0:T(8,128)(2,1)S(1)}, u32[]{:S(2)}, u32[]{:S(2)}) collective-permute-start(bf16[128,1024]{1,0:T(8,128)(2,1)S(1)} %get-tuple-element.37), channel_id=1, source_target_pairs={{0,24},{1,25},{2,26},{3,27},{4,28},{5,29},{6,30},{7,31},{8,16},{9,... | collective-permute-start | bytes 786440 | tf_op jit(solution)/shard_map/ppermute | solution.py:302
  25.8 6.8 %collective-permute-start.6 = (bf16[4,128,256]{2,1,0:T(8,128)(2,1)S(1)}, bf16[4,128,256]{2,1,0:T(8,128)(2,1)S(1)}, u32[]{:S(2)}, u32[]{:S(2)}) collective-permute-start(bf16[4,128,256]{2,1,0:T(8,128)(2,1)S(1)} %pad_maximum_fusion.2.refs_6_), channel_id=1, source_target_pairs={{0,4},{1,5},{2,6},{3,7},{4,0},{5,1},{6,2},{7,3},{8,12},{9,13},{10,... | collective-permute-start | bytes 786440 | tf_op jit(solution)/shard_map/ppermute | solution.py:302
  25.8 6.8 %collective-permute-start.11 = (bf16[4,128,256]{2,1,0:T(8,128)(2,1)S(1)}, bf16[4,128,256]{2,1,0:T(8,128)(2,1)S(1)}, u32[]{:S(2)}, u32[]{:S(2)}) collective-permute-start(bf16[4,128,256]{2,1,0:T(8,128)(2,1)S(1)} %constant_dynamic-update-slice_fusion.refs_10_), channel_id=1, source_target_pairs={{0,4},{1,5},{2,6},{3,7},{4,0},{5,1},{6,2},{7,3},{8,12},{9,13},{10,... | collective-permute-start | bytes 786440 | tf_op jit(solution)/shard_map/ppermute | solution.py:302
  26.3 6.3 %collective-permute-start.8 = (bf16[4,128,256]{2,1,0:T(8,128)(2,1)S(1)}, bf16[4,128,256]{2,1,0:T(8,128)(2,1)S(1)}, u32[]{:S(2)}, u32[]{:S(2)}) collective-permute-start(bf16[4,128,256]{2,1,0:T(8,128)(2,1)S(1)} %collective-permute-done.7.refs_8_), channel_id=1, source_target_pairs={{0,4},{1,5},{2,6},{3,7},{4,0},{5,1},{6,2},{7,3},{8,12},{9,13},{10,... | collective-permute-start | bytes 786440 | tf_op jit(solution)/shard_map/ppermute | solution.py:302
  31.5 1.5 %collective-permute-start.13 = (bf16[4,128,256]{2,1,0:T(8,128)(2,1)S(1)}, bf16[4,128,256]{2,1,0:T(8,128)(2,1)S(1)}, u32[]{:S(2)}, u32[]{:S(2)}) collective-permute-start(bf16[4,128,256]{2,1,0:T(8,128)(2,1)S(1)} %collective-permute-done.12.refs_12_), channel_id=1, source_target_pairs={{0,4},{1,5},{2,6},{3,7},{4,0},{5,1},{6,2},{7,3},{8,12},{9,13},{10,... | collective-permute-start | bytes 786440 | tf_op jit(solution)/shard_map/ppermute | solution.py:302
  44.2 2.7 %collective-permute-start.14 = (bf16[4,4,128,256]{3,2,1,0:T(8,128)(2,1)S(1)}, bf16[4,4,128,256]{3,2,1,0:T(8,128)(2,1)S(1)}, u32[]{:S(2)}, u32[]{:S(2)}) collective-permute-start(bf16[4,4,128,256]{3,2,1,0:T(8,128)(2,1)S(1)} %get-tuple-element.44), channel_id=1, source_target_pairs={{0,4},{1,5},{2,6},{3,7},{4,0},{5,1},{6,2},{7,3},{8,12},{9,13},{10,... | collective-permute-start | bytes 3145736 | tf_op jit(solution)/shard_map/ppermute | solution.py:302
  47.1 9.1 %collective-permute-start.15 = (bf16[4,128,256]{2,1,0:T(8,128)(2,1)S(1)}, bf16[4,128,256]{2,1,0:T(8,128)(2,1)S(1)}, u32[]{:S(2)}, u32[]{:S(2)}) collective-permute-start(bf16[4,128,256]{2,1,0:T(8,128)(2,1)S(1)} %get-tuple-element.66), channel_id=1, source_target_pairs={{0,1},{1,0},{2,3},{3,2},{4,5},{5,4},{6,7},{7,6},{8,9},{9,8},{10,11... | collective-permute-start | bytes 786440 | tf_op jit(solution)/shard_map/ppermute | solution.py:302
  49.6 9.9 %collective-permute-start.18 = (bf16[128,1024]{1,0:T(8,128)(2,1)S(1)}, bf16[128,1024]{1,0:T(8,128)(2,1)S(1)}, u32[]{:S(2)}, u32[]{:S(2)}) collective-permute-start(bf16[128,1024]{1,0:T(8,128)(2,1)S(1)} %get-tuple-element.46), channel_id=1, source_target_pairs={{0,8},{1,9},{2,10},{3,11},{4,12},{5,13},{6,14},{7,15},{8,0},{9,1},... | collective-permute-start | bytes 786440 | tf_op jit(solution)/shard_map/ppermute | solution.py:302
  50.1 13.4 %collective-permute-start.19 = (bf16[128,1024]{1,0:T(8,128)(2,1)S(1)}, bf16[128,1024]{1,0:T(8,128)(2,1)S(1)}, u32[]{:S(2)}, u32[]{:S(2)}) collective-permute-start(bf16[128,1024]{1,0:T(8,128)(2,1)S(1)} %get-tuple-element.47), channel_id=1, source_target_pairs={{0,16},{1,17},{2,18},{3,19},{4,20},{5,21},{6,22},{7,23},{8,24},{9,... | collective-permute-start | bytes 786440 | tf_op jit(solution)/shard_map/ppermute | solution.py:302
  50.6 12.9 %collective-permute-start.20 = (bf16[128,1024]{1,0:T(8,128)(2,1)S(1)}, bf16[128,1024]{1,0:T(8,128)(2,1)S(1)}, u32[]{:S(2)}, u32[]{:S(2)}) collective-permute-start(bf16[128,1024]{1,0:T(8,128)(2,1)S(1)} %get-tuple-element.48), channel_id=1, source_target_pairs={{0,24},{1,25},{2,26},{3,27},{4,28},{5,29},{6,30},{7,31},{8,16},{9,... | collective-permute-start | bytes 786440 | tf_op jit(solution)/shard_map/ppermute | solution.py:302
  56.2 12.1 %collective-permute-start.16 = (bf16[4,128,256]{2,1,0:T(8,128)(2,1)S(1)}, bf16[4,128,256]{2,1,0:T(8,128)(2,1)S(1)}, u32[]{:S(2)}, u32[]{:S(2)}) collective-permute-start(bf16[4,128,256]{2,1,0:T(8,128)(2,1)S(1)} %get-tuple-element.45), channel_id=1, source_target_pairs={{0,1},{1,0},{2,3},{3,2},{4,5},{5,4},{6,7},{7,6},{8,9},{9,8},{10,11... | collective-permute-start | bytes 786440 | tf_op jit(solution)/shard_map/ppermute | solution.py:302
  58.0 9.2 %collective-permute-start.17 = (bf16[3,128,256]{2,1,0:T(8,128)(2,1)S(1)}, bf16[3,128,256]{2,1,0:T(8,128)(2,1)S(1)}, u32[]{:S(2)}, u32[]{:S(2)}) collective-permute-start(bf16[3,128,256]{2,1,0:T(8,128)(2,1)S(1)} %fusion), channel_id=1, source_target_pairs={{0,2},{1,3},{2,0},{3,1},{4,6},{5,7},{6,4},{7,5},{8,10},{9,11},{10,... | collective-permute-start | bytes 589832 | tf_op jit(solution)/shard_map/ppermute | solution.py:302
  68.4 6.9 %collective-permute-start.21 = (bf16[128,256]{1,0:T(8,128)(2,1)S(1)}, bf16[128,256]{1,0:T(8,128)(2,1)S(1)}, u32[]{:S(2)}, u32[]{:S(2)}) collective-permute-start(bf16[128,256]{1,0:T(8,128)(2,1)S(1)} %get-tuple-element.56), channel_id=1, source_target_pairs={{0,2},{1,3},{2,0},{3,1},{4,6},{5,7},{6,4},{7,5},{8,10},{9,11},{10,... | collective-permute-start | bytes 196616 | tf_op jit(solution)/shard_map/ppermute | solution.py:302
  70.7 4.6 %collective-permute-start.22 = (bf16[128,256]{1,0:T(8,128)(2,1)S(1)}, bf16[128,256]{1,0:T(8,128)(2,1)S(1)}, u32[]{:S(2)}, u32[]{:S(2)}) collective-permute-start(bf16[128,256]{1,0:T(8,128)(2,1)S(1)} %get-tuple-element.57), channel_id=1, source_target_pairs={{0,8},{1,9},{2,10},{3,11},{4,12},{5,13},{6,14},{7,15},{8,0},{9,1},... | collective-permute-start | bytes 196616 | tf_op jit(solution)/shard_map/ppermute | solution.py:302
  71.3 4.3 %collective-permute-start.23 = (bf16[128,256]{1,0:T(8,128)(2,1)S(1)}, bf16[128,256]{1,0:T(8,128)(2,1)S(1)}, u32[]{:S(2)}, u32[]{:S(2)}) collective-permute-start(bf16[128,256]{1,0:T(8,128)(2,1)S(1)} %get-tuple-element.58), channel_id=1, source_target_pairs={{0,16},{1,17},{2,18},{3,19},{4,20},{5,21},{6,22},{7,23},{8,24},{9,... | collective-permute-start | bytes 196616 | tf_op jit(solution)/shard_map/ppermute | solution.py:302
  71.8 5.2 %collective-permute-start.24 = (bf16[128,256]{1,0:T(8,128)(2,1)S(1)}, bf16[128,256]{1,0:T(8,128)(2,1)S(1)}, u32[]{:S(2)}, u32[]{:S(2)}) collective-permute-start(bf16[128,256]{1,0:T(8,128)(2,1)S(1)} %get-tuple-element.59), channel_id=1, source_target_pairs={{0,24},{1,25},{2,26},{3,27},{4,28},{5,29},{6,30},{7,31},{8,16},{9,... | collective-permute-start | bytes 196616 | tf_op jit(solution)/shard_map/ppermute | solution.py:302

commit v6 on v5

--- a/solution.py
+++ b/solution.py
@@ -649,18 +649,25 @@
     od, dkv = attention(lengths, marks, qd, kv, cores, heads)
 
     both = (dkv[0], flipped(dkv[1], 1, 0))
-    third = flipped(summed(*(term[3] for term in both)), 0, 1)
-    first, _ = together((summed(*(term[1] for term in both)), third))
-    first, rest, od_moved = together(
+    third_rest = flipped(summed(*(term[3, 1:] for term in both)), 0, 1)
+    first, last, _ = together(
+        (
+            summed(*(term[1] for term in both)),
+            summed(*(term[3, 0] for term in both)),
+            third_rest,
+        )
+    )
+    first, third_own, rest, od_moved = together(
         (
             flipped(first, 0, 1),
-            flipped(summed(*(term[2, 1:] for term in both), third[1:]), 0, 2),
+            flipped(last, 0, 1),
+            flipped(summed(*(term[2, 1:] for term in both), third_rest), 0, 2),
             exchange(od)[1:],
         )
     )
     own, grads = together(
         (
-            summed(*(term[2, 0] for term in both), third[0]),
+            summed(*(term[2, 0] for term in both), third_own),
             [summed(*(term[0, s] for term in both), first[s], rest[s - 1]) for s in (1, 2, 3)],
         )
     )

time: 77.4 us -> 76.7 us (level)
  starting transfers between devices: 29.2 us -> 35 us
  Pallas kernels: 14.2 us -> 10.5 us
  waiting for transfers between devices: 30.9 us -> 27.9 us
    ppermute x25 -> x26, starting transfers between devices: 29.2 us -> 35 us  [flipped(): return lax.ppermute(value, ('ctx', 'head'), pairs)]
    pallas_call x1, Pallas kernels: 11.2 us -> 7.46 us  [attention(): pl.pallas_call(functools.partial(attention_kernel, cores, heads, tok), ou...]
    ppermute x25 -> x26, waiting for transfers between devices: 30.9 us -> 27.9 us  [flipped(): return lax.ppermute(value, ('ctx', 'head'), pairs)]
  transfers between devices with their start and end apart: 25 -> 26, of which waited for: 11 -> 8; matrix products, arithmetic and copies ran while one was open for 2% -> 2% of each run, Pallas kernels for 3% -> 3%
where the time goes in v6:
time: 76.7 us
  starting transfers between devices  35 us (46%)
  waiting for transfers between devices  27.9 us (36%)
  Pallas kernels  10.5 us (14%)
  other arithmetic  2.59 us (3%)
  between operations  0.77 us (1%)
    ppermute x26, starting transfers between devices, flipped(): return lax.ppermute(value, ('ctx', 'head'), pairs)  35 us
    ppermute x26, waiting for transfers between devices, flipped(): return lax.ppermute(value, ('ctx', 'head'), pairs)  27.9 us
    pallas_call x1, Pallas kernels, attention(): pl.pallas_call(functools.partial(attention_kernel, cores, heads, tok), ou...  7.46 us
    pallas_call x2, Pallas kernels, join_heads(): pl.pallas_call(functools.partial(join_heads_kernel, pieces, wide), out_sh...  1.81 us
  transfers between devices with their start and end apart: 26, of which 8 were waited for; matrix products, arithmetic and copies ran while one was open for 2% of the time, Pallas kernels for 3%

profile of v6, /device:TPU:0, one launch (start us, length us, event | category | flops | bytes accessed | tf_op | source)
XLA Modules:
  0.0 76.7 jit_solution(13266854891254176950)
XLA Ops:
  0.6 1.0 %pad_maximum_fusion.1.both_ref = bf16[128,1024]{1,0:T(8,128)(2,1)S(1)} fusion(bf16[128,512]{1,0:T(8,128)(2,1)} %param.7, bf16[128,512]{1,0:T(8,128)(2,1)} %param.6), kind=kLoop, calls=%fused_computation.6 | loop fusion | flops 524288 | bytes 524288 | tf_op jit(solution)/shard_map/concatenate | solution.py:333
  1.7 0.1 shard_map.85
  1.8 4.1 %collective-permute-start.9 = (bf16[1,128,256]{2,1,0:T(8,128)(2,1)S(1)}, bf16[1,128,256]{2,1,0:T(8,128)(2,1)S(1)}, u32[]{:S(2)}, u32[]{:S(2)}) collective-permute-start(bf16[1,128,256]{2,1,0:T(8,128)(2,1)S(1)} %bitcast.47), channel_id=1, source_target_pairs={{0,2},{1,3},{2,0},{3,1},{4,6},{5,7},{6,4},{7,5},{8,10},{9,11},{10,... | collective-permute-start | bytes 196616 | tf_op jit(solution)/shard_map/ppermute | solution.py:302
  5.9 1.5 %collective-permute-start.3 = (bf16[128,256]{1,0:T(8,128)(2,1)S(1)}, bf16[128,256]{1,0:T(8,128)(2,1)S(1)}, u32[]{:S(2)}, u32[]{:S(2)}) collective-permute-start(bf16[128,256]{1,0:T(8,128)(2,1)S(1)} %get-tuple-element.41), channel_id=1, source_target_pairs={{0,8},{1,9},{2,10},{3,11},{4,12},{5,13},{6,14},{7,15},{8,0},{9,1},... | collective-permute-start | bytes 196616 | tf_op jit(solution)/shard_map/ppermute | solution.py:302
  7.4 1.5 %collective-permute-start.4 = (bf16[128,256]{1,0:T(8,128)(2,1)S(1)}, bf16[128,256]{1,0:T(8,128)(2,1)S(1)}, u32[]{:S(2)}, u32[]{:S(2)}) collective-permute-start(bf16[128,256]{1,0:T(8,128)(2,1)S(1)} %get-tuple-element.42), channel_id=1, source_target_pairs={{0,16},{1,17},{2,18},{3,19},{4,20},{5,21},{6,22},{7,23},{8,24},{9,... | collective-permute-start | bytes 196616 | tf_op jit(solution)/shard_map/ppermute | solution.py:302
  8.9 0.5 collective-permute-start.5
  9.4 1.1 %pad_maximum_fusion.both_ref = bf16[128,4096]{1,0:T(8,128)(2,1)S(1)} fusion(bf16[128,2048]{1,0:T(8,128)(2,1)S(1)} %copy-done.1, bf16[128,2048]{1,0:T(8,128)(2,1)} %param.5), kind=kLoop, calls=%fused_computation | loop fusion | flops 2097152 | bytes 2097152 | tf_op jit(solution)/shard_map/concatenate | solution.py:380
  10.5 1.1 %shard_map.84 = (bf16[128,1024]{1,0:T(8,128)(2,1)S(1)}, bf16[128,1024]{1,0:T(8,128)(2,1)S(1)}, bf16[128,1024]{1,0:T(8,128)(2,1)S(1)}, bf16[128,1024]{1,0:T(8,128)(2,1)S(1)}, bf16[4096,128]{1,0:T(8,128)(2,1)S(1)}) custom-call(s32[32]{0:T(128)S(1)} %copy-done, bf16[128,4096]{1,0:T(8,128)(2,1)S(1)} %pad_maximum_fusion.both_ref), custom_call_target="tpu_custom_call" | custom-call | tf_op jit(solution)/shard_map/pallas_call | solution.py:373
  11.7 1.6 %collective-permute-start = (bf16[128,1024]{1,0:T(8,128)(2,1)S(1)}, bf16[128,1024]{1,0:T(8,128)(2,1)S(1)}, u32[]{:S(2)}, u32[]{:S(2)}) collective-permute-start(bf16[128,1024]{1,0:T(8,128)(2,1)S(1)} %get-tuple-element.37), channel_id=1, source_target_pairs={{0,8},{1,9},{2,10},{3,11},{4,12},{5,13},{6,14},{7,15},{8,0},{9,1},... | collective-permute-start | bytes 786440 | tf_op jit(solution)/shard_map/ppermute | solution.py:302
  13.2 0.0 collective-permute-done.3
  13.2 1.5 %collective-permute-start.1 = (bf16[128,1024]{1,0:T(8,128)(2,1)S(1)}, bf16[128,1024]{1,0:T(8,128)(2,1)S(1)}, u32[]{:S(2)}, u32[]{:S(2)}) collective-permute-start(bf16[128,1024]{1,0:T(8,128)(2,1)S(1)} %get-tuple-element.38), channel_id=1, source_target_pairs={{0,16},{1,17},{2,18},{3,19},{4,20},{5,21},{6,22},{7,23},{8,24},{9,... | collective-permute-start | bytes 786440 | tf_op jit(solution)/shard_map/ppermute | solution.py:302
  14.7 0.0 collective-permute-done.4
  14.7 0.0 collective-permute-done.5
  14.8 0.4 collective-permute-start.10
  15.2 1.6 %collective-permute-start.7 = (bf16[4,128,256]{2,1,0:T(8,128)(2,1)S(1)}, bf16[4,128,256]{2,1,0:T(8,128)(2,1)S(1)}, u32[]{:S(2)}, u32[]{:S(2)}) collective-permute-start(bf16[4,128,256]{2,1,0:T(8,128)(2,1)S(1)} %pad_maximum_fusion.2.refs_6_), channel_id=1, source_target_pairs={{0,1},{1,0},{2,3},{3,2},{4,5},{5,4},{6,7},{7,6},{8,9},{9,8},{10,11... | collective-permute-start | bytes 786440 | tf_op jit(solution)/shard_map/ppermute | solution.py:302
  16.9 0.0 collective-permute-done.9
  16.9 8.1 %collective-permute-done.10 = bf16[3,128,256]{2,1,0:T(8,128)(2,1)S(1)} collective-permute-done((bf16[3,128,256]{2,1,0:T(8,128)(2,1)S(1)}, bf16[3,128,256]{2,1,0:T(8,128)(2,1)S(1)}, u32[]{:S(2)}, u32[]{:S(2)}) %collective-permute-start.10) | collective-permute-done | bytes 196640 | tf_op jit(solution)/shard_map/ppermute | solution.py:302
  25.0 0.3 collective-permute-start.12
  25.3 0.5 collective-permute-start.2
  25.8 0.5 collective-permute-start.11
  26.3 0.1 collective-permute-start.8
  26.4 5.1 %collective-permute-done.12.refs_12_ = bf16[4,128,256]{2,1,0:T(8,128)(2,1)S(1)} collective-permute-done((bf16[4,128,256]{2,1,0:T(8,128)(2,1)S(1)}, bf16[4,128,256]{2,1,0:T(8,128)(2,1)S(1)}, u32[]{:S(2)}, u32[]{:S(2)}) %collective-permute-start.12) | collective-permute-done | bytes 262176 | tf_op jit(solution)/shard_map/ppermute | solution.py:302
  31.5 0.0 collective-permute-start.13
  31.5 1.1 %collective-permute-done.2.refs_5_ = bf16[128,1024]{1,0:T(8,128)(2,1)S(1)} collective-permute-done((bf16[128,1024]{1,0:T(8,128)(2,1)S(1)}, bf16[128,1024]{1,0:T(8,128)(2,1)S(1)}, u32[]{:S(2)}, u32[]{:S(2)}) %collective-permute-start.2) | collective-permute-done | bytes 262176 | tf_op jit(solution)/shard_map/ppermute | solution.py:302
  32.6 0.0 collective-permute-done.11.refs_11_
  32.6 0.4 collective-permute-done.13.refs_13_
  33.0 7.5 %shard_map.86 = (bf16[128,1024]{1,0:T(8,128)(2,1)S(1)}, bf16[128,1024]{1,0:T(8,128)(2,1)S(1)}, bf16[128,1024]{1,0:T(8,128)(2,1)S(1)}, bf16[128,1024]{1,0:T(8,128...) custom-call(s32[32]{0:T(128)S(1)} %copy-done, ...), custom_call_target="tpu_custom_call" | custom-call | tf_op jit(solution)/shard_map/pallas_call | solution.py:594
  40.5 3.9 %collective-permute-start.14 = (bf16[4,4,128,256]{3,2,1,0:T(8,128)(2,1)S(1)}, bf16[4,4,128,256]{3,2,1,0:T(8,128)(2,1)S(1)}, u32[]{:S(2)}, u32[]{:S(2)}) collective-permute-start(bf16[4,4,128,256]{3,2,1,0:T(8,128)(2,1)S(1)} %get-tuple-element.46), channel_id=1, source_target_pairs={{0,4},{1,5},{2,6},{3,7},{4,0},{5,1},{6,2},{7,3},{8,12},{9,13},{10,... | collective-permute-start | bytes 3145736 | tf_op jit(solution)/shard_map/ppermute | solution.py:302
  44.4 0.5 collective-permute-start.19
  44.9 0.5 collective-permute-start.20
  45.4 2.5 %collective-permute-start.21 = (bf16[128,1024]{1,0:T(8,128)(2,1)S(1)}, bf16[128,1024]{1,0:T(8,128)(2,1)S(1)}, u32[]{:S(2)}, u32[]{:S(2)}) collective-permute-start(bf16[128,1024]{1,0:T(8,128)(2,1)S(1)} %get-tuple-element.51), channel_id=1, source_target_pairs={{0,24},{1,25},{2,26},{3,27},{4,28},{5,29},{6,30},{7,31},{8,16},{9,... | collective-permute-start | bytes 786440 | tf_op jit(solution)/shard_map/ppermute | solution.py:302
  47.9 1.4 %collective-permute-start.15 = (bf16[3,128,256]{2,1,0:T(8,128)(2,1)S(1)}, bf16[3,128,256]{2,1,0:T(8,128)(2,1)S(1)}, u32[]{:S(2)}, u32[]{:S(2)}) collective-permute-start(bf16[3,128,256]{2,1,0:T(8,128)(2,1)S(1)} %fusion.2), channel_id=1, source_target_pairs={{0,1},{1,0},{2,3},{3,2},{4,5},{5,4},{6,7},{7,6},{8,9},{9,8},{10,11... | collective-permute-start | bytes 589832 | tf_op jit(solution)/shard_map/ppermute | solution.py:302
  49.3 0.1 fusion.1
  49.4 4.6 %collective-permute-done.15 = bf16[3,128,256]{2,1,0:T(8,128)(2,1)S(1)} collective-permute-done((bf16[3,128,256]{2,1,0:T(8,128)(2,1)S(1)}, bf16[3,128,256]{2,1,0:T(8,128)(2,1)S(1)}, u32[]{:S(2)}, u32[]{:S(2)}) %collective-permute-start.15) | collective-permute-done | bytes 196640 | tf_op jit(solution)/shard_map/ppermute | solution.py:302
  54.1 1.3 %collective-permute-start.16 = (bf16[4,128,256]{2,1,0:T(8,128)(2,1)S(1)}, bf16[4,128,256]{2,1,0:T(8,128)(2,1)S(1)}, u32[]{:S(2)}, u32[]{:S(2)}) collective-permute-start(bf16[4,128,256]{2,1,0:T(8,128)(2,1)S(1)} %fusion.1), channel_id=1, source_target_pairs={{0,1},{1,0},{2,3},{3,2},{4,5},{5,4},{6,7},{7,6},{8,9},{9,8},{10,11... | collective-permute-start | bytes 786440 | tf_op jit(solution)/shard_map/ppermute | solution.py:302
  55.4 0.1 fusion
  55.4 3.6 %collective-permute-start.18 = (bf16[3,128,256]{2,1,0:T(8,128)(2,1)S(1)}, bf16[3,128,256]{2,1,0:T(8,128)(2,1)S(1)}, u32[]{:S(2)}, u32[]{:S(2)}) collective-permute-start(bf16[3,128,256]{2,1,0:T(8,128)(2,1)S(1)} %fusion), channel_id=1, source_target_pairs={{0,2},{1,3},{2,0},{3,1},{4,6},{5,7},{6,4},{7,5},{8,10},{9,11},{10,... | collective-permute-start | bytes 589832 | tf_op jit(solution)/shard_map/ppermute | solution.py:302
  59.0 0.3 collective-permute-start.17
  59.3 6.9 %collective-permute-done.17 = bf16[128,256]{1,0:T(8,128)(2,1)S(1)} collective-permute-done((bf16[128,256]{1,0:T(8,128)(2,1)S(1)}, bf16[128,256]{1,0:T(8,128)(2,1)S(1)}, u32[]{:S(2)}, u32[]{:S(2)}) %collective-permute-start.17) | collective-permute-done | bytes 65568 | tf_op jit(solution)/shard_map/ppermute | solution.py:302
  66.2 0.1 fusion.3
  66.3 3.4 %collective-permute-start.22 = (bf16[128,256]{1,0:T(8,128)(2,1)S(1)}, bf16[128,256]{1,0:T(8,128)(2,1)S(1)}, u32[]{:S(2)}, u32[]{:S(2)}) collective-permute-start(bf16[128,256]{1,0:T(8,128)(2,1)S(1)} %get-tuple-element.60), channel_id=1, source_target_pairs={{0,2},{1,3},{2,0},{3,1},{4,6},{5,7},{6,4},{7,5},{8,10},{9,11},{10,... | collective-permute-start | bytes 196616 | tf_op jit(solution)/shard_map/ppermute | solution.py:302
  69.8 0.5 collective-permute-start.23
  70.3 0.5 collective-permute-start.24
  70.8 2.5 %collective-permute-start.25 = (bf16[128,256]{1,0:T(8,128)(2,1)S(1)}, bf16[128,256]{1,0:T(8,128)(2,1)S(1)}, u32[]{:S(2)}, u32[]{:S(2)}) collective-permute-start(bf16[128,256]{1,0:T(8,128)(2,1)S(1)} %get-tuple-element.63), channel_id=1, source_target_pairs={{0,24},{1,25},{2,26},{3,27},{4,28},{5,29},{6,30},{7,31},{8,16},{9,... | collective-permute-start | bytes 196616 | tf_op jit(solution)/shard_map/ppermute | solution.py:302
  73.3 1.1 %shard_map.87 = (bf16[128,2048]{1,0:T(8,128)(2,1)}, bf16[128,2048]{1,0:T(8,128)(2,1)}) custom-call(bf16[128,1024]{1,0:T(8,128)(2,1)S(1)} %get-tuple-element.44.refs_0_, bf16[128,1024]{1,0:T(8,128)(2,1)S(1)} %collective-permute-done.19.refs_1_, bf16[128,1024]{1,0:T(8,128)(2,1)S(1)} %collective-permute-done.20.refs_2_, ...), custom_call_target="tpu_custom_call" | custom-call | tf_op jit(solution)/shard_map/pallas_call | solution.py:339
  74.4 0.2 collective-permute-done.24.refs_2_
  74.6 1.4 %collective-permute-done.25.refs_3_ = bf16[128,256]{1,0:T(8,128)(2,1)S(1)} collective-permute-done((bf16[128,256]{1,0:T(8,128)(2,1)S(1)}, bf16[128,256]{1,0:T(8,128)(2,1)S(1)}, u32[]{:S(2)}, u32[]{:S(2)}) %collective-permute-start.25) | collective-permute-done | bytes 65568 | tf_op jit(solution)/shard_map/ppermute | solution.py:302
  76.0 0.8 shard_map.88
  (25 shorter events, 0.2 us)
Async XLA Ops:
  0.6 8.8 %copy-start.1 = (bf16[128,2048]{1,0:T(8,128)(2,1)S(1)}, bf16[128,2048]{1,0:T(8,128)(2,1)}, u32[]{:S(2)}) copy-start(bf16[128,2048]{1,0:T(8,128)(2,1)} %param.8) | copy-start | bytes 1572868
  1.8 15.1 %collective-permute-start.9 = (bf16[1,128,256]{2,1,0:T(8,128)(2,1)S(1)}, bf16[1,128,256]{2,1,0:T(8,128)(2,1)S(1)}, u32[]{:S(2)}, u32[]{:S(2)}) collective-permute-start(bf16[1,128,256]{2,1,0:T(8,128)(2,1)S(1)} %bitcast.47), channel_id=1, source_target_pairs={{0,2},{1,3},{2,0},{3,1},{4,6},{5,7},{6,4},{7,5},{8,10},{9,11},{10,... | collective-permute-start | bytes 196616 | tf_op jit(solution)/shard_map/ppermute | solution.py:302
  5.9 7.3 %collective-permute-start.3 = (bf16[128,256]{1,0:T(8,128)(2,1)S(1)}, bf16[128,256]{1,0:T(8,128)(2,1)S(1)}, u32[]{:S(2)}, u32[]{:S(2)}) collective-permute-start(bf16[128,256]{1,0:T(8,128)(2,1)S(1)} %get-tuple-element.41), channel_id=1, source_target_pairs={{0,8},{1,9},{2,10},{3,11},{4,12},{5,13},{6,14},{7,15},{8,0},{9,1},... | collective-permute-start | bytes 196616 | tf_op jit(solution)/shard_map/ppermute | solution.py:302
  7.4 7.4 %collective-permute-start.4 = (bf16[128,256]{1,0:T(8,128)(2,1)S(1)}, bf16[128,256]{1,0:T(8,128)(2,1)S(1)}, u32[]{:S(2)}, u32[]{:S(2)}) collective-permute-start(bf16[128,256]{1,0:T(8,128)(2,1)S(1)} %get-tuple-element.42), channel_id=1, source_target_pairs={{0,16},{1,17},{2,18},{3,19},{4,20},{5,21},{6,22},{7,23},{8,24},{9,... | collective-permute-start | bytes 196616 | tf_op jit(solution)/shard_map/ppermute | solution.py:302
  8.9 1.6 %copy-start = (s32[32]{0:T(128)S(1)}, s32[32]{0:T(128)}, u32[]{:S(2)}) copy-start(s32[32]{0:T(128)} %refs_0_.1) | copy-start | bytes 388
  8.9 5.8 %collective-permute-start.5 = (bf16[128,256]{1,0:T(8,128)(2,1)S(1)}, bf16[128,256]{1,0:T(8,128)(2,1)S(1)}, u32[]{:S(2)}, u32[]{:S(2)}) collective-permute-start(bf16[128,256]{1,0:T(8,128)(2,1)S(1)} %get-tuple-element.43), channel_id=1, source_target_pairs={{0,24},{1,25},{2,26},{3,27},{4,28},{5,29},{6,30},{7,31},{8,16},{9,... | collective-permute-start | bytes 196616 | tf_op jit(solution)/shard_map/ppermute | solution.py:302
  11.7 14.1 %collective-permute-start = (bf16[128,1024]{1,0:T(8,128)(2,1)S(1)}, bf16[128,1024]{1,0:T(8,128)(2,1)S(1)}, u32[]{:S(2)}, u32[]{:S(2)}) collective-permute-start(bf16[128,1024]{1,0:T(8,128)(2,1)S(1)} %get-tuple-element.37), channel_id=1, source_target_pairs={{0,8},{1,9},{2,10},{3,11},{4,12},{5,13},{6,14},{7,15},{8,0},{9,1},... | collective-permute-start | bytes 786440 | tf_op jit(solution)/shard_map/ppermute | solution.py:302
  13.2 12.6 %collective-permute-start.1 = (bf16[128,1024]{1,0:T(8,128)(2,1)S(1)}, bf16[128,1024]{1,0:T(8,128)(2,1)S(1)}, u32[]{:S(2)}, u32[]{:S(2)}) collective-permute-start(bf16[128,1024]{1,0:T(8,128)(2,1)S(1)} %get-tuple-element.38), channel_id=1, source_target_pairs={{0,16},{1,17},{2,18},{3,19},{4,20},{5,21},{6,22},{7,23},{8,24},{9,... | collective-permute-start | bytes 786440 | tf_op jit(solution)/shard_map/ppermute | solution.py:302
  14.8 10.2 %collective-permute-start.10 = (bf16[3,128,256]{2,1,0:T(8,128)(2,1)S(1)}, bf16[3,128,256]{2,1,0:T(8,128)(2,1)S(1)}, u32[]{:S(2)}, u32[]{:S(2)}) collective-permute-start(bf16[3,128,256]{2,1,0:T(8,128)(2,1)S(1)} %pad_maximum_fusion.3), channel_id=1, source_target_pairs={{0,2},{1,3},{2,0},{3,1},{4,6},{5,7},{6,4},{7,5},{8,10},{9,11},{10,... | collective-permute-start | bytes 589832 | tf_op jit(solution)/shard_map/ppermute | solution.py:302
  15.2 11.1 %collective-permute-start.7 = (bf16[4,128,256]{2,1,0:T(8,128)(2,1)S(1)}, bf16[4,128,256]{2,1,0:T(8,128)(2,1)S(1)}, u32[]{:S(2)}, u32[]{:S(2)}) collective-permute-start(bf16[4,128,256]{2,1,0:T(8,128)(2,1)S(1)} %pad_maximum_fusion.2.refs_6_), channel_id=1, source_target_pairs={{0,1},{1,0},{2,3},{3,2},{4,5},{5,4},{6,7},{7,6},{8,9},{9,8},{10,11... | collective-permute-start | bytes 786440 | tf_op jit(solution)/shard_map/ppermute | solution.py:302
  25.0 6.5 %collective-permute-start.12 = (bf16[4,128,256]{2,1,0:T(8,128)(2,1)S(1)}, bf16[4,128,256]{2,1,0:T(8,128)(2,1)S(1)}, u32[]{:S(2)}, u32[]{:S(2)}) collective-permute-start(bf16[4,128,256]{2,1,0:T(8,128)(2,1)S(1)} %constant_dynamic-update-slice_fusion.refs_10_), channel_id=1, source_target_pairs={{0,1},{1,0},{2,3},{3,2},{4,5},{5,4},{6,7},{7,6},{8,9},{9,8},{10,11... | collective-permute-start | bytes 786440 | tf_op jit(solution)/shard_map/ppermute | solution.py:302
  25.3 7.3 %collective-permute-start.2 = (bf16[128,1024]{1,0:T(8,128)(2,1)S(1)}, bf16[128,1024]{1,0:T(8,128)(2,1)S(1)}, u32[]{:S(2)}, u32[]{:S(2)}) collective-permute-start(bf16[128,1024]{1,0:T(8,128)(2,1)S(1)} %get-tuple-element.39), channel_id=1, source_target_pairs={{0,24},{1,25},{2,26},{3,27},{4,28},{5,29},{6,30},{7,31},{8,16},{9,... | collective-permute-start | bytes 786440 | tf_op jit(solution)/shard_map/ppermute | solution.py:302
  25.8 6.8 %collective-permute-start.6 = (bf16[4,128,256]{2,1,0:T(8,128)(2,1)S(1)}, bf16[4,128,256]{2,1,0:T(8,128)(2,1)S(1)}, u32[]{:S(2)}, u32[]{:S(2)}) collective-permute-start(bf16[4,128,256]{2,1,0:T(8,128)(2,1)S(1)} %pad_maximum_fusion.2.refs_6_), channel_id=1, source_target_pairs={{0,4},{1,5},{2,6},{3,7},{4,0},{5,1},{6,2},{7,3},{8,12},{9,13},{10,... | collective-permute-start | bytes 786440 | tf_op jit(solution)/shard_map/ppermute | solution.py:302
  25.8 6.8 %collective-permute-start.11 = (bf16[4,128,256]{2,1,0:T(8,128)(2,1)S(1)}, bf16[4,128,256]{2,1,0:T(8,128)(2,1)S(1)}, u32[]{:S(2)}, u32[]{:S(2)}) collective-permute-start(bf16[4,128,256]{2,1,0:T(8,128)(2,1)S(1)} %constant_dynamic-update-slice_fusion.refs_10_), channel_id=1, source_target_pairs={{0,4},{1,5},{2,6},{3,7},{4,0},{5,1},{6,2},{7,3},{8,12},{9,13},{10,... | collective-permute-start | bytes 786440 | tf_op jit(solution)/shard_map/ppermute | solution.py:302
  26.3 6.3 %collective-permute-start.8 = (bf16[4,128,256]{2,1,0:T(8,128)(2,1)S(1)}, bf16[4,128,256]{2,1,0:T(8,128)(2,1)S(1)}, u32[]{:S(2)}, u32[]{:S(2)}) collective-permute-start(bf16[4,128,256]{2,1,0:T(8,128)(2,1)S(1)} %collective-permute-done.7.refs_8_), channel_id=1, source_target_pairs={{0,4},{1,5},{2,6},{3,7},{4,0},{5,1},{6,2},{7,3},{8,12},{9,13},{10,... | collective-permute-start | bytes 786440 | tf_op jit(solution)/shard_map/ppermute | solution.py:302
  31.5 1.5 %collective-permute-start.13 = (bf16[4,128,256]{2,1,0:T(8,128)(2,1)S(1)}, bf16[4,128,256]{2,1,0:T(8,128)(2,1)S(1)}, u32[]{:S(2)}, u32[]{:S(2)}) collective-permute-start(bf16[4,128,256]{2,1,0:T(8,128)(2,1)S(1)} %collective-permute-done.12.refs_12_), channel_id=1, source_target_pairs={{0,4},{1,5},{2,6},{3,7},{4,0},{5,1},{6,2},{7,3},{8,12},{9,13},{10,... | collective-permute-start | bytes 786440 | tf_op jit(solution)/shard_map/ppermute | solution.py:302
  40.5 7.4 %collective-permute-start.14 = (bf16[4,4,128,256]{3,2,1,0:T(8,128)(2,1)S(1)}, bf16[4,4,128,256]{3,2,1,0:T(8,128)(2,1)S(1)}, u32[]{:S(2)}, u32[]{:S(2)}) collective-permute-start(bf16[4,4,128,256]{3,2,1,0:T(8,128)(2,1)S(1)} %get-tuple-element.46), channel_id=1, source_target_pairs={{0,4},{1,5},{2,6},{3,7},{4,0},{5,1},{6,2},{7,3},{8,12},{9,13},{10,... | collective-permute-start | bytes 3145736 | tf_op jit(solution)/shard_map/ppermute | solution.py:302
  44.4 14.6 %collective-permute-start.19 = (bf16[128,1024]{1,0:T(8,128)(2,1)S(1)}, bf16[128,1024]{1,0:T(8,128)(2,1)S(1)}, u32[]{:S(2)}, u32[]{:S(2)}) collective-permute-start(bf16[128,1024]{1,0:T(8,128)(2,1)S(1)} %get-tuple-element.49), channel_id=1, source_target_pairs={{0,8},{1,9},{2,10},{3,11},{4,12},{5,13},{6,14},{7,15},{8,0},{9,1},... | collective-permute-start | bytes 786440 | tf_op jit(solution)/shard_map/ppermute | solution.py:302
  44.9 14.4 %collective-permute-start.20 = (bf16[128,1024]{1,0:T(8,128)(2,1)S(1)}, bf16[128,1024]{1,0:T(8,128)(2,1)S(1)}, u32[]{:S(2)}, u32[]{:S(2)}) collective-permute-start(bf16[128,1024]{1,0:T(8,128)(2,1)S(1)} %get-tuple-element.50), channel_id=1, source_target_pairs={{0,16},{1,17},{2,18},{3,19},{4,20},{5,21},{6,22},{7,23},{8,24},{9,... | collective-permute-start | bytes 786440 | tf_op jit(solution)/shard_map/ppermute | solution.py:302
  45.4 13.9 %collective-permute-start.21 = (bf16[128,1024]{1,0:T(8,128)(2,1)S(1)}, bf16[128,1024]{1,0:T(8,128)(2,1)S(1)}, u32[]{:S(2)}, u32[]{:S(2)}) collective-permute-start(bf16[128,1024]{1,0:T(8,128)(2,1)S(1)} %get-tuple-element.51), channel_id=1, source_target_pairs={{0,24},{1,25},{2,26},{3,27},{4,28},{5,29},{6,30},{7,31},{8,16},{9,... | collective-permute-start | bytes 786440 | tf_op jit(solution)/shard_map/ppermute | solution.py:302
  47.9 6.1 %collective-permute-start.15 = (bf16[3,128,256]{2,1,0:T(8,128)(2,1)S(1)}, bf16[3,128,256]{2,1,0:T(8,128)(2,1)S(1)}, u32[]{:S(2)}, u32[]{:S(2)}) collective-permute-start(bf16[3,128,256]{2,1,0:T(8,128)(2,1)S(1)} %fusion.2), channel_id=1, source_target_pairs={{0,1},{1,0},{2,3},{3,2},{4,5},{5,4},{6,7},{7,6},{8,9},{9,8},{10,11... | collective-permute-start | bytes 589832 | tf_op jit(solution)/shard_map/ppermute | solution.py:302
  54.1 12.2 %collective-permute-start.16 = (bf16[4,128,256]{2,1,0:T(8,128)(2,1)S(1)}, bf16[4,128,256]{2,1,0:T(8,128)(2,1)S(1)}, u32[]{:S(2)}, u32[]{:S(2)}) collective-permute-start(bf16[4,128,256]{2,1,0:T(8,128)(2,1)S(1)} %fusion.1), channel_id=1, source_target_pairs={{0,1},{1,0},{2,3},{3,2},{4,5},{5,4},{6,7},{7,6},{8,9},{9,8},{10,11... | collective-permute-start | bytes 786440 | tf_op jit(solution)/shard_map/ppermute | solution.py:302
  55.4 10.8 %collective-permute-start.18 = (bf16[3,128,256]{2,1,0:T(8,128)(2,1)S(1)}, bf16[3,128,256]{2,1,0:T(8,128)(2,1)S(1)}, u32[]{:S(2)}, u32[]{:S(2)}) collective-permute-start(bf16[3,128,256]{2,1,0:T(8,128)(2,1)S(1)} %fusion), channel_id=1, source_target_pairs={{0,2},{1,3},{2,0},{3,1},{4,6},{5,7},{6,4},{7,5},{8,10},{9,11},{10,... | collective-permute-start | bytes 589832 | tf_op jit(solution)/shard_map/ppermute | solution.py:302
  59.0 7.2 %collective-permute-start.17 = (bf16[128,256]{1,0:T(8,128)(2,1)S(1)}, bf16[128,256]{1,0:T(8,128)(2,1)S(1)}, u32[]{:S(2)}, u32[]{:S(2)}) collective-permute-start(bf16[128,256]{1,0:T(8,128)(2,1)S(1)} %fusion.9), channel_id=1, source_target_pairs={{0,1},{1,0},{2,3},{3,2},{4,5},{5,4},{6,7},{7,6},{8,9},{9,8},{10,11... | collective-permute-start | bytes 196616 | tf_op jit(solution)/shard_map/ppermute | solution.py:302
  66.3 8.0 %collective-permute-start.22 = (bf16[128,256]{1,0:T(8,128)(2,1)S(1)}, bf16[128,256]{1,0:T(8,128)(2,1)S(1)}, u32[]{:S(2)}, u32[]{:S(2)}) collective-permute-start(bf16[128,256]{1,0:T(8,128)(2,1)S(1)} %get-tuple-element.60), channel_id=1, source_target_pairs={{0,2},{1,3},{2,0},{3,1},{4,6},{5,7},{6,4},{7,5},{8,10},{9,11},{10,... | collective-permute-start | bytes 196616 | tf_op jit(solution)/shard_map/ppermute | solution.py:302
  69.8 4.6 %collective-permute-start.23 = (bf16[128,256]{1,0:T(8,128)(2,1)S(1)}, bf16[128,256]{1,0:T(8,128)(2,1)S(1)}, u32[]{:S(2)}, u32[]{:S(2)}) collective-permute-start(bf16[128,256]{1,0:T(8,128)(2,1)S(1)} %get-tuple-element.61), channel_id=1, source_target_pairs={{0,8},{1,9},{2,10},{3,11},{4,12},{5,13},{6,14},{7,15},{8,0},{9,1},... | collective-permute-start | bytes 196616 | tf_op jit(solution)/shard_map/ppermute | solution.py:302
  70.3 4.3 %collective-permute-start.24 = (bf16[128,256]{1,0:T(8,128)(2,1)S(1)}, bf16[128,256]{1,0:T(8,128)(2,1)S(1)}, u32[]{:S(2)}, u32[]{:S(2)}) collective-permute-start(bf16[128,256]{1,0:T(8,128)(2,1)S(1)} %get-tuple-element.62), channel_id=1, source_target_pairs={{0,16},{1,17},{2,18},{3,19},{4,20},{5,21},{6,22},{7,23},{8,24},{9,... | collective-permute-start | bytes 196616 | tf_op jit(solution)/shard_map/ppermute | solution.py:302
  70.8 5.2 %collective-permute-start.25 = (bf16[128,256]{1,0:T(8,128)(2,1)S(1)}, bf16[128,256]{1,0:T(8,128)(2,1)S(1)}, u32[]{:S(2)}, u32[]{:S(2)}) collective-permute-start(bf16[128,256]{1,0:T(8,128)(2,1)S(1)} %get-tuple-element.63), channel_id=1, source_target_pairs={{0,24},{1,25},{2,26},{3,27},{4,28},{5,29},{6,30},{7,31},{8,16},{9,... | collective-permute-start | bytes 196616 | tf_op jit(solution)/shard_map/ppermute | solution.py:302

commit v7 on v6

--- a/solution.py
+++ b/solution.py
@@ -350,19 +350,16 @@
     split_heads_kernel(pieces, wide, both_ref, *piece_refs)
     total, docs = marks_ref.shape[0], lengths_ref.shape[0]
     lane = lax.broadcasted_iota(jnp.int32, (1, MARKS), 1)
-    begins = jnp.zeros((1, MARKS), jnp.int32)
-    ends = jnp.where(lane < docs, total, 0)
+    ends = jnp.zeros((1, MARKS), jnp.int32)
     end = jnp.int32(0)
     for number in range(docs):
-        begins = jnp.where(lane == number, end, begins)
         end = end + lengths_ref[number]
         ends = jnp.where(lane == number, end, ends)
 
     def some_rows(step, _):
         rows = pl.ds(pl.multiple_of(step * KEY_ROWS, KEY_ROWS), KEY_ROWS)
         position = step * KEY_ROWS + lax.broadcasted_iota(jnp.int32, (KEY_ROWS, MARKS), 0)
-        inside = (position >= begins) & (position < ends)
-        marks_ref[rows, :] = jnp.where(inside, 1.0, 0.0).astype(jnp.bfloat16)
+        marks_ref[rows, :] = jnp.where(position < ends, 1.0, 0.0).astype(jnp.bfloat16)
         return 0
 
     lax.fori_loop(0, total // KEY_ROWS, some_rows, 0)
@@ -382,7 +379,7 @@
 
 
 KEY_ROWS = 256
-BATCH = 4
+BATCH = 6
 MARKS = 128
 HIDDEN = -(2.0**100)
 
@@ -589,7 +586,7 @@
     lanes = group * tok
     reach = REACH * heads * tok
     pair = sum(-(-(keys + tok) // KEY_ROWS) for keys in (reach, reach // 2))
-    items = -(-KVH // 2 * pair // BATCH) * BATCH
+    items = KVH // 2 * pair
     bf16, f32 = jnp.bfloat16, jnp.float32
     results = pl.pallas_call(
         functools.partial(attention_kernel, cores, heads, tok),
@@ -614,7 +611,7 @@
             pltpu.VMEM((KVH, HD + 16, lanes), f32),
             pltpu.SMEM((3, items + BATCH), jnp.int32),
         ],
-        compiler_params=pltpu.CompilerParams(vmem_limit_bytes=36 * 1024 * 1024),
+        compiler_params=pltpu.CompilerParams(vmem_limit_bytes=42 * 1024 * 1024),
     )(lengths, marks, *qd, *kv)
     return results[: len(qd)], results[len(qd) :]
 

time: 76.7 us -> 76.9 us (level)
  starting transfers between devices: 35 us -> 33.3 us
  Pallas kernels: 10.5 us -> 12.1 us
  waiting for transfers between devices: 27.9 us -> 28.7 us
    pallas_call x1, Pallas kernels: 7.46 us -> 9.18 us  [attention(): pl.pallas_call(functools.partial(attention_kernel, cores, heads, tok), ou...]
    ppermute x26, starting transfers between devices: 35 us -> 33.3 us  [flipped(): return lax.ppermute(value, ('ctx', 'head'), pairs)]
    ppermute x26, waiting for transfers between devices: 27.9 us -> 28.7 us  [flipped(): return lax.ppermute(value, ('ctx', 'head'), pairs)]
where the time goes in v7:
time: 76.9 us; the launch traced here: 77.5 us
  starting transfers between devices  33.3 us (43%)
  waiting for transfers between devices  28.7 us (37%)
  Pallas kernels  12.1 us (16%)
  other arithmetic  2.59 us (3%)
  between operations  0.78 us (1%)
    ppermute x26, starting transfers between devices, flipped(): return lax.ppermute(value, ('ctx', 'head'), pairs)  33.3 us
    ppermute x26, waiting for transfers between devices, flipped(): return lax.ppermute(value, ('ctx', 'head'), pairs)  28.7 us
    pallas_call x1, Pallas kernels, attention(): pl.pallas_call(functools.partial(attention_kernel, cores, heads, tok), ou...  9.18 us
    pallas_call x2, Pallas kernels, join_heads(): pl.pallas_call(functools.partial(join_heads_kernel, pieces, wide), out_sh...  1.81 us
  transfers between devices with their start and end apart: 26, of which 8 were waited for; matrix products, arithmetic and copies ran while one was open for 2% of the time, Pallas kernels for 3%

profile of v7, /device:TPU:0, one launch (start us, length us, event | category | flops | bytes accessed | tf_op | source)
XLA Modules:
  0.0 77.5 jit_solution(1002011860728054844)
XLA Ops:
  0.6 1.0 %pad_maximum_fusion.1.both_ref = bf16[128,1024]{1,0:T(8,128)(2,1)S(1)} fusion(bf16[128,512]{1,0:T(8,128)(2,1)} %param.7, bf16[128,512]{1,0:T(8,128)(2,1)} %param.6), kind=kLoop, calls=%fused_computation.6 | loop fusion | flops 524288 | bytes 524288 | tf_op jit(solution)/shard_map/concatenate | solution.py:333
  1.7 0.1 shard_map.85
  1.8 4.1 %collective-permute-start.9 = (bf16[1,128,256]{2,1,0:T(8,128)(2,1)S(1)}, bf16[1,128,256]{2,1,0:T(8,128)(2,1)S(1)}, u32[]{:S(2)}, u32[]{:S(2)}) collective-permute-start(bf16[1,128,256]{2,1,0:T(8,128)(2,1)S(1)} %bitcast.47), channel_id=1, source_target_pairs={{0,2},{1,3},{2,0},{3,1},{4,6},{5,7},{6,4},{7,5},{8,10},{9,11},{10,... | collective-permute-start | bytes 196616 | tf_op jit(solution)/shard_map/ppermute | solution.py:302
  5.9 1.5 %collective-permute-start.3 = (bf16[128,256]{1,0:T(8,128)(2,1)S(1)}, bf16[128,256]{1,0:T(8,128)(2,1)S(1)}, u32[]{:S(2)}, u32[]{:S(2)}) collective-permute-start(bf16[128,256]{1,0:T(8,128)(2,1)S(1)} %get-tuple-element.41), channel_id=1, source_target_pairs={{0,8},{1,9},{2,10},{3,11},{4,12},{5,13},{6,14},{7,15},{8,0},{9,1},... | collective-permute-start | bytes 196616 | tf_op jit(solution)/shard_map/ppermute | solution.py:302
  7.4 1.5 %collective-permute-start.4 = (bf16[128,256]{1,0:T(8,128)(2,1)S(1)}, bf16[128,256]{1,0:T(8,128)(2,1)S(1)}, u32[]{:S(2)}, u32[]{:S(2)}) collective-permute-start(bf16[128,256]{1,0:T(8,128)(2,1)S(1)} %get-tuple-element.42), channel_id=1, source_target_pairs={{0,16},{1,17},{2,18},{3,19},{4,20},{5,21},{6,22},{7,23},{8,24},{9,... | collective-permute-start | bytes 196616 | tf_op jit(solution)/shard_map/ppermute | solution.py:302
  8.9 0.5 collective-permute-start.5
  9.4 1.1 %pad_maximum_fusion.both_ref = bf16[128,4096]{1,0:T(8,128)(2,1)S(1)} fusion(bf16[128,2048]{1,0:T(8,128)(2,1)S(1)} %copy-done.1, bf16[128,2048]{1,0:T(8,128)(2,1)} %param.5), kind=kLoop, calls=%fused_computation | loop fusion | flops 2097152 | bytes 2097152 | tf_op jit(solution)/shard_map/concatenate | solution.py:377
  10.5 1.0 %shard_map.84 = (bf16[128,1024]{1,0:T(8,128)(2,1)S(1)}, bf16[128,1024]{1,0:T(8,128)(2,1)S(1)}, bf16[128,1024]{1,0:T(8,128)(2,1)S(1)}, bf16[128,1024]{1,0:T(8,128)(2,1)S(1)}, bf16[4096,128]{1,0:T(8,128)(2,1)S(1)}) custom-call(s32[32]{0:T(128)S(1)} %copy-done, bf16[128,4096]{1,0:T(8,128)(2,1)S(1)} %pad_maximum_fusion.both_ref), custom_call_target="tpu_custom_call" | custom-call | tf_op jit(solution)/shard_map/pallas_call | solution.py:370
  11.5 1.6 %collective-permute-start = (bf16[128,1024]{1,0:T(8,128)(2,1)S(1)}, bf16[128,1024]{1,0:T(8,128)(2,1)S(1)}, u32[]{:S(2)}, u32[]{:S(2)}) collective-permute-start(bf16[128,1024]{1,0:T(8,128)(2,1)S(1)} %get-tuple-element.37), channel_id=1, source_target_pairs={{0,8},{1,9},{2,10},{3,11},{4,12},{5,13},{6,14},{7,15},{8,0},{9,1},... | collective-permute-start | bytes 786440 | tf_op jit(solution)/shard_map/ppermute | solution.py:302
  13.1 1.5 %collective-permute-start.1 = (bf16[128,1024]{1,0:T(8,128)(2,1)S(1)}, bf16[128,1024]{1,0:T(8,128)(2,1)S(1)}, u32[]{:S(2)}, u32[]{:S(2)}) collective-permute-start(bf16[128,1024]{1,0:T(8,128)(2,1)S(1)} %get-tuple-element.38), channel_id=1, source_target_pairs={{0,16},{1,17},{2,18},{3,19},{4,20},{5,21},{6,22},{7,23},{8,24},{9,... | collective-permute-start | bytes 786440 | tf_op jit(solution)/shard_map/ppermute | solution.py:302
  14.6 0.4 collective-permute-start.10
  15.1 1.6 %collective-permute-start.7 = (bf16[4,128,256]{2,1,0:T(8,128)(2,1)S(1)}, bf16[4,128,256]{2,1,0:T(8,128)(2,1)S(1)}, u32[]{:S(2)}, u32[]{:S(2)}) collective-permute-start(bf16[4,128,256]{2,1,0:T(8,128)(2,1)S(1)} %pad_maximum_fusion.2.refs_6_), channel_id=1, source_target_pairs={{0,1},{1,0},{2,3},{3,2},{4,5},{5,4},{6,7},{7,6},{8,9},{9,8},{10,11... | collective-permute-start | bytes 786440 | tf_op jit(solution)/shard_map/ppermute | solution.py:302
  16.7 0.0 collective-permute-done.9
  16.7 8.1 %collective-permute-done.10 = bf16[3,128,256]{2,1,0:T(8,128)(2,1)S(1)} collective-permute-done((bf16[3,128,256]{2,1,0:T(8,128)(2,1)S(1)}, bf16[3,128,256]{2,1,0:T(8,128)(2,1)S(1)}, u32[]{:S(2)}, u32[]{:S(2)}) %collective-permute-start.10) | collective-permute-done | bytes 196640 | tf_op jit(solution)/shard_map/ppermute | solution.py:302
  24.9 0.3 collective-permute-start.12
  25.2 0.5 collective-permute-start.2
  25.7 0.5 collective-permute-start.11
  26.2 0.1 collective-permute-start.8
  26.2 5.1 %collective-permute-done.12.refs_12_ = bf16[4,128,256]{2,1,0:T(8,128)(2,1)S(1)} collective-permute-done((bf16[4,128,256]{2,1,0:T(8,128)(2,1)S(1)}, bf16[4,128,256]{2,1,0:T(8,128)(2,1)S(1)}, u32[]{:S(2)}, u32[]{:S(2)}) %collective-permute-start.12) | collective-permute-done | bytes 262176 | tf_op jit(solution)/shard_map/ppermute | solution.py:302
  31.3 0.0 collective-permute-start.13
  31.3 1.1 %collective-permute-done.2.refs_5_ = bf16[128,1024]{1,0:T(8,128)(2,1)S(1)} collective-permute-done((bf16[128,1024]{1,0:T(8,128)(2,1)S(1)}, bf16[128,1024]{1,0:T(8,128)(2,1)S(1)}, u32[]{:S(2)}, u32[]{:S(2)}) %collective-permute-start.2) | collective-permute-done | bytes 262176 | tf_op jit(solution)/shard_map/ppermute | solution.py:302
  32.5 0.4 collective-permute-done.13.refs_13_
  32.9 9.2 %shard_map.86 = (bf16[128,1024]{1,0:T(8,128)(2,1)S(1)}, bf16[128,1024]{1,0:T(8,128)(2,1)S(1)}, bf16[128,1024]{1,0:T(8,128)(2,1)S(1)}, bf16[128,1024]{1,0:T(8,128...) custom-call(s32[32]{0:T(128)S(1)} %copy-done, ...), custom_call_target="tpu_custom_call" | custom-call | tf_op jit(solution)/shard_map/pallas_call | solution.py:591
  42.1 0.1 collective-permute-start.14
  42.1 0.6 collective-permute-start.19
  42.7 0.5 collective-permute-start.20
  43.2 2.4 %collective-permute-start.21 = (bf16[128,1024]{1,0:T(8,128)(2,1)S(1)}, bf16[128,1024]{1,0:T(8,128)(2,1)S(1)}, u32[]{:S(2)}, u32[]{:S(2)}) collective-permute-start(bf16[128,1024]{1,0:T(8,128)(2,1)S(1)} %get-tuple-element.51), channel_id=1, source_target_pairs={{0,24},{1,25},{2,26},{3,27},{4,28},{5,29},{6,30},{7,31},{8,16},{9,... | collective-permute-start | bytes 786440 | tf_op jit(solution)/shard_map/ppermute | solution.py:302
  45.7 0.0 collective-permute-done.14
  45.7 4.2 %collective-permute-start.15 = (bf16[3,128,256]{2,1,0:T(8,128)(2,1)S(1)}, bf16[3,128,256]{2,1,0:T(8,128)(2,1)S(1)}, u32[]{:S(2)}, u32[]{:S(2)}) collective-permute-start(bf16[3,128,256]{2,1,0:T(8,128)(2,1)S(1)} %fusion.2), channel_id=1, source_target_pairs={{0,1},{1,0},{2,3},{3,2},{4,5},{5,4},{6,7},{7,6},{8,9},{9,8},{10,11... | collective-permute-start | bytes 589832 | tf_op jit(solution)/shard_map/ppermute | solution.py:302
  49.9 0.1 fusion.1
  50.0 4.6 %collective-permute-done.15 = bf16[3,128,256]{2,1,0:T(8,128)(2,1)S(1)} collective-permute-done((bf16[3,128,256]{2,1,0:T(8,128)(2,1)S(1)}, bf16[3,128,256]{2,1,0:T(8,128)(2,1)S(1)}, u32[]{:S(2)}, u32[]{:S(2)}) %collective-permute-start.15) | collective-permute-done | bytes 196640 | tf_op jit(solution)/shard_map/ppermute | solution.py:302
  54.6 1.7 %collective-permute-start.16 = (bf16[4,128,256]{2,1,0:T(8,128)(2,1)S(1)}, bf16[4,128,256]{2,1,0:T(8,128)(2,1)S(1)}, u32[]{:S(2)}, u32[]{:S(2)}) collective-permute-start(bf16[4,128,256]{2,1,0:T(8,128)(2,1)S(1)} %fusion.1), channel_id=1, source_target_pairs={{0,1},{1,0},{2,3},{3,2},{4,5},{5,4},{6,7},{7,6},{8,9},{9,8},{10,11... | collective-permute-start | bytes 786440 | tf_op jit(solution)/shard_map/ppermute | solution.py:302
  56.4 0.1 fusion
  56.4 3.0 %collective-permute-start.18 = (bf16[3,128,256]{2,1,0:T(8,128)(2,1)S(1)}, bf16[3,128,256]{2,1,0:T(8,128)(2,1)S(1)}, u32[]{:S(2)}, u32[]{:S(2)}) collective-permute-start(bf16[3,128,256]{2,1,0:T(8,128)(2,1)S(1)} %fusion), channel_id=1, source_target_pairs={{0,2},{1,3},{2,0},{3,1},{4,6},{5,7},{6,4},{7,5},{8,10},{9,11},{10,... | collective-permute-start | bytes 589832 | tf_op jit(solution)/shard_map/ppermute | solution.py:302
  59.4 0.3 collective-permute-start.17
  59.7 0.0 collective-permute-done.20.refs_2_
  59.7 0.0 collective-permute-done.21.refs_3_
  59.7 7.8 %collective-permute-done.17 = bf16[128,256]{1,0:T(8,128)(2,1)S(1)} collective-permute-done((bf16[128,256]{1,0:T(8,128)(2,1)S(1)}, bf16[128,256]{1,0:T(8,128)(2,1)S(1)}, u32[]{:S(2)}, u32[]{:S(2)}) %collective-permute-start.17) | collective-permute-done | bytes 65568 | tf_op jit(solution)/shard_map/ppermute | solution.py:302
  67.5 0.0 collective-permute-done.18
  67.5 0.1 fusion.3
  67.6 3.0 %collective-permute-start.22 = (bf16[128,256]{1,0:T(8,128)(2,1)S(1)}, bf16[128,256]{1,0:T(8,128)(2,1)S(1)}, u32[]{:S(2)}, u32[]{:S(2)}) collective-permute-start(bf16[128,256]{1,0:T(8,128)(2,1)S(1)} %get-tuple-element.60), channel_id=1, source_target_pairs={{0,2},{1,3},{2,0},{3,1},{4,6},{5,7},{6,4},{7,5},{8,10},{9,11},{10,... | collective-permute-start | bytes 196616 | tf_op jit(solution)/shard_map/ppermute | solution.py:302
  70.5 0.5 collective-permute-start.23
  71.1 0.5 collective-permute-start.24
  71.6 2.5 %collective-permute-start.25 = (bf16[128,256]{1,0:T(8,128)(2,1)S(1)}, bf16[128,256]{1,0:T(8,128)(2,1)S(1)}, u32[]{:S(2)}, u32[]{:S(2)}) collective-permute-start(bf16[128,256]{1,0:T(8,128)(2,1)S(1)} %get-tuple-element.63), channel_id=1, source_target_pairs={{0,24},{1,25},{2,26},{3,27},{4,28},{5,29},{6,30},{7,31},{8,16},{9,... | collective-permute-start | bytes 196616 | tf_op jit(solution)/shard_map/ppermute | solution.py:302
  74.0 1.1 %shard_map.87 = (bf16[128,2048]{1,0:T(8,128)(2,1)}, bf16[128,2048]{1,0:T(8,128)(2,1)}) custom-call(bf16[128,1024]{1,0:T(8,128)(2,1)S(1)} %get-tuple-element.44.refs_0_, bf16[128,1024]{1,0:T(8,128)(2,1)S(1)} %collective-permute-done.19.refs_1_, bf16[128,1024]{1,0:T(8,128)(2,1)S(1)} %collective-permute-done.20.refs_2_, ...), custom_call_target="tpu_custom_call" | custom-call | tf_op jit(solution)/shard_map/pallas_call | solution.py:339
  75.2 0.2 collective-permute-done.24.refs_2_
  75.3 1.4 %collective-permute-done.25.refs_3_ = bf16[128,256]{1,0:T(8,128)(2,1)S(1)} collective-permute-done((bf16[128,256]{1,0:T(8,128)(2,1)S(1)}, bf16[128,256]{1,0:T(8,128)(2,1)S(1)}, u32[]{:S(2)}, u32[]{:S(2)}) %collective-permute-start.25) | collective-permute-done | bytes 65568 | tf_op jit(solution)/shard_map/ppermute | solution.py:302
  76.8 0.8 shard_map.88
  (25 shorter events, 0.2 us)
Async XLA Ops:
  0.6 8.8 %copy-start.1 = (bf16[128,2048]{1,0:T(8,128)(2,1)S(1)}, bf16[128,2048]{1,0:T(8,128)(2,1)}, u32[]{:S(2)}) copy-start(bf16[128,2048]{1,0:T(8,128)(2,1)} %param.8) | copy-start | bytes 1572868
  1.8 14.9 %collective-permute-start.9 = (bf16[1,128,256]{2,1,0:T(8,128)(2,1)S(1)}, bf16[1,128,256]{2,1,0:T(8,128)(2,1)S(1)}, u32[]{:S(2)}, u32[]{:S(2)}) collective-permute-start(bf16[1,128,256]{2,1,0:T(8,128)(2,1)S(1)} %bitcast.47), channel_id=1, source_target_pairs={{0,2},{1,3},{2,0},{3,1},{4,6},{5,7},{6,4},{7,5},{8,10},{9,11},{10,... | collective-permute-start | bytes 196616 | tf_op jit(solution)/shard_map/ppermute | solution.py:302
  5.9 7.2 %collective-permute-start.3 = (bf16[128,256]{1,0:T(8,128)(2,1)S(1)}, bf16[128,256]{1,0:T(8,128)(2,1)S(1)}, u32[]{:S(2)}, u32[]{:S(2)}) collective-permute-start(bf16[128,256]{1,0:T(8,128)(2,1)S(1)} %get-tuple-element.41), channel_id=1, source_target_pairs={{0,8},{1,9},{2,10},{3,11},{4,12},{5,13},{6,14},{7,15},{8,0},{9,1},... | collective-permute-start | bytes 196616 | tf_op jit(solution)/shard_map/ppermute | solution.py:302
  7.4 7.2 %collective-permute-start.4 = (bf16[128,256]{1,0:T(8,128)(2,1)S(1)}, bf16[128,256]{1,0:T(8,128)(2,1)S(1)}, u32[]{:S(2)}, u32[]{:S(2)}) collective-permute-start(bf16[128,256]{1,0:T(8,128)(2,1)S(1)} %get-tuple-element.42), channel_id=1, source_target_pairs={{0,16},{1,17},{2,18},{3,19},{4,20},{5,21},{6,22},{7,23},{8,24},{9,... | collective-permute-start | bytes 196616 | tf_op jit(solution)/shard_map/ppermute | solution.py:302
  8.9 1.6 %copy-start = (s32[32]{0:T(128)S(1)}, s32[32]{0:T(128)}, u32[]{:S(2)}) copy-start(s32[32]{0:T(128)} %refs_0_.1) | copy-start | bytes 388
  8.9 5.7 %collective-permute-start.5 = (bf16[128,256]{1,0:T(8,128)(2,1)S(1)}, bf16[128,256]{1,0:T(8,128)(2,1)S(1)}, u32[]{:S(2)}, u32[]{:S(2)}) collective-permute-start(bf16[128,256]{1,0:T(8,128)(2,1)S(1)} %get-tuple-element.43), channel_id=1, source_target_pairs={{0,24},{1,25},{2,26},{3,27},{4,28},{5,29},{6,30},{7,31},{8,16},{9,... | collective-permute-start | bytes 196616 | tf_op jit(solution)/shard_map/ppermute | solution.py:302
  11.5 14.1 %collective-permute-start = (bf16[128,1024]{1,0:T(8,128)(2,1)S(1)}, bf16[128,1024]{1,0:T(8,128)(2,1)S(1)}, u32[]{:S(2)}, u32[]{:S(2)}) collective-permute-start(bf16[128,1024]{1,0:T(8,128)(2,1)S(1)} %get-tuple-element.37), channel_id=1, source_target_pairs={{0,8},{1,9},{2,10},{3,11},{4,12},{5,13},{6,14},{7,15},{8,0},{9,1},... | collective-permute-start | bytes 786440 | tf_op jit(solution)/shard_map/ppermute | solution.py:302
  13.1 12.6 %collective-permute-start.1 = (bf16[128,1024]{1,0:T(8,128)(2,1)S(1)}, bf16[128,1024]{1,0:T(8,128)(2,1)S(1)}, u32[]{:S(2)}, u32[]{:S(2)}) collective-permute-start(bf16[128,1024]{1,0:T(8,128)(2,1)S(1)} %get-tuple-element.38), channel_id=1, source_target_pairs={{0,16},{1,17},{2,18},{3,19},{4,20},{5,21},{6,22},{7,23},{8,24},{9,... | collective-permute-start | bytes 786440 | tf_op jit(solution)/shard_map/ppermute | solution.py:302
  14.6 10.2 %collective-permute-start.10 = (bf16[3,128,256]{2,1,0:T(8,128)(2,1)S(1)}, bf16[3,128,256]{2,1,0:T(8,128)(2,1)S(1)}, u32[]{:S(2)}, u32[]{:S(2)}) collective-permute-start(bf16[3,128,256]{2,1,0:T(8,128)(2,1)S(1)} %pad_maximum_fusion.3), channel_id=1, source_target_pairs={{0,2},{1,3},{2,0},{3,1},{4,6},{5,7},{6,4},{7,5},{8,10},{9,11},{10,... | collective-permute-start | bytes 589832 | tf_op jit(solution)/shard_map/ppermute | solution.py:302
  15.1 11.1 %collective-permute-start.7 = (bf16[4,128,256]{2,1,0:T(8,128)(2,1)S(1)}, bf16[4,128,256]{2,1,0:T(8,128)(2,1)S(1)}, u32[]{:S(2)}, u32[]{:S(2)}) collective-permute-start(bf16[4,128,256]{2,1,0:T(8,128)(2,1)S(1)} %pad_maximum_fusion.2.refs_6_), channel_id=1, source_target_pairs={{0,1},{1,0},{2,3},{3,2},{4,5},{5,4},{6,7},{7,6},{8,9},{9,8},{10,11... | collective-permute-start | bytes 786440 | tf_op jit(solution)/shard_map/ppermute | solution.py:302
  24.9 6.5 %collective-permute-start.12 = (bf16[4,128,256]{2,1,0:T(8,128)(2,1)S(1)}, bf16[4,128,256]{2,1,0:T(8,128)(2,1)S(1)}, u32[]{:S(2)}, u32[]{:S(2)}) collective-permute-start(bf16[4,128,256]{2,1,0:T(8,128)(2,1)S(1)} %constant_dynamic-update-slice_fusion.refs_10_), channel_id=1, source_target_pairs={{0,1},{1,0},{2,3},{3,2},{4,5},{5,4},{6,7},{7,6},{8,9},{9,8},{10,11... | collective-permute-start | bytes 786440 | tf_op jit(solution)/shard_map/ppermute | solution.py:302
  25.2 7.3 %collective-permute-start.2 = (bf16[128,1024]{1,0:T(8,128)(2,1)S(1)}, bf16[128,1024]{1,0:T(8,128)(2,1)S(1)}, u32[]{:S(2)}, u32[]{:S(2)}) collective-permute-start(bf16[128,1024]{1,0:T(8,128)(2,1)S(1)} %get-tuple-element.39), channel_id=1, source_target_pairs={{0,24},{1,25},{2,26},{3,27},{4,28},{5,29},{6,30},{7,31},{8,16},{9,... | collective-permute-start | bytes 786440 | tf_op jit(solution)/shard_map/ppermute | solution.py:302
  25.7 6.8 %collective-permute-start.6 = (bf16[4,128,256]{2,1,0:T(8,128)(2,1)S(1)}, bf16[4,128,256]{2,1,0:T(8,128)(2,1)S(1)}, u32[]{:S(2)}, u32[]{:S(2)}) collective-permute-start(bf16[4,128,256]{2,1,0:T(8,128)(2,1)S(1)} %pad_maximum_fusion.2.refs_6_), channel_id=1, source_target_pairs={{0,4},{1,5},{2,6},{3,7},{4,0},{5,1},{6,2},{7,3},{8,12},{9,13},{10,... | collective-permute-start | bytes 786440 | tf_op jit(solution)/shard_map/ppermute | solution.py:302
  25.7 6.8 %collective-permute-start.11 = (bf16[4,128,256]{2,1,0:T(8,128)(2,1)S(1)}, bf16[4,128,256]{2,1,0:T(8,128)(2,1)S(1)}, u32[]{:S(2)}, u32[]{:S(2)}) collective-permute-start(bf16[4,128,256]{2,1,0:T(8,128)(2,1)S(1)} %constant_dynamic-update-slice_fusion.refs_10_), channel_id=1, source_target_pairs={{0,4},{1,5},{2,6},{3,7},{4,0},{5,1},{6,2},{7,3},{8,12},{9,13},{10,... | collective-permute-start | bytes 786440 | tf_op jit(solution)/shard_map/ppermute | solution.py:302
  26.2 6.3 %collective-permute-start.8 = (bf16[4,128,256]{2,1,0:T(8,128)(2,1)S(1)}, bf16[4,128,256]{2,1,0:T(8,128)(2,1)S(1)}, u32[]{:S(2)}, u32[]{:S(2)}) collective-permute-start(bf16[4,128,256]{2,1,0:T(8,128)(2,1)S(1)} %collective-permute-done.7.refs_8_), channel_id=1, source_target_pairs={{0,4},{1,5},{2,6},{3,7},{4,0},{5,1},{6,2},{7,3},{8,12},{9,13},{10,... | collective-permute-start | bytes 786440 | tf_op jit(solution)/shard_map/ppermute | solution.py:302
  31.3 1.5 %collective-permute-start.13 = (bf16[4,128,256]{2,1,0:T(8,128)(2,1)S(1)}, bf16[4,128,256]{2,1,0:T(8,128)(2,1)S(1)}, u32[]{:S(2)}, u32[]{:S(2)}) collective-permute-start(bf16[4,128,256]{2,1,0:T(8,128)(2,1)S(1)} %collective-permute-done.12.refs_12_), channel_id=1, source_target_pairs={{0,4},{1,5},{2,6},{3,7},{4,0},{5,1},{6,2},{7,3},{8,12},{9,13},{10,... | collective-permute-start | bytes 786440 | tf_op jit(solution)/shard_map/ppermute | solution.py:302
  42.1 3.6 %collective-permute-start.14 = (bf16[4,4,128,256]{3,2,1,0:T(8,128)(2,1)S(1)}, bf16[4,4,128,256]{3,2,1,0:T(8,128)(2,1)S(1)}, u32[]{:S(2)}, u32[]{:S(2)}) collective-permute-start(bf16[4,4,128,256]{3,2,1,0:T(8,128)(2,1)S(1)} %get-tuple-element.46), channel_id=1, source_target_pairs={{0,4},{1,5},{2,6},{3,7},{4,0},{5,1},{6,2},{7,3},{8,12},{9,13},{10,... | collective-permute-start | bytes 3145736 | tf_op jit(solution)/shard_map/ppermute | solution.py:302
  42.1 17.2 %collective-permute-start.19 = (bf16[128,1024]{1,0:T(8,128)(2,1)S(1)}, bf16[128,1024]{1,0:T(8,128)(2,1)S(1)}, u32[]{:S(2)}, u32[]{:S(2)}) collective-permute-start(bf16[128,1024]{1,0:T(8,128)(2,1)S(1)} %get-tuple-element.49), channel_id=1, source_target_pairs={{0,8},{1,9},{2,10},{3,11},{4,12},{5,13},{6,14},{7,15},{8,0},{9,1},... | collective-permute-start | bytes 786440 | tf_op jit(solution)/shard_map/ppermute | solution.py:302
  42.7 17.0 %collective-permute-start.20 = (bf16[128,1024]{1,0:T(8,128)(2,1)S(1)}, bf16[128,1024]{1,0:T(8,128)(2,1)S(1)}, u32[]{:S(2)}, u32[]{:S(2)}) collective-permute-start(bf16[128,1024]{1,0:T(8,128)(2,1)S(1)} %get-tuple-element.50), channel_id=1, source_target_pairs={{0,16},{1,17},{2,18},{3,19},{4,20},{5,21},{6,22},{7,23},{8,24},{9,... | collective-permute-start | bytes 786440 | tf_op jit(solution)/shard_map/ppermute | solution.py:302
  43.2 16.5 %collective-permute-start.21 = (bf16[128,1024]{1,0:T(8,128)(2,1)S(1)}, bf16[128,1024]{1,0:T(8,128)(2,1)S(1)}, u32[]{:S(2)}, u32[]{:S(2)}) collective-permute-start(bf16[128,1024]{1,0:T(8,128)(2,1)S(1)} %get-tuple-element.51), channel_id=1, source_target_pairs={{0,24},{1,25},{2,26},{3,27},{4,28},{5,29},{6,30},{7,31},{8,16},{9,... | collective-permute-start | bytes 786440 | tf_op jit(solution)/shard_map/ppermute | solution.py:302
  45.7 8.9 %collective-permute-start.15 = (bf16[3,128,256]{2,1,0:T(8,128)(2,1)S(1)}, bf16[3,128,256]{2,1,0:T(8,128)(2,1)S(1)}, u32[]{:S(2)}, u32[]{:S(2)}) collective-permute-start(bf16[3,128,256]{2,1,0:T(8,128)(2,1)S(1)} %fusion.2), channel_id=1, source_target_pairs={{0,1},{1,0},{2,3},{3,2},{4,5},{5,4},{6,7},{7,6},{8,9},{9,8},{10,11... | collective-permute-start | bytes 589832 | tf_op jit(solution)/shard_map/ppermute | solution.py:302
  54.6 12.9 %collective-permute-start.16 = (bf16[4,128,256]{2,1,0:T(8,128)(2,1)S(1)}, bf16[4,128,256]{2,1,0:T(8,128)(2,1)S(1)}, u32[]{:S(2)}, u32[]{:S(2)}) collective-permute-start(bf16[4,128,256]{2,1,0:T(8,128)(2,1)S(1)} %fusion.1), channel_id=1, source_target_pairs={{0,1},{1,0},{2,3},{3,2},{4,5},{5,4},{6,7},{7,6},{8,9},{9,8},{10,11... | collective-permute-start | bytes 786440 | tf_op jit(solution)/shard_map/ppermute | solution.py:302
  56.4 11.0 %collective-permute-start.18 = (bf16[3,128,256]{2,1,0:T(8,128)(2,1)S(1)}, bf16[3,128,256]{2,1,0:T(8,128)(2,1)S(1)}, u32[]{:S(2)}, u32[]{:S(2)}) collective-permute-start(bf16[3,128,256]{2,1,0:T(8,128)(2,1)S(1)} %fusion), channel_id=1, source_target_pairs={{0,2},{1,3},{2,0},{3,1},{4,6},{5,7},{6,4},{7,5},{8,10},{9,11},{10,... | collective-permute-start | bytes 589832 | tf_op jit(solution)/shard_map/ppermute | solution.py:302
  59.4 8.1 %collective-permute-start.17 = (bf16[128,256]{1,0:T(8,128)(2,1)S(1)}, bf16[128,256]{1,0:T(8,128)(2,1)S(1)}, u32[]{:S(2)}, u32[]{:S(2)}) collective-permute-start(bf16[128,256]{1,0:T(8,128)(2,1)S(1)} %fusion.9), channel_id=1, source_target_pairs={{0,1},{1,0},{2,3},{3,2},{4,5},{5,4},{6,7},{7,6},{8,9},{9,8},{10,11... | collective-permute-start | bytes 196616 | tf_op jit(solution)/shard_map/ppermute | solution.py:302
  67.6 7.5 %collective-permute-start.22 = (bf16[128,256]{1,0:T(8,128)(2,1)S(1)}, bf16[128,256]{1,0:T(8,128)(2,1)S(1)}, u32[]{:S(2)}, u32[]{:S(2)}) collective-permute-start(bf16[128,256]{1,0:T(8,128)(2,1)S(1)} %get-tuple-element.60), channel_id=1, source_target_pairs={{0,2},{1,3},{2,0},{3,1},{4,6},{5,7},{6,4},{7,5},{8,10},{9,11},{10,... | collective-permute-start | bytes 196616 | tf_op jit(solution)/shard_map/ppermute | solution.py:302
  70.5 4.6 %collective-permute-start.23 = (bf16[128,256]{1,0:T(8,128)(2,1)S(1)}, bf16[128,256]{1,0:T(8,128)(2,1)S(1)}, u32[]{:S(2)}, u32[]{:S(2)}) collective-permute-start(bf16[128,256]{1,0:T(8,128)(2,1)S(1)} %get-tuple-element.61), channel_id=1, source_target_pairs={{0,8},{1,9},{2,10},{3,11},{4,12},{5,13},{6,14},{7,15},{8,0},{9,1},... | collective-permute-start | bytes 196616 | tf_op jit(solution)/shard_map/ppermute | solution.py:302
  71.1 4.3 %collective-permute-start.24 = (bf16[128,256]{1,0:T(8,128)(2,1)S(1)}, bf16[128,256]{1,0:T(8,128)(2,1)S(1)}, u32[]{:S(2)}, u32[]{:S(2)}) collective-permute-start(bf16[128,256]{1,0:T(8,128)(2,1)S(1)} %get-tuple-element.62), channel_id=1, source_target_pairs={{0,16},{1,17},{2,18},{3,19},{4,20},{5,21},{6,22},{7,23},{8,24},{9,... | collective-permute-start | bytes 196616 | tf_op jit(solution)/shard_map/ppermute | solution.py:302
  71.6 5.2 %collective-permute-start.25 = (bf16[128,256]{1,0:T(8,128)(2,1)S(1)}, bf16[128,256]{1,0:T(8,128)(2,1)S(1)}, u32[]{:S(2)}, u32[]{:S(2)}) collective-permute-start(bf16[128,256]{1,0:T(8,128)(2,1)S(1)} %get-tuple-element.63), channel_id=1, source_target_pairs={{0,24},{1,25},{2,26},{3,27},{4,28},{5,29},{6,30},{7,31},{8,16},{9,... | collective-permute-start | bytes 196616 | tf_op jit(solution)/shard_map/ppermute | solution.py:302

commit v8 on v7

--- a/solution.py
+++ b/solution.py
@@ -345,9 +345,7 @@
     )(*parts)
 
 
-def prepare_kernel(pieces, wide, lengths_ref, both_ref, *out_refs):
-    piece_refs, marks_ref = out_refs[:pieces], out_refs[pieces]
-    split_heads_kernel(pieces, wide, both_ref, *piece_refs)
+def marks_kernel(lengths_ref, marks_ref):
     total, docs = marks_ref.shape[0], lengths_ref.shape[0]
     lane = lax.broadcasted_iota(jnp.int32, (1, MARKS), 1)
     ends = jnp.zeros((1, MARKS), jnp.int32)
@@ -357,25 +355,22 @@
         ends = jnp.where(lane == number, end, ends)
 
     def some_rows(step, _):
-        rows = pl.ds(pl.multiple_of(step * KEY_ROWS, KEY_ROWS), KEY_ROWS)
-        position = step * KEY_ROWS + lax.broadcasted_iota(jnp.int32, (KEY_ROWS, MARKS), 0)
-        marks_ref[rows, :] = jnp.where(position < ends, 1.0, 0.0).astype(jnp.bfloat16)
+        rows = pl.ds(pl.multiple_of(step * 4 * KEY_ROWS, KEY_ROWS), 4 * KEY_ROWS)
+        position = lax.broadcasted_iota(jnp.int32, (4 * KEY_ROWS, MARKS), 0)
+        marks_ref[rows, :] = jnp.where(position < ends - step * 4 * KEY_ROWS, 1.0, 0.0).astype(jnp.bfloat16)
         return 0
 
-    lax.fori_loop(0, total // KEY_ROWS, some_rows, 0)
-
-
-def prepare(lengths, left, right, pieces, total):
-    rows, wide = left.shape[0], left.shape[1] // pieces
-    results = pl.pallas_call(
-        functools.partial(prepare_kernel, pieces, wide),
-        out_shape=[jax.ShapeDtypeStruct((rows, 2 * wide), left.dtype)] * pieces
-        + [jax.ShapeDtypeStruct((total, MARKS), jnp.bfloat16)],
-        in_specs=[SMEM, VMEM],
-        out_specs=[VMEM] * (pieces + 1),
+    lax.fori_loop(0, total // (4 * KEY_ROWS), some_rows, 0)
+
+
+def document_marks(lengths, total):
+    return pl.pallas_call(
+        marks_kernel,
+        out_shape=jax.ShapeDtypeStruct((total, MARKS), jnp.bfloat16),
+        in_specs=[SMEM],
+        out_specs=VMEM,
         compiler_params=SMALL,
-    )(lengths, jnp.concatenate([left, right], axis=1))
-    return results[:pieces], results[pieces]
+    )(lengths)
 
 
 KEY_ROWS = 256
@@ -637,8 +632,8 @@
     kv_mine = jnp.stack(kv_pieces)
     far_rest = flipped(jnp.stack(kv_pieces[1:]), 0, 2)
     far = jnp.concatenate([far_own, far_rest])
-    qd, marks = prepare(lengths, queries, d_out, KVH, total)
-    qd = exchange(qd)
+    qd = exchange(split_heads(queries, d_out, KVH))
+    marks = document_marks(together((lengths, far))[0], total)
     near = flipped(kv_mine, 0, 1)
     kv = []
     for piece in (kv_mine, near, far, flipped(far, 0, 1)):

time: 76.9 us -> 77.4 us (level); the launches traced: 77.5 us -> 76.5 us
    concatenate x1 -> x2, other arithmetic: 1.04 us -> 2.17 us  [split_heads(): jnp.concatenate([left, right], axis=1)]
    concatenate x1 -> x0, other arithmetic: 1.12 us -> none  [prepare(): jnp.concatenate([left, right], axis=1)]
  transfers between devices with their start and end apart: 26 -> 26, of which waited for: 8 -> 9; matrix products, arithmetic and copies ran while one was open for 2% -> 2% of each run, Pallas kernels for 3% -> 3%
where the time goes in v8:
time: 77.4 us; the launch traced here: 76.5 us
  starting transfers between devices  32.6 us (42%)
  waiting for transfers between devices  28.5 us (37%)
  Pallas kernels  12 us (16%)
  other arithmetic  2.6 us (3%)
  between operations  0.78 us (1%)
    ppermute x26, starting transfers between devices, flipped(): return lax.ppermute(value, ('ctx', 'head'), pairs)  32.6 us
    ppermute x26, waiting for transfers between devices, flipped(): return lax.ppermute(value, ('ctx', 'head'), pairs)  28.5 us
    pallas_call x1, Pallas kernels, attention(): pl.pallas_call(functools.partial(attention_kernel, cores, heads, tok), ou...  9.17 us
    concatenate x2, other arithmetic, split_heads(): jnp.concatenate([left, right], axis=1)  2.17 us
    pallas_call x2, Pallas kernels, join_heads(): pl.pallas_call(functools.partial(join_heads_kernel, pieces, wide), out_sh...  1.81 us
  transfers between devices with their start and end apart: 26, of which 9 were waited for; matrix products, arithmetic and copies ran while one was open for 2% of the time, Pallas kernels for 3%

profile of v8, /device:TPU:0, one launch (start us, length us, event | category | flops | bytes accessed | tf_op | source)
XLA Modules:
  0.0 76.5 jit_solution(12016891378014257752)
XLA Ops:
  0.6 1.0 %pad_maximum_fusion.1.both_ref = bf16[128,1024]{1,0:T(8,128)(2,1)S(1)} fusion(bf16[128,512]{1,0:T(8,128)(2,1)} %param.7, bf16[128,512]{1,0:T(8,128)(2,1)} %param.6), kind=kLoop, calls=%fused_computation.6 | loop fusion | flops 524288 | bytes 524288 | tf_op jit(solution)/shard_map/concatenate | solution.py:333
  1.7 0.1 shard_map.84
  1.8 4.1 %collective-permute-start = (bf16[1,128,256]{2,1,0:T(8,128)(2,1)S(1)}, bf16[1,128,256]{2,1,0:T(8,128)(2,1)S(1)}, u32[]{:S(2)}, u32[]{:S(2)}) collective-permute-start(bf16[1,128,256]{2,1,0:T(8,128)(2,1)S(1)} %bitcast.47), channel_id=1, source_target_pairs={{0,2},{1,3},{2,0},{3,1},{4,6},{5,7},{6,4},{7,5},{8,10},{9,11},{10,... | collective-permute-start | bytes 196616 | tf_op jit(solution)/shard_map/ppermute | solution.py:302
  5.9 1.5 %collective-permute-start.1 = (bf16[128,256]{1,0:T(8,128)(2,1)S(1)}, bf16[128,256]{1,0:T(8,128)(2,1)S(1)}, u32[]{:S(2)}, u32[]{:S(2)}) collective-permute-start(bf16[128,256]{1,0:T(8,128)(2,1)S(1)} %get-tuple-element.36), channel_id=1, source_target_pairs={{0,8},{1,9},{2,10},{3,11},{4,12},{5,13},{6,14},{7,15},{8,0},{9,1},... | collective-permute-start | bytes 196616 | tf_op jit(solution)/shard_map/ppermute | solution.py:302
  7.4 1.5 %collective-permute-start.2 = (bf16[128,256]{1,0:T(8,128)(2,1)S(1)}, bf16[128,256]{1,0:T(8,128)(2,1)S(1)}, u32[]{:S(2)}, u32[]{:S(2)}) collective-permute-start(bf16[128,256]{1,0:T(8,128)(2,1)S(1)} %get-tuple-element.37), channel_id=1, source_target_pairs={{0,16},{1,17},{2,18},{3,19},{4,20},{5,21},{6,22},{7,23},{8,24},{9,... | collective-permute-start | bytes 196616 | tf_op jit(solution)/shard_map/ppermute | solution.py:302
  8.9 0.5 collective-permute-start.3
  9.4 1.1 %pad_maximum_fusion.both_ref = bf16[128,4096]{1,0:T(8,128)(2,1)S(1)} fusion(bf16[128,2048]{1,0:T(8,128)(2,1)S(1)} %copy-done.1, bf16[128,2048]{1,0:T(8,128)(2,1)} %param.5), kind=kLoop, calls=%fused_computation | loop fusion | flops 2097152 | bytes 2097152 | tf_op jit(solution)/shard_map/concatenate | solution.py:333
  10.5 0.0 copy-start
  10.5 0.1 shard_map.86
  10.6 1.6 %collective-permute-start.5 = (bf16[128,1024]{1,0:T(8,128)(2,1)S(1)}, bf16[128,1024]{1,0:T(8,128)(2,1)S(1)}, u32[]{:S(2)}, u32[]{:S(2)}) collective-permute-start(bf16[128,1024]{1,0:T(8,128)(2,1)S(1)} %get-tuple-element.41), channel_id=1, source_target_pairs={{0,8},{1,9},{2,10},{3,11},{4,12},{5,13},{6,14},{7,15},{8,0},{9,1},... | collective-permute-start | bytes 786440 | tf_op jit(solution)/shard_map/ppermute | solution.py:302
  12.2 1.5 %collective-permute-start.6 = (bf16[128,1024]{1,0:T(8,128)(2,1)S(1)}, bf16[128,1024]{1,0:T(8,128)(2,1)S(1)}, u32[]{:S(2)}, u32[]{:S(2)}) collective-permute-start(bf16[128,1024]{1,0:T(8,128)(2,1)S(1)} %get-tuple-element.42), channel_id=1, source_target_pairs={{0,16},{1,17},{2,18},{3,19},{4,20},{5,21},{6,22},{7,23},{8,24},{9,... | collective-permute-start | bytes 786440 | tf_op jit(solution)/shard_map/ppermute | solution.py:302
  13.7 1.0 %collective-permute-done.3 = bf16[128,256]{1,0:T(8,128)(2,1)S(1)} collective-permute-done((bf16[128,256]{1,0:T(8,128)(2,1)S(1)}, bf16[128,256]{1,0:T(8,128)(2,1)S(1)}, u32[]{:S(2)}, u32[]{:S(2)}) %collective-permute-start.3) | collective-permute-done | bytes 65568 | tf_op jit(solution)/shard_map/ppermute | solution.py:302
  14.7 0.4 collective-permute-start.4
  15.1 1.6 %collective-permute-start.9 = (bf16[4,128,256]{2,1,0:T(8,128)(2,1)S(1)}, bf16[4,128,256]{2,1,0:T(8,128)(2,1)S(1)}, u32[]{:S(2)}, u32[]{:S(2)}) collective-permute-start(bf16[4,128,256]{2,1,0:T(8,128)(2,1)S(1)} %pad_maximum_fusion.2.refs_6_), channel_id=1, source_target_pairs={{0,1},{1,0},{2,3},{3,2},{4,5},{5,4},{6,7},{7,6},{8,9},{9,8},{10,11... | collective-permute-start | bytes 786440 | tf_op jit(solution)/shard_map/ppermute | solution.py:302
  16.8 7.4 %collective-permute-done.4 = bf16[3,128,256]{2,1,0:T(8,128)(2,1)S(1)} collective-permute-done((bf16[3,128,256]{2,1,0:T(8,128)(2,1)S(1)}, bf16[3,128,256]{2,1,0:T(8,128)(2,1)S(1)}, u32[]{:S(2)}, u32[]{:S(2)}) %collective-permute-start.4) | collective-permute-done | bytes 196640 | tf_op jit(solution)/shard_map/ppermute | solution.py:302
  24.2 0.2 collective-permute-start.12
  24.4 1.0 %collective-permute-start.7 = (bf16[128,1024]{1,0:T(8,128)(2,1)S(1)}, bf16[128,1024]{1,0:T(8,128)(2,1)S(1)}, u32[]{:S(2)}, u32[]{:S(2)}) collective-permute-start(bf16[128,1024]{1,0:T(8,128)(2,1)S(1)} %get-tuple-element.43), channel_id=1, source_target_pairs={{0,24},{1,25},{2,26},{3,27},{4,28},{5,29},{6,30},{7,31},{8,16},{9,... | collective-permute-start | bytes 786440 | tf_op jit(solution)/shard_map/ppermute | solution.py:302
  25.4 0.0 collective-permute-done.5.refs_3_
  25.5 0.5 collective-permute-start.11
  26.0 0.0 collective-permute-done.9.refs_8_
  26.0 0.1 collective-permute-start.10
  26.0 4.6 %collective-permute-done.12.refs_12_ = bf16[4,128,256]{2,1,0:T(8,128)(2,1)S(1)} collective-permute-done((bf16[4,128,256]{2,1,0:T(8,128)(2,1)S(1)}, bf16[4,128,256]{2,1,0:T(8,128)(2,1)S(1)}, u32[]{:S(2)}, u32[]{:S(2)}) %collective-permute-start.12) | collective-permute-done | bytes 262176 | tf_op jit(solution)/shard_map/ppermute | solution.py:302
  30.7 0.8 %shard_map.85.refs_1_ = bf16[4096,128]{1,0:T(8,128)(2,1)S(1)} custom-call(s32[32]{0:T(128)S(1)} %copy-done), custom_call_target="tpu_custom_call" | custom-call | tf_op jit(solution)/shard_map/pallas_call | solution.py:367
  31.5 0.2 collective-permute-done.7.refs_5_
  31.7 0.0 collective-permute-done.8.refs_7_
  31.7 0.5 collective-permute-done.13.refs_13_
  32.2 9.2 %shard_map.87 = (bf16[128,1024]{1,0:T(8,128)(2,1)S(1)}, bf16[128,1024]{1,0:T(8,128)(2,1)S(1)}, bf16[128,1024]{1,0:T(8,128)(2,1)S(1)}, bf16[128,1024]{1,0:T(8,128...) custom-call(s32[32]{0:T(128)S(1)} %copy-done, ...), custom_call_target="tpu_custom_call" | custom-call | tf_op jit(solution)/shard_map/pallas_call | solution.py:586
  41.4 1.6 %collective-permute-start.14 = (bf16[4,4,128,256]{3,2,1,0:T(8,128)(2,1)S(1)}, bf16[4,4,128,256]{3,2,1,0:T(8,128)(2,1)S(1)}, u32[]{:S(2)}, u32[]{:S(2)}) collective-permute-start(bf16[4,4,128,256]{3,2,1,0:T(8,128)(2,1)S(1)} %get-tuple-element.46), channel_id=1, source_target_pairs={{0,4},{1,5},{2,6},{3,7},{4,0},{5,1},{6,2},{7,3},{8,12},{9,13},{10,... | collective-permute-start | bytes 3145736 | tf_op jit(solution)/shard_map/ppermute | solution.py:302
  43.0 1.2 %collective-permute-start.19 = (bf16[128,1024]{1,0:T(8,128)(2,1)S(1)}, bf16[128,1024]{1,0:T(8,128)(2,1)S(1)}, u32[]{:S(2)}, u32[]{:S(2)}) collective-permute-start(bf16[128,1024]{1,0:T(8,128)(2,1)S(1)} %get-tuple-element.49), channel_id=1, source_target_pairs={{0,8},{1,9},{2,10},{3,11},{4,12},{5,13},{6,14},{7,15},{8,0},{9,1},... | collective-permute-start | bytes 786440 | tf_op jit(solution)/shard_map/ppermute | solution.py:302
  44.1 0.7 collective-permute-start.20
  44.8 1.6 %collective-permute-start.21 = (bf16[128,1024]{1,0:T(8,128)(2,1)S(1)}, bf16[128,1024]{1,0:T(8,128)(2,1)S(1)}, u32[]{:S(2)}, u32[]{:S(2)}) collective-permute-start(bf16[128,1024]{1,0:T(8,128)(2,1)S(1)} %get-tuple-element.51), channel_id=1, source_target_pairs={{0,24},{1,25},{2,26},{3,27},{4,28},{5,29},{6,30},{7,31},{8,16},{9,... | collective-permute-start | bytes 786440 | tf_op jit(solution)/shard_map/ppermute | solution.py:302
  46.5 0.2 collective-permute-start.15
  46.7 0.1 fusion.1
  46.8 5.8 %collective-permute-done.15 = bf16[3,128,256]{2,1,0:T(8,128)(2,1)S(1)} collective-permute-done((bf16[3,128,256]{2,1,0:T(8,128)(2,1)S(1)}, bf16[3,128,256]{2,1,0:T(8,128)(2,1)S(1)}, u32[]{:S(2)}, u32[]{:S(2)}) %collective-permute-start.15) | collective-permute-done | bytes 196640 | tf_op jit(solution)/shard_map/ppermute | solution.py:302
  52.6 0.4 collective-permute-start.16
  53.0 0.1 fusion
  53.1 3.3 %collective-permute-start.18 = (bf16[3,128,256]{2,1,0:T(8,128)(2,1)S(1)}, bf16[3,128,256]{2,1,0:T(8,128)(2,1)S(1)}, u32[]{:S(2)}, u32[]{:S(2)}) collective-permute-start(bf16[3,128,256]{2,1,0:T(8,128)(2,1)S(1)} %fusion), channel_id=1, source_target_pairs={{0,2},{1,3},{2,0},{3,1},{4,6},{5,7},{6,4},{7,5},{8,10},{9,11},{10,... | collective-permute-start | bytes 589832 | tf_op jit(solution)/shard_map/ppermute | solution.py:302
  56.4 1.7 %collective-permute-start.17 = (bf16[128,256]{1,0:T(8,128)(2,1)S(1)}, bf16[128,256]{1,0:T(8,128)(2,1)S(1)}, u32[]{:S(2)}, u32[]{:S(2)}) collective-permute-start(bf16[128,256]{1,0:T(8,128)(2,1)S(1)} %fusion.9), channel_id=1, source_target_pairs={{0,1},{1,0},{2,3},{3,2},{4,5},{5,4},{6,7},{7,6},{8,9},{9,8},{10,11... | collective-permute-start | bytes 196616 | tf_op jit(solution)/shard_map/ppermute | solution.py:302
  58.1 6.6 %collective-permute-done.17 = bf16[128,256]{1,0:T(8,128)(2,1)S(1)} collective-permute-done((bf16[128,256]{1,0:T(8,128)(2,1)S(1)}, bf16[128,256]{1,0:T(8,128)(2,1)S(1)}, u32[]{:S(2)}, u32[]{:S(2)}) %collective-permute-start.17) | collective-permute-done | bytes 65568 | tf_op jit(solution)/shard_map/ppermute | solution.py:302
  64.8 0.1 fusion.3
  64.9 4.0 %collective-permute-start.22 = (bf16[128,256]{1,0:T(8,128)(2,1)S(1)}, bf16[128,256]{1,0:T(8,128)(2,1)S(1)}, u32[]{:S(2)}, u32[]{:S(2)}) collective-permute-start(bf16[128,256]{1,0:T(8,128)(2,1)S(1)} %get-tuple-element.60), channel_id=1, source_target_pairs={{0,2},{1,3},{2,0},{3,1},{4,6},{5,7},{6,4},{7,5},{8,10},{9,11},{10,... | collective-permute-start | bytes 196616 | tf_op jit(solution)/shard_map/ppermute | solution.py:302
  68.9 1.1 %collective-permute-start.23 = (bf16[128,256]{1,0:T(8,128)(2,1)S(1)}, bf16[128,256]{1,0:T(8,128)(2,1)S(1)}, u32[]{:S(2)}, u32[]{:S(2)}) collective-permute-start(bf16[128,256]{1,0:T(8,128)(2,1)S(1)} %get-tuple-element.61), channel_id=1, source_target_pairs={{0,8},{1,9},{2,10},{3,11},{4,12},{5,13},{6,14},{7,15},{8,0},{9,1},... | collective-permute-start | bytes 196616 | tf_op jit(solution)/shard_map/ppermute | solution.py:302
  70.0 0.6 collective-permute-start.24
  70.6 1.8 %collective-permute-start.25 = (bf16[128,256]{1,0:T(8,128)(2,1)S(1)}, bf16[128,256]{1,0:T(8,128)(2,1)S(1)}, u32[]{:S(2)}, u32[]{:S(2)}) collective-permute-start(bf16[128,256]{1,0:T(8,128)(2,1)S(1)} %get-tuple-element.63), channel_id=1, source_target_pairs={{0,24},{1,25},{2,26},{3,27},{4,28},{5,29},{6,30},{7,31},{8,16},{9,... | collective-permute-start | bytes 196616 | tf_op jit(solution)/shard_map/ppermute | solution.py:302
  72.4 1.1 %shard_map.88 = (bf16[128,2048]{1,0:T(8,128)(2,1)}, bf16[128,2048]{1,0:T(8,128)(2,1)}) custom-call(bf16[128,1024]{1,0:T(8,128)(2,1)S(1)} %get-tuple-element.44.refs_0_, bf16[128,1024]{1,0:T(8,128)(2,1)S(1)} %collective-permute-done.19.refs_1_, bf16[128,1024]{1,0:T(8,128)(2,1)S(1)} %collective-permute-done.20.refs_2_, ...), custom_call_target="tpu_custom_call" | custom-call | tf_op jit(solution)/shard_map/pallas_call | solution.py:339
  73.5 0.8 %collective-permute-done.24.refs_2_ = bf16[128,256]{1,0:T(8,128)(2,1)S(1)} collective-permute-done((bf16[128,256]{1,0:T(8,128)(2,1)S(1)}, bf16[128,256]{1,0:T(8,128)(2,1)S(1)}, u32[]{:S(2)}, u32[]{:S(2)}) %collective-permute-start.24) | collective-permute-done | bytes 65568 | tf_op jit(solution)/shard_map/ppermute | solution.py:302
  74.2 1.5 %collective-permute-done.25.refs_3_ = bf16[128,256]{1,0:T(8,128)(2,1)S(1)} collective-permute-done((bf16[128,256]{1,0:T(8,128)(2,1)S(1)}, bf16[128,256]{1,0:T(8,128)(2,1)S(1)}, u32[]{:S(2)}, u32[]{:S(2)}) %collective-permute-start.25) | collective-permute-done | bytes 65568 | tf_op jit(solution)/shard_map/ppermute | solution.py:302
  75.7 0.8 shard_map.89
  (26 shorter events, 0.2 us)
Async XLA Ops:
  0.6 8.8 %copy-start.1 = (bf16[128,2048]{1,0:T(8,128)(2,1)S(1)}, bf16[128,2048]{1,0:T(8,128)(2,1)}, u32[]{:S(2)}) copy-start(bf16[128,2048]{1,0:T(8,128)(2,1)} %param.8) | copy-start | bytes 1572868
  1.8 15.0 %collective-permute-start = (bf16[1,128,256]{2,1,0:T(8,128)(2,1)S(1)}, bf16[1,128,256]{2,1,0:T(8,128)(2,1)S(1)}, u32[]{:S(2)}, u32[]{:S(2)}) collective-permute-start(bf16[1,128,256]{2,1,0:T(8,128)(2,1)S(1)} %bitcast.47), channel_id=1, source_target_pairs={{0,2},{1,3},{2,0},{3,1},{4,6},{5,7},{6,4},{7,5},{8,10},{9,11},{10,... | collective-permute-start | bytes 196616 | tf_op jit(solution)/shard_map/ppermute | solution.py:302
  5.9 6.3 %collective-permute-start.1 = (bf16[128,256]{1,0:T(8,128)(2,1)S(1)}, bf16[128,256]{1,0:T(8,128)(2,1)S(1)}, u32[]{:S(2)}, u32[]{:S(2)}) collective-permute-start(bf16[128,256]{1,0:T(8,128)(2,1)S(1)} %get-tuple-element.36), channel_id=1, source_target_pairs={{0,8},{1,9},{2,10},{3,11},{4,12},{5,13},{6,14},{7,15},{8,0},{9,1},... | collective-permute-start | bytes 196616 | tf_op jit(solution)/shard_map/ppermute | solution.py:302
  7.4 6.3 %collective-permute-start.2 = (bf16[128,256]{1,0:T(8,128)(2,1)S(1)}, bf16[128,256]{1,0:T(8,128)(2,1)S(1)}, u32[]{:S(2)}, u32[]{:S(2)}) collective-permute-start(bf16[128,256]{1,0:T(8,128)(2,1)S(1)} %get-tuple-element.37), channel_id=1, source_target_pairs={{0,16},{1,17},{2,18},{3,19},{4,20},{5,21},{6,22},{7,23},{8,24},{9,... | collective-permute-start | bytes 196616 | tf_op jit(solution)/shard_map/ppermute | solution.py:302
  8.9 5.8 %collective-permute-start.3 = (bf16[128,256]{1,0:T(8,128)(2,1)S(1)}, bf16[128,256]{1,0:T(8,128)(2,1)S(1)}, u32[]{:S(2)}, u32[]{:S(2)}) collective-permute-start(bf16[128,256]{1,0:T(8,128)(2,1)S(1)} %get-tuple-element.38), channel_id=1, source_target_pairs={{0,24},{1,25},{2,26},{3,27},{4,28},{5,29},{6,30},{7,31},{8,16},{9,... | collective-permute-start | bytes 196616 | tf_op jit(solution)/shard_map/ppermute | solution.py:302
  10.5 20.2 %copy-start = (s32[32]{0:T(128)S(1)}, s32[32]{0:T(128)}, u32[]{:S(2)}) copy-start(s32[32]{0:T(128)} %refs_0_.1) | copy-start | bytes 388
  10.6 14.8 %collective-permute-start.5 = (bf16[128,1024]{1,0:T(8,128)(2,1)S(1)}, bf16[128,1024]{1,0:T(8,128)(2,1)S(1)}, u32[]{:S(2)}, u32[]{:S(2)}) collective-permute-start(bf16[128,1024]{1,0:T(8,128)(2,1)S(1)} %get-tuple-element.41), channel_id=1, source_target_pairs={{0,8},{1,9},{2,10},{3,11},{4,12},{5,13},{6,14},{7,15},{8,0},{9,1},... | collective-permute-start | bytes 786440 | tf_op jit(solution)/shard_map/ppermute | solution.py:302
  12.2 13.3 %collective-permute-start.6 = (bf16[128,1024]{1,0:T(8,128)(2,1)S(1)}, bf16[128,1024]{1,0:T(8,128)(2,1)S(1)}, u32[]{:S(2)}, u32[]{:S(2)}) collective-permute-start(bf16[128,1024]{1,0:T(8,128)(2,1)S(1)} %get-tuple-element.42), channel_id=1, source_target_pairs={{0,16},{1,17},{2,18},{3,19},{4,20},{5,21},{6,22},{7,23},{8,24},{9,... | collective-permute-start | bytes 786440 | tf_op jit(solution)/shard_map/ppermute | solution.py:302
  14.7 9.5 %collective-permute-start.4 = (bf16[3,128,256]{2,1,0:T(8,128)(2,1)S(1)}, bf16[3,128,256]{2,1,0:T(8,128)(2,1)S(1)}, u32[]{:S(2)}, u32[]{:S(2)}) collective-permute-start(bf16[3,128,256]{2,1,0:T(8,128)(2,1)S(1)} %pad_maximum_fusion.3), channel_id=1, source_target_pairs={{0,2},{1,3},{2,0},{3,1},{4,6},{5,7},{6,4},{7,5},{8,10},{9,11},{10,... | collective-permute-start | bytes 589832 | tf_op jit(solution)/shard_map/ppermute | solution.py:302
  15.1 10.8 %collective-permute-start.9 = (bf16[4,128,256]{2,1,0:T(8,128)(2,1)S(1)}, bf16[4,128,256]{2,1,0:T(8,128)(2,1)S(1)}, u32[]{:S(2)}, u32[]{:S(2)}) collective-permute-start(bf16[4,128,256]{2,1,0:T(8,128)(2,1)S(1)} %pad_maximum_fusion.2.refs_6_), channel_id=1, source_target_pairs={{0,1},{1,0},{2,3},{3,2},{4,5},{5,4},{6,7},{7,6},{8,9},{9,8},{10,11... | collective-permute-start | bytes 786440 | tf_op jit(solution)/shard_map/ppermute | solution.py:302
  24.2 6.4 %collective-permute-start.12 = (bf16[4,128,256]{2,1,0:T(8,128)(2,1)S(1)}, bf16[4,128,256]{2,1,0:T(8,128)(2,1)S(1)}, u32[]{:S(2)}, u32[]{:S(2)}) collective-permute-start(bf16[4,128,256]{2,1,0:T(8,128)(2,1)S(1)} %constant_dynamic-update-slice_fusion.refs_10_), channel_id=1, source_target_pairs={{0,1},{1,0},{2,3},{3,2},{4,5},{5,4},{6,7},{7,6},{8,9},{9,8},{10,11... | collective-permute-start | bytes 786440 | tf_op jit(solution)/shard_map/ppermute | solution.py:302
  24.4 7.3 %collective-permute-start.7 = (bf16[128,1024]{1,0:T(8,128)(2,1)S(1)}, bf16[128,1024]{1,0:T(8,128)(2,1)S(1)}, u32[]{:S(2)}, u32[]{:S(2)}) collective-permute-start(bf16[128,1024]{1,0:T(8,128)(2,1)S(1)} %get-tuple-element.43), channel_id=1, source_target_pairs={{0,24},{1,25},{2,26},{3,27},{4,28},{5,29},{6,30},{7,31},{8,16},{9,... | collective-permute-start | bytes 786440 | tf_op jit(solution)/shard_map/ppermute | solution.py:302
  25.4 6.3 %collective-permute-start.8 = (bf16[4,128,256]{2,1,0:T(8,128)(2,1)S(1)}, bf16[4,128,256]{2,1,0:T(8,128)(2,1)S(1)}, u32[]{:S(2)}, u32[]{:S(2)}) collective-permute-start(bf16[4,128,256]{2,1,0:T(8,128)(2,1)S(1)} %pad_maximum_fusion.2.refs_6_), channel_id=1, source_target_pairs={{0,4},{1,5},{2,6},{3,7},{4,0},{5,1},{6,2},{7,3},{8,12},{9,13},{10,... | collective-permute-start | bytes 786440 | tf_op jit(solution)/shard_map/ppermute | solution.py:302
  25.5 6.3 %collective-permute-start.11 = (bf16[4,128,256]{2,1,0:T(8,128)(2,1)S(1)}, bf16[4,128,256]{2,1,0:T(8,128)(2,1)S(1)}, u32[]{:S(2)}, u32[]{:S(2)}) collective-permute-start(bf16[4,128,256]{2,1,0:T(8,128)(2,1)S(1)} %constant_dynamic-update-slice_fusion.refs_10_), channel_id=1, source_target_pairs={{0,4},{1,5},{2,6},{3,7},{4,0},{5,1},{6,2},{7,3},{8,12},{9,13},{10,... | collective-permute-start | bytes 786440 | tf_op jit(solution)/shard_map/ppermute | solution.py:302
  26.0 5.7 %collective-permute-start.10 = (bf16[4,128,256]{2,1,0:T(8,128)(2,1)S(1)}, bf16[4,128,256]{2,1,0:T(8,128)(2,1)S(1)}, u32[]{:S(2)}, u32[]{:S(2)}) collective-permute-start(bf16[4,128,256]{2,1,0:T(8,128)(2,1)S(1)} %collective-permute-done.9.refs_8_), channel_id=1, source_target_pairs={{0,4},{1,5},{2,6},{3,7},{4,0},{5,1},{6,2},{7,3},{8,12},{9,13},{10,... | collective-permute-start | bytes 786440 | tf_op jit(solution)/shard_map/ppermute | solution.py:302
  30.7 1.5 %collective-permute-start.13 = (bf16[4,128,256]{2,1,0:T(8,128)(2,1)S(1)}, bf16[4,128,256]{2,1,0:T(8,128)(2,1)S(1)}, u32[]{:S(2)}, u32[]{:S(2)}) collective-permute-start(bf16[4,128,256]{2,1,0:T(8,128)(2,1)S(1)} %collective-permute-done.12.refs_12_), channel_id=1, source_target_pairs={{0,4},{1,5},{2,6},{3,7},{4,0},{5,1},{6,2},{7,3},{8,12},{9,13},{10,... | collective-permute-start | bytes 786440 | tf_op jit(solution)/shard_map/ppermute | solution.py:302
  41.4 5.1 %collective-permute-start.14 = (bf16[4,4,128,256]{3,2,1,0:T(8,128)(2,1)S(1)}, bf16[4,4,128,256]{3,2,1,0:T(8,128)(2,1)S(1)}, u32[]{:S(2)}, u32[]{:S(2)}) collective-permute-start(bf16[4,4,128,256]{3,2,1,0:T(8,128)(2,1)S(1)} %get-tuple-element.46), channel_id=1, source_target_pairs={{0,4},{1,5},{2,6},{3,7},{4,0},{5,1},{6,2},{7,3},{8,12},{9,13},{10,... | collective-permute-start | bytes 3145736 | tf_op jit(solution)/shard_map/ppermute | solution.py:302
  43.0 13.4 %collective-permute-start.19 = (bf16[128,1024]{1,0:T(8,128)(2,1)S(1)}, bf16[128,1024]{1,0:T(8,128)(2,1)S(1)}, u32[]{:S(2)}, u32[]{:S(2)}) collective-permute-start(bf16[128,1024]{1,0:T(8,128)(2,1)S(1)} %get-tuple-element.49), channel_id=1, source_target_pairs={{0,8},{1,9},{2,10},{3,11},{4,12},{5,13},{6,14},{7,15},{8,0},{9,1},... | collective-permute-start | bytes 786440 | tf_op jit(solution)/shard_map/ppermute | solution.py:302
  44.1 14.0 %collective-permute-start.20 = (bf16[128,1024]{1,0:T(8,128)(2,1)S(1)}, bf16[128,1024]{1,0:T(8,128)(2,1)S(1)}, u32[]{:S(2)}, u32[]{:S(2)}) collective-permute-start(bf16[128,1024]{1,0:T(8,128)(2,1)S(1)} %get-tuple-element.50), channel_id=1, source_target_pairs={{0,16},{1,17},{2,18},{3,19},{4,20},{5,21},{6,22},{7,23},{8,24},{9,... | collective-permute-start | bytes 786440 | tf_op jit(solution)/shard_map/ppermute | solution.py:302
  44.8 13.3 %collective-permute-start.21 = (bf16[128,1024]{1,0:T(8,128)(2,1)S(1)}, bf16[128,1024]{1,0:T(8,128)(2,1)S(1)}, u32[]{:S(2)}, u32[]{:S(2)}) collective-permute-start(bf16[128,1024]{1,0:T(8,128)(2,1)S(1)} %get-tuple-element.51), channel_id=1, source_target_pairs={{0,24},{1,25},{2,26},{3,27},{4,28},{5,29},{6,30},{7,31},{8,16},{9,... | collective-permute-start | bytes 786440 | tf_op jit(solution)/shard_map/ppermute | solution.py:302
  46.5 6.1 %collective-permute-start.15 = (bf16[3,128,256]{2,1,0:T(8,128)(2,1)S(1)}, bf16[3,128,256]{2,1,0:T(8,128)(2,1)S(1)}, u32[]{:S(2)}, u32[]{:S(2)}) collective-permute-start(bf16[3,128,256]{2,1,0:T(8,128)(2,1)S(1)} %fusion.2), channel_id=1, source_target_pairs={{0,1},{1,0},{2,3},{3,2},{4,5},{5,4},{6,7},{7,6},{8,9},{9,8},{10,11... | collective-permute-start | bytes 589832 | tf_op jit(solution)/shard_map/ppermute | solution.py:302
  52.6 12.2 %collective-permute-start.16 = (bf16[4,128,256]{2,1,0:T(8,128)(2,1)S(1)}, bf16[4,128,256]{2,1,0:T(8,128)(2,1)S(1)}, u32[]{:S(2)}, u32[]{:S(2)}) collective-permute-start(bf16[4,128,256]{2,1,0:T(8,128)(2,1)S(1)} %fusion.1), channel_id=1, source_target_pairs={{0,1},{1,0},{2,3},{3,2},{4,5},{5,4},{6,7},{7,6},{8,9},{9,8},{10,11... | collective-permute-start | bytes 786440 | tf_op jit(solution)/shard_map/ppermute | solution.py:302
  53.1 11.7 %collective-permute-start.18 = (bf16[3,128,256]{2,1,0:T(8,128)(2,1)S(1)}, bf16[3,128,256]{2,1,0:T(8,128)(2,1)S(1)}, u32[]{:S(2)}, u32[]{:S(2)}) collective-permute-start(bf16[3,128,256]{2,1,0:T(8,128)(2,1)S(1)} %fusion), channel_id=1, source_target_pairs={{0,2},{1,3},{2,0},{3,1},{4,6},{5,7},{6,4},{7,5},{8,10},{9,11},{10,... | collective-permute-start | bytes 589832 | tf_op jit(solution)/shard_map/ppermute | solution.py:302
  56.4 8.4 %collective-permute-start.17 = (bf16[128,256]{1,0:T(8,128)(2,1)S(1)}, bf16[128,256]{1,0:T(8,128)(2,1)S(1)}, u32[]{:S(2)}, u32[]{:S(2)}) collective-permute-start(bf16[128,256]{1,0:T(8,128)(2,1)S(1)} %fusion.9), channel_id=1, source_target_pairs={{0,1},{1,0},{2,3},{3,2},{4,5},{5,4},{6,7},{7,6},{8,9},{9,8},{10,11... | collective-permute-start | bytes 196616 | tf_op jit(solution)/shard_map/ppermute | solution.py:302
  64.9 8.5 %collective-permute-start.22 = (bf16[128,256]{1,0:T(8,128)(2,1)S(1)}, bf16[128,256]{1,0:T(8,128)(2,1)S(1)}, u32[]{:S(2)}, u32[]{:S(2)}) collective-permute-start(bf16[128,256]{1,0:T(8,128)(2,1)S(1)} %get-tuple-element.60), channel_id=1, source_target_pairs={{0,2},{1,3},{2,0},{3,1},{4,6},{5,7},{6,4},{7,5},{8,10},{9,11},{10,... | collective-permute-start | bytes 196616 | tf_op jit(solution)/shard_map/ppermute | solution.py:302
  68.9 4.6 %collective-permute-start.23 = (bf16[128,256]{1,0:T(8,128)(2,1)S(1)}, bf16[128,256]{1,0:T(8,128)(2,1)S(1)}, u32[]{:S(2)}, u32[]{:S(2)}) collective-permute-start(bf16[128,256]{1,0:T(8,128)(2,1)S(1)} %get-tuple-element.61), channel_id=1, source_target_pairs={{0,8},{1,9},{2,10},{3,11},{4,12},{5,13},{6,14},{7,15},{8,0},{9,1},... | collective-permute-start | bytes 196616 | tf_op jit(solution)/shard_map/ppermute | solution.py:302
  70.0 4.3 %collective-permute-start.24 = (bf16[128,256]{1,0:T(8,128)(2,1)S(1)}, bf16[128,256]{1,0:T(8,128)(2,1)S(1)}, u32[]{:S(2)}, u32[]{:S(2)}) collective-permute-start(bf16[128,256]{1,0:T(8,128)(2,1)S(1)} %get-tuple-element.62), channel_id=1, source_target_pairs={{0,16},{1,17},{2,18},{3,19},{4,20},{5,21},{6,22},{7,23},{8,24},{9,... | collective-permute-start | bytes 196616 | tf_op jit(solution)/shard_map/ppermute | solution.py:302
  70.6 5.2 %collective-permute-start.25 = (bf16[128,256]{1,0:T(8,128)(2,1)S(1)}, bf16[128,256]{1,0:T(8,128)(2,1)S(1)}, u32[]{:S(2)}, u32[]{:S(2)}) collective-permute-start(bf16[128,256]{1,0:T(8,128)(2,1)S(1)} %get-tuple-element.63), channel_id=1, source_target_pairs={{0,24},{1,25},{2,26},{3,27},{4,28},{5,29},{6,30},{7,31},{8,16},{9,... | collective-permute-start | bytes 196616 | tf_op jit(solution)/shard_map/ppermute | solution.py:302

commit v9 on v7

--- a/solution.py
+++ b/solution.py
@@ -357,12 +357,12 @@
         ends = jnp.where(lane == number, end, ends)
 
     def some_rows(step, _):
-        rows = pl.ds(pl.multiple_of(step * KEY_ROWS, KEY_ROWS), KEY_ROWS)
-        position = step * KEY_ROWS + lax.broadcasted_iota(jnp.int32, (KEY_ROWS, MARKS), 0)
-        marks_ref[rows, :] = jnp.where(position < ends, 1.0, 0.0).astype(jnp.bfloat16)
+        rows = pl.ds(pl.multiple_of(step * 4 * KEY_ROWS, KEY_ROWS), 4 * KEY_ROWS)
+        position = lax.broadcasted_iota(jnp.int32, (4 * KEY_ROWS, MARKS), 0)
+        marks_ref[rows, :] = jnp.where(position < ends - step * 4 * KEY_ROWS, 1.0, 0.0).astype(jnp.bfloat16)
         return 0
 
-    lax.fori_loop(0, total // KEY_ROWS, some_rows, 0)
+    lax.fori_loop(0, total // (4 * KEY_ROWS), some_rows, 0)
 
 
 def prepare(lengths, left, right, pieces, total):

time: 76.9 us -> 76.7 us (level)
  no operation moved by 1% of the time
where the time goes in v9:
time: 76.7 us; the launch traced here: 76.9 us
  starting transfers between devices  33.6 us (44%)
  waiting for transfers between devices  28 us (37%)
  Pallas kernels  12 us (16%)
  other arithmetic  2.59 us (3%)
  between operations  0.78 us (1%)
    ppermute x26, starting transfers between devices, flipped(): return lax.ppermute(value, ('ctx', 'head'), pairs)  33.6 us
    ppermute x26, waiting for transfers between devices, flipped(): return lax.ppermute(value, ('ctx', 'head'), pairs)  28 us
    pallas_call x1, Pallas kernels, attention(): pl.pallas_call(functools.partial(attention_kernel, cores, heads, tok), ou...  9.18 us
    pallas_call x2, Pallas kernels, join_heads(): pl.pallas_call(functools.partial(join_heads_kernel, pieces, wide), out_sh...  1.81 us
  transfers between devices with their start and end apart: 26, of which 8 were waited for; matrix products, arithmetic and copies ran while one was open for 2% of the time, Pallas kernels for 3%

profile of v9, /device:TPU:0, one launch (start us, length us, event | category | flops | bytes accessed | tf_op | source)
XLA Modules:
  0.0 76.9 jit_solution(10902568886490137102)
XLA Ops:
  0.6 1.0 %pad_maximum_fusion.1.both_ref = bf16[128,1024]{1,0:T(8,128)(2,1)S(1)} fusion(bf16[128,512]{1,0:T(8,128)(2,1)} %param.7, bf16[128,512]{1,0:T(8,128)(2,1)} %param.6), kind=kLoop, calls=%fused_computation.6 | loop fusion | flops 524288 | bytes 524288 | tf_op jit(solution)/shard_map/concatenate | solution.py:333
  1.7 0.1 shard_map.85
  1.8 4.1 %collective-permute-start.9 = (bf16[1,128,256]{2,1,0:T(8,128)(2,1)S(1)}, bf16[1,128,256]{2,1,0:T(8,128)(2,1)S(1)}, u32[]{:S(2)}, u32[]{:S(2)}) collective-permute-start(bf16[1,128,256]{2,1,0:T(8,128)(2,1)S(1)} %bitcast.47), channel_id=1, source_target_pairs={{0,2},{1,3},{2,0},{3,1},{4,6},{5,7},{6,4},{7,5},{8,10},{9,11},{10,... | collective-permute-start | bytes 196616 | tf_op jit(solution)/shard_map/ppermute | solution.py:302
  5.9 1.5 %collective-permute-start.3 = (bf16[128,256]{1,0:T(8,128)(2,1)S(1)}, bf16[128,256]{1,0:T(8,128)(2,1)S(1)}, u32[]{:S(2)}, u32[]{:S(2)}) collective-permute-start(bf16[128,256]{1,0:T(8,128)(2,1)S(1)} %get-tuple-element.41), channel_id=1, source_target_pairs={{0,8},{1,9},{2,10},{3,11},{4,12},{5,13},{6,14},{7,15},{8,0},{9,1},... | collective-permute-start | bytes 196616 | tf_op jit(solution)/shard_map/ppermute | solution.py:302
  7.4 1.5 %collective-permute-start.4 = (bf16[128,256]{1,0:T(8,128)(2,1)S(1)}, bf16[128,256]{1,0:T(8,128)(2,1)S(1)}, u32[]{:S(2)}, u32[]{:S(2)}) collective-permute-start(bf16[128,256]{1,0:T(8,128)(2,1)S(1)} %get-tuple-element.42), channel_id=1, source_target_pairs={{0,16},{1,17},{2,18},{3,19},{4,20},{5,21},{6,22},{7,23},{8,24},{9,... | collective-permute-start | bytes 196616 | tf_op jit(solution)/shard_map/ppermute | solution.py:302
  8.9 0.5 collective-permute-start.5
  9.4 1.1 %pad_maximum_fusion.both_ref = bf16[128,4096]{1,0:T(8,128)(2,1)S(1)} fusion(bf16[128,2048]{1,0:T(8,128)(2,1)S(1)} %copy-done.1, bf16[128,2048]{1,0:T(8,128)(2,1)} %param.5), kind=kLoop, calls=%fused_computation | loop fusion | flops 2097152 | bytes 2097152 | tf_op jit(solution)/shard_map/concatenate | solution.py:377
  10.5 0.9 %shard_map.84 = (bf16[128,1024]{1,0:T(8,128)(2,1)S(1)}, bf16[128,1024]{1,0:T(8,128)(2,1)S(1)}, bf16[128,1024]{1,0:T(8,128)(2,1)S(1)}, bf16[128,1024]{1,0:T(8,128)(2,1)S(1)}, bf16[4096,128]{1,0:T(8,128)(2,1)S(1)}) custom-call(s32[32]{0:T(128)S(1)} %copy-done, bf16[128,4096]{1,0:T(8,128)(2,1)S(1)} %pad_maximum_fusion.both_ref), custom_call_target="tpu_custom_call" | custom-call | tf_op jit(solution)/shard_map/pallas_call | solution.py:370
  11.4 1.6 %collective-permute-start = (bf16[128,1024]{1,0:T(8,128)(2,1)S(1)}, bf16[128,1024]{1,0:T(8,128)(2,1)S(1)}, u32[]{:S(2)}, u32[]{:S(2)}) collective-permute-start(bf16[128,1024]{1,0:T(8,128)(2,1)S(1)} %get-tuple-element.37), channel_id=1, source_target_pairs={{0,8},{1,9},{2,10},{3,11},{4,12},{5,13},{6,14},{7,15},{8,0},{9,1},... | collective-permute-start | bytes 786440 | tf_op jit(solution)/shard_map/ppermute | solution.py:302
  13.0 1.5 %collective-permute-start.1 = (bf16[128,1024]{1,0:T(8,128)(2,1)S(1)}, bf16[128,1024]{1,0:T(8,128)(2,1)S(1)}, u32[]{:S(2)}, u32[]{:S(2)}) collective-permute-start(bf16[128,1024]{1,0:T(8,128)(2,1)S(1)} %get-tuple-element.38), channel_id=1, source_target_pairs={{0,16},{1,17},{2,18},{3,19},{4,20},{5,21},{6,22},{7,23},{8,24},{9,... | collective-permute-start | bytes 786440 | tf_op jit(solution)/shard_map/ppermute | solution.py:302
  14.5 0.0 collective-permute-done.4
  14.5 0.0 collective-permute-done.5
  14.5 0.4 collective-permute-start.10
  15.0 1.6 %collective-permute-start.7 = (bf16[4,128,256]{2,1,0:T(8,128)(2,1)S(1)}, bf16[4,128,256]{2,1,0:T(8,128)(2,1)S(1)}, u32[]{:S(2)}, u32[]{:S(2)}) collective-permute-start(bf16[4,128,256]{2,1,0:T(8,128)(2,1)S(1)} %pad_maximum_fusion.2.refs_6_), channel_id=1, source_target_pairs={{0,1},{1,0},{2,3},{3,2},{4,5},{5,4},{6,7},{7,6},{8,9},{9,8},{10,11... | collective-permute-start | bytes 786440 | tf_op jit(solution)/shard_map/ppermute | solution.py:302
  16.6 8.1 %collective-permute-done.10 = bf16[3,128,256]{2,1,0:T(8,128)(2,1)S(1)} collective-permute-done((bf16[3,128,256]{2,1,0:T(8,128)(2,1)S(1)}, bf16[3,128,256]{2,1,0:T(8,128)(2,1)S(1)}, u32[]{:S(2)}, u32[]{:S(2)}) %collective-permute-start.10) | collective-permute-done | bytes 196640 | tf_op jit(solution)/shard_map/ppermute | solution.py:302
  24.8 0.3 collective-permute-start.12
  25.1 0.4 collective-permute-start.2
  25.5 0.0 collective-permute-done.refs_3_
  25.5 0.5 collective-permute-start.11
  26.0 0.0 collective-permute-done.7.refs_8_
  26.0 0.1 collective-permute-start.8
  26.1 5.2 %collective-permute-done.12.refs_12_ = bf16[4,128,256]{2,1,0:T(8,128)(2,1)S(1)} collective-permute-done((bf16[4,128,256]{2,1,0:T(8,128)(2,1)S(1)}, bf16[4,128,256]{2,1,0:T(8,128)(2,1)S(1)}, u32[]{:S(2)}, u32[]{:S(2)}) %collective-permute-start.12) | collective-permute-done | bytes 262176 | tf_op jit(solution)/shard_map/ppermute | solution.py:302
  31.2 1.1 %collective-permute-done.2.refs_5_ = bf16[128,1024]{1,0:T(8,128)(2,1)S(1)} collective-permute-done((bf16[128,1024]{1,0:T(8,128)(2,1)S(1)}, bf16[128,1024]{1,0:T(8,128)(2,1)S(1)}, u32[]{:S(2)}, u32[]{:S(2)}) %collective-permute-start.2) | collective-permute-done | bytes 262176 | tf_op jit(solution)/shard_map/ppermute | solution.py:302
  32.3 0.0 collective-permute-done.6.refs_7_
  32.3 0.0 collective-permute-done.11.refs_11_
  32.4 0.4 collective-permute-done.13.refs_13_
  32.8 9.2 %shard_map.86 = (bf16[128,1024]{1,0:T(8,128)(2,1)S(1)}, bf16[128,1024]{1,0:T(8,128)(2,1)S(1)}, bf16[128,1024]{1,0:T(8,128)(2,1)S(1)}, bf16[128,1024]{1,0:T(8,128...) custom-call(s32[32]{0:T(128)S(1)} %copy-done, ...), custom_call_target="tpu_custom_call" | custom-call | tf_op jit(solution)/shard_map/pallas_call | solution.py:591
  41.9 0.1 collective-permute-start.14
  42.0 0.6 collective-permute-start.19
  42.6 0.6 collective-permute-start.20
  43.2 2.4 %collective-permute-start.21 = (bf16[128,1024]{1,0:T(8,128)(2,1)S(1)}, bf16[128,1024]{1,0:T(8,128)(2,1)S(1)}, u32[]{:S(2)}, u32[]{:S(2)}) collective-permute-start(bf16[128,1024]{1,0:T(8,128)(2,1)S(1)} %get-tuple-element.51), channel_id=1, source_target_pairs={{0,24},{1,25},{2,26},{3,27},{4,28},{5,29},{6,30},{7,31},{8,16},{9,... | collective-permute-start | bytes 786440 | tf_op jit(solution)/shard_map/ppermute | solution.py:302
  45.6 2.8 %collective-permute-start.15 = (bf16[3,128,256]{2,1,0:T(8,128)(2,1)S(1)}, bf16[3,128,256]{2,1,0:T(8,128)(2,1)S(1)}, u32[]{:S(2)}, u32[]{:S(2)}) collective-permute-start(bf16[3,128,256]{2,1,0:T(8,128)(2,1)S(1)} %fusion.2), channel_id=1, source_target_pairs={{0,1},{1,0},{2,3},{3,2},{4,5},{5,4},{6,7},{7,6},{8,9},{9,8},{10,11... | collective-permute-start | bytes 589832 | tf_op jit(solution)/shard_map/ppermute | solution.py:302
  48.5 0.1 fusion.1
  48.6 4.6 %collective-permute-done.15 = bf16[3,128,256]{2,1,0:T(8,128)(2,1)S(1)} collective-permute-done((bf16[3,128,256]{2,1,0:T(8,128)(2,1)S(1)}, bf16[3,128,256]{2,1,0:T(8,128)(2,1)S(1)}, u32[]{:S(2)}, u32[]{:S(2)}) %collective-permute-start.15) | collective-permute-done | bytes 196640 | tf_op jit(solution)/shard_map/ppermute | solution.py:302
  53.1 1.7 %collective-permute-start.16 = (bf16[4,128,256]{2,1,0:T(8,128)(2,1)S(1)}, bf16[4,128,256]{2,1,0:T(8,128)(2,1)S(1)}, u32[]{:S(2)}, u32[]{:S(2)}) collective-permute-start(bf16[4,128,256]{2,1,0:T(8,128)(2,1)S(1)} %fusion.1), channel_id=1, source_target_pairs={{0,1},{1,0},{2,3},{3,2},{4,5},{5,4},{6,7},{7,6},{8,9},{9,8},{10,11... | collective-permute-start | bytes 786440 | tf_op jit(solution)/shard_map/ppermute | solution.py:302
  54.9 0.1 fusion
  55.0 3.8 %collective-permute-start.18 = (bf16[3,128,256]{2,1,0:T(8,128)(2,1)S(1)}, bf16[3,128,256]{2,1,0:T(8,128)(2,1)S(1)}, u32[]{:S(2)}, u32[]{:S(2)}) collective-permute-start(bf16[3,128,256]{2,1,0:T(8,128)(2,1)S(1)} %fusion), channel_id=1, source_target_pairs={{0,2},{1,3},{2,0},{3,1},{4,6},{5,7},{6,4},{7,5},{8,10},{9,11},{10,... | collective-permute-start | bytes 589832 | tf_op jit(solution)/shard_map/ppermute | solution.py:302
  58.8 0.3 collective-permute-start.17
  59.1 6.9 %collective-permute-done.17 = bf16[128,256]{1,0:T(8,128)(2,1)S(1)} collective-permute-done((bf16[128,256]{1,0:T(8,128)(2,1)S(1)}, bf16[128,256]{1,0:T(8,128)(2,1)S(1)}, u32[]{:S(2)}, u32[]{:S(2)}) %collective-permute-start.17) | collective-permute-done | bytes 65568 | tf_op jit(solution)/shard_map/ppermute | solution.py:302
  66.0 0.1 fusion.3
  66.1 3.8 %collective-permute-start.22 = (bf16[128,256]{1,0:T(8,128)(2,1)S(1)}, bf16[128,256]{1,0:T(8,128)(2,1)S(1)}, u32[]{:S(2)}, u32[]{:S(2)}) collective-permute-start(bf16[128,256]{1,0:T(8,128)(2,1)S(1)} %get-tuple-element.60), channel_id=1, source_target_pairs={{0,2},{1,3},{2,0},{3,1},{4,6},{5,7},{6,4},{7,5},{8,10},{9,11},{10,... | collective-permute-start | bytes 196616 | tf_op jit(solution)/shard_map/ppermute | solution.py:302
  69.9 0.5 collective-permute-start.23
  70.5 0.5 collective-permute-start.24
  71.0 2.4 %collective-permute-start.25 = (bf16[128,256]{1,0:T(8,128)(2,1)S(1)}, bf16[128,256]{1,0:T(8,128)(2,1)S(1)}, u32[]{:S(2)}, u32[]{:S(2)}) collective-permute-start(bf16[128,256]{1,0:T(8,128)(2,1)S(1)} %get-tuple-element.63), channel_id=1, source_target_pairs={{0,24},{1,25},{2,26},{3,27},{4,28},{5,29},{6,30},{7,31},{8,16},{9,... | collective-permute-start | bytes 196616 | tf_op jit(solution)/shard_map/ppermute | solution.py:302
  73.4 1.1 %shard_map.87 = (bf16[128,2048]{1,0:T(8,128)(2,1)}, bf16[128,2048]{1,0:T(8,128)(2,1)}) custom-call(bf16[128,1024]{1,0:T(8,128)(2,1)S(1)} %get-tuple-element.44.refs_0_, bf16[128,1024]{1,0:T(8,128)(2,1)S(1)} %collective-permute-done.19.refs_1_, bf16[128,1024]{1,0:T(8,128)(2,1)S(1)} %collective-permute-done.20.refs_2_, ...), custom_call_target="tpu_custom_call" | custom-call | tf_op jit(solution)/shard_map/pallas_call | solution.py:339
  74.5 0.2 collective-permute-done.24.refs_2_
  74.7 1.4 %collective-permute-done.25.refs_3_ = bf16[128,256]{1,0:T(8,128)(2,1)S(1)} collective-permute-done((bf16[128,256]{1,0:T(8,128)(2,1)S(1)}, bf16[128,256]{1,0:T(8,128)(2,1)S(1)}, u32[]{:S(2)}, u32[]{:S(2)}) %collective-permute-start.25) | collective-permute-done | bytes 65568 | tf_op jit(solution)/shard_map/ppermute | solution.py:302
  76.2 0.8 shard_map.88
  (25 shorter events, 0.2 us)
Async XLA Ops:
  0.6 8.8 %copy-start.1 = (bf16[128,2048]{1,0:T(8,128)(2,1)S(1)}, bf16[128,2048]{1,0:T(8,128)(2,1)}, u32[]{:S(2)}) copy-start(bf16[128,2048]{1,0:T(8,128)(2,1)} %param.8) | copy-start | bytes 1572868
  1.8 14.8 %collective-permute-start.9 = (bf16[1,128,256]{2,1,0:T(8,128)(2,1)S(1)}, bf16[1,128,256]{2,1,0:T(8,128)(2,1)S(1)}, u32[]{:S(2)}, u32[]{:S(2)}) collective-permute-start(bf16[1,128,256]{2,1,0:T(8,128)(2,1)S(1)} %bitcast.47), channel_id=1, source_target_pairs={{0,2},{1,3},{2,0},{3,1},{4,6},{5,7},{6,4},{7,5},{8,10},{9,11},{10,... | collective-permute-start | bytes 196616 | tf_op jit(solution)/shard_map/ppermute | solution.py:302
  5.9 7.1 %collective-permute-start.3 = (bf16[128,256]{1,0:T(8,128)(2,1)S(1)}, bf16[128,256]{1,0:T(8,128)(2,1)S(1)}, u32[]{:S(2)}, u32[]{:S(2)}) collective-permute-start(bf16[128,256]{1,0:T(8,128)(2,1)S(1)} %get-tuple-element.41), channel_id=1, source_target_pairs={{0,8},{1,9},{2,10},{3,11},{4,12},{5,13},{6,14},{7,15},{8,0},{9,1},... | collective-permute-start | bytes 196616 | tf_op jit(solution)/shard_map/ppermute | solution.py:302
  7.4 7.1 %collective-permute-start.4 = (bf16[128,256]{1,0:T(8,128)(2,1)S(1)}, bf16[128,256]{1,0:T(8,128)(2,1)S(1)}, u32[]{:S(2)}, u32[]{:S(2)}) collective-permute-start(bf16[128,256]{1,0:T(8,128)(2,1)S(1)} %get-tuple-element.42), channel_id=1, source_target_pairs={{0,16},{1,17},{2,18},{3,19},{4,20},{5,21},{6,22},{7,23},{8,24},{9,... | collective-permute-start | bytes 196616 | tf_op jit(solution)/shard_map/ppermute | solution.py:302
  8.9 1.6 %copy-start = (s32[32]{0:T(128)S(1)}, s32[32]{0:T(128)}, u32[]{:S(2)}) copy-start(s32[32]{0:T(128)} %refs_0_.1) | copy-start | bytes 388
  8.9 5.6 %collective-permute-start.5 = (bf16[128,256]{1,0:T(8,128)(2,1)S(1)}, bf16[128,256]{1,0:T(8,128)(2,1)S(1)}, u32[]{:S(2)}, u32[]{:S(2)}) collective-permute-start(bf16[128,256]{1,0:T(8,128)(2,1)S(1)} %get-tuple-element.43), channel_id=1, source_target_pairs={{0,24},{1,25},{2,26},{3,27},{4,28},{5,29},{6,30},{7,31},{8,16},{9,... | collective-permute-start | bytes 196616 | tf_op jit(solution)/shard_map/ppermute | solution.py:302
  11.4 14.1 %collective-permute-start = (bf16[128,1024]{1,0:T(8,128)(2,1)S(1)}, bf16[128,1024]{1,0:T(8,128)(2,1)S(1)}, u32[]{:S(2)}, u32[]{:S(2)}) collective-permute-start(bf16[128,1024]{1,0:T(8,128)(2,1)S(1)} %get-tuple-element.37), channel_id=1, source_target_pairs={{0,8},{1,9},{2,10},{3,11},{4,12},{5,13},{6,14},{7,15},{8,0},{9,1},... | collective-permute-start | bytes 786440 | tf_op jit(solution)/shard_map/ppermute | solution.py:302
  13.0 12.5 %collective-permute-start.1 = (bf16[128,1024]{1,0:T(8,128)(2,1)S(1)}, bf16[128,1024]{1,0:T(8,128)(2,1)S(1)}, u32[]{:S(2)}, u32[]{:S(2)}) collective-permute-start(bf16[128,1024]{1,0:T(8,128)(2,1)S(1)} %get-tuple-element.38), channel_id=1, source_target_pairs={{0,16},{1,17},{2,18},{3,19},{4,20},{5,21},{6,22},{7,23},{8,24},{9,... | collective-permute-start | bytes 786440 | tf_op jit(solution)/shard_map/ppermute | solution.py:302
  14.5 10.2 %collective-permute-start.10 = (bf16[3,128,256]{2,1,0:T(8,128)(2,1)S(1)}, bf16[3,128,256]{2,1,0:T(8,128)(2,1)S(1)}, u32[]{:S(2)}, u32[]{:S(2)}) collective-permute-start(bf16[3,128,256]{2,1,0:T(8,128)(2,1)S(1)} %pad_maximum_fusion.3), channel_id=1, source_target_pairs={{0,2},{1,3},{2,0},{3,1},{4,6},{5,7},{6,4},{7,5},{8,10},{9,11},{10,... | collective-permute-start | bytes 589832 | tf_op jit(solution)/shard_map/ppermute | solution.py:302
  15.0 11.0 %collective-permute-start.7 = (bf16[4,128,256]{2,1,0:T(8,128)(2,1)S(1)}, bf16[4,128,256]{2,1,0:T(8,128)(2,1)S(1)}, u32[]{:S(2)}, u32[]{:S(2)}) collective-permute-start(bf16[4,128,256]{2,1,0:T(8,128)(2,1)S(1)} %pad_maximum_fusion.2.refs_6_), channel_id=1, source_target_pairs={{0,1},{1,0},{2,3},{3,2},{4,5},{5,4},{6,7},{7,6},{8,9},{9,8},{10,11... | collective-permute-start | bytes 786440 | tf_op jit(solution)/shard_map/ppermute | solution.py:302
  24.8 6.5 %collective-permute-start.12 = (bf16[4,128,256]{2,1,0:T(8,128)(2,1)S(1)}, bf16[4,128,256]{2,1,0:T(8,128)(2,1)S(1)}, u32[]{:S(2)}, u32[]{:S(2)}) collective-permute-start(bf16[4,128,256]{2,1,0:T(8,128)(2,1)S(1)} %constant_dynamic-update-slice_fusion.refs_10_), channel_id=1, source_target_pairs={{0,1},{1,0},{2,3},{3,2},{4,5},{5,4},{6,7},{7,6},{8,9},{9,8},{10,11... | collective-permute-start | bytes 786440 | tf_op jit(solution)/shard_map/ppermute | solution.py:302
  25.1 7.3 %collective-permute-start.2 = (bf16[128,1024]{1,0:T(8,128)(2,1)S(1)}, bf16[128,1024]{1,0:T(8,128)(2,1)S(1)}, u32[]{:S(2)}, u32[]{:S(2)}) collective-permute-start(bf16[128,1024]{1,0:T(8,128)(2,1)S(1)} %get-tuple-element.39), channel_id=1, source_target_pairs={{0,24},{1,25},{2,26},{3,27},{4,28},{5,29},{6,30},{7,31},{8,16},{9,... | collective-permute-start | bytes 786440 | tf_op jit(solution)/shard_map/ppermute | solution.py:302
  25.5 6.9 %collective-permute-start.6 = (bf16[4,128,256]{2,1,0:T(8,128)(2,1)S(1)}, bf16[4,128,256]{2,1,0:T(8,128)(2,1)S(1)}, u32[]{:S(2)}, u32[]{:S(2)}) collective-permute-start(bf16[4,128,256]{2,1,0:T(8,128)(2,1)S(1)} %pad_maximum_fusion.2.refs_6_), channel_id=1, source_target_pairs={{0,4},{1,5},{2,6},{3,7},{4,0},{5,1},{6,2},{7,3},{8,12},{9,13},{10,... | collective-permute-start | bytes 786440 | tf_op jit(solution)/shard_map/ppermute | solution.py:302
  25.5 6.9 %collective-permute-start.11 = (bf16[4,128,256]{2,1,0:T(8,128)(2,1)S(1)}, bf16[4,128,256]{2,1,0:T(8,128)(2,1)S(1)}, u32[]{:S(2)}, u32[]{:S(2)}) collective-permute-start(bf16[4,128,256]{2,1,0:T(8,128)(2,1)S(1)} %constant_dynamic-update-slice_fusion.refs_10_), channel_id=1, source_target_pairs={{0,4},{1,5},{2,6},{3,7},{4,0},{5,1},{6,2},{7,3},{8,12},{9,13},{10,... | collective-permute-start | bytes 786440 | tf_op jit(solution)/shard_map/ppermute | solution.py:302
  26.0 6.4 %collective-permute-start.8 = (bf16[4,128,256]{2,1,0:T(8,128)(2,1)S(1)}, bf16[4,128,256]{2,1,0:T(8,128)(2,1)S(1)}, u32[]{:S(2)}, u32[]{:S(2)}) collective-permute-start(bf16[4,128,256]{2,1,0:T(8,128)(2,1)S(1)} %collective-permute-done.7.refs_8_), channel_id=1, source_target_pairs={{0,4},{1,5},{2,6},{3,7},{4,0},{5,1},{6,2},{7,3},{8,12},{9,13},{10,... | collective-permute-start | bytes 786440 | tf_op jit(solution)/shard_map/ppermute | solution.py:302
  31.2 1.5 %collective-permute-start.13 = (bf16[4,128,256]{2,1,0:T(8,128)(2,1)S(1)}, bf16[4,128,256]{2,1,0:T(8,128)(2,1)S(1)}, u32[]{:S(2)}, u32[]{:S(2)}) collective-permute-start(bf16[4,128,256]{2,1,0:T(8,128)(2,1)S(1)} %collective-permute-done.12.refs_12_), channel_id=1, source_target_pairs={{0,4},{1,5},{2,6},{3,7},{4,0},{5,1},{6,2},{7,3},{8,12},{9,13},{10,... | collective-permute-start | bytes 786440 | tf_op jit(solution)/shard_map/ppermute | solution.py:302
  41.9 3.6 %collective-permute-start.14 = (bf16[4,4,128,256]{3,2,1,0:T(8,128)(2,1)S(1)}, bf16[4,4,128,256]{3,2,1,0:T(8,128)(2,1)S(1)}, u32[]{:S(2)}, u32[]{:S(2)}) collective-permute-start(bf16[4,4,128,256]{3,2,1,0:T(8,128)(2,1)S(1)} %get-tuple-element.46), channel_id=1, source_target_pairs={{0,4},{1,5},{2,6},{3,7},{4,0},{5,1},{6,2},{7,3},{8,12},{9,13},{10,... | collective-permute-start | bytes 3145736 | tf_op jit(solution)/shard_map/ppermute | solution.py:302
  42.0 16.8 %collective-permute-start.19 = (bf16[128,1024]{1,0:T(8,128)(2,1)S(1)}, bf16[128,1024]{1,0:T(8,128)(2,1)S(1)}, u32[]{:S(2)}, u32[]{:S(2)}) collective-permute-start(bf16[128,1024]{1,0:T(8,128)(2,1)S(1)} %get-tuple-element.49), channel_id=1, source_target_pairs={{0,8},{1,9},{2,10},{3,11},{4,12},{5,13},{6,14},{7,15},{8,0},{9,1},... | collective-permute-start | bytes 786440 | tf_op jit(solution)/shard_map/ppermute | solution.py:302
  42.6 16.5 %collective-permute-start.20 = (bf16[128,1024]{1,0:T(8,128)(2,1)S(1)}, bf16[128,1024]{1,0:T(8,128)(2,1)S(1)}, u32[]{:S(2)}, u32[]{:S(2)}) collective-permute-start(bf16[128,1024]{1,0:T(8,128)(2,1)S(1)} %get-tuple-element.50), channel_id=1, source_target_pairs={{0,16},{1,17},{2,18},{3,19},{4,20},{5,21},{6,22},{7,23},{8,24},{9,... | collective-permute-start | bytes 786440 | tf_op jit(solution)/shard_map/ppermute | solution.py:302
  43.2 15.9 %collective-permute-start.21 = (bf16[128,1024]{1,0:T(8,128)(2,1)S(1)}, bf16[128,1024]{1,0:T(8,128)(2,1)S(1)}, u32[]{:S(2)}, u32[]{:S(2)}) collective-permute-start(bf16[128,1024]{1,0:T(8,128)(2,1)S(1)} %get-tuple-element.51), channel_id=1, source_target_pairs={{0,24},{1,25},{2,26},{3,27},{4,28},{5,29},{6,30},{7,31},{8,16},{9,... | collective-permute-start | bytes 786440 | tf_op jit(solution)/shard_map/ppermute | solution.py:302
  45.6 7.5 %collective-permute-start.15 = (bf16[3,128,256]{2,1,0:T(8,128)(2,1)S(1)}, bf16[3,128,256]{2,1,0:T(8,128)(2,1)S(1)}, u32[]{:S(2)}, u32[]{:S(2)}) collective-permute-start(bf16[3,128,256]{2,1,0:T(8,128)(2,1)S(1)} %fusion.2), channel_id=1, source_target_pairs={{0,1},{1,0},{2,3},{3,2},{4,5},{5,4},{6,7},{7,6},{8,9},{9,8},{10,11... | collective-permute-start | bytes 589832 | tf_op jit(solution)/shard_map/ppermute | solution.py:302
  53.1 12.9 %collective-permute-start.16 = (bf16[4,128,256]{2,1,0:T(8,128)(2,1)S(1)}, bf16[4,128,256]{2,1,0:T(8,128)(2,1)S(1)}, u32[]{:S(2)}, u32[]{:S(2)}) collective-permute-start(bf16[4,128,256]{2,1,0:T(8,128)(2,1)S(1)} %fusion.1), channel_id=1, source_target_pairs={{0,1},{1,0},{2,3},{3,2},{4,5},{5,4},{6,7},{7,6},{8,9},{9,8},{10,11... | collective-permute-start | bytes 786440 | tf_op jit(solution)/shard_map/ppermute | solution.py:302
  55.0 11.0 %collective-permute-start.18 = (bf16[3,128,256]{2,1,0:T(8,128)(2,1)S(1)}, bf16[3,128,256]{2,1,0:T(8,128)(2,1)S(1)}, u32[]{:S(2)}, u32[]{:S(2)}) collective-permute-start(bf16[3,128,256]{2,1,0:T(8,128)(2,1)S(1)} %fusion), channel_id=1, source_target_pairs={{0,2},{1,3},{2,0},{3,1},{4,6},{5,7},{6,4},{7,5},{8,10},{9,11},{10,... | collective-permute-start | bytes 589832 | tf_op jit(solution)/shard_map/ppermute | solution.py:302
  58.8 7.2 %collective-permute-start.17 = (bf16[128,256]{1,0:T(8,128)(2,1)S(1)}, bf16[128,256]{1,0:T(8,128)(2,1)S(1)}, u32[]{:S(2)}, u32[]{:S(2)}) collective-permute-start(bf16[128,256]{1,0:T(8,128)(2,1)S(1)} %fusion.9), channel_id=1, source_target_pairs={{0,1},{1,0},{2,3},{3,2},{4,5},{5,4},{6,7},{7,6},{8,9},{9,8},{10,11... | collective-permute-start | bytes 196616 | tf_op jit(solution)/shard_map/ppermute | solution.py:302
  66.1 8.4 %collective-permute-start.22 = (bf16[128,256]{1,0:T(8,128)(2,1)S(1)}, bf16[128,256]{1,0:T(8,128)(2,1)S(1)}, u32[]{:S(2)}, u32[]{:S(2)}) collective-permute-start(bf16[128,256]{1,0:T(8,128)(2,1)S(1)} %get-tuple-element.60), channel_id=1, source_target_pairs={{0,2},{1,3},{2,0},{3,1},{4,6},{5,7},{6,4},{7,5},{8,10},{9,11},{10,... | collective-permute-start | bytes 196616 | tf_op jit(solution)/shard_map/ppermute | solution.py:302
  69.9 4.6 %collective-permute-start.23 = (bf16[128,256]{1,0:T(8,128)(2,1)S(1)}, bf16[128,256]{1,0:T(8,128)(2,1)S(1)}, u32[]{:S(2)}, u32[]{:S(2)}) collective-permute-start(bf16[128,256]{1,0:T(8,128)(2,1)S(1)} %get-tuple-element.61), channel_id=1, source_target_pairs={{0,8},{1,9},{2,10},{3,11},{4,12},{5,13},{6,14},{7,15},{8,0},{9,1},... | collective-permute-start | bytes 196616 | tf_op jit(solution)/shard_map/ppermute | solution.py:302
  70.5 4.3 %collective-permute-start.24 = (bf16[128,256]{1,0:T(8,128)(2,1)S(1)}, bf16[128,256]{1,0:T(8,128)(2,1)S(1)}, u32[]{:S(2)}, u32[]{:S(2)}) collective-permute-start(bf16[128,256]{1,0:T(8,128)(2,1)S(1)} %get-tuple-element.62), channel_id=1, source_target_pairs={{0,16},{1,17},{2,18},{3,19},{4,20},{5,21},{6,22},{7,23},{8,24},{9,... | collective-permute-start | bytes 196616 | tf_op jit(solution)/shard_map/ppermute | solution.py:302
  71.0 5.2 %collective-permute-start.25 = (bf16[128,256]{1,0:T(8,128)(2,1)S(1)}, bf16[128,256]{1,0:T(8,128)(2,1)S(1)}, u32[]{:S(2)}, u32[]{:S(2)}) collective-permute-start(bf16[128,256]{1,0:T(8,128)(2,1)S(1)} %get-tuple-element.63), channel_id=1, source_target_pairs={{0,24},{1,25},{2,26},{3,27},{4,28},{5,29},{6,30},{7,31},{8,16},{9,... | collective-permute-start | bytes 196616 | tf_op jit(solution)/shard_map/ppermute | solution.py:302
